TPU v7x, 512 devices: a whole 4x4x16 slice. The times are simulated.
512 devices in a mesh: dp: 64 (over z, x_hi, core), rep: 8 (over y, x_lo).
Axes of the slice: x: 4 (x_hi: 2, x_lo: 2; x = x_hi * 2 + x_lo), y: 4, z: 16, core: 2. Of those that a mesh axis runs over, the one named last changes fastest.
Arguments:
- grad_out: bfloat16 [49152, 2048], P('dp', 'rep'), may hold values from -16 to 16
- pre_act: bfloat16 [49152, 3072], P('dp', 'rep'), may hold values from -6 to 6
- up_weight: bfloat16 [3072, 2048], P('rep'), may hold values from -0.125 to 0.125
- down_weight: bfloat16 [2048, 3072], P(None, 'rep'), may hold values from -0.109375 to 0.109375
- slot_counts: int32 [64], P('dp'), may hold values from 384 to 768, as said below
Outputs:
- input_grad: bfloat16 [49152, 2048], P('dp')
- down_grad: float32 [2048, 3072], P('dp', 'rep')
Inputs may be any that keep to these rules, and one draw needn't show every extreme that they name: Row i * 768 + j is live exactly when j < slot_counts[i]; some index has all 768 slots live and some index exactly 384.
All inputs are finite; a program needn't handle non-finite values.
Results may differ from a plain program's by a relative error of at most 0.0049.
Values may be sent and summed in bfloat16 or wider, within the bound.
No kernel may reach another device: no remote copies, remote signals or barrier semaphores. Data moves between devices by JAX's collectives and lax.ppermute only.
A program may use at most 64 MiB of HBM per device.

v0:
```python
import jax
import jax.numpy as jnp
from jax import lax
from jax.sharding import Mesh
from jax.sharding import PartitionSpec as P

REP = ("rep_0", "rep_1")


def whole_of(array, axes, dim):
    if not axes:
        return array
    nearer = lax.all_gather(array, axes[-1], axis=dim, tiled=True)
    return whole_of(nearer, axes[:-1], dim)


def on_device(grad_out, pre_act, up_weight, down_weight, slot_counts):
    slot_rows = grad_out.shape[0]
    live_rows = (lax.iota(jnp.int32, slot_rows) < slot_counts[0])[:, None]
    grad_full = whole_of(grad_out, REP, 1)
    grad_live = jnp.where(live_rows, grad_full, jnp.zeros_like(grad_full))
    zero_pre = jnp.zeros_like(pre_act)
    hidden = jnp.where(live_rows, jnp.maximum(pre_act, zero_pre), zero_pre)
    data_ranks = lax.axis_size("dp")
    down_sum = lax.psum_scatter(
        lax.dot_general(
            grad_live, hidden, (((0,), (0,)), ((), ())), preferred_element_type=jnp.float32
        ),
        "dp",
        scatter_dimension=0,
        tiled=True,
    )
    down_grad = down_sum / data_ranks
    hidden_grad = jnp.dot(grad_live, down_weight, preferred_element_type=jnp.float32)
    pre_grad = jnp.where(pre_act > 0, hidden_grad, jnp.zeros_like(hidden_grad)).astype(jnp.bfloat16)
    partial_terms = jnp.dot(pre_grad, up_weight, preferred_element_type=jnp.float32)
    input_sum = lax.psum(partial_terms, REP)
    input_grad = input_sum.astype(jnp.bfloat16)
    return (input_grad, down_grad)


def solution(mesh):
    finer = Mesh(mesh.devices.reshape(mesh.shape["dp"], 4, 2), ("dp", "rep_0", "rep_1"))
    in_specs = (P("dp", REP), P("dp", REP), P(REP, None), P(None, REP), P("dp"))
    out_specs = (P("dp", None), P("dp", REP))
    return jax.shard_map(
        on_device, mesh=finer, in_specs=in_specs, out_specs=out_specs, check_vma=False
    )
```

profile of v0, /device:TPU:6, one launch (start us, length us, event | category | flops | bytes accessed | tf_op | source)
XLA Modules:
  0.0 349.7 jit_solution(8490427789314710554)
XLA Ops:
  7.2 0.0 copy-start
  7.2 0.0 all-gather.2.cloned.1.call-start
  7.2 12.8 %all_gather.6 = bf16[768,512]{1,0:T(8,128)(2,1)} all-gather(bf16[768,256]{1,0:T(8,128)(2,1)} %param.5), channel_id=1, replica_groups=mesh['dp'=64,'rep_0'=4,'rep_1'=2] {'rep_1'}, dimensions={1}, use_global_device_ids=true | all-gather | bytes 1179648 | tf_op jit(solution)/shard_map/all_gather | solution.py:13
  20.0 0.0 all-gather.2.cloned.1.call-update
  20.0 0.0 reduce-scatter.2.cloned.1.call-start
  20.7 51.5 %all-gather.2.cloned.1.call-done = bf16[768,2048]{1,0:T(8,128)(2,1)} async-done(((bf16[768,512]{1,0:T(8,128)(2,1)}), bf16[768,2048]{1,0:T(8,128)(2,1)}) %all-gather.2.cloned.1.call-update) | async-done | bytes 3145744 | tf_op jit(solution)/shard_map/all_gather | solution.py:13
  72.2 5.6 %fusion.1 = f32[2048,384]{1,0:T(8,128)} fusion(bf16[768,2048]{1,0:T(8,128)(2,1)} %all-gather.2.cloned.1.call-done, pred[768]{0:T(1024)(128)(4,1)S(1)} %iota_compare_fusion, bf16[768,384]{1,0:T(8,128)(2,1)} %param.6), kind=kOutput, calls=%fused_computation.3 | convolution fusion | flops 1210122240 | bytes 6882048 | tf_op jit(solution)/shard_map/dot_general | solution.py:26
  77.8 0.0 copy-start.1
  77.8 0.0 reduce-scatter.2.cloned.1.call-update
  77.8 0.0 copy-done
  77.8 1.4 copy-done.1
  79.2 8.1 %fusion.2 = f32[768,2048]{1,0:T(8,128)} fusion(bf16[384,2048]{1,0:T(8,128)(2,1)S(1)} %copy-done, bf16[2048,384]{1,0:T(8,128)(2,1)S(1)} %copy-done.1, bf16[768,2048]{1,0:T(8,128)(2,1)} %all-gather.2.cloned.1.call-done, pred[768]{0:T(1024)(128)(4,1)S(1)} %iota_compare_fusion, bf16[768,384]{1,0:T(8,128)(2,1)} %param.6), kind=kOutput, calls=%fused_computation.4 | convolution fusion | flops 2418376704 | bytes 13173504 | tf_op jit(solution)/shard_map/dot_general | solution.py:36
  87.3 254.1 %all-reduce.1 = bf16[768,2048]{1,0:T(8,128)(2,1)} all-reduce(f32[768,2048]{1,0:T(8,128)} %fusion.2), channel_id=1, replica_groups=mesh['dp'=64,'rep_0'=4,'rep_1'=2] {'rep_0','rep_1'}, use_global_device_ids=true, to_apply=%region_0.1 | all-reduce | flops 1572864 | bytes 9437184 | tf_op jit(solution)/shard_map/psum | solution.py:37
  341.4 0.0 reduce-scatter.2.cloned.1.call-done
  341.4 1.4 broadcast_multiply_fusion
  (1 shorter events, 0.0 us)
Async XLA Ops:
  7.2 70.7 %copy-start = (bf16[384,2048]{1,0:T(8,128)(2,1)S(1)}, bf16[384,2048]{1,0:T(8,128)(2,1)}, u32[]{:S(2)}) copy-start(bf16[384,2048]{1,0:T(8,128)(2,1)} %param.7) | copy-start | bytes 4718596
  7.2 65.0 %all-gather.2.cloned.1.call-start = ((), (), s32[]{:S(2)}) async-start(), calls=%async_computation.1 | async-start | bytes 3932160 | tf_op jit(solution)/shard_map/all_gather | solution.py:13
  20.0 321.4 %reduce-scatter.2.cloned.1.call-start = ((), (), s32[]{:S(2)}) async-start(), calls=%async_computation.2 | async-start | bytes 3194880 | tf_op jit(solution)/shard_map/reduce_scatter | solution.py:25
  77.8 1.4 copy-start.1
Sparse Core Ops, SparseCore 0:
  20.1 51.9 all-gather.1
  78.0 225.7 reduce-scatter.1
where the time goes:
time: 351 us; the launch traced here: 350 us
  blocking collectives  267 us (76%)
  waiting for transfers between devices  51.5 us (15%)
  between operations  14.7 us (4%)
  matrix products  13.7 us (4%)
    psum x1, blocking collectives, on_device(): input_sum = lax.psum(partial_terms, REP)  254 us
    all_gather x1, waiting for transfers between devices, whole_of(): nearer = lax.all_gather(array, axes[-1], axis=dim, tiled=True)  51.5 us
    all_gather x1, blocking collectives, whole_of(): nearer = lax.all_gather(array, axes[-1], axis=dim, tiled=True)  12.8 us
    dot_general x1, matrix products, on_device(): jnp.dot(pre_grad, up_weight, preferred_element_type=jnp.float32)  8.12 us
  transfers between devices with their start and end apart: 2, of which 1 were waited for; matrix products, arithmetic and copies ran while one was open for 2% of the time, Pallas kernels for 0%

commit v1 on v0

v1 whole, which is shorter than its diff:
```python
import jax
import jax.numpy as jnp
from jax import lax
from jax.sharding import Mesh
from jax.sharding import PartitionSpec as P

DP = ("z", "xh", "core")
REP = ("y", "xl")
PAIR = [(0, 1), (1, 0)]


def to_all(block, axes, ranks):
    copies = jnp.broadcast_to(block[None], (ranks, *block.shape))
    return lax.all_to_all(copies, axes, 0, 0, tiled=True)


def on_device(grad_out, pre_act, up_weight, down_weight, slot_counts):
    slot_rows, features = grad_out.shape
    hidden_units = pre_act.shape[1]
    reps = lax.axis_size(REP)
    data_ranks = lax.axis_size(DP)
    model_width = features * reps
    live_rows = (lax.iota(jnp.int32, slot_rows) < slot_counts[0])[:, None]
    grad_live = jnp.where(live_rows, grad_out, jnp.zeros_like(grad_out))
    zero_pre = jnp.zeros_like(pre_act)
    hidden = jnp.where(live_rows, jnp.maximum(pre_act, zero_pre), zero_pre)

    grads = to_all(grad_live, REP, reps)

    weights = down_weight.reshape(reps, features, hidden_units)
    hidden_grad = sum(
        jnp.dot(grads[j], weights[j], preferred_element_type=jnp.float32) for j in range(reps)
    )
    pre_grad = jnp.where(pre_act > 0, hidden_grad, 0.0).astype(jnp.bfloat16)
    terms = jnp.dot(pre_grad, up_weight, preferred_element_type=jnp.float32).astype(jnp.bfloat16)
    terms = lax.all_to_all(terms, REP, 0, 0, tiled=True)
    terms = terms.reshape(reps, slot_rows // reps, model_width)
    own_rows = jnp.sum(terms.astype(jnp.float32), axis=0).astype(jnp.bfloat16)
    input_grad = to_all(own_rows, REP, reps).reshape(slot_rows, model_width)

    down_terms = lax.dot_general(
        grads, hidden, (((1,), (0,)), ((), ())), preferred_element_type=jnp.float32
    ).astype(jnp.bfloat16)
    share = model_width // data_ranks
    down_terms = down_terms.reshape(data_ranks // 2, 2, share, hidden_units)
    core = lax.axis_index("core")
    kept = lax.dynamic_index_in_dim(down_terms, core, 1, keepdims=False)
    sent = lax.dynamic_index_in_dim(down_terms, 1 - core, 1, keepdims=False)
    came = lax.ppermute(sent, "core", PAIR)
    chip_terms = kept.astype(jnp.float32) + came.astype(jnp.float32)
    z_terms = chip_terms.reshape(-1, hidden_units)
    z_sum = lax.psum_scatter(z_terms, "z", scatter_dimension=0, tiled=True)
    z_sum = z_sum.reshape(2, share, hidden_units)
    xh = lax.axis_index("xh")
    kept = lax.dynamic_index_in_dim(z_sum, xh, 0, keepdims=False)
    sent = lax.dynamic_index_in_dim(z_sum, 1 - xh, 0, keepdims=False)
    down_grad = (kept + lax.ppermute(sent, "xh", PAIR)) / data_ranks
    return (input_grad, down_grad)


def solution(mesh):
    z_ranks = mesh.shape["dp"] // 4
    y_ranks = mesh.shape["rep"] // 2
    finer = Mesh(mesh.devices.reshape(z_ranks, 2, 2, y_ranks, 2), (*DP, *REP))
    in_specs = (P(DP, REP), P(DP, REP), P(REP, None), P(None, REP), P(DP))
    out_specs = (P(DP, None), P(DP, REP))
    return jax.shard_map(
        on_device, mesh=finer, in_specs=in_specs, out_specs=out_specs, check_vma=False
    )
```

time: 351 us -> 176 us (0.50)
  blocking collectives: 267 us -> 43 us
  waiting for transfers between devices: 51.5 us -> 72.5 us
  starting transfers between devices: 0.08 us -> 16.6 us
  local copies, waits for them, and re-layouts: 1.38 us -> 8.2 us
  other arithmetic: 1.43 us -> 7.57 us
    psum x1 -> x0, blocking collectives: 254 us -> none  [on_device(): input_sum = lax.psum(partial_terms, REP)]
    all_gather x1 -> x0, waiting for transfers between devices: 51.5 us -> none  [whole_of(): nearer = lax.all_gather(array, axes[-1], axis=dim, tiled=True)]
    all_to_all x0 -> x1, blocking collectives: none -> 43 us  [to_all(): return lax.all_to_all(copies, axes, 0, 0, tiled=True)]
    reduce_scatter x1, waiting for transfers between devices: 0.01 us -> 41.4 us  [on_device(): z_sum = lax.psum_scatter(z_terms, 'z', scatter_dimension=0, tiled=True)]
    all_to_all x0 -> x2, waiting for transfers between devices: none -> 24.3 us  [the longest x1 24.3 us: on_device(): terms = lax.all_to_all(terms, REP, 0, 0, tiled=True)]
    all_gather x1 -> x0, blocking collectives: 12.8 us -> none  [whole_of(): nearer = lax.all_gather(array, axes[-1], axis=dim, tiled=True)]
    all_to_all x0 -> x2, starting transfers between devices: none -> 11.4 us  [the longest x1 5.83 us: on_device(): terms = lax.all_to_all(terms, REP, 0, 0, tiled=True)]
    ppermute x0 -> x2, waiting for transfers between devices: none -> 6.79 us  [the longest x1 4.2 us: on_device(): down_grad = (kept + lax.ppermute(sent, 'xh', PAIR)) / data_ranks]
  transfers between devices with their start and end apart: 2 -> 5, of which waited for: 1 -> 4; matrix products, arithmetic and copies ran while one was open for 2% -> 8% of each run, Pallas kernels for 0% -> 0%
where the time goes in v1:
time: 176 us
  waiting for transfers between devices  72.5 us (41%)
  blocking collectives  43 us (24%)
  starting transfers between devices  16.6 us (9%)
  between operations  14.9 us (8%)
  matrix products  12.9 us (7%)
  local copies, waits for them, and re-layouts  8.2 us (5%)
  other arithmetic  7.57 us (4%)
    all_to_all x1, blocking collectives, to_all(): return lax.all_to_all(copies, axes, 0, 0, tiled=True)  43 us
    reduce_scatter x1, waiting for transfers between devices, on_device(): z_sum = lax.psum_scatter(z_terms, 'z', scatter_dimension=0, tiled=True)  41.4 us
    all_to_all x1, waiting for transfers between devices, on_device(): terms = lax.all_to_all(terms, REP, 0, 0, tiled=True)  24.3 us
    all_to_all x1, starting transfers between devices, on_device(): terms = lax.all_to_all(terms, REP, 0, 0, tiled=True)  5.83 us
    all_to_all x1, starting transfers between devices, to_all(): return lax.all_to_all(copies, axes, 0, 0, tiled=True)  5.56 us
    dot_general x1, matrix products, on_device(): jnp.dot(pre_grad, up_weight, preferred_element_type=jnp.float32)  5.21 us
    ppermute x1, waiting for transfers between devices, on_device(): down_grad = (kept + lax.ppermute(sent, 'xh', PAIR)) / data_ranks  4.2 us
    unnamed x7, local copies, waits for them, and re-layouts  3.99 us
  transfers between devices with their start and end apart: 5, of which 4 were waited for; matrix products, arithmetic and copies ran while one was open for 8% of the time, Pallas kernels for 0%

profile of v1, /device:TPU:6, one launch (start us, length us, event | category | flops | bytes accessed | tf_op | source)
XLA Modules:
  0.0 175.6 jit_solution(7372151911817153773)
XLA Ops:
  7.2 0.0 copy-start
  8.0 1.2 broadcast_select_fusion
  9.1 0.2 copy.7
  9.3 0.2 broadcast_in_dim.38
  9.5 0.0 copy-start.2
  9.5 43.0 %all_to_all.19 = bf16[8,768,256]{1,2,0:T(8,128)(2,1)S(1)} all-to-all(bf16[8,768,256]{1,2,0:T(8,128)(2,1)S(1)} %broadcast_in_dim.38), channel_id=1, replica_groups=mesh['z'=16,'xh'=2,'core'=2,'y'=4,'xl'=2] {'y','xl'}, dimensions={0} | all-to-all | bytes 6291456 | tf_op jit(solution)/shard_map/all_to_all | solution.py:14
  52.5 0.0 copy-done.2
  52.5 0.0 copy-start.1
  52.5 0.4 fusion.8
  52.9 0.4 convolution_add_fusion.6
  53.3 0.4 convolution_add_fusion.5
  53.7 0.4 convolution_add_fusion.4
  54.1 0.4 convolution_add_fusion.3
  54.5 0.4 convolution_add_fusion.2
  54.9 0.0 copy-done.1
  54.9 1.4 convolution_add_fusion.1
  56.4 0.0 copy-done
  56.4 5.2 %convolution_convert_fusion = bf16[768,2048]{1,0:T(8,128)(2,1)} fusion(bf16[384,2048]{1,0:T(8,128)(2,1)S(1)} %copy-done, f32[768,384]{1,0:T(8,128)} %convolution_add_fusion.1, bf16[768,384]{1,0:T(8,128)(2,1)} %param.6, bf16[8,768,256]{1,2,0:T(8,128)(2,1)} %copy-done.1, bf16[2048,384]{1,0:T(8,128)(2,1)S(1)} %copy-done.2), kind=kOutput, calls=%fused_computation | convolution fusion | flops 1361707008 | bytes 7077888 | tf_op jit(solution)/shard_map/dot_general | solution.py:35
  61.6 5.8 %all-to-all-start.1 = ((bf16[8,96,2048]{2,1,0:T(8,128)(2,1)}), bf16[8,96,2048]{2,1,0:T(8,128)(2,1)}, u32[]{:S(2)}, u32[]{:S(2)}) async-start(bf16[8,96,2048]{2,1,0:T(8,128)(2,1)} %bitcast.49), calls=%async_computation.1 | async-start | bytes 6291456 | tf_op jit(solution)/shard_map/all_to_all | solution.py:36
  67.4 0.0 reduce-scatter.2.cloned.1.call-start
  67.4 3.9 %convolution_convert_fusion.1 = bf16[8,256,384]{2,1,0:T(8,128)(2,1)S(1)} fusion(bf16[8,768,256]{1,2,0:T(8,128)(2,1)} %copy-done.1, bf16[768,384]{1,0:T(8,128)(2,1)} %param.6, pred[768]{0:T(1024)(128)(4,1)S(1)} %iota_compare_fusion), kind=kOutput, calls=%fused_computation.1 | convolution fusion | flops 1209335808 | bytes 5309184 | tf_op jit(solution)/shard_map/dot_general | solution.py:41
  71.3 1.0 dynamic-slice_bitcast_fusion
  72.3 1.9 %collective-permute-start = (bf16[32,32,384]{2,1,0:T(8,128)(2,1)}, bf16[32,32,384]{2,1,0:T(8,128)(2,1)}, u32[]{:S(2)}, u32[]{:S(2)}) collective-permute-start(bf16[32,32,384]{2,1,0:T(8,128)(2,1)} %dynamic-slice_bitcast_fusion), channel_id=1, source_target_pairs={{0,8},{8,0},{1,9},{9,1},{2,10},{10,2},{3,11},{11,3},{4,12},{12,4},... | collective-permute-start | bytes 2359304 | tf_op jit(solution)/shard_map/ppermute | solution.py:49
  74.2 2.6 %collective-permute-done = bf16[32,32,384]{2,1,0:T(8,128)(2,1)} collective-permute-done((bf16[32,32,384]{2,1,0:T(8,128)(2,1)}, bf16[32,32,384]{2,1,0:T(8,128)(2,1)}, u32[]{:S(2)}, u32[]{:S(2)}) %collective-permute-start) | collective-permute-done | bytes 786464 | tf_op jit(solution)/shard_map/ppermute | solution.py:49
  76.8 2.5 %convert_add_fusion = f32[32,32,384]{2,1,0:T(8,128)} fusion(bf16[32,32,384]{2,1,0:T(8,128)(2,1)} %collective-permute-done, bf16[32,2,32,384]{3,2,1,0:T(8,128)(2,1)S(1)} %bitcast.51, s32[]{:T(128)S(6)} %select_n.29), kind=kLoop, calls=%fused_computation.2 | loop fusion | flops 1179648 | bytes 3145732 | tf_op jit(solution)/shard_map/add | solution.py:50
  79.3 0.0 reduce-scatter.2.cloned.1.call-update
  79.3 24.3 %all-to-all-done.1 = bf16[8,96,2048]{2,1,0:T(8,128)(2,1)} async-done(((bf16[8,96,2048]{2,1,0:T(8,128)(2,1)}), bf16[8,96,2048]{2,1,0:T(8,128)(2,1)}, u32[]{:S(2)}, u32[]{:S(2)}) %all-to-all-start.1) | async-done | bytes 3145760 | tf_op jit(solution)/shard_map/all_to_all | solution.py:36
  103.6 2.5 %reduce_sum.12 = bf16[96,2048]{1,0:T(8,128)(2,1)S(1)} reduce(bf16[8,96,2048]{2,1,0:T(8,128)(2,1)} %all-to-all-done.1, bf16[]{:T(256)} %constant.28.clone.1), dimensions={0}, to_apply=%region_0.1 | reduce | flops 1376256 | bytes 3538946 | tf_op jit(solution)/shard_map/reduce_sum | solution.py:38
  106.1 2.1 %broadcast_in_dim.40 = bf16[8,96,2048]{2,1,0:T(8,128)(2,1)} broadcast(bf16[96,2048]{1,0:T(8,128)(2,1)S(1)} %reduce_sum.12), dimensions={1,2} | broadcast | bytes 3538944 | tf_op jit(solution)/shard_map/broadcast_in_dim | solution.py:13
  108.2 5.6 %all-to-all-start.2 = ((bf16[8,96,2048]{2,1,0:T(8,128)(2,1)}), bf16[8,96,2048]{2,1,0:T(8,128)(2,1)}, u32[]{:S(2)}, u32[]{:S(2)}) async-start(bf16[8,96,2048]{2,1,0:T(8,128)(2,1)} %broadcast_in_dim.40), calls=%async_computation.2 | async-start | bytes 6291456 | tf_op jit(solution)/shard_map/all_to_all | solution.py:14
  113.7 41.4 %reduce-scatter.2.cloned.1.call-done = f32[64,384]{1,0:T(8,128)} async-done(((f32[1024,384]{1,0:T(8,128)}), f32[64,384]{1,0:T(8,128)}) %reduce-scatter.2.cloned.1.call-update) | async-done | bytes 98320 | tf_op jit(solution)/shard_map/reduce_scatter | solution.py:52
  155.1 0.8 dynamic-slice_bitcast_fusion.1
  155.9 3.3 %collective-permute-start.1 = (f32[32,384]{1,0:T(8,128)S(1)}, f32[32,384]{1,0:T(8,128)S(1)}, u32[]{:S(2)}, u32[]{:S(2)}) collective-permute-start(f32[32,384]{1,0:T(8,128)S(1)} %dynamic-slice_bitcast_fusion.1), channel_id=1, source_target_pairs={{0,16},{16,0},{1,17},{17,1},{2,18},{18,2},{3,19},{19,3},{4,20},{20... | collective-permute-start | bytes 147464 | tf_op jit(solution)/shard_map/ppermute | solution.py:57
  159.2 4.2 %collective-permute-done.1 = f32[32,384]{1,0:T(8,128)S(1)} collective-permute-done((f32[32,384]{1,0:T(8,128)S(1)}, f32[32,384]{1,0:T(8,128)S(1)}, u32[]{:S(2)}, u32[]{:S(2)}) %collective-permute-start.1) | collective-permute-done | bytes 49184 | tf_op jit(solution)/shard_map/ppermute | solution.py:57
  163.4 1.4 fusion.20
  164.8 0.0 all-to-all-done.2
  164.8 4.0 %copy.10 = bf16[768,2048]{1,0:T(8,128)(2,1)} copy(bf16[768,2048]{1,0:T(8,128)(2,1)} %bitcast.10) | data formatting | bytes 6291456
  (1 shorter events, 0.0 us)
Async XLA Ops:
  7.2 49.2 %copy-start = (bf16[384,2048]{1,0:T(8,128)(2,1)S(1)}, bf16[384,2048]{1,0:T(8,128)(2,1)}, u32[]{:S(2)}) copy-start(bf16[384,2048]{1,0:T(8,128)(2,1)} %param.7) | copy-start | bytes 4718596
  9.5 43.0 %copy-start.2 = (bf16[2048,384]{1,0:T(8,128)(2,1)S(1)}, bf16[2048,384]{1,0:T(8,128)(2,1)}, u32[]{:S(2)}) copy-start(bf16[2048,384]{1,0:T(8,128)(2,1)} %param.8) | copy-start | bytes 4718596
  52.5 2.4 %copy-start.1 = (bf16[8,768,256]{1,2,0:T(8,128)(2,1)}, bf16[8,768,256]{1,2,0:T(8,128)(2,1)S(1)}, u32[]{:S(2)}) copy-start(bf16[8,768,256]{1,2,0:T(8,128)(2,1)S(1)} %all_to_all.19) | copy-start | bytes 9437188
  61.6 42.1 %all-to-all-start.1 = ((bf16[8,96,2048]{2,1,0:T(8,128)(2,1)}), bf16[8,96,2048]{2,1,0:T(8,128)(2,1)}, u32[]{:S(2)}, u32[]{:S(2)}) async-start(bf16[8,96,2048]{2,1,0:T(8,128)(2,1)} %bitcast.49), calls=%async_computation.1 | async-start | bytes 6291456 | tf_op jit(solution)/shard_map/all_to_all | solution.py:36
  67.4 87.7 %reduce-scatter.2.cloned.1.call-start = ((), (), s32[]{:S(2)}) async-start(), calls=%async_computation.4 | async-start | bytes 1671168 | tf_op jit(solution)/shard_map/reduce_scatter | solution.py:52
  72.3 4.5 %collective-permute-start = (bf16[32,32,384]{2,1,0:T(8,128)(2,1)}, bf16[32,32,384]{2,1,0:T(8,128)(2,1)}, u32[]{:S(2)}, u32[]{:S(2)}) collective-permute-start(bf16[32,32,384]{2,1,0:T(8,128)(2,1)} %dynamic-slice_bitcast_fusion), channel_id=1, source_target_pairs={{0,8},{8,0},{1,9},{9,1},{2,10},{10,2},{3,11},{11,3},{4,12},{12,4},... | collective-permute-start | bytes 2359304 | tf_op jit(solution)/shard_map/ppermute | solution.py:49
  108.2 56.6 %all-to-all-start.2 = ((bf16[8,96,2048]{2,1,0:T(8,128)(2,1)}), bf16[8,96,2048]{2,1,0:T(8,128)(2,1)}, u32[]{:S(2)}, u32[]{:S(2)}) async-start(bf16[8,96,2048]{2,1,0:T(8,128)(2,1)} %broadcast_in_dim.40), calls=%async_computation.2 | async-start | bytes 6291456 | tf_op jit(solution)/shard_map/all_to_all | solution.py:14
  155.9 7.5 %collective-permute-start.1 = (f32[32,384]{1,0:T(8,128)S(1)}, f32[32,384]{1,0:T(8,128)S(1)}, u32[]{:S(2)}, u32[]{:S(2)}) collective-permute-start(f32[32,384]{1,0:T(8,128)S(1)} %dynamic-slice_bitcast_fusion.1), channel_id=1, source_target_pairs={{0,16},{16,0},{1,17},{17,1},{2,18},{18,2},{3,19},{19,3},{4,20},{20... | collective-permute-start | bytes 147464 | tf_op jit(solution)/shard_map/ppermute | solution.py:57
Sparse Core Ops, SparseCore 0:
  79.4 75.5 reduce-scatter.1

commit v2 on v0

v2 whole, which is shorter than its diff:
```python
import jax
import jax.numpy as jnp
from jax import lax
from jax.experimental import pallas as pl
from jax.experimental.pallas import tpu as pltpu
from jax.sharding import Mesh
from jax.sharding import PartitionSpec as P

DP = ("z", "xh", "core")
REP = ("y", "xl")
RING = ("xh", "xl")
NEAR = [(0, 1), (1, 0)]
FAR = [(0, 3), (3, 0), (1, 2), (2, 1)]
ACROSS = [(0, 2), (2, 0), (1, 3), (3, 1)]
VMEM = pl.BlockSpec(memory_space=pltpu.VMEM)
SMEM = pl.BlockSpec(memory_space=pltpu.SMEM)
ANY = pl.BlockSpec(memory_space=pl.ANY)
LIMIT = 40 * 1024 * 1024


def dot(a, b):
    return jnp.dot(a, b, preferred_element_type=jnp.float32)


def terms_kernel(place, grads, pre_own, pre_far, down_own, down_mine, down_other, up_own, up_mine, up_other, terms):
    core = place[0]
    blocks, features = grads.shape[0], grads.shape[2]
    half = blocks // 2
    own = sum(dot(grads[j], down_own[j * features:(j + 1) * features, :]) for j in range(blocks))
    far = sum(
        dot(grads[core * half + j], down_mine[j * features:(j + 1) * features, :]) for j in range(half)
    ) + sum(
        dot(grads[(1 - core) * half + j], down_other[j * features:(j + 1) * features, :]) for j in range(half)
    )
    own = jnp.where(pre_own[...] > 0, own, 0.0).astype(jnp.bfloat16)
    far = jnp.where(pre_far[...] > 0, far, 0.0).astype(jnp.bfloat16)
    columns = up_mine.shape[1]
    for up_part, start in ((up_mine, core * columns), (up_other, (1 - core) * columns)):
        at = pl.ds(pl.multiple_of(start, columns), columns)
        terms[:, at] = (dot(own, up_own[:, at]) + dot(far, up_part[...])).astype(terms.dtype)


def down_kernel(place, grads, pre_own, pre_far, kept, sent):
    core, xh, xl, live = place[0], place[1], place[2], place[3]
    blocks, rows, features = grads.shape
    share = kept.shape[2]
    groups = features // (4 * share)
    at = lax.broadcasted_iota(jnp.int32, pre_own.shape, 0)
    part = rows // 4
    row = at + (at // part + xl) * part
    for t, pre in ((0, pre_own), (1, pre_far)):
        hidden = jnp.where(row < live, jnp.maximum(pre[...], 0), 0).astype(jnp.bfloat16)
        for j in range(blocks):
            block = lax.dot_general(
                grads[j], hidden, (((0,), (0,)), ((), ())), preferred_element_type=jnp.float32
            ).astype(kept.dtype)
            for g in range(groups):
                z = j * groups + g
                for h in range(2):
                    first = (g * 4 + h * 2) * share
                    kind = t * 2 + jnp.abs(xh - h)
                    low = block[first:first + share, :]
                    high = block[first + share:first + 2 * share, :]

                    @pl.when(core == 0)
                    def _():
                        kept[kind, z] = low
                        sent[kind, z] = high

                    @pl.when(core != 0)
                    def _():
                        kept[kind, z] = high
                        sent[kind, z] = low


def place_kernel(place, own, near, below, above, far_low, far_high, near_below, near_above, near_far, out, sems):
    y, xl = place[4], place[2]
    rows = own.shape[0]
    half = rows // 2
    ranks = out.shape[0] // (2 * rows)

    def start(dy, dx, offset):
        at = ((y + dy) % ranks) * 2 + (1 - xl if dx else xl)
        return pl.multiple_of(at * rows + offset, 16)

    copies = [
        (own, 0, 0, 0), (near, 0, 1, 0), (below, ranks - 1, 0, 0), (above, 1, 0, 0),
        (far_low, 2, 0, 0), (far_high, 2, 0, half),
        (near_below, ranks - 1, 1, 0), (near_above, 1, 1, 0), (near_far, 2, 1, 0),
    ]
    running = []
    for i, (block, dy, dx, offset) in enumerate(copies):
        copy = pltpu.make_async_copy(
            block, out.at[pl.ds(start(dy, dx, offset), block.shape[0])], sems.at[i]
        )
        copy.start()
        running.append(copy)
    for copy in running:
        copy.wait()


def own_part(array, index, axis):
    return lax.dynamic_index_in_dim(array, index, axis, keepdims=False)


def on_device(grad_out, pre_act, up_weight, down_weight, slot_counts):
    slot_rows, features = grad_out.shape
    hidden_units = pre_act.shape[1]
    ys, zs = lax.axis_size("y"), lax.axis_size("z")
    reps = 2 * ys
    width = features * reps
    rows = slot_rows // reps
    half_rows = slot_rows // 2
    core, xh, xl, y = (lax.axis_index(a) for a in ("core", "xh", "xl", "y"))
    place = jnp.stack([core, xh, xl, slot_counts[0], y]).astype(jnp.int32)
    bf16 = jnp.bfloat16

    def turn(by):
        return [(i, (i + by) % ys) for i in range(ys)]

    live_rows = (lax.iota(jnp.int32, slot_rows) < slot_counts[0])[:, None]
    grad_live = jnp.where(live_rows, grad_out, jnp.zeros_like(grad_out))
    by_set = grad_live.reshape(ys, 2, rows, features).transpose(1, 0, 2, 3).reshape(2, half_rows, features)
    grads = jnp.broadcast_to(by_set[None], (ys, 2, half_rows, features)).reshape(reps, half_rows, features)
    grads = lax.all_to_all(grads, REP, 0, 0, tiled=True)

    pre_sets = pre_act.reshape(ys, 2, rows, hidden_units)
    pre_own = own_part(pre_sets, xl, 1).reshape(half_rows, hidden_units)
    pre_far = lax.ppermute(own_part(pre_sets, 1 - xl, 1).reshape(half_rows, hidden_units), "xl", NEAR)

    down_mine = lax.ppermute(own_part(down_weight.reshape(2, width // 2, hidden_units), core, 0), RING, FAR)
    up_mine = lax.ppermute(
        lax.dynamic_slice_in_dim(up_weight, core * (width // 2), width // 2, 1), RING, FAR
    )
    down_other = lax.ppermute(down_mine, "core", NEAR)
    up_other = lax.ppermute(up_mine, "core", NEAR)

    terms = pl.pallas_call(
        terms_kernel,
        out_shape=jax.ShapeDtypeStruct((half_rows, width), bf16),
        in_specs=[SMEM] + [VMEM] * 9,
        out_specs=VMEM,
        compiler_params=pltpu.CompilerParams(vmem_limit_bytes=LIMIT),
        cost_estimate=pl.CostEstimate(
            flops=8 * half_rows * width * hidden_units, bytes_accessed=16 * width * hidden_units, transcendentals=0
        ),
        name="terms",
    )(place, grads, pre_own, pre_far, down_weight, down_mine, down_other, up_weight, up_mine, up_other)

    share = width // (4 * zs)
    laid_out = jax.ShapeDtypeStruct((4, zs, share, hidden_units), bf16)
    kept, sent = pl.pallas_call(
        down_kernel,
        out_shape=(laid_out, laid_out),
        in_specs=[SMEM] + [VMEM] * 3,
        out_specs=(VMEM, VMEM),
        compiler_params=pltpu.CompilerParams(vmem_limit_bytes=LIMIT),
        cost_estimate=pl.CostEstimate(
            flops=4 * half_rows * width * hidden_units, bytes_accessed=8 * width * hidden_units, transcendentals=0
        ),
        name="down_terms",
    )(place, grads, pre_own, pre_far)

    came = lax.all_to_all(terms.reshape(ys, rows, width), "y", 0, 0, tiled=True)
    f32 = jnp.float32
    own = sum(came[i].astype(f32) for i in range(ys)).astype(bf16)

    other = lax.ppermute(sent, "core", NEAR)
    chip = [(kept[k].astype(f32) + other[k].astype(f32)) for k in range(4)]
    ring = [
        lax.ppermute(chip[2].astype(bf16), "xl", NEAR),
        lax.ppermute(chip[1].astype(bf16), RING, ACROSS),
        lax.ppermute(chip[3].astype(bf16), RING, FAR),
    ]
    ring_sum = (chip[0] + sum(part.astype(f32) for part in ring)).astype(bf16)
    z_terms = lax.all_to_all(ring_sum, "z", 0, 0, tiled=True)
    down_grad = jnp.sum(z_terms.astype(f32), axis=0) / (4 * zs)

    near = lax.ppermute(own, "xl", NEAR)
    below = lax.ppermute(own, "y", turn(1))
    above = lax.ppermute(own, "y", turn(-1))
    far_low = lax.ppermute(below[:rows // 2], "y", turn(1))
    far_high = lax.ppermute(above[rows // 2:], "y", turn(-1))
    near_below = lax.ppermute(below, "xl", NEAR)
    near_above = lax.ppermute(above, "xl", NEAR)
    near_far = lax.ppermute(near, "y", turn(2))
    input_grad = pl.pallas_call(
        place_kernel,
        out_shape=jax.ShapeDtypeStruct((slot_rows, width), bf16),
        in_specs=[SMEM] + [ANY] * 9,
        out_specs=ANY,
        scratch_shapes=[pltpu.SemaphoreType.DMA((9,))],
        name="place",
    )(place, own, near, below, above, far_low, far_high, near_below, near_above, near_far)
    return (input_grad, down_grad)


def solution(mesh):
    zs = mesh.shape["dp"] // 4
    ys = mesh.shape["rep"] // 2
    finer = Mesh(mesh.devices.reshape(zs, 2, 2, ys, 2), (*DP, *REP))
    in_specs = (P(DP, REP), P(DP, REP), P(REP, None), P(None, REP), P(DP))
    out_specs = (P(DP, None), P(DP, REP))
    return jax.shard_map(
        on_device, mesh=finer, in_specs=in_specs, out_specs=out_specs, check_vma=False
    )
```

time: 351 us -> 251 us (0.72)
  blocking collectives: 267 us -> 0 us
  Pallas kernels: 0 us -> 111 us
  starting transfers between devices: 0.08 us -> 78.2 us
  matrix products: 13.7 us -> 0 us
  between operations: 14.7 us -> 1.61 us
  waiting for transfers between devices: 51.5 us -> 41.3 us
  local copies, waits for them, and re-layouts: 1.38 us -> 9.22 us
  other arithmetic: 1.43 us -> 5.61 us
    psum x1 -> x0, blocking collectives: 254 us -> none  [on_device(): input_sum = lax.psum(partial_terms, REP)]
    pallas_call x0 -> x3, Pallas kernels: none -> 111 us  [the longest x1 97.1 us: on_device(): pl.pallas_call(place_kernel, out_shape=jax.ShapeDtypeStruct((slot_rows, w...]
    ppermute x0 -> x17, starting transfers between devices: none -> 52.7 us  [the longest x1 5.43 us: on_device(): lax.ppermute(lax.dynamic_slice_in_dim(up_weight, core * (width // 2), wid...]
    all_gather x1 -> x0, waiting for transfers between devices: 51.5 us -> none  [whole_of(): nearer = lax.all_gather(array, axes[-1], axis=dim, tiled=True)]
    ppermute x0 -> x17, waiting for transfers between devices: none -> 41.3 us  [the longest x1 8.28 us: on_device(): lax.ppermute(own_part(pre_sets, 1 - xl, 1).reshape(half_rows, hidden_unit...]
    all_to_all x0 -> x3, starting transfers between devices: none -> 25.5 us  [the longest x1 15.2 us: on_device(): z_terms = lax.all_to_all(ring_sum, 'z', 0, 0, tiled=True)]
    dot_general x2 -> x0, matrix products: 13.7 us -> none  [the longest x1 8.12 us: on_device(): jnp.dot(pre_grad, up_weight, preferred_element_type=jnp.float32)]
    all_gather x1 -> x0, blocking collectives: 12.8 us -> none  [whole_of(): nearer = lax.all_gather(array, axes[-1], axis=dim, tiled=True)]
  transfers between devices with their start and end apart: 2 -> 20, of which waited for: 1 -> 11; matrix products, arithmetic and copies ran while one was open for 2% -> 4% of each run, Pallas kernels for 0% -> 45%
where the time goes in v2:
time: 251 us; the launch traced here: 247 us
  Pallas kernels  111 us (44%)
  starting transfers between devices  78.2 us (31%)
  waiting for transfers between devices  41.3 us (16%)
  local copies, waits for them, and re-layouts  9.22 us (4%)
  other arithmetic  5.61 us (2%)
    pallas_call x1, Pallas kernels, on_device(): pl.pallas_call(place_kernel, out_shape=jax.ShapeDtypeStruct((slot_rows, w...  97.1 us
    all_to_all x1, starting transfers between devices, on_device(): z_terms = lax.all_to_all(ring_sum, 'z', 0, 0, tiled=True)  15.2 us
    ppermute x1, waiting for transfers between devices, on_device(): lax.ppermute(own_part(pre_sets, 1 - xl, 1).reshape(half_rows, hidden_unit...  8.28 us
    pallas_call x1, Pallas kernels, on_device(): pl.pallas_call(down_kernel, out_shape=(laid_out, laid_out), in_specs=[SME...  7.93 us
    ppermute x1, waiting for transfers between devices, on_device(): lax.ppermute(chip[1].astype(bf16), RING, ACROSS)  7.35 us
    ppermute x1, waiting for transfers between devices, on_device(): lax.ppermute(chip[3].astype(bf16), RING, FAR)  6.4 us
    pallas_call x1, Pallas kernels, on_device(): pl.pallas_call(terms_kernel, out_shape=jax.ShapeDtypeStruct((half_rows, w...  6.08 us
    all_to_all x1, starting transfers between devices, on_device(): grads = lax.all_to_all(grads, REP, 0, 0, tiled=True)  5.93 us
  transfers between devices with their start and end apart: 20, of which 11 were waited for; matrix products, arithmetic and copies ran while one was open for 4% of the time, Pallas kernels for 45%

profile of v2, /device:TPU:6, one launch (start us, length us, event | category | flops | bytes accessed | tf_op | source)
XLA Modules:
  0.0 247.1 jit_solution(7711169015056555431)
XLA Ops:
  1.3 1.2 broadcast_select_fusion
  2.5 1.2 broadcast_in_dim.22
  3.7 5.9 %all-to-all-start = ((bf16[8,384,256]{2,1,0:T(8,128)(2,1)}), bf16[8,384,256]{2,1,0:T(8,128)(2,1)S(1)}, u32[]{:S(2)}, u32[]{:S(2)}) async-start(bf16[8,384,256]{2,1,0:T(8,128)(2,1)} %bitcast.8), calls=%async_computation | async-start | bytes 3145728 | tf_op jit(solution)/shard_map/all_to_all | solution.py:125
  9.7 2.2 constant_dynamic-slice_fusion
  11.9 5.4 %collective-permute-start.3 = (bf16[384,1024]{1,0:T(8,128)(2,1)}, bf16[384,1024]{1,0:T(8,128)(2,1)}, u32[]{:S(2)}, u32[]{:S(2)}) collective-permute-start(bf16[384,1024]{1,0:T(8,128)(2,1)} %constant_dynamic-slice_fusion), channel_id=1, source_target_pairs={{0,17},{17,0},{1,16},{16,1},{2,19},{19,2},{3,18},{18,3},{4,21},{21... | collective-permute-start | bytes 2359304 | tf_op jit(solution)/shard_map/ppermute | solution.py:132
  17.3 1.0 dynamic-slice_bitcast_fusion
  18.3 1.9 collective-permute-start.1
  20.2 1.8 constant_dynamic-slice_fusion.1
  22.1 3.2 %collective-permute-start = (bf16[384,384]{1,0:T(8,128)(2,1)}, bf16[384,384]{1,0:T(8,128)(2,1)}, u32[]{:S(2)}, u32[]{:S(2)}) collective-permute-start(bf16[384,384]{1,0:T(8,128)(2,1)} %bitcast.11), channel_id=1, source_target_pairs={{0,1},{1,0},{2,3},{3,2},{4,5},{5,4},{6,7},{7,6},{8,9},{9,8},{10,11... | collective-permute-start | bytes 884744 | tf_op jit(solution)/shard_map/ppermute | solution.py:129
  25.4 8.3 %collective-permute-done.pre_far = bf16[384,384]{1,0:T(8,128)(2,1)} collective-permute-done((bf16[384,384]{1,0:T(8,128)(2,1)}, bf16[384,384]{1,0:T(8,128)(2,1)}, u32[]{:S(2)}, u32[]{:S(2)}) %collective-permute-start) | collective-permute-done | bytes 294944 | tf_op jit(solution)/shard_map/ppermute | solution.py:129
  33.7 7.9 %down_terms.1 = (bf16[4,16,32,384]{3,2,1,0:T(8,128)(2,1)S(1)}, bf16[4,16,32,384]{3,2,1,0:T(8,128)(2,1)}) custom-call(s32[5]{0:T(128)S(1)} %stack.19.place, bf16[8,384,256]{2,1,0:T(8,128)(2,1)S(1)} %all-to-all-done.grads, bf16[384,384]{1,0:T(8,128)(2,1)S(1)} %bitcast.35, bf16[384,384]{1,0:T(8,128)(2,1)} %collective-permute-done.pre_far), custom_call_target="tpu_custom_call" | custom-call | flops 1207959552 | bytes 6291456 | tf_op jit(solution)/shard_map/down_terms/pallas_call | solution.py:152
  41.6 1.1 copy-done.2
  42.7 1.9 collective-permute-start.13
  44.7 2.4 collective-permute-start.4
  47.1 3.8 %collective-permute-done.1.down_mine = bf16[1024,384]{1,0:T(8,128)(2,1)} collective-permute-done((bf16[1024,384]{1,0:T(8,128)(2,1)}, bf16[1024,384]{1,0:T(8,128)(2,1)}, u32[]{:S(2)}, u32[]{:S(2)}) %collective-permute-start.1) | collective-permute-done | bytes 786464 | tf_op jit(solution)/shard_map/ppermute | solution.py:131
  50.8 1.9 collective-permute-start.2
  52.8 2.5 collective-permute-done.2.down_other
  55.2 6.1 %terms.1 = bf16[384,2048]{1,0:T(8,128)(2,1)} custom-call(s32[5]{0:T(128)S(1)} %stack.19.place, bf16[8,384,256]{2,1,0:T(8,128)(2,1)S(1)} %all-to-all-done.grads, bf16[384,384]{1,0:T(8,128)(2,1)S(1)} %bitcast.36, bf16[384,384]{1,0:T(8,128)(2,1)} %collective-permute-done.pre_far, bf16[2048,384]{1,0:T(8,128)(2,1)S(1)} %copy-done, ...), custom_call_target="tpu_custom_call" | custom-call | flops 2415919104 | bytes 12582912 | tf_op jit(solution)/shard_map/terms/pallas_call | solution.py:138
  61.3 4.4 %all-to-all-start.1 = ((bf16[4,96,2048]{2,1,0:T(8,128)(2,1)}), bf16[4,96,2048]{2,1,0:T(8,128)(2,1)S(1)}, u32[]{:S(2)}, u32[]{:S(2)}) async-start(bf16[4,96,2048]{2,1,0:T(8,128)(2,1)} %bitcast.14), calls=%async_computation.1 | async-start | bytes 3145728 | tf_op jit(solution)/shard_map/all_to_all | solution.py:164
  65.7 1.5 fusion.2
  67.2 1.9 collective-permute-start.14
  69.2 3.9 %collective-permute-start.15 = (bf16[16,32,384]{2,1,0:T(8,128)(2,1)S(1)}, bf16[16,32,384]{2,1,0:T(8,128)(2,1)S(1)}, u32[]{:S(2)}, u32[]{:S(2)}) collective-permute-start(bf16[16,32,384]{2,1,0:T(8,128)(2,1)S(1)} %get-tuple-element.8), channel_id=1, source_target_pairs={{0,16},{16,0},{1,17},{17,1},{2,18},{18,2},{3,19},{19,3},{4,20},{20... | collective-permute-start | bytes 1179656 | tf_op jit(solution)/shard_map/ppermute | solution.py:172
  73.0 4.6 %collective-permute-start.16 = (bf16[16,32,384]{2,1,0:T(8,128)(2,1)S(1)}, bf16[16,32,384]{2,1,0:T(8,128)(2,1)S(1)}, u32[]{:S(2)}, u32[]{:S(2)}) collective-permute-start(bf16[16,32,384]{2,1,0:T(8,128)(2,1)S(1)} %get-tuple-element.7), channel_id=1, source_target_pairs={{0,17},{17,0},{1,16},{16,1},{2,19},{19,2},{3,18},{18,3},{4,21},{21... | collective-permute-start | bytes 1179656 | tf_op jit(solution)/shard_map/ppermute | solution.py:173
  77.7 3.4 %collective-permute-done.14 = bf16[16,32,384]{2,1,0:T(8,128)(2,1)S(1)} collective-permute-done((bf16[16,32,384]{2,1,0:T(8,128)(2,1)S(1)}, bf16[16,32,384]{2,1,0:T(8,128)(2,1)S(1)}, u32[]{:S(2)}, u32[]{:S(2)}) %collective-permute-start.14) | collective-permute-done | bytes 393248 | tf_op jit(solution)/shard_map/ppermute | solution.py:171
  81.1 7.4 %collective-permute-done.15 = bf16[16,32,384]{2,1,0:T(8,128)(2,1)S(1)} collective-permute-done((bf16[16,32,384]{2,1,0:T(8,128)(2,1)S(1)}, bf16[16,32,384]{2,1,0:T(8,128)(2,1)S(1)}, u32[]{:S(2)}, u32[]{:S(2)}) %collective-permute-start.15) | collective-permute-done | bytes 393248 | tf_op jit(solution)/shard_map/ppermute | solution.py:172
  88.5 6.4 %collective-permute-done.16 = bf16[16,32,384]{2,1,0:T(8,128)(2,1)S(1)} collective-permute-done((bf16[16,32,384]{2,1,0:T(8,128)(2,1)S(1)}, bf16[16,32,384]{2,1,0:T(8,128)(2,1)S(1)}, u32[]{:S(2)}, u32[]{:S(2)}) %collective-permute-start.16) | collective-permute-done | bytes 393248 | tf_op jit(solution)/shard_map/ppermute | solution.py:173
  94.9 2.0 fusion
  96.9 15.2 %all-to-all-start.2 = ((bf16[16,32,384]{2,1,0:T(8,128)(2,1)}), bf16[16,32,384]{2,1,0:T(8,128)(2,1)S(1)}, u32[]{:S(2)}, u32[]{:S(2)}) async-start(bf16[16,32,384]{2,1,0:T(8,128)(2,1)} %fusion), calls=%async_computation.2 | async-start | bytes 786432 | tf_op jit(solution)/shard_map/all_to_all | solution.py:176
  112.1 0.2 fusion.1.own
  112.3 3.6 %collective-permute-start.6 = (bf16[96,2048]{1,0:T(8,128)(2,1)S(1)}, bf16[96,2048]{1,0:T(8,128)(2,1)S(1)}, u32[]{:S(2)}, u32[]{:S(2)}) collective-permute-start(bf16[96,2048]{1,0:T(8,128)(2,1)S(1)} %fusion.1.own), channel_id=1, source_target_pairs={{0,2},{2,4},{4,6},{6,0},{1,3},{3,5},{5,7},{7,1},{8,10},{10,12},{12... | collective-permute-start | bytes 1179656 | tf_op jit(solution)/shard_map/ppermute | solution.py:180
  116.0 3.4 %collective-permute-start.7 = (bf16[96,2048]{1,0:T(8,128)(2,1)S(1)}, bf16[96,2048]{1,0:T(8,128)(2,1)S(1)}, u32[]{:S(2)}, u32[]{:S(2)}) collective-permute-start(bf16[96,2048]{1,0:T(8,128)(2,1)S(1)} %fusion.1.own), channel_id=1, source_target_pairs={{0,6},{2,0},{4,2},{6,4},{1,7},{3,1},{5,3},{7,5},{8,14},{10,8},{12,... | collective-permute-start | bytes 1179656 | tf_op jit(solution)/shard_map/ppermute | solution.py:181
  119.4 1.9 collective-permute-start.5
  121.3 3.7 %collective-permute-done.6.below = bf16[96,2048]{1,0:T(8,128)(2,1)S(1)} collective-permute-done((bf16[96,2048]{1,0:T(8,128)(2,1)S(1)}, bf16[96,2048]{1,0:T(8,128)(2,1)S(1)}, u32[]{:S(2)}, u32[]{:S(2)}) %collective-permute-start.6) | collective-permute-done | bytes 393248 | tf_op jit(solution)/shard_map/ppermute | solution.py:180
  125.0 1.9 collective-permute-start.10
  126.9 0.2 collective-permute-done.7.above
  127.2 3.7 %collective-permute-start.11 = (bf16[96,2048]{1,0:T(8,128)(2,1)S(1)}, bf16[96,2048]{1,0:T(8,128)(2,1)S(1)}, u32[]{:S(2)}, u32[]{:S(2)}) collective-permute-start(bf16[96,2048]{1,0:T(8,128)(2,1)S(1)} %collective-permute-done.7.above), channel_id=1, source_target_pairs={{0,1},{1,0},{2,3},{3,2},{4,5},{5,4},{6,7},{7,6},{8,9},{9,8},{10,11... | collective-permute-start | bytes 1179656 | tf_op jit(solution)/shard_map/ppermute | solution.py:185
  130.9 2.5 collective-permute-done.5.near
  133.3 3.9 %collective-permute-start.12 = (bf16[96,2048]{1,0:T(8,128)(2,1)S(1)}, bf16[96,2048]{1,0:T(8,128)(2,1)S(1)}, u32[]{:S(2)}, u32[]{:S(2)}) collective-permute-start(bf16[96,2048]{1,0:T(8,128)(2,1)S(1)} %collective-permute-done.5.near), channel_id=1, source_target_pairs={{0,4},{2,6},{4,0},{6,2},{1,5},{3,7},{5,1},{7,3},{8,12},{10,14},{12... | collective-permute-start | bytes 1179656 | tf_op jit(solution)/shard_map/ppermute | solution.py:186
  137.3 2.5 %collective-permute-start.8 = (bf16[48,2048]{1,0:T(8,128)(2,1)S(1)}, bf16[48,2048]{1,0:T(8,128)(2,1)S(1)}, u32[]{:S(2)}, u32[]{:S(2)}) collective-permute-start(bf16[48,2048]{1,0:T(8,128)(2,1)S(1)} %slice.60), channel_id=1, source_target_pairs={{0,2},{2,4},{4,6},{6,0},{1,3},{3,5},{5,7},{7,1},{8,10},{10,12},{12... | collective-permute-start | bytes 589832 | tf_op jit(solution)/shard_map/ppermute | solution.py:182
  139.8 4.6 %collective-permute-start.9 = (bf16[48,2048]{1,0:T(8,128)(2,1)S(1)}, bf16[48,2048]{1,0:T(8,128)(2,1)S(1)}, u32[]{:S(2)}, u32[]{:S(2)}) collective-permute-start(bf16[48,2048]{1,0:T(8,128)(2,1)S(1)} %slice.61), channel_id=1, source_target_pairs={{0,6},{2,0},{4,2},{6,4},{1,7},{3,1},{5,3},{7,5},{8,14},{10,8},{12,... | collective-permute-start | bytes 589832 | tf_op jit(solution)/shard_map/ppermute | solution.py:183
  144.4 2.2 collective-permute-done.8.far_low
  146.6 0.9 collective-permute-done.9.far_high
  147.6 0.6 copy-done.13
  148.2 0.1 copy-done.9
  148.4 0.1 copy-done.10
  148.5 0.8 copy-done.11
  149.3 97.1 %place.1 = bf16[768,2048]{1,0:T(8,128)(2,1)} custom-call(s32[5]{0:T(128)} %copy-done.4, bf16[96,2048]{1,0:T(8,128)(2,1)} %copy-done.5, bf16[96,2048]{1,0:T(8,128)(2,1)} %copy-done.8, bf16[96,2048]{1,0:T(8,128)(2,1)} %copy-done.6, bf16[96,2048]{1,0:T(8,128)(2,1)} %copy-done.7, bf16[48,2048]{1,0:T(8,128)(2,1)} %copy-done.12, bf16[48,2048]{1,0:T(8,128)(2,1)} %copy-done.13, ...), custom_call_target="tpu_custom_call" | custom-call | tf_op jit(solution)/shard_map/place/pallas_call | solution.py:187
  246.5 0.6 broadcast_multiply_fusion
  (38 shorter events, 0.3 us)
Async XLA Ops:
  3.7 29.9 %all-to-all-start = ((bf16[8,384,256]{2,1,0:T(8,128)(2,1)}), bf16[8,384,256]{2,1,0:T(8,128)(2,1)S(1)}, u32[]{:S(2)}, u32[]{:S(2)}) async-start(bf16[8,384,256]{2,1,0:T(8,128)(2,1)} %bitcast.8), calls=%async_computation | async-start | bytes 3145728 | tf_op jit(solution)/shard_map/all_to_all | solution.py:125
  9.7 7.6 %copy-start = (bf16[2048,384]{1,0:T(8,128)(2,1)S(1)}, bf16[2048,384]{1,0:T(8,128)(2,1)}, u32[]{:S(2)}) copy-start(bf16[2048,384]{1,0:T(8,128)(2,1)} %down_own.1) | copy-start | bytes 4718596
  11.9 32.8 %collective-permute-start.3 = (bf16[384,1024]{1,0:T(8,128)(2,1)}, bf16[384,1024]{1,0:T(8,128)(2,1)}, u32[]{:S(2)}, u32[]{:S(2)}) collective-permute-start(bf16[384,1024]{1,0:T(8,128)(2,1)} %constant_dynamic-slice_fusion), channel_id=1, source_target_pairs={{0,17},{17,0},{1,16},{16,1},{2,19},{19,2},{3,18},{18,3},{4,21},{21... | collective-permute-start | bytes 2359304 | tf_op jit(solution)/shard_map/ppermute | solution.py:132
  18.3 32.5 %collective-permute-start.1 = (bf16[1024,384]{1,0:T(8,128)(2,1)}, bf16[1024,384]{1,0:T(8,128)(2,1)}, u32[]{:S(2)}, u32[]{:S(2)}) collective-permute-start(bf16[1024,384]{1,0:T(8,128)(2,1)} %dynamic-slice_bitcast_fusion), channel_id=1, source_target_pairs={{0,17},{17,0},{1,16},{16,1},{2,19},{19,2},{3,18},{18,3},{4,21},{21... | collective-permute-start | bytes 2359304 | tf_op jit(solution)/shard_map/ppermute | solution.py:131
  22.1 11.6 %collective-permute-start = (bf16[384,384]{1,0:T(8,128)(2,1)}, bf16[384,384]{1,0:T(8,128)(2,1)}, u32[]{:S(2)}, u32[]{:S(2)}) collective-permute-start(bf16[384,384]{1,0:T(8,128)(2,1)} %bitcast.11), channel_id=1, source_target_pairs={{0,1},{1,0},{2,3},{3,2},{4,5},{5,4},{6,7},{7,6},{8,9},{9,8},{10,11... | collective-permute-start | bytes 884744 | tf_op jit(solution)/shard_map/ppermute | solution.py:129
  25.4 29.9 %copy-start.4 = (s32[5]{0:T(128)}, s32[5]{0:T(128)S(1)}, u32[]{:S(2)}) copy-start(s32[5]{0:T(128)S(1)} %stack.19.place) | copy-start | bytes 64
  33.7 21.6 %copy-start.1 = (bf16[384,2048]{1,0:T(8,128)(2,1)S(1)}, bf16[384,2048]{1,0:T(8,128)(2,1)}, u32[]{:S(2)}) copy-start(bf16[384,2048]{1,0:T(8,128)(2,1)} %up_own.1) | copy-start | bytes 4718596
  41.6 1.1 copy-start.2
  42.7 22.9 %collective-permute-start.13 = (bf16[4,16,32,384]{3,2,1,0:T(8,128)(2,1)}, bf16[4,16,32,384]{3,2,1,0:T(8,128)(2,1)}, u32[]{:S(2)}, u32[]{:S(2)}) collective-permute-start(bf16[4,16,32,384]{3,2,1,0:T(8,128)(2,1)} %get-tuple-element.5), channel_id=1, source_target_pairs={{0,8},{8,0},{1,9},{9,1},{2,10},{10,2},{3,11},{11,3},{4,12},{12,4},... | collective-permute-start | bytes 4718600 | tf_op jit(solution)/shard_map/ppermute | solution.py:168
  44.7 8.1 %collective-permute-start.4 = (bf16[384,1024]{1,0:T(8,128)(2,1)}, bf16[384,1024]{1,0:T(8,128)(2,1)S(1)}, u32[]{:S(2)}, u32[]{:S(2)}) collective-permute-start(bf16[384,1024]{1,0:T(8,128)(2,1)} %collective-permute-done.3.up_mine), channel_id=1, source_target_pairs={{0,8},{8,0},{1,9},{9,1},{2,10},{10,2},{3,11},{11,3},{4,12},{12,4},... | collective-permute-start | bytes 2359304 | tf_op jit(solution)/shard_map/ppermute | solution.py:136
  50.8 4.4 %collective-permute-start.2 = (bf16[1024,384]{1,0:T(8,128)(2,1)}, bf16[1024,384]{1,0:T(8,128)(2,1)S(1)}, u32[]{:S(2)}, u32[]{:S(2)}) collective-permute-start(bf16[1024,384]{1,0:T(8,128)(2,1)} %collective-permute-done.1.down_mine), channel_id=1, source_target_pairs={{0,8},{8,0},{1,9},{9,1},{2,10},{10,2},{3,11},{11,3},{4,12},{12,4},... | collective-permute-start | bytes 2359304 | tf_op jit(solution)/shard_map/ppermute | solution.py:135
  61.3 4.4 %copy-start.3 = (bf16[4,16,32,384]{3,2,1,0:T(8,128)(2,1)S(1)}, bf16[4,16,32,384]{3,2,1,0:T(8,128)(2,1)}, u32[]{:S(2)}) copy-start(bf16[4,16,32,384]{3,2,1,0:T(8,128)(2,1)} %copy-done.2) | copy-start | bytes 4718596
  61.3 35.6 %all-to-all-start.1 = ((bf16[4,96,2048]{2,1,0:T(8,128)(2,1)}), bf16[4,96,2048]{2,1,0:T(8,128)(2,1)S(1)}, u32[]{:S(2)}, u32[]{:S(2)}) async-start(bf16[4,96,2048]{2,1,0:T(8,128)(2,1)} %bitcast.14), calls=%async_computation.1 | async-start | bytes 3145728 | tf_op jit(solution)/shard_map/all_to_all | solution.py:164
  67.2 13.9 %collective-permute-start.14 = (bf16[16,32,384]{2,1,0:T(8,128)(2,1)S(1)}, bf16[16,32,384]{2,1,0:T(8,128)(2,1)S(1)}, u32[]{:S(2)}, u32[]{:S(2)}) collective-permute-start(bf16[16,32,384]{2,1,0:T(8,128)(2,1)S(1)} %get-tuple-element.6), channel_id=1, source_target_pairs={{0,1},{1,0},{2,3},{3,2},{4,5},{5,4},{6,7},{7,6},{8,9},{9,8},{10,11... | collective-permute-start | bytes 1179656 | tf_op jit(solution)/shard_map/ppermute | solution.py:171
  69.2 19.3 %collective-permute-start.15 = (bf16[16,32,384]{2,1,0:T(8,128)(2,1)S(1)}, bf16[16,32,384]{2,1,0:T(8,128)(2,1)S(1)}, u32[]{:S(2)}, u32[]{:S(2)}) collective-permute-start(bf16[16,32,384]{2,1,0:T(8,128)(2,1)S(1)} %get-tuple-element.8), channel_id=1, source_target_pairs={{0,16},{16,0},{1,17},{17,1},{2,18},{18,2},{3,19},{19,3},{4,20},{20... | collective-permute-start | bytes 1179656 | tf_op jit(solution)/shard_map/ppermute | solution.py:172
  73.0 21.8 %collective-permute-start.16 = (bf16[16,32,384]{2,1,0:T(8,128)(2,1)S(1)}, bf16[16,32,384]{2,1,0:T(8,128)(2,1)S(1)}, u32[]{:S(2)}, u32[]{:S(2)}) collective-permute-start(bf16[16,32,384]{2,1,0:T(8,128)(2,1)S(1)} %get-tuple-element.7), channel_id=1, source_target_pairs={{0,17},{17,0},{1,16},{16,1},{2,19},{19,2},{3,18},{18,3},{4,21},{21... | collective-permute-start | bytes 1179656 | tf_op jit(solution)/shard_map/ppermute | solution.py:173
  96.9 149.5 %all-to-all-start.2 = ((bf16[16,32,384]{2,1,0:T(8,128)(2,1)}), bf16[16,32,384]{2,1,0:T(8,128)(2,1)S(1)}, u32[]{:S(2)}, u32[]{:S(2)}) async-start(bf16[16,32,384]{2,1,0:T(8,128)(2,1)} %fusion), calls=%async_computation.2 | async-start | bytes 786432 | tf_op jit(solution)/shard_map/all_to_all | solution.py:176
  112.3 35.3 %copy-start.5 = (bf16[96,2048]{1,0:T(8,128)(2,1)}, bf16[96,2048]{1,0:T(8,128)(2,1)S(1)}, u32[]{:S(2)}) copy-start(bf16[96,2048]{1,0:T(8,128)(2,1)S(1)} %fusion.1.own) | copy-start | bytes 1179652
  112.3 12.7 %collective-permute-start.6 = (bf16[96,2048]{1,0:T(8,128)(2,1)S(1)}, bf16[96,2048]{1,0:T(8,128)(2,1)S(1)}, u32[]{:S(2)}, u32[]{:S(2)}) collective-permute-start(bf16[96,2048]{1,0:T(8,128)(2,1)S(1)} %fusion.1.own), channel_id=1, source_target_pairs={{0,2},{2,4},{4,6},{6,0},{1,3},{3,5},{5,7},{7,1},{8,10},{10,12},{12... | collective-permute-start | bytes 1179656 | tf_op jit(solution)/shard_map/ppermute | solution.py:180
  116.0 11.2 %collective-permute-start.7 = (bf16[96,2048]{1,0:T(8,128)(2,1)S(1)}, bf16[96,2048]{1,0:T(8,128)(2,1)S(1)}, u32[]{:S(2)}, u32[]{:S(2)}) collective-permute-start(bf16[96,2048]{1,0:T(8,128)(2,1)S(1)} %fusion.1.own), channel_id=1, source_target_pairs={{0,6},{2,0},{4,2},{6,4},{1,7},{3,1},{5,3},{7,5},{8,14},{10,8},{12,... | collective-permute-start | bytes 1179656 | tf_op jit(solution)/shard_map/ppermute | solution.py:181
  119.4 13.9 %collective-permute-start.5 = (bf16[96,2048]{1,0:T(8,128)(2,1)S(1)}, bf16[96,2048]{1,0:T(8,128)(2,1)S(1)}, u32[]{:S(2)}, u32[]{:S(2)}) collective-permute-start(bf16[96,2048]{1,0:T(8,128)(2,1)S(1)} %fusion.1.own), channel_id=1, source_target_pairs={{0,1},{1,0},{2,3},{3,2},{4,5},{5,4},{6,7},{7,6},{8,9},{9,8},{10,11... | collective-permute-start | bytes 1179656 | tf_op jit(solution)/shard_map/ppermute | solution.py:179
  125.0 22.6 %copy-start.6 = (bf16[96,2048]{1,0:T(8,128)(2,1)}, bf16[96,2048]{1,0:T(8,128)(2,1)S(1)}, u32[]{:S(2)}) copy-start(bf16[96,2048]{1,0:T(8,128)(2,1)S(1)} %collective-permute-done.6.below) | copy-start | bytes 1179652
  125.0 22.5 %collective-permute-start.10 = (bf16[96,2048]{1,0:T(8,128)(2,1)S(1)}, bf16[96,2048]{1,0:T(8,128)(2,1)S(1)}, u32[]{:S(2)}, u32[]{:S(2)}) collective-permute-start(bf16[96,2048]{1,0:T(8,128)(2,1)S(1)} %collective-permute-done.6.below), channel_id=1, source_target_pairs={{0,1},{1,0},{2,3},{3,2},{4,5},{5,4},{6,7},{7,6},{8,9},{9,8},{10,11... | collective-permute-start | bytes 1179656 | tf_op jit(solution)/shard_map/ppermute | solution.py:184
  127.2 20.4 %copy-start.7 = (bf16[96,2048]{1,0:T(8,128)(2,1)}, bf16[96,2048]{1,0:T(8,128)(2,1)S(1)}, u32[]{:S(2)}) copy-start(bf16[96,2048]{1,0:T(8,128)(2,1)S(1)} %collective-permute-done.7.above) | copy-start | bytes 1179652
  127.2 20.4 %collective-permute-start.11 = (bf16[96,2048]{1,0:T(8,128)(2,1)S(1)}, bf16[96,2048]{1,0:T(8,128)(2,1)S(1)}, u32[]{:S(2)}, u32[]{:S(2)}) collective-permute-start(bf16[96,2048]{1,0:T(8,128)(2,1)S(1)} %collective-permute-done.7.above), channel_id=1, source_target_pairs={{0,1},{1,0},{2,3},{3,2},{4,5},{5,4},{6,7},{7,6},{8,9},{9,8},{10,11... | collective-permute-start | bytes 1179656 | tf_op jit(solution)/shard_map/ppermute | solution.py:185
  133.3 14.3 %copy-start.8 = (bf16[96,2048]{1,0:T(8,128)(2,1)}, bf16[96,2048]{1,0:T(8,128)(2,1)S(1)}, u32[]{:S(2)}) copy-start(bf16[96,2048]{1,0:T(8,128)(2,1)S(1)} %collective-permute-done.5.near) | copy-start | bytes 1179652
  133.3 14.2 %collective-permute-start.12 = (bf16[96,2048]{1,0:T(8,128)(2,1)S(1)}, bf16[96,2048]{1,0:T(8,128)(2,1)S(1)}, u32[]{:S(2)}, u32[]{:S(2)}) collective-permute-start(bf16[96,2048]{1,0:T(8,128)(2,1)S(1)} %collective-permute-done.5.near), channel_id=1, source_target_pairs={{0,4},{2,6},{4,0},{6,2},{1,5},{3,7},{5,1},{7,3},{8,12},{10,14},{12... | collective-permute-start | bytes 1179656 | tf_op jit(solution)/shard_map/ppermute | solution.py:186
  137.3 9.3 %collective-permute-start.8 = (bf16[48,2048]{1,0:T(8,128)(2,1)S(1)}, bf16[48,2048]{1,0:T(8,128)(2,1)S(1)}, u32[]{:S(2)}, u32[]{:S(2)}) collective-permute-start(bf16[48,2048]{1,0:T(8,128)(2,1)S(1)} %slice.60), channel_id=1, source_target_pairs={{0,2},{2,4},{4,6},{6,0},{1,3},{3,5},{5,7},{7,1},{8,10},{10,12},{12... | collective-permute-start | bytes 589832 | tf_op jit(solution)/shard_map/ppermute | solution.py:182
  139.8 7.8 %collective-permute-start.9 = (bf16[48,2048]{1,0:T(8,128)(2,1)S(1)}, bf16[48,2048]{1,0:T(8,128)(2,1)S(1)}, u32[]{:S(2)}, u32[]{:S(2)}) collective-permute-start(bf16[48,2048]{1,0:T(8,128)(2,1)S(1)} %slice.61), channel_id=1, source_target_pairs={{0,6},{2,0},{4,2},{6,4},{1,7},{3,1},{5,3},{7,5},{8,14},{10,8},{12,... | collective-permute-start | bytes 589832 | tf_op jit(solution)/shard_map/ppermute | solution.py:183
  146.6 1.0 copy-start.12
  147.6 0.7 copy-start.13
  147.6 0.8 copy-start.9
  147.6 0.9 copy-start.10
  148.5 0.8 copy-start.11

commit v3 on v2

v3 whole, which is shorter than its diff:
```python
import jax
import jax.numpy as jnp
from jax import lax
from jax.experimental import pallas as pl
from jax.experimental.pallas import tpu as pltpu
from jax.sharding import Mesh
from jax.sharding import PartitionSpec as P

DP = ("z", "xh", "core")
REP = ("y", "xl")
RING = ("xh", "xl")
NEAR = [(0, 1), (1, 0)]
FAR = [(0, 3), (3, 0), (1, 2), (2, 1)]
MIXED = [(i, i ^ 1 if i // 2 % 2 == 0 else i ^ 5) for i in range(8)]
ACROSS = [(0, 2), (2, 0), (1, 3), (3, 1)]
VMEM = pl.BlockSpec(memory_space=pltpu.VMEM)
SMEM = pl.BlockSpec(memory_space=pltpu.SMEM)
ANY = pl.BlockSpec(memory_space=pl.ANY)
LIMIT = 40 * 1024 * 1024


def dot(a, b):
    return jnp.dot(a, b, preferred_element_type=jnp.float32)


def own_kernel(grads, pre, down, out):
    blocks, _, features = grads.shape
    hidden = sum(dot(grads[j], down[j * features:(j + 1) * features, :]) for j in range(blocks))
    out[...] = jnp.where(pre[...] > 0, hidden, 0.0).astype(out.dtype)


def terms_kernel(place, grads, own, pre_far, down_mine, down_other, up_own, up_mine, up_other, terms, up_far):
    core = place[0]
    blocks, features = grads.shape[0], grads.shape[2]
    half = blocks // 2
    units = up_mine.shape[0]
    up_far[pl.ds(pl.multiple_of(core * units, 16), units), :] = up_mine[...]
    up_far[pl.ds(pl.multiple_of((1 - core) * units, 16), units), :] = up_other[...]
    far = sum(
        dot(grads[core * half + j], down_mine[j * features:(j + 1) * features, :]) for j in range(half)
    ) + sum(
        dot(grads[(1 - core) * half + j], down_other[j * features:(j + 1) * features, :]) for j in range(half)
    )
    far = jnp.where(pre_far[...] > 0, far, 0.0).astype(jnp.bfloat16)
    terms[...] = (dot(own[...], up_own[...]) + dot(far, up_far[...])).astype(terms.dtype)


def down_kernel(place, grads, pre_own, pre_far, kept, sent):
    core, xh, xl, live = place[0], place[1], place[2], place[3]
    blocks, rows, features = grads.shape
    units = pre_own.shape[1]
    share = kept.shape[2]
    groups = features // (4 * share)
    at = lax.broadcasted_iota(jnp.int32, pre_own.shape, 0)
    part = rows // 4
    row = at + (at // part + xl) * part
    hidden = jnp.concatenate(
        [jnp.where(row < live, jnp.maximum(pre[...], 0), 0).astype(jnp.bfloat16) for pre in (pre_own, pre_far)],
        axis=1,
    )
    for j in range(blocks):
        block = lax.dot_general(
            grads[j], hidden, (((0,), (0,)), ((), ())), preferred_element_type=jnp.float32
        ).astype(kept.dtype)
        for g in range(groups):
            z = j * groups + g
            for h in range(2):
                first = (g * 4 + h * 2) * share
                low = block[first:first + share, :]
                high = block[first + share:first + 2 * share, :]
                mine = jnp.where(core == 0, low, high)
                other = jnp.where(core == 0, high, low)
                for t in range(2):
                    kind = t * 2 + jnp.abs(xh - h)
                    kept[kind, z] = mine[:, t * units:(t + 1) * units]
                    sent[kind, z] = other[:, t * units:(t + 1) * units]


def put(place, blocks, out, sems):
    y, xl = place[4], place[2]
    rows = blocks[0][0].shape[0] if len(blocks[0]) == 3 else blocks[0][4]
    ranks = out.shape[0] // (2 * rows)
    running = []
    for i, (block, dy, dx, *rest) in enumerate(blocks):
        at = ((y + dy + ranks) % ranks) * 2 + (1 - xl if dx else xl)
        start = pl.multiple_of(at * rows, 16)
        source = block.at[pl.ds(rest[0], rows)] if rest else block
        copy = pltpu.make_async_copy(source, out.at[pl.ds(start, rows)], sems.at[i])
        copy.start()
        running.append(copy)
    for copy in running:
        copy.wait()


def first_kernel(place, own, near, below, above, out, sems):
    put(place, [(own, 0, 0), (near, 0, 1), (below, -1, 0), (above, 1, 0)], out, sems)


def last_kernel(place, partial, across, beside, out, sems):
    rows = across.shape[0] // 2
    put(
        place,
        [(across, 2, 0, 0, rows), (across, 2, 1, rows, rows), (beside, -1, 1, 0, rows), (beside, 1, 1, rows, rows)],
        out,
        sems,
    )


def own_part(array, index, axis):
    return lax.dynamic_index_in_dim(array, index, axis, keepdims=False)


def on_device(grad_out, pre_act, up_weight, down_weight, slot_counts):
    slot_rows, features = grad_out.shape
    hidden_units = pre_act.shape[1]
    ys, zs = lax.axis_size("y"), lax.axis_size("z")
    reps = 2 * ys
    width = features * reps
    rows = slot_rows // reps
    half_rows = slot_rows // 2
    core, xh, xl, y = (lax.axis_index(a) for a in ("core", "xh", "xl", "y"))
    place = jnp.stack([core, xh, xl, slot_counts[0], y]).astype(jnp.int32)
    bf16 = jnp.bfloat16

    def turn(by):
        return [(i, (i + by) % ys) for i in range(ys)]

    live_rows = (lax.iota(jnp.int32, slot_rows) < slot_counts[0])[:, None]
    grad_live = jnp.where(live_rows, grad_out, jnp.zeros_like(grad_out))
    by_set = grad_live.reshape(ys, 2, rows, features).transpose(1, 0, 2, 3).reshape(2, half_rows, features)
    grads = jnp.broadcast_to(by_set[None], (ys, 2, half_rows, features)).reshape(reps, half_rows, features)
    grads = lax.all_to_all(grads, REP, 0, 0, tiled=True)

    pre_sets = pre_act.reshape(ys, 2, rows, hidden_units)
    pre_own = own_part(pre_sets, xl, 1).reshape(half_rows, hidden_units)
    pre_far = lax.ppermute(own_part(pre_sets, 1 - xl, 1).reshape(half_rows, hidden_units), "xl", NEAR)

    down_mine = lax.ppermute(own_part(down_weight.reshape(2, width // 2, hidden_units), core, 0), RING, FAR)
    up_mine = lax.ppermute(
        own_part(up_weight.reshape(2, hidden_units // 2, width), core, 0), ("xh", "core", "xl"), MIXED
    )
    down_other = lax.ppermute(down_mine, "core", NEAR)
    up_other = lax.ppermute(up_mine, "core", NEAR)

    pre_grad = pl.pallas_call(
        own_kernel,
        out_shape=jax.ShapeDtypeStruct((half_rows, hidden_units), bf16),
        in_specs=[VMEM] * 3,
        out_specs=VMEM,
        compiler_params=pltpu.CompilerParams(vmem_limit_bytes=LIMIT),
        cost_estimate=pl.CostEstimate(
            flops=2 * half_rows * width * hidden_units, bytes_accessed=4 * width * hidden_units, transcendentals=0
        ),
        name="own_grad",
    )(grads, pre_own, down_weight)
    terms = pl.pallas_call(
        terms_kernel,
        out_shape=jax.ShapeDtypeStruct((half_rows, width), bf16),
        in_specs=[SMEM] + [VMEM] * 8,
        out_specs=VMEM,
        scratch_shapes=[pltpu.VMEM((hidden_units, width), bf16)],
        compiler_params=pltpu.CompilerParams(vmem_limit_bytes=LIMIT),
        cost_estimate=pl.CostEstimate(
            flops=6 * half_rows * width * hidden_units, bytes_accessed=12 * width * hidden_units, transcendentals=0
        ),
        name="terms",
    )(place, grads, pre_grad, pre_far, down_mine, down_other, up_weight, up_mine, up_other)

    share = width // (4 * zs)
    laid_out = jax.ShapeDtypeStruct((4, zs, share, hidden_units), bf16)
    kept, sent = pl.pallas_call(
        down_kernel,
        out_shape=(laid_out, laid_out),
        in_specs=[SMEM] + [VMEM] * 3,
        out_specs=(VMEM, VMEM),
        compiler_params=pltpu.CompilerParams(vmem_limit_bytes=LIMIT),
        cost_estimate=pl.CostEstimate(
            flops=4 * half_rows * width * hidden_units, bytes_accessed=8 * width * hidden_units, transcendentals=0
        ),
        name="down_terms",
    )(place, grads, pre_own, pre_far)

    f32 = jnp.float32
    came = lax.all_to_all(terms.reshape(ys, rows, width), "y", 0, 0, tiled=True)
    own = sum(came[i].astype(f32) for i in range(ys)).astype(bf16)

    other = lax.ppermute(sent, "core", NEAR)
    chip = [(kept[k].astype(f32) + other[k].astype(f32)) for k in range(4)]
    ring = [
        lax.ppermute(chip[2].astype(bf16), "xl", NEAR),
        lax.ppermute(chip[3].astype(bf16), RING, FAR),
        lax.ppermute(chip[1].astype(bf16), RING, ACROSS),
    ]

    near = lax.ppermute(own, "xl", NEAR)
    below = lax.ppermute(own, "y", turn(1))
    above = lax.ppermute(own, "y", turn(-1))

    own_chip, ring, _ = lax.optimization_barrier((chip[0].astype(bf16), ring, own))
    ring_sum = (own_chip.astype(f32) + sum(part.astype(f32) for part in ring)).astype(bf16)
    z_terms = lax.all_to_all(ring_sum, "z", 0, 0, tiled=True)
    down_grad = jnp.sum(z_terms.astype(f32), axis=0) / (4 * zs)

    across = lax.ppermute(jnp.concatenate([own, near]), "y", turn(2))
    beside = lax.ppermute(jnp.concatenate([below, above]), "xl", NEAR)
    whole = jax.ShapeDtypeStruct((slot_rows, width), bf16)
    params = pltpu.CompilerParams(vmem_limit_bytes=LIMIT)
    first = pl.pallas_call(
        first_kernel,
        out_shape=whole,
        in_specs=[SMEM] + [VMEM] * 4,
        out_specs=ANY,
        scratch_shapes=[pltpu.SemaphoreType.DMA((4,))],
        compiler_params=params,
        name="place_first",
    )(place, own, near, below, above)
    input_grad = pl.pallas_call(
        last_kernel,
        out_shape=whole,
        in_specs=[SMEM, ANY] + [VMEM] * 2,
        out_specs=ANY,
        scratch_shapes=[pltpu.SemaphoreType.DMA((4,))],
        input_output_aliases={1: 0},
        compiler_params=params,
        name="place_last",
    )(place, first, across, beside)
    return (input_grad, down_grad)


def solution(mesh):
    zs = mesh.shape["dp"] // 4
    ys = mesh.shape["rep"] // 2
    finer = Mesh(mesh.devices.reshape(zs, 2, 2, ys, 2), (*DP, *REP))
    in_specs = (P(DP, REP), P(DP, REP), P(REP, None), P(None, REP), P(DP))
    out_specs = (P(DP, None), P(DP, REP))
    return jax.shard_map(
        on_device, mesh=finer, in_specs=in_specs, out_specs=out_specs, check_vma=False
    )
```

time: 251 us -> 143 us (0.57); the launches traced: 247 us -> 142 us
  Pallas kernels: 111 us -> 14.1 us
  starting transfers between devices: 78.2 us -> 72.5 us
  local copies, waits for them, and re-layouts: 9.22 us -> 6.36 us
    pallas_call x1 -> x3, Pallas kernels: 97.1 us -> 4.41 us  [the longest x1 1.72 us: on_device(): pl.pallas_call(first_kernel, out_shape=whole, in_specs=[SMEM] + [VMEM] *...]
    ppermute x6 -> x3, starting transfers between devices: 22 us -> 10.9 us  [the longest x1 5.01 us: on_device(): across = lax.ppermute(jnp.concatenate([own, near]), 'y', turn(2))]
    ppermute x6 -> x3, waiting for transfers between devices: 3.17 us -> 13.6 us  [the longest x1 7.68 us: on_device(): beside = lax.ppermute(jnp.concatenate([below, above]), 'xl', NEAR)]
    all_to_all x1, waiting for transfers between devices: 0.01 us -> 8.89 us  [on_device(): came = lax.all_to_all(terms.reshape(ys, rows, width), 'y', 0, 0, tiled=True)]
    ppermute x1, waiting for transfers between devices: 8.28 us -> 0.01 us  [on_device(): lax.ppermute(own_part(pre_sets, 1 - xl, 1).reshape(half_rows, hidden_unit...]
    ppermute x1, waiting for transfers between devices: 7.35 us -> 0.01 us  [on_device(): lax.ppermute(chip[1].astype(bf16), RING, ACROSS)]
    ppermute x1, waiting for transfers between devices: 6.4 us -> 0.01 us  [on_device(): lax.ppermute(chip[3].astype(bf16), RING, FAR)]
    ppermute x1, waiting for transfers between devices: 3.76 us -> 10 us  [on_device(): lax.ppermute(own_part(down_weight.reshape(2, width // 2, hidden_units), c...]
  transfers between devices with their start and end apart: 20 -> 17, of which waited for: 11 -> 6; matrix products, arithmetic and copies ran while one was open for 4% -> 6% of each run, Pallas kernels for 45% -> 10%
where the time goes in v3:
time: 143 us; the launch traced here: 142 us
  starting transfers between devices  72.5 us (51%)
  waiting for transfers between devices  40.6 us (28%)
  Pallas kernels  14.1 us (10%)
  other arithmetic  6.91 us (5%)
  local copies, waits for them, and re-layouts  6.36 us (4%)
  between operations  1.57 us (1%)
    all_to_all x1, starting transfers between devices, on_device(): z_terms = lax.all_to_all(ring_sum, 'z', 0, 0, tiled=True)  15.2 us
    ppermute x1, waiting for transfers between devices, on_device(): lax.ppermute(own_part(down_weight.reshape(2, width // 2, hidden_units), c...  10 us
    all_to_all x1, waiting for transfers between devices, on_device(): came = lax.all_to_all(terms.reshape(ys, rows, width), 'y', 0, 0, tiled=True)  8.89 us
    ppermute x1, waiting for transfers between devices, on_device(): near = lax.ppermute(own, 'xl', NEAR)  8.01 us
    ppermute x1, waiting for transfers between devices, on_device(): beside = lax.ppermute(jnp.concatenate([below, above]), 'xl', NEAR)  7.68 us
    all_to_all x1, starting transfers between devices, on_device(): grads = lax.all_to_all(grads, REP, 0, 0, tiled=True)  6.06 us
    pallas_call x1, Pallas kernels, on_device(): pl.pallas_call(terms_kernel, out_shape=jax.ShapeDtypeStruct((half_rows, w...  5.72 us
    ppermute x1, starting transfers between devices, on_device(): lax.ppermute(own_part(down_weight.reshape(2, width // 2, hidden_units), c...  5.44 us
  transfers between devices with their start and end apart: 17, of which 6 were waited for; matrix products, arithmetic and copies ran while one was open for 6% of the time, Pallas kernels for 10%

profile of v3, /device:TPU:6, one launch (start us, length us, event | category | flops | bytes accessed | tf_op | source)
XLA Modules:
  0.0 142.1 jit_solution(5531710050079980401)
XLA Ops:
  1.3 1.2 broadcast_select_fusion
  2.5 1.2 broadcast_in_dim.22
  3.7 6.1 %all-to-all-start = ((bf16[8,384,256]{2,1,0:T(8,128)(2,1)}), bf16[8,384,256]{2,1,0:T(8,128)(2,1)S(1)}, u32[]{:S(2)}, u32[]{:S(2)}) async-start(bf16[8,384,256]{2,1,0:T(8,128)(2,1)} %bitcast.39), calls=%async_computation | async-start | bytes 3145728 | tf_op jit(solution)/shard_map/all_to_all | solution.py:132
  9.8 1.0 dynamic-slice_bitcast_fusion.1
  10.8 5.4 %collective-permute-start.1 = (bf16[1024,384]{1,0:T(8,128)(2,1)}, bf16[1024,384]{1,0:T(8,128)(2,1)}, u32[]{:S(2)}, u32[]{:S(2)}) collective-permute-start(bf16[1024,384]{1,0:T(8,128)(2,1)} %dynamic-slice_bitcast_fusion.1), channel_id=1, source_target_pairs={{0,17},{17,0},{1,16},{16,1},{2,19},{19,2},{3,18},{18,3},{4,21},{21... | collective-permute-start | bytes 2359304 | tf_op jit(solution)/shard_map/ppermute | solution.py:138
  16.2 1.0 dynamic-slice_bitcast_fusion
  17.2 3.2 %collective-permute-start.3 = (bf16[192,2048]{1,0:T(8,128)(2,1)}, bf16[192,2048]{1,0:T(8,128)(2,1)}, u32[]{:S(2)}, u32[]{:S(2)}) collective-permute-start(bf16[192,2048]{1,0:T(8,128)(2,1)} %dynamic-slice_bitcast_fusion), channel_id=1, source_target_pairs={{0,1},{1,0},{8,25},{9,24},{16,17},{17,16},{24,9},{25,8},{2,3},{3,2... | collective-permute-start | bytes 2359304 | tf_op jit(solution)/shard_map/ppermute | solution.py:139
  20.4 1.8 %constant_dynamic-slice_fusion = (bf16[4,1,96,384]{3,2,1,0:T(8,128)(2,1)}, bf16[4,1,96,384]{3,2,1,0:T(8,128)(2,1)S(1)}) fusion(bf16[4,2,96,384]{3,2,1,0:T(8,128)(2,1)} %bitcast.42, s32[]{:T(128)S(6)} %select_n.19, s32[]{:T(128)S(6)} %select_n.18), kind=kLoop, calls=%fused_computation.19 | loop fusion | bytes 1179656 | tf_op jit(solution)/shard_map/jit(dynamic_index_in_dim)/dynamic_slice | solution.py:110
  22.3 2.6 %collective-permute-start = (bf16[384,384]{1,0:T(8,128)(2,1)}, bf16[384,384]{1,0:T(8,128)(2,1)}, u32[]{:S(2)}, u32[]{:S(2)}) collective-permute-start(bf16[384,384]{1,0:T(8,128)(2,1)} %bitcast.11), channel_id=1, source_target_pairs={{0,1},{1,0},{2,3},{3,2},{4,5},{5,4},{6,7},{7,6},{8,9},{9,8},{10,11... | collective-permute-start | bytes 884744 | tf_op jit(solution)/shard_map/ppermute | solution.py:136
  24.9 10.0 %collective-permute-done.1.down_mine = bf16[1024,384]{1,0:T(8,128)(2,1)} collective-permute-done((bf16[1024,384]{1,0:T(8,128)(2,1)}, bf16[1024,384]{1,0:T(8,128)(2,1)}, u32[]{:S(2)}, u32[]{:S(2)}) %collective-permute-start.1) | collective-permute-done | bytes 786464 | tf_op jit(solution)/shard_map/ppermute | solution.py:138
  35.0 1.9 %collective-permute-start.2 = (bf16[1024,384]{1,0:T(8,128)(2,1)}, bf16[1024,384]{1,0:T(8,128)(2,1)}, u32[]{:S(2)}, u32[]{:S(2)}) collective-permute-start(bf16[1024,384]{1,0:T(8,128)(2,1)} %collective-permute-done.1.down_mine), channel_id=1, source_target_pairs={{0,8},{8,0},{1,9},{9,1},{2,10},{10,2},{3,11},{11,3},{4,12},{12,4},... | collective-permute-start | bytes 2359304 | tf_op jit(solution)/shard_map/ppermute | solution.py:142
  36.9 2.2 %collective-permute-done.3.up_mine = bf16[192,2048]{1,0:T(8,128)(2,1)} collective-permute-done((bf16[192,2048]{1,0:T(8,128)(2,1)}, bf16[192,2048]{1,0:T(8,128)(2,1)}, u32[]{:S(2)}, u32[]{:S(2)}) %collective-permute-start.3) | collective-permute-done | bytes 786464 | tf_op jit(solution)/shard_map/ppermute | solution.py:139
  39.1 4.0 %collective-permute-start.4 = (bf16[192,2048]{1,0:T(8,128)(2,1)}, bf16[192,2048]{1,0:T(8,128)(2,1)}, u32[]{:S(2)}, u32[]{:S(2)}) collective-permute-start(bf16[192,2048]{1,0:T(8,128)(2,1)} %collective-permute-done.3.up_mine), channel_id=1, source_target_pairs={{0,8},{8,0},{1,9},{9,1},{2,10},{10,2},{3,11},{11,3},{4,12},{12,4},... | collective-permute-start | bytes 2359304 | tf_op jit(solution)/shard_map/ppermute | solution.py:143
  43.1 0.1 stack.19.place
  43.1 4.0 %down_terms.1 = (bf16[4,16,32,384]{3,2,1,0:T(8,128)(2,1)S(1)}, bf16[4,16,32,384]{3,2,1,0:T(8,128)(2,1)}) custom-call(s32[5]{0:T(128)S(1)} %stack.19.place, bf16[8,384,256]{2,1,0:T(8,128)(2,1)S(1)} %all-to-all-done.grads, bf16[384,384]{1,0:T(8,128)(2,1)S(1)} %bitcast.37, bf16[384,384]{1,0:T(8,128)(2,1)} %collective-permute-done.pre_far), custom_call_target="tpu_custom_call" | custom-call | flops 1207959552 | bytes 6291456 | tf_op jit(solution)/shard_map/down_terms/pallas_call | solution.py:171
  47.2 1.2 copy-done.3
  48.3 2.0 %collective-permute-start.10 = (bf16[4,16,32,384]{3,2,1,0:T(8,128)(2,1)}, bf16[4,16,32,384]{3,2,1,0:T(8,128)(2,1)}, u32[]{:S(2)}, u32[]{:S(2)}) collective-permute-start(bf16[4,16,32,384]{3,2,1,0:T(8,128)(2,1)} %get-tuple-element.9), channel_id=1, source_target_pairs={{0,8},{8,0},{1,9},{9,1},{2,10},{10,2},{3,11},{11,3},{4,12},{12,4},... | collective-permute-start | bytes 4718600 | tf_op jit(solution)/shard_map/ppermute | solution.py:187
  50.4 1.0 own_grad.1.own
  51.4 0.0 collective-permute-done.2.down_other
  51.4 5.7 %terms.1 = bf16[384,2048]{1,0:T(8,128)(2,1)} custom-call(s32[5]{0:T(128)S(1)} %stack.19.place, bf16[8,384,256]{2,1,0:T(8,128)(2,1)S(1)} %all-to-all-done.grads, bf16[384,384]{1,0:T(8,128)(2,1)S(1)} %own_grad.1.own, bf16[384,384]{1,0:T(8,128)(2,1)} %collective-permute-done.pre_far, bf16[1024,384]{1,0:T(8,128)(2,1)} %collective-permute-done.1.down_mine, ...), custom_call_target="tpu_custom_call" | custom-call | flops 1811939328 | bytes 9437184 | tf_op jit(solution)/shard_map/terms/pallas_call | solution.py:156
  57.1 4.4 %all-to-all-start.1 = ((bf16[4,96,2048]{2,1,0:T(8,128)(2,1)}), bf16[4,96,2048]{2,1,0:T(8,128)(2,1)S(1)}, u32[]{:S(2)}, u32[]{:S(2)}) async-start(bf16[4,96,2048]{2,1,0:T(8,128)(2,1)} %bitcast.16), calls=%async_computation.1 | async-start | bytes 3145728 | tf_op jit(solution)/shard_map/all_to_all | solution.py:184
  61.5 0.0 collective-permute-done.10
  61.5 2.6 %fusion.4 = (bf16[16,32,384]{2,1,0:T(8,128)(2,1)}, bf16[16,32,384]{2,1,0:T(8,128)(2,1)}, bf16[16,32,384]{2,1,0:T(8,128)(2,1)}, bf16[16,32,384]{2,1,0:T(8,128)(2,1)S(1)}) fusion(bf16[4,16,32,384]{3,2,1,0:T(8,128)(2,1)} %collective-permute-done.10, bf16[4,16,32,384]{3,2,1,0:T(8,128)(2,1)S(1)} %copy-done.4), kind=kLoop, calls=%fused_computation.15 | loop fusion | flops 3145728 | bytes 4718592 | tf_op jit(solution)/shard_map/convert_element_type | solution.py:192
  64.1 3.1 %collective-permute-start.11 = (bf16[16,32,384]{2,1,0:T(8,128)(2,1)}, bf16[16,32,384]{2,1,0:T(8,128)(2,1)S(1)}, u32[]{:S(2)}, u32[]{:S(2)}) collective-permute-start(bf16[16,32,384]{2,1,0:T(8,128)(2,1)} %get-tuple-element.16), channel_id=1, source_target_pairs={{0,1},{1,0},{2,3},{3,2},{4,5},{5,4},{6,7},{7,6},{8,9},{9,8},{10,11... | collective-permute-start | bytes 1179656 | tf_op jit(solution)/shard_map/ppermute | solution.py:190
  67.2 2.0 %collective-permute-start.12 = (bf16[16,32,384]{2,1,0:T(8,128)(2,1)}, bf16[16,32,384]{2,1,0:T(8,128)(2,1)}, u32[]{:S(2)}, u32[]{:S(2)}) collective-permute-start(bf16[16,32,384]{2,1,0:T(8,128)(2,1)} %get-tuple-element.15), channel_id=1, source_target_pairs={{0,17},{17,0},{1,16},{16,1},{2,19},{19,2},{3,18},{18,3},{4,21},{21... | collective-permute-start | bytes 1179656 | tf_op jit(solution)/shard_map/ppermute | solution.py:191
  69.3 4.7 %collective-permute-start.13 = (bf16[16,32,384]{2,1,0:T(8,128)(2,1)}, bf16[16,32,384]{2,1,0:T(8,128)(2,1)}, u32[]{:S(2)}, u32[]{:S(2)}) collective-permute-start(bf16[16,32,384]{2,1,0:T(8,128)(2,1)} %get-tuple-element.14), channel_id=1, source_target_pairs={{0,16},{16,0},{1,17},{17,1},{2,18},{18,2},{3,19},{19,3},{4,20},{20... | collective-permute-start | bytes 1179656 | tf_op jit(solution)/shard_map/ppermute | solution.py:192
  74.0 8.9 %all-to-all-done.1 = bf16[4,96,2048]{2,1,0:T(8,128)(2,1)S(1)} async-done(((bf16[4,96,2048]{2,1,0:T(8,128)(2,1)}), bf16[4,96,2048]{2,1,0:T(8,128)(2,1)S(1)}, u32[]{:S(2)}, u32[]{:S(2)}) %all-to-all-start.1) | async-done | bytes 1572896 | tf_op jit(solution)/shard_map/all_to_all | solution.py:184
  82.9 0.2 fusion.own
  83.1 2.5 %collective-permute-start.6 = (bf16[96,2048]{1,0:T(8,128)(2,1)S(1)}, bf16[96,2048]{1,0:T(8,128)(2,1)S(1)}, u32[]{:S(2)}, u32[]{:S(2)}) collective-permute-start(bf16[96,2048]{1,0:T(8,128)(2,1)S(1)} %fusion.own), channel_id=1, source_target_pairs={{0,2},{2,4},{4,6},{6,0},{1,3},{3,5},{5,7},{7,1},{8,10},{10,12},{12... | collective-permute-start | bytes 1179656 | tf_op jit(solution)/shard_map/ppermute | solution.py:196
  85.6 4.6 %collective-permute-start.7 = (bf16[96,2048]{1,0:T(8,128)(2,1)S(1)}, bf16[96,2048]{1,0:T(8,128)(2,1)S(1)}, u32[]{:S(2)}, u32[]{:S(2)}) collective-permute-start(bf16[96,2048]{1,0:T(8,128)(2,1)S(1)} %fusion.own), channel_id=1, source_target_pairs={{0,6},{2,0},{4,2},{6,4},{1,7},{3,1},{5,3},{7,5},{8,14},{10,8},{12,... | collective-permute-start | bytes 1179656 | tf_op jit(solution)/shard_map/ppermute | solution.py:197
  90.2 0.0 collective-permute-done.11
  90.2 0.0 collective-permute-done.12
  90.2 2.1 %add_convert_fusion = bf16[16,32,384]{2,1,0:T(8,128)(2,1)} fusion(bf16[16,32,384]{2,1,0:T(8,128)(2,1)} %collective-permute-done.13, bf16[16,32,384]{2,1,0:T(8,128)(2,1)} %collective-permute-done.12, bf16[16,32,384]{2,1,0:T(8,128)(2,1)S(1)} %collective-permute-done.11, bf16[16,32,384]{2,1,0:T(8,128)(2,1)S(1)} %get-tuple-element.10), kind=kLoop, calls=%fused_computation.3 | loop fusion | flops 1572864 | bytes 1966080 | tf_op jit(solution)/shard_map/convert_element_type | solution.py:200
  92.3 15.2 %all-to-all-start.2 = ((bf16[16,32,384]{2,1,0:T(8,128)(2,1)}), bf16[16,32,384]{2,1,0:T(8,128)(2,1)S(1)}, u32[]{:S(2)}, u32[]{:S(2)}) async-start(bf16[16,32,384]{2,1,0:T(8,128)(2,1)} %add_convert_fusion), calls=%async_computation.2 | async-start | bytes 786432 | tf_op jit(solution)/shard_map/all_to_all | solution.py:201
  107.5 3.1 %collective-permute-start.5 = (bf16[96,2048]{1,0:T(8,128)(2,1)S(1)}, bf16[96,2048]{1,0:T(8,128)(2,1)S(1)}, u32[]{:S(2)}, u32[]{:S(2)}) collective-permute-start(bf16[96,2048]{1,0:T(8,128)(2,1)S(1)} %fusion.own), channel_id=1, source_target_pairs={{0,1},{1,0},{2,3},{3,2},{4,5},{5,4},{6,7},{7,6},{8,9},{9,8},{10,11... | collective-permute-start | bytes 1179656 | tf_op jit(solution)/shard_map/ppermute | solution.py:195
  110.6 0.0 collective-permute-done.6.below
  110.6 0.1 pad_maximum_fusion.1
  110.7 2.7 %collective-permute-start.9 = (bf16[192,2048]{1,0:T(8,128)(2,1)S(1)}, bf16[192,2048]{1,0:T(8,128)(2,1)S(1)}, u32[]{:S(2)}, u32[]{:S(2)}) collective-permute-start(bf16[192,2048]{1,0:T(8,128)(2,1)S(1)} %pad_maximum_fusion.1), channel_id=1, source_target_pairs={{0,1},{1,0},{2,3},{3,2},{4,5},{5,4},{6,7},{7,6},{8,9},{9,8},{10,11... | collective-permute-start | bytes 2359304 | tf_op jit(solution)/shard_map/ppermute | solution.py:205
  113.4 8.0 %collective-permute-done.5.near = bf16[96,2048]{1,0:T(8,128)(2,1)S(1)} collective-permute-done((bf16[96,2048]{1,0:T(8,128)(2,1)S(1)}, bf16[96,2048]{1,0:T(8,128)(2,1)S(1)}, u32[]{:S(2)}, u32[]{:S(2)}) %collective-permute-start.5) | collective-permute-done | bytes 393248 | tf_op jit(solution)/shard_map/ppermute | solution.py:195
  121.4 0.1 pad_maximum_fusion
  121.5 5.0 %collective-permute-start.8 = (bf16[192,2048]{1,0:T(8,128)(2,1)S(1)}, bf16[192,2048]{1,0:T(8,128)(2,1)S(1)}, u32[]{:S(2)}, u32[]{:S(2)}) collective-permute-start(bf16[192,2048]{1,0:T(8,128)(2,1)S(1)} %pad_maximum_fusion), channel_id=1, source_target_pairs={{0,4},{2,6},{4,0},{6,2},{1,5},{3,7},{5,1},{7,3},{8,12},{10,14},{12... | collective-permute-start | bytes 2359304 | tf_op jit(solution)/shard_map/ppermute | solution.py:204
  126.5 1.7 %place_first.1.partial = bf16[768,2048]{1,0:T(8,128)(2,1)} custom-call(s32[5]{0:T(128)S(1)} %stack.19.place, bf16[96,2048]{1,0:T(8,128)(2,1)S(1)} %fusion.own, bf16[96,2048]{1,0:T(8,128)(2,1)S(1)} %collective-permute-done.5.near, bf16[96,2048]{1,0:T(8,128)(2,1)S(1)} %collective-permute-done.6.below, bf16[96,2048]{1,0:T(8,128)(2,1)S(1)} %collective-permute-done.7.above), custom_call_target="tpu_custom_call" | custom-call | tf_op jit(solution)/shard_map/place_first/pallas_call | solution.py:208
  128.2 7.7 %collective-permute-done.9.beside = bf16[192,2048]{1,0:T(8,128)(2,1)S(1)} collective-permute-done((bf16[192,2048]{1,0:T(8,128)(2,1)S(1)}, bf16[192,2048]{1,0:T(8,128)(2,1)S(1)}, u32[]{:S(2)}, u32[]{:S(2)}) %collective-permute-start.9) | collective-permute-done | bytes 786464 | tf_op jit(solution)/shard_map/ppermute | solution.py:205
  135.9 3.8 %collective-permute-done.8.across = bf16[192,2048]{1,0:T(8,128)(2,1)S(1)} collective-permute-done((bf16[192,2048]{1,0:T(8,128)(2,1)S(1)}, bf16[192,2048]{1,0:T(8,128)(2,1)S(1)}, u32[]{:S(2)}, u32[]{:S(2)}) %collective-permute-start.8) | collective-permute-done | bytes 786464 | tf_op jit(solution)/shard_map/ppermute | solution.py:204
  139.7 1.7 %place_last.1 = bf16[768,2048]{1,0:T(8,128)(2,1)} custom-call(s32[5]{0:T(128)S(1)} %stack.19.place, bf16[768,2048]{1,0:T(8,128)(2,1)} %place_first.1.partial, bf16[192,2048]{1,0:T(8,128)(2,1)S(1)} %collective-permute-done.8.across, bf16[192,2048]{1,0:T(8,128)(2,1)S(1)} %collective-permute-done.9.beside), custom_call_target="tpu_custom_call", output_to_operand_aliasing={{}: (1, {})} | custom-call | tf_op jit(solution)/shard_map/place_last/pallas_call | solution.py:217
  141.4 0.0 all-to-all-done.2
  141.4 0.1 convert_reduce_fusion
  141.5 0.6 broadcast_multiply_fusion
  (16 shorter events, 0.1 us)
Async XLA Ops:
  3.7 6.1 %copy-start = (bf16[2048,384]{1,0:T(8,128)(2,1)S(1)}, bf16[2048,384]{1,0:T(8,128)(2,1)}, u32[]{:S(2)}) copy-start(bf16[2048,384]{1,0:T(8,128)(2,1)} %down.1) | copy-start | bytes 4718596
  3.7 39.4 %all-to-all-start = ((bf16[8,384,256]{2,1,0:T(8,128)(2,1)}), bf16[8,384,256]{2,1,0:T(8,128)(2,1)S(1)}, u32[]{:S(2)}, u32[]{:S(2)}) async-start(bf16[8,384,256]{2,1,0:T(8,128)(2,1)} %bitcast.39), calls=%async_computation | async-start | bytes 3145728 | tf_op jit(solution)/shard_map/all_to_all | solution.py:132
  9.8 6.4 %copy-start.1 = (bf16[384,2048]{1,0:T(8,128)(2,1)S(1)}, bf16[384,2048]{1,0:T(8,128)(2,1)}, u32[]{:S(2)}) copy-start(bf16[384,2048]{1,0:T(8,128)(2,1)} %up_own.1) | copy-start | bytes 4718596
  10.8 24.2 %collective-permute-start.1 = (bf16[1024,384]{1,0:T(8,128)(2,1)}, bf16[1024,384]{1,0:T(8,128)(2,1)}, u32[]{:S(2)}, u32[]{:S(2)}) collective-permute-start(bf16[1024,384]{1,0:T(8,128)(2,1)} %dynamic-slice_bitcast_fusion.1), channel_id=1, source_target_pairs={{0,17},{17,0},{1,16},{16,1},{2,19},{19,2},{3,18},{18,3},{4,21},{21... | collective-permute-start | bytes 2359304 | tf_op jit(solution)/shard_map/ppermute | solution.py:138
  17.2 21.8 %collective-permute-start.3 = (bf16[192,2048]{1,0:T(8,128)(2,1)}, bf16[192,2048]{1,0:T(8,128)(2,1)}, u32[]{:S(2)}, u32[]{:S(2)}) collective-permute-start(bf16[192,2048]{1,0:T(8,128)(2,1)} %dynamic-slice_bitcast_fusion), channel_id=1, source_target_pairs={{0,1},{1,0},{8,25},{9,24},{16,17},{17,16},{24,9},{25,8},{2,3},{3,2... | collective-permute-start | bytes 2359304 | tf_op jit(solution)/shard_map/ppermute | solution.py:139
  22.3 20.9 %collective-permute-start = (bf16[384,384]{1,0:T(8,128)(2,1)}, bf16[384,384]{1,0:T(8,128)(2,1)}, u32[]{:S(2)}, u32[]{:S(2)}) collective-permute-start(bf16[384,384]{1,0:T(8,128)(2,1)} %bitcast.11), channel_id=1, source_target_pairs={{0,1},{1,0},{2,3},{3,2},{4,5},{5,4},{6,7},{7,6},{8,9},{9,8},{10,11... | collective-permute-start | bytes 884744 | tf_op jit(solution)/shard_map/ppermute | solution.py:136
  35.0 16.4 %collective-permute-start.2 = (bf16[1024,384]{1,0:T(8,128)(2,1)}, bf16[1024,384]{1,0:T(8,128)(2,1)}, u32[]{:S(2)}, u32[]{:S(2)}) collective-permute-start(bf16[1024,384]{1,0:T(8,128)(2,1)} %collective-permute-done.1.down_mine), channel_id=1, source_target_pairs={{0,8},{8,0},{1,9},{9,1},{2,10},{10,2},{3,11},{11,3},{4,12},{12,4},... | collective-permute-start | bytes 2359304 | tf_op jit(solution)/shard_map/ppermute | solution.py:142
  39.1 12.3 %collective-permute-start.4 = (bf16[192,2048]{1,0:T(8,128)(2,1)}, bf16[192,2048]{1,0:T(8,128)(2,1)}, u32[]{:S(2)}, u32[]{:S(2)}) collective-permute-start(bf16[192,2048]{1,0:T(8,128)(2,1)} %collective-permute-done.3.up_mine), channel_id=1, source_target_pairs={{0,8},{8,0},{1,9},{9,1},{2,10},{10,2},{3,11},{11,3},{4,12},{12,4},... | collective-permute-start | bytes 2359304 | tf_op jit(solution)/shard_map/ppermute | solution.py:143
  47.2 1.2 copy-start.3
  48.3 3.1 %copy-start.2 = (bf16[384,2048]{1,0:T(8,128)(2,1)S(1)}, bf16[384,2048]{1,0:T(8,128)(2,1)}, u32[]{:S(2)}) copy-start(bf16[384,2048]{1,0:T(8,128)(2,1)} %up_own.1) | copy-start | bytes 4718596
  48.3 13.2 %collective-permute-start.10 = (bf16[4,16,32,384]{3,2,1,0:T(8,128)(2,1)}, bf16[4,16,32,384]{3,2,1,0:T(8,128)(2,1)}, u32[]{:S(2)}, u32[]{:S(2)}) collective-permute-start(bf16[4,16,32,384]{3,2,1,0:T(8,128)(2,1)} %get-tuple-element.9), channel_id=1, source_target_pairs={{0,8},{8,0},{1,9},{9,1},{2,10},{10,2},{3,11},{11,3},{4,12},{12,4},... | collective-permute-start | bytes 4718600 | tf_op jit(solution)/shard_map/ppermute | solution.py:187
  57.1 4.4 %copy-start.4 = (bf16[4,16,32,384]{3,2,1,0:T(8,128)(2,1)S(1)}, bf16[4,16,32,384]{3,2,1,0:T(8,128)(2,1)}, u32[]{:S(2)}) copy-start(bf16[4,16,32,384]{3,2,1,0:T(8,128)(2,1)} %copy-done.3) | copy-start | bytes 4718596
  57.1 25.7 %all-to-all-start.1 = ((bf16[4,96,2048]{2,1,0:T(8,128)(2,1)}), bf16[4,96,2048]{2,1,0:T(8,128)(2,1)S(1)}, u32[]{:S(2)}, u32[]{:S(2)}) async-start(bf16[4,96,2048]{2,1,0:T(8,128)(2,1)} %bitcast.16), calls=%async_computation.1 | async-start | bytes 3145728 | tf_op jit(solution)/shard_map/all_to_all | solution.py:184
  64.1 26.0 %collective-permute-start.11 = (bf16[16,32,384]{2,1,0:T(8,128)(2,1)}, bf16[16,32,384]{2,1,0:T(8,128)(2,1)S(1)}, u32[]{:S(2)}, u32[]{:S(2)}) collective-permute-start(bf16[16,32,384]{2,1,0:T(8,128)(2,1)} %get-tuple-element.16), channel_id=1, source_target_pairs={{0,1},{1,0},{2,3},{3,2},{4,5},{5,4},{6,7},{7,6},{8,9},{9,8},{10,11... | collective-permute-start | bytes 1179656 | tf_op jit(solution)/shard_map/ppermute | solution.py:190
  67.2 22.9 %collective-permute-start.12 = (bf16[16,32,384]{2,1,0:T(8,128)(2,1)}, bf16[16,32,384]{2,1,0:T(8,128)(2,1)}, u32[]{:S(2)}, u32[]{:S(2)}) collective-permute-start(bf16[16,32,384]{2,1,0:T(8,128)(2,1)} %get-tuple-element.15), channel_id=1, source_target_pairs={{0,17},{17,0},{1,16},{16,1},{2,19},{19,2},{3,18},{18,3},{4,21},{21... | collective-permute-start | bytes 1179656 | tf_op jit(solution)/shard_map/ppermute | solution.py:191
  69.3 20.9 %collective-permute-start.13 = (bf16[16,32,384]{2,1,0:T(8,128)(2,1)}, bf16[16,32,384]{2,1,0:T(8,128)(2,1)}, u32[]{:S(2)}, u32[]{:S(2)}) collective-permute-start(bf16[16,32,384]{2,1,0:T(8,128)(2,1)} %get-tuple-element.14), channel_id=1, source_target_pairs={{0,16},{16,0},{1,17},{17,1},{2,18},{18,2},{3,19},{19,3},{4,20},{20... | collective-permute-start | bytes 1179656 | tf_op jit(solution)/shard_map/ppermute | solution.py:192
  83.1 27.5 %collective-permute-start.6 = (bf16[96,2048]{1,0:T(8,128)(2,1)S(1)}, bf16[96,2048]{1,0:T(8,128)(2,1)S(1)}, u32[]{:S(2)}, u32[]{:S(2)}) collective-permute-start(bf16[96,2048]{1,0:T(8,128)(2,1)S(1)} %fusion.own), channel_id=1, source_target_pairs={{0,2},{2,4},{4,6},{6,0},{1,3},{3,5},{5,7},{7,1},{8,10},{10,12},{12... | collective-permute-start | bytes 1179656 | tf_op jit(solution)/shard_map/ppermute | solution.py:196
  85.6 25.1 %collective-permute-start.7 = (bf16[96,2048]{1,0:T(8,128)(2,1)S(1)}, bf16[96,2048]{1,0:T(8,128)(2,1)S(1)}, u32[]{:S(2)}, u32[]{:S(2)}) collective-permute-start(bf16[96,2048]{1,0:T(8,128)(2,1)S(1)} %fusion.own), channel_id=1, source_target_pairs={{0,6},{2,0},{4,2},{6,4},{1,7},{3,1},{5,3},{7,5},{8,14},{10,8},{12,... | collective-permute-start | bytes 1179656 | tf_op jit(solution)/shard_map/ppermute | solution.py:197
  92.3 49.1 %all-to-all-start.2 = ((bf16[16,32,384]{2,1,0:T(8,128)(2,1)}), bf16[16,32,384]{2,1,0:T(8,128)(2,1)S(1)}, u32[]{:S(2)}, u32[]{:S(2)}) async-start(bf16[16,32,384]{2,1,0:T(8,128)(2,1)} %add_convert_fusion), calls=%async_computation.2 | async-start | bytes 786432 | tf_op jit(solution)/shard_map/all_to_all | solution.py:201
  107.5 13.9 %collective-permute-start.5 = (bf16[96,2048]{1,0:T(8,128)(2,1)S(1)}, bf16[96,2048]{1,0:T(8,128)(2,1)S(1)}, u32[]{:S(2)}, u32[]{:S(2)}) collective-permute-start(bf16[96,2048]{1,0:T(8,128)(2,1)S(1)} %fusion.own), channel_id=1, source_target_pairs={{0,1},{1,0},{2,3},{3,2},{4,5},{5,4},{6,7},{7,6},{8,9},{9,8},{10,11... | collective-permute-start | bytes 1179656 | tf_op jit(solution)/shard_map/ppermute | solution.py:195
  110.7 25.2 %collective-permute-start.9 = (bf16[192,2048]{1,0:T(8,128)(2,1)S(1)}, bf16[192,2048]{1,0:T(8,128)(2,1)S(1)}, u32[]{:S(2)}, u32[]{:S(2)}) collective-permute-start(bf16[192,2048]{1,0:T(8,128)(2,1)S(1)} %pad_maximum_fusion.1), channel_id=1, source_target_pairs={{0,1},{1,0},{2,3},{3,2},{4,5},{5,4},{6,7},{7,6},{8,9},{9,8},{10,11... | collective-permute-start | bytes 2359304 | tf_op jit(solution)/shard_map/ppermute | solution.py:205
  121.5 18.2 %collective-permute-start.8 = (bf16[192,2048]{1,0:T(8,128)(2,1)S(1)}, bf16[192,2048]{1,0:T(8,128)(2,1)S(1)}, u32[]{:S(2)}, u32[]{:S(2)}) collective-permute-start(bf16[192,2048]{1,0:T(8,128)(2,1)S(1)} %pad_maximum_fusion), channel_id=1, source_target_pairs={{0,4},{2,6},{4,0},{6,2},{1,5},{3,7},{5,1},{7,3},{8,12},{10,14},{12... | collective-permute-start | bytes 2359304 | tf_op jit(solution)/shard_map/ppermute | solution.py:204

commit v4 on v3

--- a/solution.py
+++ b/solution.py
@@ -21,6 +21,26 @@
 
 def dot(a, b):
     return jnp.dot(a, b, preferred_element_type=jnp.float32)
+
+
+def split_kernel(place, grad_out, pre_act, own_set, other_set, pre_own, pre_sent):
+    xl, live = place[2], place[3]
+    part = own_set.shape[0] // 4
+    for y in range(4):
+        to = slice(y * part, (y + 1) * part)
+        for x, grads, pre in ((xl, own_set, pre_own), (1 - xl, other_set, pre_sent)):
+            first = pl.multiple_of((y * 2 + x) * part, 16)
+            at = pl.ds(first, part)
+            row = first + lax.broadcasted_iota(jnp.int32, (part, grads.shape[1]), 0)
+            grads[to, :] = jnp.where(row < live, grad_out[at, :], 0).astype(grads.dtype)
+            pre[to, :] = pre_act[at, :]
+
+
+def spread_kernel(place, own_set, near_set, out):
+    xl = place[2]
+    for y in range(out.shape[0]):
+        out[y, xl] = own_set[...]
+        out[y, 1 - xl] = near_set[...]
 
 
 def own_kernel(grads, pre, down, out):
@@ -125,15 +145,28 @@
     def turn(by):
         return [(i, (i + by) % ys) for i in range(ys)]
 
-    live_rows = (lax.iota(jnp.int32, slot_rows) < slot_counts[0])[:, None]
-    grad_live = jnp.where(live_rows, grad_out, jnp.zeros_like(grad_out))
-    by_set = grad_live.reshape(ys, 2, rows, features).transpose(1, 0, 2, 3).reshape(2, half_rows, features)
-    grads = jnp.broadcast_to(by_set[None], (ys, 2, half_rows, features)).reshape(reps, half_rows, features)
-    grads = lax.all_to_all(grads, REP, 0, 0, tiled=True)
-
-    pre_sets = pre_act.reshape(ys, 2, rows, hidden_units)
-    pre_own = own_part(pre_sets, xl, 1).reshape(half_rows, hidden_units)
-    pre_far = lax.ppermute(own_part(pre_sets, 1 - xl, 1).reshape(half_rows, hidden_units), "xl", NEAR)
+    params = pltpu.CompilerParams(vmem_limit_bytes=LIMIT)
+    set_shape = jax.ShapeDtypeStruct((half_rows, features), bf16)
+    pre_shape = jax.ShapeDtypeStruct((half_rows, hidden_units), bf16)
+    own_set, other_set, pre_own, pre_sent = pl.pallas_call(
+        split_kernel,
+        out_shape=(set_shape, set_shape, pre_shape, pre_shape),
+        in_specs=[SMEM] + [VMEM] * 2,
+        out_specs=(VMEM,) * 4,
+        compiler_params=params,
+        name="split",
+    )(place, grad_out, pre_act)
+    near_set = lax.ppermute(other_set, "xl", NEAR)
+    grads = pl.pallas_call(
+        spread_kernel,
+        out_shape=jax.ShapeDtypeStruct((ys, 2, half_rows, features), bf16),
+        in_specs=[SMEM] + [VMEM] * 2,
+        out_specs=VMEM,
+        compiler_params=params,
+        name="spread",
+    )(place, own_set, near_set)
+    grads = lax.all_to_all(grads, "y", 0, 0, tiled=True).reshape(reps, half_rows, features)
+    pre_far = lax.ppermute(pre_sent, "xl", NEAR)
 
     down_mine = lax.ppermute(own_part(down_weight.reshape(2, width // 2, hidden_units), core, 0), RING, FAR)
     up_mine = lax.ppermute(
@@ -153,19 +186,6 @@
         ),
         name="own_grad",
     )(grads, pre_own, down_weight)
-    terms = pl.pallas_call(
-        terms_kernel,
-        out_shape=jax.ShapeDtypeStruct((half_rows, width), bf16),
-        in_specs=[SMEM] + [VMEM] * 8,
-        out_specs=VMEM,
-        scratch_shapes=[pltpu.VMEM((hidden_units, width), bf16)],
-        compiler_params=pltpu.CompilerParams(vmem_limit_bytes=LIMIT),
-        cost_estimate=pl.CostEstimate(
-            flops=6 * half_rows * width * hidden_units, bytes_accessed=12 * width * hidden_units, transcendentals=0
-        ),
-        name="terms",
-    )(place, grads, pre_grad, pre_far, down_mine, down_other, up_weight, up_mine, up_other)
-
     share = width // (4 * zs)
     laid_out = jax.ShapeDtypeStruct((4, zs, share, hidden_units), bf16)
     kept, sent = pl.pallas_call(
@@ -180,6 +200,19 @@
         name="down_terms",
     )(place, grads, pre_own, pre_far)
 
+    terms = pl.pallas_call(
+        terms_kernel,
+        out_shape=jax.ShapeDtypeStruct((half_rows, width), bf16),
+        in_specs=[SMEM] + [VMEM] * 8,
+        out_specs=VMEM,
+        scratch_shapes=[pltpu.VMEM((hidden_units, width), bf16)],
+        compiler_params=pltpu.CompilerParams(vmem_limit_bytes=LIMIT),
+        cost_estimate=pl.CostEstimate(
+            flops=6 * half_rows * width * hidden_units, bytes_accessed=12 * width * hidden_units, transcendentals=0
+        ),
+        name="terms",
+    )(place, grads, pre_grad, pre_far, down_mine, down_other, up_weight, up_mine, up_other)
+
     f32 = jnp.float32
     came = lax.all_to_all(terms.reshape(ys, rows, width), "y", 0, 0, tiled=True)
     own = sum(came[i].astype(f32) for i in range(ys)).astype(bf16)
@@ -201,10 +234,10 @@
     z_terms = lax.all_to_all(ring_sum, "z", 0, 0, tiled=True)
     down_grad = jnp.sum(z_terms.astype(f32), axis=0) / (4 * zs)
 
+    near, below, above = lax.optimization_barrier((near, below, above))
     across = lax.ppermute(jnp.concatenate([own, near]), "y", turn(2))
     beside = lax.ppermute(jnp.concatenate([below, above]), "xl", NEAR)
     whole = jax.ShapeDtypeStruct((slot_rows, width), bf16)
-    params = pltpu.CompilerParams(vmem_limit_bytes=LIMIT)
     first = pl.pallas_call(
         first_kernel,
         out_shape=whole,

time: 143 us -> 139 us (0.972)
  waiting for transfers between devices: 40.6 us -> 34.3 us
  Pallas kernels: 14.1 us -> 16.1 us
  local copies, waits for them, and re-layouts: 6.36 us -> 7.89 us
    ppermute x1, waiting for transfers between devices: 8.01 us -> 0.01 us  [on_device(): near = lax.ppermute(own, 'xl', NEAR)]
    ppermute x1, waiting for transfers between devices: 7.68 us -> 12.3 us  [on_device(): beside = lax.ppermute(jnp.concatenate([below, above]), 'xl', NEAR)]
    unnamed x10 -> x22, local copies, waits for them, and re-layouts: 1.18 us -> 5.63 us
    ppermute x1, starting transfers between devices: 5.01 us -> 1.92 us  [on_device(): across = lax.ppermute(jnp.concatenate([own, near]), 'y', turn(2))]
    ppermute x1, waiting for transfers between devices: 10 us -> 7.29 us  [on_device(): lax.ppermute(own_part(down_weight.reshape(2, width // 2, hidden_units), c...]
    ppermute x1 -> x2, starting transfers between devices: 2.64 us -> 5.25 us  [the longest x1 2.72 us: on_device(): near_set = lax.ppermute(other_set, 'xl', NEAR)]
    pallas_call x0 -> x2, Pallas kernels: none -> 2.45 us  [the longest x1 1.8 us: on_device(): pl.pallas_call(spread_kernel, out_shape=jax.ShapeDtypeStruct((ys, 2, half...]
    all_to_all x1, starting transfers between devices: 6.06 us -> 3.69 us  [on_device(): lax.all_to_all(grads, 'y', 0, 0, tiled=True)]
  transfers between devices with their start and end apart: 17 -> 18, of which waited for: 6 -> 5; matrix products, arithmetic and copies ran while one was open for 6% -> 5% of each run, Pallas kernels for 10% -> 11%
where the time goes in v4:
time: 139 us; the launch traced here: 137 us
  starting transfers between devices  71.4 us (51%)
  waiting for transfers between devices  34.3 us (25%)
  Pallas kernels  16.1 us (12%)
  local copies, waits for them, and re-layouts  7.89 us (6%)
  other arithmetic  5.97 us (4%)
  between operations  1.64 us (1%)
    all_to_all x1, starting transfers between devices, on_device(): z_terms = lax.all_to_all(ring_sum, 'z', 0, 0, tiled=True)  15.2 us
    ppermute x1, waiting for transfers between devices, on_device(): beside = lax.ppermute(jnp.concatenate([below, above]), 'xl', NEAR)  12.3 us
    all_to_all x1, waiting for transfers between devices, on_device(): came = lax.all_to_all(terms.reshape(ys, rows, width), 'y', 0, 0, tiled=True)  8.78 us
    ppermute x1, waiting for transfers between devices, on_device(): lax.ppermute(own_part(down_weight.reshape(2, width // 2, hidden_units), c...  7.29 us
    ppermute x1, starting transfers between devices, on_device(): lax.ppermute(own_part(down_weight.reshape(2, width // 2, hidden_units), c...  6.93 us
    pallas_call x1, Pallas kernels, on_device(): pl.pallas_call(terms_kernel, out_shape=jax.ShapeDtypeStruct((half_rows, w...  5.65 us
    unnamed x22, local copies, waits for them, and re-layouts  5.63 us
    ppermute x1, waiting for transfers between devices, on_device(): across = lax.ppermute(jnp.concatenate([own, near]), 'y', turn(2))  4.95 us
  transfers between devices with their start and end apart: 18, of which 5 were waited for; matrix products, arithmetic and copies ran while one was open for 5% of the time, Pallas kernels for 11%

profile of v4, /device:TPU:6, one launch (start us, length us, event | category | flops | bytes accessed | tf_op | source)
XLA Modules:
  0.0 137.4 jit_solution(3963548779875694767)
XLA Ops:
  1.3 0.1 stack.19.place
  1.4 1.1 copy-done.4
  2.4 1.0 copy-done.5
  3.4 0.7 split.1
  4.1 0.7 copy-done.8
  4.8 2.7 %collective-permute-start = (bf16[384,256]{1,0:T(8,128)(2,1)S(1)}, bf16[384,256]{1,0:T(8,128)(2,1)S(1)}, u32[]{:S(2)}, u32[]{:S(2)}) collective-permute-start(bf16[384,256]{1,0:T(8,128)(2,1)S(1)} %get-tuple-element.16), channel_id=1, source_target_pairs={{0,1},{1,0},{2,3},{3,2},{4,5},{5,4},{6,7},{7,6},{8,9},{9,8},{10,11... | collective-permute-start | bytes 589832 | tf_op jit(solution)/shard_map/ppermute | solution.py:159
  7.5 2.1 %dynamic-slice_bitcast_fusion.1 = bf16[1024,384]{1,0:T(8,128)(2,1)} fusion(bf16[2,1024,384]{2,1,0:T(8,128)(2,1)} %bitcast.25, s32[]{:T(128)S(6)} %select_n.6), kind=kLoop, calls=%fused_computation.10 | loop fusion | bytes 1572868 | tf_op jit(solution)/shard_map/jit(dynamic_index_in_dim)/squeeze | solution.py:130
  9.7 6.9 %collective-permute-start.2 = (bf16[1024,384]{1,0:T(8,128)(2,1)}, bf16[1024,384]{1,0:T(8,128)(2,1)}, u32[]{:S(2)}, u32[]{:S(2)}) collective-permute-start(bf16[1024,384]{1,0:T(8,128)(2,1)} %dynamic-slice_bitcast_fusion.1), channel_id=1, source_target_pairs={{0,17},{17,0},{1,16},{16,1},{2,19},{19,2},{3,18},{18,3},{4,21},{21... | collective-permute-start | bytes 2359304 | tf_op jit(solution)/shard_map/ppermute | solution.py:171
  16.6 0.0 collective-permute-done.near_set
  16.6 1.8 %spread.1 = bf16[4,2,384,256]{3,2,1,0:T(8,128)(2,1)} custom-call(s32[5]{0:T(128)S(1)} %stack.19.place, bf16[384,256]{1,0:T(8,128)(2,1)S(1)} %get-tuple-element.15.own_set, bf16[384,256]{1,0:T(8,128)(2,1)S(1)} %collective-permute-done.near_set), custom_call_target="tpu_custom_call" | custom-call | tf_op jit(solution)/shard_map/spread/pallas_call | solution.py:160
  18.4 3.7 %all-to-all-start = ((bf16[4,2,384,256]{3,2,1,0:T(8,128)(2,1)}), bf16[4,2,384,256]{3,2,1,0:T(8,128)(2,1)S(1)}, u32[]{:S(2)}, u32[]{:S(2)}) async-start(bf16[4,2,384,256]{3,2,1,0:T(8,128)(2,1)} %spread.1), calls=%async_computation | async-start | bytes 3145728 | tf_op jit(solution)/shard_map/all_to_all | solution.py:168
  22.1 0.1 dynamic-slice_bitcast_fusion
  22.2 3.3 %collective-permute-start.4 = (bf16[192,2048]{1,0:T(8,128)(2,1)S(1)}, bf16[192,2048]{1,0:T(8,128)(2,1)}, u32[]{:S(2)}, u32[]{:S(2)}) collective-permute-start(bf16[192,2048]{1,0:T(8,128)(2,1)S(1)} %dynamic-slice_bitcast_fusion), channel_id=1, source_target_pairs={{0,1},{1,0},{8,25},{9,24},{16,17},{17,16},{24,9},{25,8},{2,3},{3,2... | collective-permute-start | bytes 2359304 | tf_op jit(solution)/shard_map/ppermute | solution.py:172
  25.5 2.5 %collective-permute-start.1 = (bf16[384,384]{1,0:T(8,128)(2,1)S(1)}, bf16[384,384]{1,0:T(8,128)(2,1)S(1)}, u32[]{:S(2)}, u32[]{:S(2)}) collective-permute-start(bf16[384,384]{1,0:T(8,128)(2,1)S(1)} %copy-done.9), channel_id=1, source_target_pairs={{0,1},{1,0},{2,3},{3,2},{4,5},{5,4},{6,7},{7,6},{8,9},{9,8},{10,11... | collective-permute-start | bytes 884744 | tf_op jit(solution)/shard_map/ppermute | solution.py:169
  28.1 7.3 %collective-permute-done.2.down_mine = bf16[1024,384]{1,0:T(8,128)(2,1)} collective-permute-done((bf16[1024,384]{1,0:T(8,128)(2,1)}, bf16[1024,384]{1,0:T(8,128)(2,1)}, u32[]{:S(2)}, u32[]{:S(2)}) %collective-permute-start.2) | collective-permute-done | bytes 786464 | tf_op jit(solution)/shard_map/ppermute | solution.py:171
  35.4 1.9 %collective-permute-start.3 = (bf16[1024,384]{1,0:T(8,128)(2,1)}, bf16[1024,384]{1,0:T(8,128)(2,1)}, u32[]{:S(2)}, u32[]{:S(2)}) collective-permute-start(bf16[1024,384]{1,0:T(8,128)(2,1)} %collective-permute-done.2.down_mine), channel_id=1, source_target_pairs={{0,8},{8,0},{1,9},{9,1},{2,10},{10,2},{3,11},{11,3},{4,12},{12,4},... | collective-permute-start | bytes 2359304 | tf_op jit(solution)/shard_map/ppermute | solution.py:175
  37.3 0.9 collective-permute-done.4.up_mine
  38.2 4.0 %collective-permute-start.5 = (bf16[192,2048]{1,0:T(8,128)(2,1)}, bf16[192,2048]{1,0:T(8,128)(2,1)}, u32[]{:S(2)}, u32[]{:S(2)}) collective-permute-start(bf16[192,2048]{1,0:T(8,128)(2,1)} %collective-permute-done.4.up_mine), channel_id=1, source_target_pairs={{0,8},{8,0},{1,9},{9,1},{2,10},{10,2},{3,11},{11,3},{4,12},{12,4},... | collective-permute-start | bytes 2359304 | tf_op jit(solution)/shard_map/ppermute | solution.py:176
  42.2 0.0 collective-permute-done.1.pre_far
  42.2 0.7 copy-done.6
  42.9 1.0 copy-done.7
  43.9 3.6 %down_terms.1 = (bf16[4,16,32,384]{3,2,1,0:T(8,128)(2,1)S(1)}, bf16[4,16,32,384]{3,2,1,0:T(8,128)(2,1)}) custom-call(s32[5]{0:T(128)S(1)} %stack.19.place, bf16[8,384,256]{2,1,0:T(8,128)(2,1)S(1)} %bitcast.22, bf16[384,384]{1,0:T(8,128)(2,1)S(1)} %get-tuple-element.17.pre.pre_own, bf16[384,384]{1,0:T(8,128)(2,1)S(1)} %copy-done.7), custom_call_target="tpu_custom_call" | custom-call | flops 1207959552 | bytes 6291456 | tf_op jit(solution)/shard_map/down_terms/pallas_call | solution.py:191
  47.5 1.2 copy-done.2
  48.7 1.9 %collective-permute-start.11 = (bf16[4,16,32,384]{3,2,1,0:T(8,128)(2,1)}, bf16[4,16,32,384]{3,2,1,0:T(8,128)(2,1)}, u32[]{:S(2)}, u32[]{:S(2)}) collective-permute-start(bf16[4,16,32,384]{3,2,1,0:T(8,128)(2,1)} %get-tuple-element.23), channel_id=1, source_target_pairs={{0,8},{8,0},{1,9},{9,1},{2,10},{10,2},{3,11},{11,3},{4,12},{12,4},... | collective-permute-start | bytes 4718600 | tf_op jit(solution)/shard_map/ppermute | solution.py:220
  50.6 1.0 own_grad.1.own
  51.6 5.6 %terms.1 = bf16[384,2048]{1,0:T(8,128)(2,1)} custom-call(s32[5]{0:T(128)S(1)} %stack.19.place, bf16[8,384,256]{2,1,0:T(8,128)(2,1)S(1)} %bitcast.24, bf16[384,384]{1,0:T(8,128)(2,1)S(1)} %own_grad.1.own, bf16[384,384]{1,0:T(8,128)(2,1)S(1)} %copy-done.7, bf16[1024,384]{1,0:T(8,128)(2,1)} %collective-permute-done.2.down_mine, ...), custom_call_target="tpu_custom_call" | custom-call | flops 1811939328 | bytes 9437184 | tf_op jit(solution)/shard_map/terms/pallas_call | solution.py:203
  57.2 4.6 %all-to-all-start.1 = ((bf16[4,96,2048]{2,1,0:T(8,128)(2,1)}), bf16[4,96,2048]{2,1,0:T(8,128)(2,1)S(1)}, u32[]{:S(2)}, u32[]{:S(2)}) async-start(bf16[4,96,2048]{2,1,0:T(8,128)(2,1)} %bitcast.9), calls=%async_computation.1 | async-start | bytes 3145728 | tf_op jit(solution)/shard_map/all_to_all | solution.py:217
  61.8 2.7 %fusion.4 = (bf16[16,32,384]{2,1,0:T(8,128)(2,1)}, bf16[16,32,384]{2,1,0:T(8,128)(2,1)}, bf16[16,32,384]{2,1,0:T(8,128)(2,1)}, bf16[16,32,384]{2,1,0:T(8,128)(2,1)}) fusion(bf16[4,16,32,384]{3,2,1,0:T(8,128)(2,1)} %collective-permute-done.11, bf16[4,16,32,384]{3,2,1,0:T(8,128)(2,1)S(1)} %copy-done.3), kind=kLoop, calls=%fused_computation.15 | loop fusion | flops 3145728 | bytes 4718592 | tf_op jit(solution)/shard_map/convert_element_type | solution.py:225
  64.6 2.1 %collective-permute-start.12 = (bf16[16,32,384]{2,1,0:T(8,128)(2,1)}, bf16[16,32,384]{2,1,0:T(8,128)(2,1)}, u32[]{:S(2)}, u32[]{:S(2)}) collective-permute-start(bf16[16,32,384]{2,1,0:T(8,128)(2,1)} %get-tuple-element.30), channel_id=1, source_target_pairs={{0,1},{1,0},{2,3},{3,2},{4,5},{5,4},{6,7},{7,6},{8,9},{9,8},{10,11... | collective-permute-start | bytes 1179656 | tf_op jit(solution)/shard_map/ppermute | solution.py:223
  66.7 2.9 %collective-permute-start.13 = (bf16[16,32,384]{2,1,0:T(8,128)(2,1)}, bf16[16,32,384]{2,1,0:T(8,128)(2,1)}, u32[]{:S(2)}, u32[]{:S(2)}) collective-permute-start(bf16[16,32,384]{2,1,0:T(8,128)(2,1)} %get-tuple-element.29), channel_id=1, source_target_pairs={{0,17},{17,0},{1,16},{16,1},{2,19},{19,2},{3,18},{18,3},{4,21},{21... | collective-permute-start | bytes 1179656 | tf_op jit(solution)/shard_map/ppermute | solution.py:224
  69.6 4.9 %collective-permute-start.14 = (bf16[16,32,384]{2,1,0:T(8,128)(2,1)}, bf16[16,32,384]{2,1,0:T(8,128)(2,1)}, u32[]{:S(2)}, u32[]{:S(2)}) collective-permute-start(bf16[16,32,384]{2,1,0:T(8,128)(2,1)} %get-tuple-element.28), channel_id=1, source_target_pairs={{0,16},{16,0},{1,17},{17,1},{2,18},{18,2},{3,19},{19,3},{4,20},{20... | collective-permute-start | bytes 1179656 | tf_op jit(solution)/shard_map/ppermute | solution.py:225
  74.4 8.8 %all-to-all-done.1 = bf16[4,96,2048]{2,1,0:T(8,128)(2,1)S(1)} async-done(((bf16[4,96,2048]{2,1,0:T(8,128)(2,1)}), bf16[4,96,2048]{2,1,0:T(8,128)(2,1)S(1)}, u32[]{:S(2)}, u32[]{:S(2)}) %all-to-all-start.1) | async-done | bytes 1572896 | tf_op jit(solution)/shard_map/all_to_all | solution.py:217
  83.2 0.2 fusion.own
  83.5 2.1 %collective-permute-start.6 = (bf16[96,2048]{1,0:T(8,128)(2,1)S(1)}, bf16[96,2048]{1,0:T(8,128)(2,1)S(1)}, u32[]{:S(2)}, u32[]{:S(2)}) collective-permute-start(bf16[96,2048]{1,0:T(8,128)(2,1)S(1)} %fusion.own), channel_id=1, source_target_pairs={{0,1},{1,0},{2,3},{3,2},{4,5},{5,4},{6,7},{7,6},{8,9},{9,8},{10,11... | collective-permute-start | bytes 1179656 | tf_op jit(solution)/shard_map/ppermute | solution.py:228
  85.5 2.5 %collective-permute-start.7 = (bf16[96,2048]{1,0:T(8,128)(2,1)S(1)}, bf16[96,2048]{1,0:T(8,128)(2,1)S(1)}, u32[]{:S(2)}, u32[]{:S(2)}) collective-permute-start(bf16[96,2048]{1,0:T(8,128)(2,1)S(1)} %fusion.own), channel_id=1, source_target_pairs={{0,2},{2,4},{4,6},{6,0},{1,3},{3,5},{5,7},{7,1},{8,10},{10,12},{12... | collective-permute-start | bytes 1179656 | tf_op jit(solution)/shard_map/ppermute | solution.py:229
  88.0 4.6 %collective-permute-start.8 = (bf16[96,2048]{1,0:T(8,128)(2,1)S(1)}, bf16[96,2048]{1,0:T(8,128)(2,1)S(1)}, u32[]{:S(2)}, u32[]{:S(2)}) collective-permute-start(bf16[96,2048]{1,0:T(8,128)(2,1)S(1)} %fusion.own), channel_id=1, source_target_pairs={{0,6},{2,0},{4,2},{6,4},{1,7},{3,1},{5,3},{7,5},{8,14},{10,8},{12,... | collective-permute-start | bytes 1179656 | tf_op jit(solution)/shard_map/ppermute | solution.py:230
  92.7 2.2 %add_convert_fusion = bf16[16,32,384]{2,1,0:T(8,128)(2,1)} fusion(bf16[16,32,384]{2,1,0:T(8,128)(2,1)} %collective-permute-done.14, bf16[16,32,384]{2,1,0:T(8,128)(2,1)} %collective-permute-done.13, bf16[16,32,384]{2,1,0:T(8,128)(2,1)} %collective-permute-done.12, bf16[16,32,384]{2,1,0:T(8,128)(2,1)S(1)} %copy-done.10), kind=kLoop, calls=%fused_computation.3 | loop fusion | flops 1572864 | bytes 1966080 | tf_op jit(solution)/shard_map/convert_element_type | solution.py:233
  94.8 15.2 %all-to-all-start.2 = ((bf16[16,32,384]{2,1,0:T(8,128)(2,1)}), bf16[16,32,384]{2,1,0:T(8,128)(2,1)S(1)}, u32[]{:S(2)}, u32[]{:S(2)}) async-start(bf16[16,32,384]{2,1,0:T(8,128)(2,1)} %add_convert_fusion), calls=%async_computation.2 | async-start | bytes 786432 | tf_op jit(solution)/shard_map/all_to_all | solution.py:234
  110.1 0.1 pad_maximum_fusion.1
  110.1 3.8 %collective-permute-start.10 = (bf16[192,2048]{1,0:T(8,128)(2,1)S(1)}, bf16[192,2048]{1,0:T(8,128)(2,1)S(1)}, u32[]{:S(2)}, u32[]{:S(2)}) collective-permute-start(bf16[192,2048]{1,0:T(8,128)(2,1)S(1)} %pad_maximum_fusion.1), channel_id=1, source_target_pairs={{0,1},{1,0},{2,3},{3,2},{4,5},{5,4},{6,7},{7,6},{8,9},{9,8},{10,11... | collective-permute-start | bytes 2359304 | tf_op jit(solution)/shard_map/ppermute | solution.py:239
  113.9 0.1 pad_maximum_fusion
  114.0 1.9 %collective-permute-start.9 = (bf16[192,2048]{1,0:T(8,128)(2,1)S(1)}, bf16[192,2048]{1,0:T(8,128)(2,1)S(1)}, u32[]{:S(2)}, u32[]{:S(2)}) collective-permute-start(bf16[192,2048]{1,0:T(8,128)(2,1)S(1)} %pad_maximum_fusion), channel_id=1, source_target_pairs={{0,4},{2,6},{4,0},{6,2},{1,5},{3,7},{5,1},{7,3},{8,12},{10,14},{12... | collective-permute-start | bytes 2359304 | tf_op jit(solution)/shard_map/ppermute | solution.py:238
  115.9 1.7 %place_first.1.partial = bf16[768,2048]{1,0:T(8,128)(2,1)} custom-call(s32[5]{0:T(128)S(1)} %stack.19.place, bf16[96,2048]{1,0:T(8,128)(2,1)S(1)} %fusion.own, bf16[96,2048]{1,0:T(8,128)(2,1)S(1)} %collective-permute-done.6.near, bf16[96,2048]{1,0:T(8,128)(2,1)S(1)} %collective-permute-done.7.below, bf16[96,2048]{1,0:T(8,128)(2,1)S(1)} %collective-permute-done.8.above), custom_call_target="tpu_custom_call" | custom-call | tf_op jit(solution)/shard_map/place_first/pallas_call | solution.py:241
  117.6 12.3 %collective-permute-done.10.beside = bf16[192,2048]{1,0:T(8,128)(2,1)S(1)} collective-permute-done((bf16[192,2048]{1,0:T(8,128)(2,1)S(1)}, bf16[192,2048]{1,0:T(8,128)(2,1)S(1)}, u32[]{:S(2)}, u32[]{:S(2)}) %collective-permute-start.10) | collective-permute-done | bytes 786464 | tf_op jit(solution)/shard_map/ppermute | solution.py:239
  130.0 5.0 %collective-permute-done.9.across = bf16[192,2048]{1,0:T(8,128)(2,1)S(1)} collective-permute-done((bf16[192,2048]{1,0:T(8,128)(2,1)S(1)}, bf16[192,2048]{1,0:T(8,128)(2,1)S(1)}, u32[]{:S(2)}, u32[]{:S(2)}) %collective-permute-start.9) | collective-permute-done | bytes 786464 | tf_op jit(solution)/shard_map/ppermute | solution.py:238
  134.9 1.7 %place_last.1 = bf16[768,2048]{1,0:T(8,128)(2,1)} custom-call(s32[5]{0:T(128)S(1)} %stack.19.place, bf16[768,2048]{1,0:T(8,128)(2,1)} %place_first.1.partial, bf16[192,2048]{1,0:T(8,128)(2,1)S(1)} %collective-permute-done.9.across, bf16[192,2048]{1,0:T(8,128)(2,1)S(1)} %collective-permute-done.10.beside), custom_call_target="tpu_custom_call", output_to_operand_aliasing={{}: (1, {})} | custom-call | tf_op jit(solution)/shard_map/place_last/pallas_call | solution.py:250
  136.7 0.1 convert_reduce_fusion
  136.7 0.6 broadcast_multiply_fusion
  (27 shorter events, 0.1 us)
Async XLA Ops:
  1.4 1.1 copy-start.4
  2.4 1.0 copy-start.5
  4.1 0.7 copy-start.8
  4.8 11.8 %collective-permute-start = (bf16[384,256]{1,0:T(8,128)(2,1)S(1)}, bf16[384,256]{1,0:T(8,128)(2,1)S(1)}, u32[]{:S(2)}, u32[]{:S(2)}) collective-permute-start(bf16[384,256]{1,0:T(8,128)(2,1)S(1)} %get-tuple-element.16), channel_id=1, source_target_pairs={{0,1},{1,0},{2,3},{3,2},{4,5},{5,4},{6,7},{7,6},{8,9},{9,8},{10,11... | collective-permute-start | bytes 589832 | tf_op jit(solution)/shard_map/ppermute | solution.py:159
  9.7 25.7 %collective-permute-start.2 = (bf16[1024,384]{1,0:T(8,128)(2,1)}, bf16[1024,384]{1,0:T(8,128)(2,1)}, u32[]{:S(2)}, u32[]{:S(2)}) collective-permute-start(bf16[1024,384]{1,0:T(8,128)(2,1)} %dynamic-slice_bitcast_fusion.1), channel_id=1, source_target_pairs={{0,17},{17,0},{1,16},{16,1},{2,19},{19,2},{3,18},{18,3},{4,21},{21... | collective-permute-start | bytes 2359304 | tf_op jit(solution)/shard_map/ppermute | solution.py:171
  18.4 3.7 %copy-start.1 = (bf16[384,2048]{1,0:T(8,128)(2,1)S(1)}, bf16[384,2048]{1,0:T(8,128)(2,1)}, u32[]{:S(2)}) copy-start(bf16[384,2048]{1,0:T(8,128)(2,1)} %up_own.1) | copy-start | bytes 4718596
  18.4 24.5 %all-to-all-start = ((bf16[4,2,384,256]{3,2,1,0:T(8,128)(2,1)}), bf16[4,2,384,256]{3,2,1,0:T(8,128)(2,1)S(1)}, u32[]{:S(2)}, u32[]{:S(2)}) async-start(bf16[4,2,384,256]{3,2,1,0:T(8,128)(2,1)} %spread.1), calls=%async_computation | async-start | bytes 3145728 | tf_op jit(solution)/shard_map/all_to_all | solution.py:168
  22.1 3.4 %copy-start.9 = (bf16[384,384]{1,0:T(8,128)(2,1)S(1)}, bf16[384,384]{1,0:T(8,128)(2,1)}, u32[]{:S(2)}) copy-start(bf16[384,384]{1,0:T(8,128)(2,1)} %copy-done.8) | copy-start | bytes 884740
  22.2 16.0 %collective-permute-start.4 = (bf16[192,2048]{1,0:T(8,128)(2,1)S(1)}, bf16[192,2048]{1,0:T(8,128)(2,1)}, u32[]{:S(2)}, u32[]{:S(2)}) collective-permute-start(bf16[192,2048]{1,0:T(8,128)(2,1)S(1)} %dynamic-slice_bitcast_fusion), channel_id=1, source_target_pairs={{0,1},{1,0},{8,25},{9,24},{16,17},{17,16},{24,9},{25,8},{2,3},{3,2... | collective-permute-start | bytes 2359304 | tf_op jit(solution)/shard_map/ppermute | solution.py:172
  25.5 16.7 %collective-permute-start.1 = (bf16[384,384]{1,0:T(8,128)(2,1)S(1)}, bf16[384,384]{1,0:T(8,128)(2,1)S(1)}, u32[]{:S(2)}, u32[]{:S(2)}) collective-permute-start(bf16[384,384]{1,0:T(8,128)(2,1)S(1)} %copy-done.9), channel_id=1, source_target_pairs={{0,1},{1,0},{2,3},{3,2},{4,5},{5,4},{6,7},{7,6},{8,9},{9,8},{10,11... | collective-permute-start | bytes 884744 | tf_op jit(solution)/shard_map/ppermute | solution.py:169
  35.4 16.2 %collective-permute-start.3 = (bf16[1024,384]{1,0:T(8,128)(2,1)}, bf16[1024,384]{1,0:T(8,128)(2,1)}, u32[]{:S(2)}, u32[]{:S(2)}) collective-permute-start(bf16[1024,384]{1,0:T(8,128)(2,1)} %collective-permute-done.2.down_mine), channel_id=1, source_target_pairs={{0,8},{8,0},{1,9},{9,1},{2,10},{10,2},{3,11},{11,3},{4,12},{12,4},... | collective-permute-start | bytes 2359304 | tf_op jit(solution)/shard_map/ppermute | solution.py:175
  38.2 13.4 %collective-permute-start.5 = (bf16[192,2048]{1,0:T(8,128)(2,1)}, bf16[192,2048]{1,0:T(8,128)(2,1)}, u32[]{:S(2)}, u32[]{:S(2)}) collective-permute-start(bf16[192,2048]{1,0:T(8,128)(2,1)} %collective-permute-done.4.up_mine), channel_id=1, source_target_pairs={{0,8},{8,0},{1,9},{9,1},{2,10},{10,2},{3,11},{11,3},{4,12},{12,4},... | collective-permute-start | bytes 2359304 | tf_op jit(solution)/shard_map/ppermute | solution.py:176
  42.2 0.7 copy-start.6
  42.9 1.0 copy-start.7
  43.9 6.7 %copy-start = (bf16[2048,384]{1,0:T(8,128)(2,1)S(1)}, bf16[2048,384]{1,0:T(8,128)(2,1)}, u32[]{:S(2)}) copy-start(bf16[2048,384]{1,0:T(8,128)(2,1)} %down.1) | copy-start | bytes 4718596
  47.5 1.2 copy-start.2
  48.7 13.2 %collective-permute-start.11 = (bf16[4,16,32,384]{3,2,1,0:T(8,128)(2,1)}, bf16[4,16,32,384]{3,2,1,0:T(8,128)(2,1)}, u32[]{:S(2)}, u32[]{:S(2)}) collective-permute-start(bf16[4,16,32,384]{3,2,1,0:T(8,128)(2,1)} %get-tuple-element.23), channel_id=1, source_target_pairs={{0,8},{8,0},{1,9},{9,1},{2,10},{10,2},{3,11},{11,3},{4,12},{12,4},... | collective-permute-start | bytes 4718600 | tf_op jit(solution)/shard_map/ppermute | solution.py:220
  57.2 4.6 %copy-start.3 = (bf16[4,16,32,384]{3,2,1,0:T(8,128)(2,1)S(1)}, bf16[4,16,32,384]{3,2,1,0:T(8,128)(2,1)}, u32[]{:S(2)}) copy-start(bf16[4,16,32,384]{3,2,1,0:T(8,128)(2,1)} %copy-done.2) | copy-start | bytes 4718596
  57.2 26.0 %all-to-all-start.1 = ((bf16[4,96,2048]{2,1,0:T(8,128)(2,1)}), bf16[4,96,2048]{2,1,0:T(8,128)(2,1)S(1)}, u32[]{:S(2)}, u32[]{:S(2)}) async-start(bf16[4,96,2048]{2,1,0:T(8,128)(2,1)} %bitcast.9), calls=%async_computation.1 | async-start | bytes 3145728 | tf_op jit(solution)/shard_map/all_to_all | solution.py:217
  64.6 23.4 %collective-permute-start.12 = (bf16[16,32,384]{2,1,0:T(8,128)(2,1)}, bf16[16,32,384]{2,1,0:T(8,128)(2,1)}, u32[]{:S(2)}, u32[]{:S(2)}) collective-permute-start(bf16[16,32,384]{2,1,0:T(8,128)(2,1)} %get-tuple-element.30), channel_id=1, source_target_pairs={{0,1},{1,0},{2,3},{3,2},{4,5},{5,4},{6,7},{7,6},{8,9},{9,8},{10,11... | collective-permute-start | bytes 1179656 | tf_op jit(solution)/shard_map/ppermute | solution.py:223
  66.7 26.0 %collective-permute-start.13 = (bf16[16,32,384]{2,1,0:T(8,128)(2,1)}, bf16[16,32,384]{2,1,0:T(8,128)(2,1)}, u32[]{:S(2)}, u32[]{:S(2)}) collective-permute-start(bf16[16,32,384]{2,1,0:T(8,128)(2,1)} %get-tuple-element.29), channel_id=1, source_target_pairs={{0,17},{17,0},{1,16},{16,1},{2,19},{19,2},{3,18},{18,3},{4,21},{21... | collective-permute-start | bytes 1179656 | tf_op jit(solution)/shard_map/ppermute | solution.py:224
  69.6 23.1 %collective-permute-start.14 = (bf16[16,32,384]{2,1,0:T(8,128)(2,1)}, bf16[16,32,384]{2,1,0:T(8,128)(2,1)}, u32[]{:S(2)}, u32[]{:S(2)}) collective-permute-start(bf16[16,32,384]{2,1,0:T(8,128)(2,1)} %get-tuple-element.28), channel_id=1, source_target_pairs={{0,16},{16,0},{1,17},{17,1},{2,18},{18,2},{3,19},{19,3},{4,20},{20... | collective-permute-start | bytes 1179656 | tf_op jit(solution)/shard_map/ppermute | solution.py:225
  83.2 9.4 %copy-start.10 = (bf16[16,32,384]{2,1,0:T(8,128)(2,1)S(1)}, bf16[16,32,384]{2,1,0:T(8,128)(2,1)}, u32[]{:S(2)}) copy-start(bf16[16,32,384]{2,1,0:T(8,128)(2,1)} %get-tuple-element.24) | copy-start | bytes 1179652
  83.5 26.6 %collective-permute-start.6 = (bf16[96,2048]{1,0:T(8,128)(2,1)S(1)}, bf16[96,2048]{1,0:T(8,128)(2,1)S(1)}, u32[]{:S(2)}, u32[]{:S(2)}) collective-permute-start(bf16[96,2048]{1,0:T(8,128)(2,1)S(1)} %fusion.own), channel_id=1, source_target_pairs={{0,1},{1,0},{2,3},{3,2},{4,5},{5,4},{6,7},{7,6},{8,9},{9,8},{10,11... | collective-permute-start | bytes 1179656 | tf_op jit(solution)/shard_map/ppermute | solution.py:228
  85.5 24.5 %collective-permute-start.7 = (bf16[96,2048]{1,0:T(8,128)(2,1)S(1)}, bf16[96,2048]{1,0:T(8,128)(2,1)S(1)}, u32[]{:S(2)}, u32[]{:S(2)}) collective-permute-start(bf16[96,2048]{1,0:T(8,128)(2,1)S(1)} %fusion.own), channel_id=1, source_target_pairs={{0,2},{2,4},{4,6},{6,0},{1,3},{3,5},{5,7},{7,1},{8,10},{10,12},{12... | collective-permute-start | bytes 1179656 | tf_op jit(solution)/shard_map/ppermute | solution.py:229
  88.0 22.0 %collective-permute-start.8 = (bf16[96,2048]{1,0:T(8,128)(2,1)S(1)}, bf16[96,2048]{1,0:T(8,128)(2,1)S(1)}, u32[]{:S(2)}, u32[]{:S(2)}) collective-permute-start(bf16[96,2048]{1,0:T(8,128)(2,1)S(1)} %fusion.own), channel_id=1, source_target_pairs={{0,6},{2,0},{4,2},{6,4},{1,7},{3,1},{5,3},{7,5},{8,14},{10,8},{12,... | collective-permute-start | bytes 1179656 | tf_op jit(solution)/shard_map/ppermute | solution.py:230
  94.8 41.8 %all-to-all-start.2 = ((bf16[16,32,384]{2,1,0:T(8,128)(2,1)}), bf16[16,32,384]{2,1,0:T(8,128)(2,1)S(1)}, u32[]{:S(2)}, u32[]{:S(2)}) async-start(bf16[16,32,384]{2,1,0:T(8,128)(2,1)} %add_convert_fusion), calls=%async_computation.2 | async-start | bytes 786432 | tf_op jit(solution)/shard_map/all_to_all | solution.py:234
  110.1 19.8 %collective-permute-start.10 = (bf16[192,2048]{1,0:T(8,128)(2,1)S(1)}, bf16[192,2048]{1,0:T(8,128)(2,1)S(1)}, u32[]{:S(2)}, u32[]{:S(2)}) collective-permute-start(bf16[192,2048]{1,0:T(8,128)(2,1)S(1)} %pad_maximum_fusion.1), channel_id=1, source_target_pairs={{0,1},{1,0},{2,3},{3,2},{4,5},{5,4},{6,7},{7,6},{8,9},{9,8},{10,11... | collective-permute-start | bytes 2359304 | tf_op jit(solution)/shard_map/ppermute | solution.py:239
  114.0 20.9 %collective-permute-start.9 = (bf16[192,2048]{1,0:T(8,128)(2,1)S(1)}, bf16[192,2048]{1,0:T(8,128)(2,1)S(1)}, u32[]{:S(2)}, u32[]{:S(2)}) collective-permute-start(bf16[192,2048]{1,0:T(8,128)(2,1)S(1)} %pad_maximum_fusion), channel_id=1, source_target_pairs={{0,4},{2,6},{4,0},{6,2},{1,5},{3,7},{5,1},{7,3},{8,12},{10,14},{12... | collective-permute-start | bytes 2359304 | tf_op jit(solution)/shard_map/ppermute | solution.py:238

commit v5 on v4

--- a/solution.py
+++ b/solution.py
@@ -6,7 +6,7 @@
 from jax.sharding import Mesh
 from jax.sharding import PartitionSpec as P
 
-DP = ("z", "xh", "core")
+DP = ("zh", "zl", "xh", "core")
 REP = ("y", "xl")
 RING = ("xh", "xl")
 NEAR = [(0, 1), (1, 0)]
@@ -16,24 +16,29 @@
 VMEM = pl.BlockSpec(memory_space=pltpu.VMEM)
 SMEM = pl.BlockSpec(memory_space=pltpu.SMEM)
 ANY = pl.BlockSpec(memory_space=pl.ANY)
-LIMIT = 40 * 1024 * 1024
+LIMIT = 12 * 1024 * 1024
 
 
 def dot(a, b):
     return jnp.dot(a, b, preferred_element_type=jnp.float32)
 
 
-def split_kernel(place, grad_out, pre_act, own_set, other_set, pre_own, pre_sent):
+def split_kernel(place, whole, own, other):
+    xl = place[2]
+    part = own.shape[0] // 4
+    for y in range(4):
+        for x, out in ((xl, own), (1 - xl, other)):
+            out[y * part:(y + 1) * part, :] = whole[pl.ds(pl.multiple_of((y * 2 + x) * part, 16), part), :]
+
+
+def live_kernel(place, whole, own, other):
     xl, live = place[2], place[3]
-    part = own_set.shape[0] // 4
+    part = own.shape[0] // 4
     for y in range(4):
-        to = slice(y * part, (y + 1) * part)
-        for x, grads, pre in ((xl, own_set, pre_own), (1 - xl, other_set, pre_sent)):
+        for x, out in ((xl, own), (1 - xl, other)):
             first = pl.multiple_of((y * 2 + x) * part, 16)
-            at = pl.ds(first, part)
-            row = first + lax.broadcasted_iota(jnp.int32, (part, grads.shape[1]), 0)
-            grads[to, :] = jnp.where(row < live, grad_out[at, :], 0).astype(grads.dtype)
-            pre[to, :] = pre_act[at, :]
+            row = first + lax.broadcasted_iota(jnp.int32, (part, out.shape[1]), 0)
+            out[y * part:(y + 1) * part, :] = jnp.where(row < live, whole[pl.ds(first, part), :], 0).astype(out.dtype)
 
 
 def spread_kernel(place, own_set, near_set, out):
@@ -83,7 +88,8 @@
             grads[j], hidden, (((0,), (0,)), ((), ())), preferred_element_type=jnp.float32
         ).astype(kept.dtype)
         for g in range(groups):
-            z = j * groups + g
+            zh, zl = divmod(j * groups + g, 4)
+            z = zl * (kept.shape[1] // 4) + zh
             for h in range(2):
                 first = (g * 4 + h * 2) * share
                 low = block[first:first + share, :]
@@ -94,6 +100,11 @@
                     kind = t * 2 + jnp.abs(xh - h)
                     kept[kind, z] = mine[:, t * units:(t + 1) * units]
                     sent[kind, z] = other[:, t * units:(t + 1) * units]
+
+
+def ring_kernel(own, near, far, across, out):
+    total = own[...].astype(jnp.float32) + near[...].astype(jnp.float32)
+    out[...] = (total + far[...].astype(jnp.float32) + across[...].astype(jnp.float32)).astype(out.dtype)
 
 
 def put(place, blocks, out, sems):
@@ -133,7 +144,7 @@
 def on_device(grad_out, pre_act, up_weight, down_weight, slot_counts):
     slot_rows, features = grad_out.shape
     hidden_units = pre_act.shape[1]
-    ys, zs = lax.axis_size("y"), lax.axis_size("z")
+    ys, zs = lax.axis_size("y"), lax.axis_size(("zh", "zl"))
     reps = 2 * ys
     width = features * reps
     rows = slot_rows // reps
@@ -148,14 +159,22 @@
     params = pltpu.CompilerParams(vmem_limit_bytes=LIMIT)
     set_shape = jax.ShapeDtypeStruct((half_rows, features), bf16)
     pre_shape = jax.ShapeDtypeStruct((half_rows, hidden_units), bf16)
-    own_set, other_set, pre_own, pre_sent = pl.pallas_call(
+    own_set, other_set = pl.pallas_call(
+        live_kernel,
+        out_shape=(set_shape, set_shape),
+        in_specs=[SMEM, VMEM],
+        out_specs=(VMEM, VMEM),
+        compiler_params=params,
+        name="live_sets",
+    )(place, grad_out)
+    pre_own, pre_sent = pl.pallas_call(
         split_kernel,
-        out_shape=(set_shape, set_shape, pre_shape, pre_shape),
-        in_specs=[SMEM] + [VMEM] * 2,
-        out_specs=(VMEM,) * 4,
-        compiler_params=params,
-        name="split",
-    )(place, grad_out, pre_act)
+        out_shape=(pre_shape, pre_shape),
+        in_specs=[SMEM, VMEM],
+        out_specs=(VMEM, VMEM),
+        compiler_params=params,
+        name="pre_sets",
+    )(place, pre_act)
     near_set = lax.ppermute(other_set, "xl", NEAR)
     grads = pl.pallas_call(
         spread_kernel,
@@ -200,6 +219,21 @@
         name="down_terms",
     )(place, grads, pre_own, pre_far)
 
+    share = width // (4 * zs)
+    laid_out = jax.ShapeDtypeStruct((4, zs, share, hidden_units), bf16)
+    kept, sent = pl.pallas_call(
+        down_kernel,
+        out_shape=(laid_out, laid_out),
+        in_specs=[SMEM] + [VMEM] * 3,
+        out_specs=(VMEM, VMEM),
+        compiler_params=pltpu.CompilerParams(vmem_limit_bytes=LIMIT),
+        cost_estimate=pl.CostEstimate(
+            flops=4 * half_rows * width * hidden_units, bytes_accessed=8 * width * hidden_units, transcendentals=0
+        ),
+        name="down_terms",
+    )(place, grads, pre_own, pre_far)
+
+    pre_later, sent = lax.optimization_barrier((pre_far, sent))
     terms = pl.pallas_call(
         terms_kernel,
         out_shape=jax.ShapeDtypeStruct((half_rows, width), bf16),
@@ -211,7 +245,7 @@
             flops=6 * half_rows * width * hidden_units, bytes_accessed=12 * width * hidden_units, transcendentals=0
         ),
         name="terms",
-    )(place, grads, pre_grad, pre_far, down_mine, down_other, up_weight, up_mine, up_other)
+    )(place, grads, pre_grad, pre_later, down_mine, down_other, up_weight, up_mine, up_other)
 
     f32 = jnp.float32
     came = lax.all_to_all(terms.reshape(ys, rows, width), "y", 0, 0, tiled=True)
@@ -230,9 +264,24 @@
     above = lax.ppermute(own, "y", turn(-1))
 
     own_chip, ring, _ = lax.optimization_barrier((chip[0].astype(bf16), ring, own))
-    ring_sum = (own_chip.astype(f32) + sum(part.astype(f32) for part in ring)).astype(bf16)
-    z_terms = lax.all_to_all(ring_sum, "z", 0, 0, tiled=True)
-    down_grad = jnp.sum(z_terms.astype(f32), axis=0) / (4 * zs)
+    ring_sum = pl.pallas_call(
+        ring_kernel,
+        out_shape=jax.ShapeDtypeStruct((zs, share, hidden_units), bf16),
+        in_specs=[VMEM] * 4,
+        out_specs=VMEM,
+        compiler_params=params,
+        cost_estimate=pl.CostEstimate(flops=2 * width * hidden_units, bytes_accessed=10 * width * hidden_units, transcendentals=0),
+        name="ring_sum",
+    )(own_chip, *ring)
+    low_terms = lax.all_to_all(ring_sum, "zl", 0, 0, tiled=True).reshape(4, zs // 4, share, hidden_units)
+    low_sum = sum(low_terms[i].astype(f32) for i in range(4))
+    highs = zs // 4
+    high = lax.axis_index("zh")
+    high_sum = own_part(low_sum, high, 0)
+    for step in range(1, highs):
+        part = own_part(low_sum, lax.rem(high + step, highs), 0)
+        high_sum += lax.ppermute(part, "zh", [(i, (i + step) % highs) for i in range(highs)])
+    down_grad = high_sum / (4 * zs)
 
     near, below, above = lax.optimization_barrier((near, below, above))
     across = lax.ppermute(jnp.concatenate([own, near]), "y", turn(2))
@@ -263,7 +312,7 @@
 def solution(mesh):
     zs = mesh.shape["dp"] // 4
     ys = mesh.shape["rep"] // 2
-    finer = Mesh(mesh.devices.reshape(zs, 2, 2, ys, 2), (*DP, *REP))
+    finer = Mesh(mesh.devices.reshape(zs // 4, 4, 2, 2, ys, 2), (*DP, *REP))
     in_specs = (P(DP, REP), P(DP, REP), P(REP, None), P(None, REP), P(DP))
     out_specs = (P(DP, None), P(DP, REP))
     return jax.shard_map(

time: 139 us -> 145 us (1.043)
  the two profiles are of different devices: /device:TPU:6 before, /device:TPU:40 now
where the time goes in v5:
time: 145 us; the launch traced here: 144 us
  starting transfers between devices  89.6 us (62%)
  waiting for transfers between devices  20 us (14%)
  Pallas kernels  17.6 us (12%)
  other arithmetic  8.66 us (6%)
  local copies, waits for them, and re-layouts  6.1 us (4%)
  between operations  1.66 us (1%)
    ppermute x3, starting transfers between devices, on_device(): lax.ppermute(part, 'zh', [(i, (i + step) % highs) for i in range(highs)])  24.6 us
    all_to_all x1, waiting for transfers between devices, on_device(): came = lax.all_to_all(terms.reshape(ys, rows, width), 'y', 0, 0, tiled=True)  7.74 us
    ppermute x1, starting transfers between devices, on_device(): across = lax.ppermute(jnp.concatenate([own, near]), 'y', turn(2))  6.23 us
    all_to_all x1, starting transfers between devices, on_device(): lax.all_to_all(ring_sum, 'zl', 0, 0, tiled=True)  6 us
    pallas_call x1, Pallas kernels, on_device(): pl.pallas_call(terms_kernel, out_shape=jax.ShapeDtypeStruct((half_rows, w...  5.64 us
    ppermute x1, waiting for transfers between devices, on_device(): lax.ppermute(own_part(down_weight.reshape(2, width // 2, hidden_units), c...  5.64 us
    all_to_all x1, starting transfers between devices, on_device(): came = lax.all_to_all(terms.reshape(ys, rows, width), 'y', 0, 0, tiled=True)  5.05 us
    all_to_all x1, starting transfers between devices, on_device(): lax.all_to_all(grads, 'y', 0, 0, tiled=True)  5.04 us
  transfers between devices with their start and end apart: 21, of which 5 were waited for; matrix products, arithmetic and copies ran while one was open for 7% of the time, Pallas kernels for 12%

profile of v5, /device:TPU:40, one launch (start us, length us, event | category | flops | bytes accessed | tf_op | source)
XLA Modules:
  0.0 143.7 jit_solution(14140304696119776914)
XLA Ops:
  1.3 0.1 stack.19.place
  1.4 1.0 copy-done.5
  2.4 0.6 live_sets.1
  3.0 3.4 %collective-permute-start = (bf16[384,256]{1,0:T(8,128)(2,1)S(1)}, bf16[384,256]{1,0:T(8,128)(2,1)S(1)}, u32[]{:S(2)}, u32[]{:S(2)}) collective-permute-start(bf16[384,256]{1,0:T(8,128)(2,1)S(1)} %get-tuple-element.18), channel_id=1, source_target_pairs={{0,1},{1,0},{2,3},{3,2},{4,5},{5,4},{6,7},{7,6},{8,9},{9,8},{10,11... | collective-permute-start | bytes 589832 | tf_op jit(solution)/shard_map/ppermute | solution.py:178
  6.4 2.1 %dynamic-slice_bitcast_fusion.1 = bf16[1024,384]{1,0:T(8,128)(2,1)} fusion(bf16[2,1024,384]{2,1,0:T(8,128)(2,1)} %bitcast.39, s32[]{:T(128)S(6)} %select_n.19), kind=kLoop, calls=%fused_computation.8 | loop fusion | bytes 1572868 | tf_op jit(solution)/shard_map/jit(dynamic_index_in_dim)/squeeze | solution.py:141
  8.5 4.0 %collective-permute-start.2 = (bf16[1024,384]{1,0:T(8,128)(2,1)}, bf16[1024,384]{1,0:T(8,128)(2,1)}, u32[]{:S(2)}, u32[]{:S(2)}) collective-permute-start(bf16[1024,384]{1,0:T(8,128)(2,1)} %dynamic-slice_bitcast_fusion.1), channel_id=1, source_target_pairs={{0,17},{17,0},{1,16},{16,1},{2,19},{19,2},{3,18},{18,3},{4,21},{21... | collective-permute-start | bytes 2359304 | tf_op jit(solution)/shard_map/ppermute | solution.py:190
  12.5 1.8 %spread.1 = bf16[4,2,384,256]{3,2,1,0:T(8,128)(2,1)} custom-call(s32[5]{0:T(128)S(1)} %stack.19.place, bf16[384,256]{1,0:T(8,128)(2,1)S(1)} %get-tuple-element.17.own_set, bf16[384,256]{1,0:T(8,128)(2,1)S(1)} %collective-permute-done.near_set), custom_call_target="tpu_custom_call" | custom-call | tf_op jit(solution)/shard_map/spread/pallas_call | solution.py:179
  14.3 5.0 %all-to-all-start = ((bf16[4,2,384,256]{3,2,1,0:T(8,128)(2,1)}), bf16[4,2,384,256]{3,2,1,0:T(8,128)(2,1)S(1)}, u32[]{:S(2)}, u32[]{:S(2)}) async-start(bf16[4,2,384,256]{3,2,1,0:T(8,128)(2,1)} %spread.1), calls=%async_computation | async-start | bytes 3145728 | tf_op jit(solution)/shard_map/all_to_all | solution.py:187
  19.3 0.1 dynamic-slice_bitcast_fusion
  19.4 2.6 %collective-permute-start.4 = (bf16[192,2048]{1,0:T(8,128)(2,1)S(1)}, bf16[192,2048]{1,0:T(8,128)(2,1)}, u32[]{:S(2)}, u32[]{:S(2)}) collective-permute-start(bf16[192,2048]{1,0:T(8,128)(2,1)S(1)} %dynamic-slice_bitcast_fusion), channel_id=1, source_target_pairs={{0,1},{1,0},{8,25},{9,24},{16,17},{17,16},{24,9},{25,8},{2,3},{3,2... | collective-permute-start | bytes 2359304 | tf_op jit(solution)/shard_map/ppermute | solution.py:191
  22.1 0.6 pre_sets.1
  22.7 0.7 copy-done.6
  23.4 3.3 %collective-permute-start.1 = (bf16[384,384]{1,0:T(8,128)(2,1)S(1)}, bf16[384,384]{1,0:T(8,128)(2,1)S(1)}, u32[]{:S(2)}, u32[]{:S(2)}) collective-permute-start(bf16[384,384]{1,0:T(8,128)(2,1)S(1)} %get-tuple-element.20), channel_id=1, source_target_pairs={{0,1},{1,0},{2,3},{3,2},{4,5},{5,4},{6,7},{7,6},{8,9},{9,8},{10,11... | collective-permute-start | bytes 884744 | tf_op jit(solution)/shard_map/ppermute | solution.py:188
  26.7 5.6 %collective-permute-done.2.down_mine = bf16[1024,384]{1,0:T(8,128)(2,1)} collective-permute-done((bf16[1024,384]{1,0:T(8,128)(2,1)}, bf16[1024,384]{1,0:T(8,128)(2,1)}, u32[]{:S(2)}, u32[]{:S(2)}) %collective-permute-start.2) | collective-permute-done | bytes 786464 | tf_op jit(solution)/shard_map/ppermute | solution.py:190
  32.4 1.9 %collective-permute-start.3 = (bf16[1024,384]{1,0:T(8,128)(2,1)}, bf16[1024,384]{1,0:T(8,128)(2,1)}, u32[]{:S(2)}, u32[]{:S(2)}) collective-permute-start(bf16[1024,384]{1,0:T(8,128)(2,1)} %collective-permute-done.2.down_mine), channel_id=1, source_target_pairs={{0,8},{8,0},{1,9},{9,1},{2,10},{10,2},{3,11},{11,3},{4,12},{12,4},... | collective-permute-start | bytes 2359304 | tf_op jit(solution)/shard_map/ppermute | solution.py:194
  34.3 2.4 %collective-permute-done.4.up_mine = bf16[192,2048]{1,0:T(8,128)(2,1)} collective-permute-done((bf16[192,2048]{1,0:T(8,128)(2,1)S(1)}, bf16[192,2048]{1,0:T(8,128)(2,1)}, u32[]{:S(2)}, u32[]{:S(2)}) %collective-permute-start.4) | collective-permute-done | bytes 786464 | tf_op jit(solution)/shard_map/ppermute | solution.py:191
  36.7 4.4 %collective-permute-start.5 = (bf16[192,2048]{1,0:T(8,128)(2,1)}, bf16[192,2048]{1,0:T(8,128)(2,1)}, u32[]{:S(2)}, u32[]{:S(2)}) collective-permute-start(bf16[192,2048]{1,0:T(8,128)(2,1)} %collective-permute-done.4.up_mine), channel_id=1, source_target_pairs={{0,8},{8,0},{1,9},{9,1},{2,10},{10,2},{3,11},{11,3},{4,12},{12,4},... | collective-permute-start | bytes 2359304 | tf_op jit(solution)/shard_map/ppermute | solution.py:195
  41.1 1.0 copy-done.7
  42.0 3.6 %down_terms.1 = (bf16[4,16,32,384]{3,2,1,0:T(8,128)(2,1)S(1)}, bf16[4,16,32,384]{3,2,1,0:T(8,128)(2,1)}) custom-call(s32[5]{0:T(128)S(1)} %stack.19.place, bf16[8,384,256]{2,1,0:T(8,128)(2,1)S(1)} %bitcast.36, bf16[384,384]{1,0:T(8,128)(2,1)S(1)} %copy-done.7, bf16[384,384]{1,0:T(8,128)(2,1)S(1)} %collective-permute-done.1.pre_far), custom_call_target="tpu_custom_call" | custom-call | flops 1207959552 | bytes 6291456 | tf_op jit(solution)/shard_map/down_terms/pallas_call | solution.py:224
  45.6 1.2 copy-done.2
  46.8 1.9 %collective-permute-start.11 = (bf16[4,16,32,384]{3,2,1,0:T(8,128)(2,1)}, bf16[4,16,32,384]{3,2,1,0:T(8,128)(2,1)}, u32[]{:S(2)}, u32[]{:S(2)}) collective-permute-start(bf16[4,16,32,384]{3,2,1,0:T(8,128)(2,1)} %get-tuple-element.27), channel_id=1, source_target_pairs={{0,8},{8,0},{1,9},{9,1},{2,10},{10,2},{3,11},{11,3},{4,12},{12,4},... | collective-permute-start | bytes 4718600 | tf_op jit(solution)/shard_map/ppermute | solution.py:254
  48.7 1.0 own_grad.1.own
  49.7 5.6 %terms.1 = bf16[384,2048]{1,0:T(8,128)(2,1)} custom-call(s32[5]{0:T(128)S(1)} %stack.19.place, bf16[8,384,256]{2,1,0:T(8,128)(2,1)S(1)} %bitcast.38, bf16[384,384]{1,0:T(8,128)(2,1)S(1)} %own_grad.1.own, bf16[384,384]{1,0:T(8,128)(2,1)S(1)} %collective-permute-done.1.pre_far, bf16[1024,384]{1,0:T(8,128)(2,1)} %collective-permute-done.2.down_mine, ...), custom_call_target="tpu_custom_call" | custom-call | flops 1811939328 | bytes 9437184 | tf_op jit(solution)/shard_map/terms/pallas_call | solution.py:237
  55.4 5.1 %all-to-all-start.1 = ((bf16[4,96,2048]{2,1,0:T(8,128)(2,1)}), bf16[4,96,2048]{2,1,0:T(8,128)(2,1)}, u32[]{:S(2)}, u32[]{:S(2)}) async-start(bf16[4,96,2048]{2,1,0:T(8,128)(2,1)} %bitcast.9), calls=%async_computation.1 | async-start | bytes 3145728 | tf_op jit(solution)/shard_map/all_to_all | solution.py:251
  60.4 2.6 %fusion.4 = (bf16[16,32,384]{2,1,0:T(8,128)(2,1)}, bf16[16,32,384]{2,1,0:T(8,128)(2,1)}, bf16[16,32,384]{2,1,0:T(8,128)(2,1)}, bf16[16,32,384]{2,1,0:T(8,128)(2,1)S(1)}) fusion(bf16[4,16,32,384]{3,2,1,0:T(8,128)(2,1)} %collective-permute-done.11, bf16[4,16,32,384]{3,2,1,0:T(8,128)(2,1)S(1)} %copy-done.3), kind=kLoop, calls=%fused_computation.13 | loop fusion | flops 3145728 | bytes 4718592 | tf_op jit(solution)/shard_map/convert_element_type | solution.py:259
  63.1 1.9 %collective-permute-start.12 = (bf16[16,32,384]{2,1,0:T(8,128)(2,1)}, bf16[16,32,384]{2,1,0:T(8,128)(2,1)S(1)}, u32[]{:S(2)}, u32[]{:S(2)}) collective-permute-start(bf16[16,32,384]{2,1,0:T(8,128)(2,1)} %get-tuple-element.34), channel_id=1, source_target_pairs={{0,1},{1,0},{2,3},{3,2},{4,5},{5,4},{6,7},{7,6},{8,9},{9,8},{10,11... | collective-permute-start | bytes 1179656 | tf_op jit(solution)/shard_map/ppermute | solution.py:257
  65.0 4.2 %collective-permute-start.13 = (bf16[16,32,384]{2,1,0:T(8,128)(2,1)}, bf16[16,32,384]{2,1,0:T(8,128)(2,1)S(1)}, u32[]{:S(2)}, u32[]{:S(2)}) collective-permute-start(bf16[16,32,384]{2,1,0:T(8,128)(2,1)} %get-tuple-element.33), channel_id=1, source_target_pairs={{0,17},{17,0},{1,16},{16,1},{2,19},{19,2},{3,18},{18,3},{4,21},{21... | collective-permute-start | bytes 1179656 | tf_op jit(solution)/shard_map/ppermute | solution.py:258
  69.1 3.7 %collective-permute-start.14 = (bf16[16,32,384]{2,1,0:T(8,128)(2,1)}, bf16[16,32,384]{2,1,0:T(8,128)(2,1)S(1)}, u32[]{:S(2)}, u32[]{:S(2)}) collective-permute-start(bf16[16,32,384]{2,1,0:T(8,128)(2,1)} %get-tuple-element.32), channel_id=1, source_target_pairs={{0,16},{16,0},{1,17},{17,1},{2,18},{18,2},{3,19},{19,3},{4,20},{20... | collective-permute-start | bytes 1179656 | tf_op jit(solution)/shard_map/ppermute | solution.py:259
  72.9 7.7 %all-to-all-done.1 = bf16[4,96,2048]{2,1,0:T(8,128)(2,1)} async-done(((bf16[4,96,2048]{2,1,0:T(8,128)(2,1)}), bf16[4,96,2048]{2,1,0:T(8,128)(2,1)}, u32[]{:S(2)}, u32[]{:S(2)}) %all-to-all-start.1) | async-done | bytes 1572896 | tf_op jit(solution)/shard_map/all_to_all | solution.py:251
  80.6 1.6 %fusion.own = bf16[96,2048]{1,0:T(8,128)(2,1)S(1)} fusion(bf16[4,96,2048]{2,1,0:T(8,128)(2,1)} %all-to-all-done.1), kind=kLoop, calls=%fused_computation.9 | loop fusion | flops 1572864 | bytes 1966080 | tf_op jit(solution)/shard_map/add | solution.py:252
  82.2 1.9 %collective-permute-start.6 = (bf16[96,2048]{1,0:T(8,128)(2,1)S(1)}, bf16[96,2048]{1,0:T(8,128)(2,1)S(1)}, u32[]{:S(2)}, u32[]{:S(2)}) collective-permute-start(bf16[96,2048]{1,0:T(8,128)(2,1)S(1)} %fusion.own), channel_id=1, source_target_pairs={{0,1},{1,0},{2,3},{3,2},{4,5},{5,4},{6,7},{7,6},{8,9},{9,8},{10,11... | collective-permute-start | bytes 1179656 | tf_op jit(solution)/shard_map/ppermute | solution.py:262
  84.1 1.9 %collective-permute-start.7 = (bf16[96,2048]{1,0:T(8,128)(2,1)S(1)}, bf16[96,2048]{1,0:T(8,128)(2,1)S(1)}, u32[]{:S(2)}, u32[]{:S(2)}) collective-permute-start(bf16[96,2048]{1,0:T(8,128)(2,1)S(1)} %fusion.own), channel_id=1, source_target_pairs={{0,2},{2,4},{4,6},{6,0},{1,3},{3,5},{5,7},{7,1},{8,10},{10,12},{12... | collective-permute-start | bytes 1179656 | tf_op jit(solution)/shard_map/ppermute | solution.py:263
  86.1 3.9 %collective-permute-start.8 = (bf16[96,2048]{1,0:T(8,128)(2,1)S(1)}, bf16[96,2048]{1,0:T(8,128)(2,1)S(1)}, u32[]{:S(2)}, u32[]{:S(2)}) collective-permute-start(bf16[96,2048]{1,0:T(8,128)(2,1)S(1)} %fusion.own), channel_id=1, source_target_pairs={{0,6},{2,0},{4,2},{6,4},{1,7},{3,1},{5,3},{7,5},{8,14},{10,8},{12,... | collective-permute-start | bytes 1179656 | tf_op jit(solution)/shard_map/ppermute | solution.py:264
  90.0 0.9 ring_sum.1
  91.0 6.0 %all-to-all-start.2 = ((bf16[16,32,384]{2,1,0:T(8,128)(2,1)}), bf16[16,32,384]{2,1,0:T(8,128)(2,1)}, u32[]{:S(2)}, u32[]{:S(2)}) async-start(bf16[16,32,384]{2,1,0:T(8,128)(2,1)} %ring_sum.1), calls=%async_computation.2 | async-start | bytes 786432 | tf_op jit(solution)/shard_map/all_to_all | solution.py:276
  97.0 1.6 %collective-permute-done.8.above = bf16[96,2048]{1,0:T(8,128)(2,1)S(1)} collective-permute-done((bf16[96,2048]{1,0:T(8,128)(2,1)S(1)}, bf16[96,2048]{1,0:T(8,128)(2,1)S(1)}, u32[]{:S(2)}, u32[]{:S(2)}) %collective-permute-start.8) | collective-permute-done | bytes 393248 | tf_op jit(solution)/shard_map/ppermute | solution.py:264
  98.6 0.9 pad_maximum_fusion.1
  99.6 3.6 %collective-permute-start.10 = (bf16[192,2048]{1,0:T(8,128)(2,1)}, bf16[192,2048]{1,0:T(8,128)(2,1)S(1)}, u32[]{:S(2)}, u32[]{:S(2)}) collective-permute-start(bf16[192,2048]{1,0:T(8,128)(2,1)} %pad_maximum_fusion.1), channel_id=1, source_target_pairs={{0,1},{1,0},{2,3},{3,2},{4,5},{5,4},{6,7},{7,6},{8,9},{9,8},{10,11... | collective-permute-start | bytes 2359304 | tf_op jit(solution)/shard_map/ppermute | solution.py:288
  103.2 0.9 pad_maximum_fusion
  104.1 6.2 %collective-permute-start.9 = (bf16[192,2048]{1,0:T(8,128)(2,1)}, bf16[192,2048]{1,0:T(8,128)(2,1)S(1)}, u32[]{:S(2)}, u32[]{:S(2)}) collective-permute-start(bf16[192,2048]{1,0:T(8,128)(2,1)} %pad_maximum_fusion), channel_id=1, source_target_pairs={{0,4},{2,6},{4,0},{6,2},{1,5},{3,7},{5,1},{7,3},{8,12},{10,14},{12... | collective-permute-start | bytes 2359304 | tf_op jit(solution)/shard_map/ppermute | solution.py:287
  110.4 1.1 convert_add_fusion
  111.5 9.1 %collective-permute-start.15 = (f32[32,384]{1,0:T(8,128)S(1)}, f32[32,384]{1,0:T(8,128)S(1)}, u32[]{:S(2)}, u32[]{:S(2)}) collective-permute-start(f32[32,384]{1,0:T(8,128)S(1)} %get-tuple-element.36), channel_id=1, source_target_pairs={{0,128},{128,256},{256,384},{384,0},{1,129},{129,257},{257,385},{3... | collective-permute-start | bytes 147464 | tf_op jit(solution)/shard_map/ppermute | solution.py:283
  120.6 10.0 %collective-permute-start.16 = (f32[32,384]{1,0:T(8,128)S(1)}, f32[32,384]{1,0:T(8,128)}, u32[]{:S(2)}, u32[]{:S(2)}) collective-permute-start(f32[32,384]{1,0:T(8,128)S(1)} %get-tuple-element.38), channel_id=1, source_target_pairs={{0,256},{128,384},{256,0},{384,128},{1,257},{129,385},{257,1},{385... | collective-permute-start | bytes 147464 | tf_op jit(solution)/shard_map/ppermute | solution.py:283
  130.7 5.5 %collective-permute-start.17 = (f32[32,384]{1,0:T(8,128)S(1)}, f32[32,384]{1,0:T(8,128)}, u32[]{:S(2)}, u32[]{:S(2)}) collective-permute-start(f32[32,384]{1,0:T(8,128)S(1)} %get-tuple-element.37), channel_id=1, source_target_pairs={{0,384},{128,0},{256,128},{384,256},{1,385},{129,1},{257,129},{385... | collective-permute-start | bytes 147464 | tf_op jit(solution)/shard_map/ppermute | solution.py:283
  136.1 1.7 %place_first.1.partial = bf16[768,2048]{1,0:T(8,128)(2,1)} custom-call(s32[5]{0:T(128)S(1)} %stack.19.place, bf16[96,2048]{1,0:T(8,128)(2,1)S(1)} %fusion.own, bf16[96,2048]{1,0:T(8,128)(2,1)S(1)} %collective-permute-done.6.near, bf16[96,2048]{1,0:T(8,128)(2,1)S(1)} %collective-permute-done.7.below, bf16[96,2048]{1,0:T(8,128)(2,1)S(1)} %collective-permute-done.8.above), custom_call_target="tpu_custom_call" | custom-call | tf_op jit(solution)/shard_map/place_first/pallas_call | solution.py:290
  137.9 1.7 %place_last.1 = bf16[768,2048]{1,0:T(8,128)(2,1)} custom-call(s32[5]{0:T(128)S(1)} %stack.19.place, bf16[768,2048]{1,0:T(8,128)(2,1)} %place_first.1.partial, bf16[192,2048]{1,0:T(8,128)(2,1)S(1)} %collective-permute-done.9.across, bf16[192,2048]{1,0:T(8,128)(2,1)S(1)} %collective-permute-done.10.beside), custom_call_target="tpu_custom_call", output_to_operand_aliasing={{}: (1, {})} | custom-call | tf_op jit(solution)/shard_map/place_last/pallas_call | solution.py:299
  139.6 2.6 %collective-permute-done.17 = f32[32,384]{1,0:T(8,128)} collective-permute-done((f32[32,384]{1,0:T(8,128)S(1)}, f32[32,384]{1,0:T(8,128)}, u32[]{:S(2)}, u32[]{:S(2)}) %collective-permute-start.17) | collective-permute-done | bytes 49184 | tf_op jit(solution)/shard_map/ppermute | solution.py:283
  142.2 1.5 %fusion.7 = f32[32,384]{1,0:T(8,128)} fusion(f32[32,384]{1,0:T(8,128)} %collective-permute-done.17, f32[32,384]{1,0:T(8,128)} %collective-permute-done.16, f32[32,384]{1,0:T(8,128)S(1)} %collective-permute-done.15, f32[4,32,384]{2,1,0:T(8,128)S(1)} %convert_add_fusion, s32[]{:T(128)S(6)} %select_n.20), kind=kLoop, calls=%fused_computation.18 | loop fusion | flops 49152 | bytes 245764 | tf_op jit(solution)/shard_map/div | solution.py:284
  (29 shorter events, 0.1 us)
Async XLA Ops:
  1.4 1.0 copy-start.5
  3.0 9.5 %collective-permute-start = (bf16[384,256]{1,0:T(8,128)(2,1)S(1)}, bf16[384,256]{1,0:T(8,128)(2,1)S(1)}, u32[]{:S(2)}, u32[]{:S(2)}) collective-permute-start(bf16[384,256]{1,0:T(8,128)(2,1)S(1)} %get-tuple-element.18), channel_id=1, source_target_pairs={{0,1},{1,0},{2,3},{3,2},{4,5},{5,4},{6,7},{7,6},{8,9},{9,8},{10,11... | collective-permute-start | bytes 589832 | tf_op jit(solution)/shard_map/ppermute | solution.py:178
  8.5 23.9 %collective-permute-start.2 = (bf16[1024,384]{1,0:T(8,128)(2,1)}, bf16[1024,384]{1,0:T(8,128)(2,1)}, u32[]{:S(2)}, u32[]{:S(2)}) collective-permute-start(bf16[1024,384]{1,0:T(8,128)(2,1)} %dynamic-slice_bitcast_fusion.1), channel_id=1, source_target_pairs={{0,17},{17,0},{1,16},{16,1},{2,19},{19,2},{3,18},{18,3},{4,21},{21... | collective-permute-start | bytes 2359304 | tf_op jit(solution)/shard_map/ppermute | solution.py:190
  14.3 5.0 %copy-start.1 = (bf16[384,2048]{1,0:T(8,128)(2,1)S(1)}, bf16[384,2048]{1,0:T(8,128)(2,1)}, u32[]{:S(2)}) copy-start(bf16[384,2048]{1,0:T(8,128)(2,1)} %up_own.1) | copy-start | bytes 4718596
  14.3 26.8 %all-to-all-start = ((bf16[4,2,384,256]{3,2,1,0:T(8,128)(2,1)}), bf16[4,2,384,256]{3,2,1,0:T(8,128)(2,1)S(1)}, u32[]{:S(2)}, u32[]{:S(2)}) async-start(bf16[4,2,384,256]{3,2,1,0:T(8,128)(2,1)} %spread.1), calls=%async_computation | async-start | bytes 3145728 | tf_op jit(solution)/shard_map/all_to_all | solution.py:187
  19.3 2.7 %copy-start.4 = (bf16[768,384]{1,0:T(8,128)(2,1)S(1)}, bf16[768,384]{1,0:T(8,128)(2,1)}, u32[]{:S(2)}) copy-start(bf16[768,384]{1,0:T(8,128)(2,1)} %whole.3) | copy-start | bytes 1769476
  19.4 17.3 %collective-permute-start.4 = (bf16[192,2048]{1,0:T(8,128)(2,1)S(1)}, bf16[192,2048]{1,0:T(8,128)(2,1)}, u32[]{:S(2)}, u32[]{:S(2)}) collective-permute-start(bf16[192,2048]{1,0:T(8,128)(2,1)S(1)} %dynamic-slice_bitcast_fusion), channel_id=1, source_target_pairs={{0,1},{1,0},{8,25},{9,24},{16,17},{17,16},{24,9},{25,8},{2,3},{3,2... | collective-permute-start | bytes 2359304 | tf_op jit(solution)/shard_map/ppermute | solution.py:191
  22.7 0.7 copy-start.6
  23.4 17.7 %collective-permute-start.1 = (bf16[384,384]{1,0:T(8,128)(2,1)S(1)}, bf16[384,384]{1,0:T(8,128)(2,1)S(1)}, u32[]{:S(2)}, u32[]{:S(2)}) collective-permute-start(bf16[384,384]{1,0:T(8,128)(2,1)S(1)} %get-tuple-element.20), channel_id=1, source_target_pairs={{0,1},{1,0},{2,3},{3,2},{4,5},{5,4},{6,7},{7,6},{8,9},{9,8},{10,11... | collective-permute-start | bytes 884744 | tf_op jit(solution)/shard_map/ppermute | solution.py:188
  32.4 17.3 %collective-permute-start.3 = (bf16[1024,384]{1,0:T(8,128)(2,1)}, bf16[1024,384]{1,0:T(8,128)(2,1)}, u32[]{:S(2)}, u32[]{:S(2)}) collective-permute-start(bf16[1024,384]{1,0:T(8,128)(2,1)} %collective-permute-done.2.down_mine), channel_id=1, source_target_pairs={{0,8},{8,0},{1,9},{9,1},{2,10},{10,2},{3,11},{11,3},{4,12},{12,4},... | collective-permute-start | bytes 2359304 | tf_op jit(solution)/shard_map/ppermute | solution.py:194
  36.7 13.0 %collective-permute-start.5 = (bf16[192,2048]{1,0:T(8,128)(2,1)}, bf16[192,2048]{1,0:T(8,128)(2,1)}, u32[]{:S(2)}, u32[]{:S(2)}) collective-permute-start(bf16[192,2048]{1,0:T(8,128)(2,1)} %collective-permute-done.4.up_mine), channel_id=1, source_target_pairs={{0,8},{8,0},{1,9},{9,1},{2,10},{10,2},{3,11},{11,3},{4,12},{12,4},... | collective-permute-start | bytes 2359304 | tf_op jit(solution)/shard_map/ppermute | solution.py:195
  41.1 1.0 copy-start.7
  42.0 6.7 %copy-start = (bf16[2048,384]{1,0:T(8,128)(2,1)S(1)}, bf16[2048,384]{1,0:T(8,128)(2,1)}, u32[]{:S(2)}) copy-start(bf16[2048,384]{1,0:T(8,128)(2,1)} %down.1) | copy-start | bytes 4718596
  45.6 1.2 copy-start.2
  46.8 13.6 %collective-permute-start.11 = (bf16[4,16,32,384]{3,2,1,0:T(8,128)(2,1)}, bf16[4,16,32,384]{3,2,1,0:T(8,128)(2,1)}, u32[]{:S(2)}, u32[]{:S(2)}) collective-permute-start(bf16[4,16,32,384]{3,2,1,0:T(8,128)(2,1)} %get-tuple-element.27), channel_id=1, source_target_pairs={{0,8},{8,0},{1,9},{9,1},{2,10},{10,2},{3,11},{11,3},{4,12},{12,4},... | collective-permute-start | bytes 4718600 | tf_op jit(solution)/shard_map/ppermute | solution.py:254
  55.3 5.1 %copy-start.3 = (bf16[4,16,32,384]{3,2,1,0:T(8,128)(2,1)S(1)}, bf16[4,16,32,384]{3,2,1,0:T(8,128)(2,1)}, u32[]{:S(2)}) copy-start(bf16[4,16,32,384]{3,2,1,0:T(8,128)(2,1)} %copy-done.2) | copy-start | bytes 4718596
  55.4 25.3 %all-to-all-start.1 = ((bf16[4,96,2048]{2,1,0:T(8,128)(2,1)}), bf16[4,96,2048]{2,1,0:T(8,128)(2,1)}, u32[]{:S(2)}, u32[]{:S(2)}) async-start(bf16[4,96,2048]{2,1,0:T(8,128)(2,1)} %bitcast.9), calls=%async_computation.1 | async-start | bytes 3145728 | tf_op jit(solution)/shard_map/all_to_all | solution.py:251
  63.1 23.0 %collective-permute-start.12 = (bf16[16,32,384]{2,1,0:T(8,128)(2,1)}, bf16[16,32,384]{2,1,0:T(8,128)(2,1)S(1)}, u32[]{:S(2)}, u32[]{:S(2)}) collective-permute-start(bf16[16,32,384]{2,1,0:T(8,128)(2,1)} %get-tuple-element.34), channel_id=1, source_target_pairs={{0,1},{1,0},{2,3},{3,2},{4,5},{5,4},{6,7},{7,6},{8,9},{9,8},{10,11... | collective-permute-start | bytes 1179656 | tf_op jit(solution)/shard_map/ppermute | solution.py:257
  65.0 25.0 %collective-permute-start.13 = (bf16[16,32,384]{2,1,0:T(8,128)(2,1)}, bf16[16,32,384]{2,1,0:T(8,128)(2,1)S(1)}, u32[]{:S(2)}, u32[]{:S(2)}) collective-permute-start(bf16[16,32,384]{2,1,0:T(8,128)(2,1)} %get-tuple-element.33), channel_id=1, source_target_pairs={{0,17},{17,0},{1,16},{16,1},{2,19},{19,2},{3,18},{18,3},{4,21},{21... | collective-permute-start | bytes 1179656 | tf_op jit(solution)/shard_map/ppermute | solution.py:258
  69.1 20.9 %collective-permute-start.14 = (bf16[16,32,384]{2,1,0:T(8,128)(2,1)}, bf16[16,32,384]{2,1,0:T(8,128)(2,1)S(1)}, u32[]{:S(2)}, u32[]{:S(2)}) collective-permute-start(bf16[16,32,384]{2,1,0:T(8,128)(2,1)} %get-tuple-element.32), channel_id=1, source_target_pairs={{0,16},{16,0},{1,17},{17,1},{2,18},{18,2},{3,19},{19,3},{4,20},{20... | collective-permute-start | bytes 1179656 | tf_op jit(solution)/shard_map/ppermute | solution.py:259
  82.2 14.8 %collective-permute-start.6 = (bf16[96,2048]{1,0:T(8,128)(2,1)S(1)}, bf16[96,2048]{1,0:T(8,128)(2,1)S(1)}, u32[]{:S(2)}, u32[]{:S(2)}) collective-permute-start(bf16[96,2048]{1,0:T(8,128)(2,1)S(1)} %fusion.own), channel_id=1, source_target_pairs={{0,1},{1,0},{2,3},{3,2},{4,5},{5,4},{6,7},{7,6},{8,9},{9,8},{10,11... | collective-permute-start | bytes 1179656 | tf_op jit(solution)/shard_map/ppermute | solution.py:262
  84.1 12.8 %collective-permute-start.7 = (bf16[96,2048]{1,0:T(8,128)(2,1)S(1)}, bf16[96,2048]{1,0:T(8,128)(2,1)S(1)}, u32[]{:S(2)}, u32[]{:S(2)}) collective-permute-start(bf16[96,2048]{1,0:T(8,128)(2,1)S(1)} %fusion.own), channel_id=1, source_target_pairs={{0,2},{2,4},{4,6},{6,0},{1,3},{3,5},{5,7},{7,1},{8,10},{10,12},{12... | collective-permute-start | bytes 1179656 | tf_op jit(solution)/shard_map/ppermute | solution.py:263
  86.1 12.5 %collective-permute-start.8 = (bf16[96,2048]{1,0:T(8,128)(2,1)S(1)}, bf16[96,2048]{1,0:T(8,128)(2,1)S(1)}, u32[]{:S(2)}, u32[]{:S(2)}) collective-permute-start(bf16[96,2048]{1,0:T(8,128)(2,1)S(1)} %fusion.own), channel_id=1, source_target_pairs={{0,6},{2,0},{4,2},{6,4},{1,7},{3,1},{5,3},{7,5},{8,14},{10,8},{12,... | collective-permute-start | bytes 1179656 | tf_op jit(solution)/shard_map/ppermute | solution.py:264
  91.0 19.4 %all-to-all-start.2 = ((bf16[16,32,384]{2,1,0:T(8,128)(2,1)}), bf16[16,32,384]{2,1,0:T(8,128)(2,1)}, u32[]{:S(2)}, u32[]{:S(2)}) async-start(bf16[16,32,384]{2,1,0:T(8,128)(2,1)} %ring_sum.1), calls=%async_computation.2 | async-start | bytes 786432 | tf_op jit(solution)/shard_map/all_to_all | solution.py:276
  99.6 38.3 %collective-permute-start.10 = (bf16[192,2048]{1,0:T(8,128)(2,1)}, bf16[192,2048]{1,0:T(8,128)(2,1)S(1)}, u32[]{:S(2)}, u32[]{:S(2)}) collective-permute-start(bf16[192,2048]{1,0:T(8,128)(2,1)} %pad_maximum_fusion.1), channel_id=1, source_target_pairs={{0,1},{1,0},{2,3},{3,2},{4,5},{5,4},{6,7},{7,6},{8,9},{9,8},{10,11... | collective-permute-start | bytes 2359304 | tf_op jit(solution)/shard_map/ppermute | solution.py:288
  104.1 33.7 %collective-permute-start.9 = (bf16[192,2048]{1,0:T(8,128)(2,1)}, bf16[192,2048]{1,0:T(8,128)(2,1)S(1)}, u32[]{:S(2)}, u32[]{:S(2)}) collective-permute-start(bf16[192,2048]{1,0:T(8,128)(2,1)} %pad_maximum_fusion), channel_id=1, source_target_pairs={{0,4},{2,6},{4,0},{6,2},{1,5},{3,7},{5,1},{7,3},{8,12},{10,14},{12... | collective-permute-start | bytes 2359304 | tf_op jit(solution)/shard_map/ppermute | solution.py:287
  111.5 28.1 %collective-permute-start.15 = (f32[32,384]{1,0:T(8,128)S(1)}, f32[32,384]{1,0:T(8,128)S(1)}, u32[]{:S(2)}, u32[]{:S(2)}) collective-permute-start(f32[32,384]{1,0:T(8,128)S(1)} %get-tuple-element.36), channel_id=1, source_target_pairs={{0,128},{128,256},{256,384},{384,0},{1,129},{129,257},{257,385},{3... | collective-permute-start | bytes 147464 | tf_op jit(solution)/shard_map/ppermute | solution.py:283
  120.6 19.0 %collective-permute-start.16 = (f32[32,384]{1,0:T(8,128)S(1)}, f32[32,384]{1,0:T(8,128)}, u32[]{:S(2)}, u32[]{:S(2)}) collective-permute-start(f32[32,384]{1,0:T(8,128)S(1)} %get-tuple-element.38), channel_id=1, source_target_pairs={{0,256},{128,384},{256,0},{384,128},{1,257},{129,385},{257,1},{385... | collective-permute-start | bytes 147464 | tf_op jit(solution)/shard_map/ppermute | solution.py:283
  130.7 11.5 %collective-permute-start.17 = (f32[32,384]{1,0:T(8,128)S(1)}, f32[32,384]{1,0:T(8,128)}, u32[]{:S(2)}, u32[]{:S(2)}) collective-permute-start(f32[32,384]{1,0:T(8,128)S(1)} %get-tuple-element.37), channel_id=1, source_target_pairs={{0,384},{128,0},{256,128},{384,256},{1,385},{129,1},{257,129},{385... | collective-permute-start | bytes 147464 | tf_op jit(solution)/shard_map/ppermute | solution.py:283

commit v6 on v3

v6 whole, which is shorter than its diff:
```python
import jax
import jax.numpy as jnp
from jax import lax
from jax.experimental import pallas as pl
from jax.experimental.pallas import tpu as pltpu
from jax.sharding import Mesh
from jax.sharding import PartitionSpec as P

DP = ("zh", "zl", "xh", "core")
REP = ("y", "xl")
RING = ("xh", "xl")
NEAR = [(0, 1), (1, 0)]
FAR = [(0, 3), (3, 0), (1, 2), (2, 1)]
MIXED = [(i, i ^ 1 if i // 2 % 2 == 0 else i ^ 5) for i in range(8)]
ACROSS = [(0, 2), (2, 0), (1, 3), (3, 1)]
VMEM = pl.BlockSpec(memory_space=pltpu.VMEM)
SMEM = pl.BlockSpec(memory_space=pltpu.SMEM)
ANY = pl.BlockSpec(memory_space=pl.ANY)
FIRST = 400
LIMIT = 12 * 1024 * 1024


def dot(a, b):
    return jnp.dot(a, b, preferred_element_type=jnp.float32)


def own_rows(ref, xl):
    part = ref.shape[0] // 8
    return jnp.concatenate(
        [ref[pl.ds(pl.multiple_of((y * 2 + xl) * part, 16), part), :] for y in range(4)], axis=0
    )


def sent_kernel(place, whole, other):
    other[...] = own_rows(whole, 1 - place[2])


def live_kernel(place, whole, own, other):
    xl, live = place[2], place[3]
    ranks = own.shape[0]
    part = other.shape[0] // 4
    for y in range(4):
        for x in (0, 1):
            first = pl.multiple_of((y * 2 + (1 - xl if x else xl)) * part, 16)
            row = first + lax.broadcasted_iota(jnp.int32, (part, other.shape[1]), 0)
            rows = jnp.where(row < live, whole[pl.ds(first, part), :], 0).astype(other.dtype)
            if x:
                other[y * part:(y + 1) * part, :] = rows
            else:
                for rank in range(ranks):
                    own[rank, y * part:(y + 1) * part, :] = rows


def spread_kernel(block, out):
    for rank in range(out.shape[0]):
        out[rank] = block[...]


def own_kernel(place, grads, grads_near, pre, down, out):
    xl = place[2]
    blocks, _, features = grads.shape
    hidden = sum(
        dot(g[j], down[pl.ds(pl.multiple_of((2 * j + x) * features, 16), features), :])
        for g, x in ((grads, xl), (grads_near, 1 - xl))
        for j in range(blocks)
    )
    out[...] = jnp.where(own_rows(pre, xl) > 0, hidden, 0.0).astype(out.dtype)


def terms_kernel(
    place, grads, grads_near, own, pre_far, down_mine, down_other, up_own, up_mine, up_other, terms, up_far
):
    core, xl = place[0], place[2]
    blocks, features = grads.shape[0], grads.shape[2]
    half = blocks // 2
    units = up_mine.shape[0]
    up_far[pl.ds(pl.multiple_of(core * units, 16), units), :] = up_mine[...]
    up_far[pl.ds(pl.multiple_of((1 - core) * units, 16), units), :] = up_other[...]
    far = sum(
        dot(g[c * half + j], down[pl.ds(pl.multiple_of((2 * j + x) * features, 16), features), :])
        for g, x in ((grads, xl), (grads_near, 1 - xl))
        for c, down in ((core, down_mine), (1 - core, down_other))
        for j in range(half)
    )
    far = jnp.where(pre_far[...] > 0, far, 0.0).astype(jnp.bfloat16)
    columns = terms.shape[1] // 4
    for i in range(4):
        at = slice(i * columns, (i + 1) * columns)
        terms[:, at] = (dot(own[...], up_own[:, at]) + dot(far, up_far[:, at])).astype(terms.dtype)


def down_kernel(place, grads, pre_own, pre_far, kept, sent):
    core, xh, xl, live = place[0], place[1], place[2], place[3]
    blocks, rows, features = grads.shape
    units = pre_far.shape[1]
    share = kept.shape[3]
    groups = features // (4 * share)
    at = lax.broadcasted_iota(jnp.int32, pre_far.shape, 0)
    part = rows // 4
    row = at + (at // part + xl) * part
    hidden = jnp.concatenate(
        [
            jnp.where(row < live, jnp.maximum(pre, 0), 0).astype(jnp.bfloat16)
            for pre in (own_rows(pre_own, xl), pre_far[...])
        ],
        axis=1,
    )
    for j in range(blocks):
        block = lax.dot_general(
            grads[j], hidden, (((0,), (0,)), ((), ())), preferred_element_type=jnp.float32
        ).astype(kept.dtype)
        for g in range(groups):
            for h in range(2):
                first = (g * 4 + h * 2) * share
                low = block[first:first + share, :]
                high = block[first + share:first + 2 * share, :]
                mine = jnp.where(core == 0, low, high)
                other = jnp.where(core == 0, high, low)
                for t in range(2):
                    kind = t * 2 + jnp.abs(xh - h)
                    kept[kind, g, j] = mine[:, t * units:(t + 1) * units]
                    sent[kind, g, j] = other[:, t * units:(t + 1) * units]


def chip_kernel(place, kept, came, kept_near, came_near, *outs):
    xl = place[2]
    groups = kept.shape[1]
    for kind, out in enumerate(outs):
        for ours, theirs, x in ((kept, came, xl), (kept_near, came_near, 1 - xl)):
            for g in range(groups):
                total = ours[kind, g].astype(jnp.float32) + theirs[kind, g].astype(jnp.float32)
                out[x * groups + g] = total.astype(out.dtype)


def ring_kernel(own, near, far, across, out):
    total = own[...].astype(jnp.float32) + near[...].astype(jnp.float32)
    out[...] = (total + far[...].astype(jnp.float32) + across[...].astype(jnp.float32)).astype(out.dtype)


def rows_kernel(came, out):
    out[...] = sum(came[i].astype(jnp.float32) for i in range(came.shape[0])).astype(out.dtype)


def put(place, blocks, out, sems):
    y, xl = place[4], place[2]
    rows = blocks[0][0].shape[0] if len(blocks[0]) == 3 else blocks[0][4]
    ranks = out.shape[0] // (2 * rows)
    running = []
    for i, (block, dy, dx, *rest) in enumerate(blocks):
        at = ((y + dy + ranks) % ranks) * 2 + (1 - xl if dx else xl)
        start = pl.multiple_of(at * rows, 16)
        source = block.at[pl.ds(rest[0], rows)] if rest else block
        copy = pltpu.make_async_copy(source, out.at[pl.ds(start, rows)], sems.at[i])
        copy.start()
        running.append(copy)
    for copy in running:
        copy.wait()


def first_kernel(place, own, near, below, above, out, sems):
    put(place, [(own, 0, 0), (near, 0, 1), (below, -1, 0), (above, 1, 0)], out, sems)


def last_kernel(place, partial, across, beside, out, sems):
    rows = across.shape[0] // 2
    put(
        place,
        [(across, 2, 0, 0, rows), (across, 2, 1, rows, rows), (beside, -1, 1, 0, rows), (beside, 1, 1, rows, rows)],
        out,
        sems,
    )


def own_part(array, index, axis):
    return lax.dynamic_index_in_dim(array, index, axis, keepdims=False)


def on_device(grad_out, pre_act, up_weight, down_weight, slot_counts):
    slot_rows, features = grad_out.shape
    hidden_units = pre_act.shape[1]
    ys, zs = lax.axis_size("y"), lax.axis_size(("zh", "zl"))
    reps = 2 * ys
    width = features * reps
    rows = slot_rows // reps
    half_rows = slot_rows // 2
    core, xh, xl, y = (lax.axis_index(a) for a in ("core", "xh", "xl", "y"))
    place = jnp.stack([core, xh, xl, slot_counts[0], y]).astype(jnp.int32)
    bf16 = jnp.bfloat16

    def turn(by):
        return [(i, (i + by) % ys) for i in range(ys)]

    f32 = jnp.float32

    def call(kernel, name, outs, *operands, flops=0, scratch=()):
        size = sum(x.size * x.dtype.itemsize for x in operands)
        return pl.pallas_call(
            kernel,
            out_shape=outs,
            in_specs=[SMEM if x is place else VMEM for x in operands],
            out_specs=tuple(VMEM for _ in outs) if isinstance(outs, tuple) else VMEM,
            scratch_shapes=list(scratch),
            compiler_params=pltpu.CompilerParams(vmem_limit_bytes=LIMIT),
            cost_estimate=pl.CostEstimate(flops=flops, bytes_accessed=size, transcendentals=0),
            name=name,
        )(*operands)

    def like(*shape):
        return jax.ShapeDtypeStruct(shape, bf16)

    own_sets, other_set = call(
        live_kernel, "live_sets", (like(ys, half_rows, features), like(half_rows, features)), place, grad_out
    )
    grads = lax.all_to_all(own_sets, "y", 0, 0, tiled=True)
    pre_sent = call(sent_kernel, "pre_sent", like(half_rows, hidden_units), place, pre_act)
    pre_far = lax.ppermute(pre_sent, "xl", NEAR)
    down_tied, other_set = lax.optimization_barrier((down_weight, other_set))
    near_set = lax.ppermute(other_set, "xl", NEAR)
    up_tied, near_set = lax.optimization_barrier((up_weight, near_set))
    near_sets = call(spread_kernel, "spread", like(ys, half_rows, features), near_set)
    grads, near_sets, pre_far = lax.optimization_barrier((grads, near_sets, pre_far))
    grads_near = lax.all_to_all(near_sets, "y", 0, 0, tiled=True)
    down_mine = lax.ppermute(own_part(down_tied.reshape(2, width // 2, hidden_units), core, 0), RING, FAR)
    up_mine = lax.ppermute(
        own_part(up_tied.reshape(2, hidden_units // 2, width), core, 0), ("xh", "core", "xl"), MIXED
    )

    share = width // (4 * zs)
    laid_out = like(4, 2, zs // 4, share, hidden_units)
    flops = half_rows * width * hidden_units
    kept, sent = call(down_kernel, "down_own", (laid_out, laid_out), place, grads, pre_act, pre_far, flops=FIRST * flops)
    down_mine, up_mine, grads_near, sent = lax.optimization_barrier((down_mine, up_mine, grads_near, sent))
    down_other = lax.ppermute(down_mine, "core", NEAR)
    up_other = lax.ppermute(up_mine, "core", NEAR)
    came = lax.ppermute(sent, "core", NEAR)
    kept_near, sent_near = call(
        down_kernel, "down_near", (laid_out, laid_out), place, grads_near, pre_act, pre_far, flops=2 * flops
    )
    came_near = lax.ppermute(sent_near, "core", NEAR)

    pre_grad = call(
        own_kernel, "own_grad", like(half_rows, hidden_units), place, grads, grads_near, pre_act, down_weight,
        flops=2 * flops,
    )
    pre_later, sent_near = lax.optimization_barrier((pre_far, sent_near))
    terms = call(
        terms_kernel, "terms", like(half_rows, width),
        place, grads, grads_near, pre_grad, pre_later, down_mine, down_other, up_weight, up_mine, up_other,
        flops=6 * flops, scratch=[pltpu.VMEM((hidden_units, width), bf16)],
    )
    terms = lax.all_to_all(terms.reshape(ys, rows, width), "y", 0, 0, tiled=True)
    own = call(rows_kernel, "own_rows", like(rows, width), terms)

    kind = like(4, zs // 4, share, hidden_units)
    own_chip, across_chip, near_chip, far_chip = call(
        chip_kernel, "chip_sum", (kind,) * 4, place, kept, came, kept_near, came_near
    )
    ring = [
        lax.ppermute(near_chip, "xl", NEAR),
        lax.ppermute(far_chip, RING, FAR),
        lax.ppermute(across_chip, RING, ACROSS),
    ]

    near = lax.ppermute(own, "xl", NEAR)
    below = lax.ppermute(own, "y", turn(1))
    above = lax.ppermute(own, "y", turn(-1))

    own_chip, ring, _ = lax.optimization_barrier((own_chip, ring, own))
    ring_sum = call(ring_kernel, "ring_sum", kind, own_chip, *ring)
    low_terms = lax.all_to_all(ring_sum, "zl", 0, 0, tiled=True)
    low_sum = call(rows_kernel, "low_sum", like(zs // 4, share, hidden_units), low_terms)
    high_terms = lax.all_to_all(low_sum, "zh", 0, 0, tiled=True)
    down_grad = sum(high_terms[i].astype(f32) for i in range(zs // 4)) / (4 * zs)

    near, below, above = lax.optimization_barrier((near, below, above))
    across = lax.ppermute(jnp.concatenate([own, near]), "y", turn(2))
    beside = lax.ppermute(jnp.concatenate([below, above]), "xl", NEAR)
    whole = jax.ShapeDtypeStruct((slot_rows, width), bf16)
    first = pl.pallas_call(
        first_kernel,
        out_shape=whole,
        in_specs=[SMEM] + [VMEM] * 4,
        out_specs=ANY,
        scratch_shapes=[pltpu.SemaphoreType.DMA((4,))],
        compiler_params=pltpu.CompilerParams(vmem_limit_bytes=LIMIT),
        name="place_first",
    )(place, own, near, below, above)
    input_grad = pl.pallas_call(
        last_kernel,
        out_shape=whole,
        in_specs=[SMEM, ANY] + [VMEM] * 2,
        out_specs=ANY,
        scratch_shapes=[pltpu.SemaphoreType.DMA((4,))],
        input_output_aliases={1: 0},
        compiler_params=pltpu.CompilerParams(vmem_limit_bytes=LIMIT),
        name="place_last",
    )(place, first, across, beside)
    return (input_grad, down_grad)


def solution(mesh):
    zs = mesh.shape["dp"] // 4
    ys = mesh.shape["rep"] // 2
    finer = Mesh(mesh.devices.reshape(zs // 4, 4, 2, 2, ys, 2), (*DP, *REP))
    in_specs = (P(DP, REP), P(DP, REP), P(REP, None), P(None, REP), P(DP))
    out_specs = (P(DP, None), P(DP, REP))
    return jax.shard_map(
        on_device, mesh=finer, in_specs=in_specs, out_specs=out_specs, check_vma=False
    )
```

time: 143 us -> 151 us (1.056)
  starting transfers between devices: 72.5 us -> 88.7 us
  waiting for transfers between devices: 40.6 us -> 24.5 us
  Pallas kernels: 14.1 us -> 20.9 us
  other arithmetic: 6.91 us -> 2.53 us
  local copies, waits for them, and re-layouts: 6.36 us -> 10.4 us
    all_to_all x3 -> x5, waiting for transfers between devices: 8.9 us -> 18 us  [the longest x1 9.72 us: on_device(): high_terms = lax.all_to_all(low_sum, 'zh', 0, 0, tiled=True)]
    all_to_all x3 -> x5, starting transfers between devices: 25.6 us -> 34.6 us  [the longest x1 14.8 us: on_device(): high_terms = lax.all_to_all(low_sum, 'zh', 0, 0, tiled=True)]
    ppermute x1, waiting for transfers between devices: 8.01 us -> 0.01 us  [on_device(): near = lax.ppermute(own, 'xl', NEAR)]
    ppermute x1, waiting for transfers between devices: 7.68 us -> 0.01 us  [on_device(): beside = lax.ppermute(jnp.concatenate([below, above]), 'xl', NEAR)]
    pallas_call x3 -> x11, Pallas kernels: 10.7 us -> 17.5 us  [call(): pl.pallas_call(kernel, out_shape=outs, in_specs=[SMEM if x is place else...]
    ppermute x7 -> x9, waiting for transfers between devices: 12.2 us -> 5.68 us  [the longest x1 5.66 us: on_device(): lax.ppermute(own_part(down_tied.reshape(2, width // 2, hidden_units), cor...]
    unnamed x10 -> x30, local copies, waits for them, and re-layouts: 1.18 us -> 7.2 us
    ppermute x7 -> x9, starting transfers between devices: 23.1 us -> 28.9 us  [the longest x1 6.81 us: on_device(): lax.ppermute(own_part(down_tied.reshape(2, width // 2, hidden_units), cor...]
  transfers between devices with their start and end apart: 17 -> 21, of which waited for: 6 -> 5; matrix products, arithmetic and copies ran while one was open for 6% -> 3% of each run, Pallas kernels for 10% -> 13%
where the time goes in v6:
time: 151 us; the launch traced here: 149 us
  starting transfers between devices  88.7 us (59%)
  waiting for transfers between devices  24.5 us (16%)
  Pallas kernels  20.9 us (14%)
  local copies, waits for them, and re-layouts  10.4 us (7%)
  other arithmetic  2.53 us (2%)
  between operations  1.71 us (1%)
    pallas_call x11, Pallas kernels, call(): pl.pallas_call(kernel, out_shape=outs, in_specs=[SMEM if x is place else...  17.5 us
    all_to_all x1, starting transfers between devices, on_device(): high_terms = lax.all_to_all(low_sum, 'zh', 0, 0, tiled=True)  14.8 us
    all_to_all x1, waiting for transfers between devices, on_device(): high_terms = lax.all_to_all(low_sum, 'zh', 0, 0, tiled=True)  9.72 us
    all_to_all x1, waiting for transfers between devices, on_device(): lax.all_to_all(terms.reshape(ys, rows, width), 'y', 0, 0, tiled=True)  8.04 us
    unnamed x30, local copies, waits for them, and re-layouts  7.2 us
    ppermute x1, starting transfers between devices, on_device(): lax.ppermute(own_part(down_tied.reshape(2, width // 2, hidden_units), cor...  6.81 us
    ppermute x1, starting transfers between devices, on_device(): down_other = lax.ppermute(down_mine, 'core', NEAR)  6.55 us
    all_to_all x1, starting transfers between devices, on_device(): low_terms = lax.all_to_all(ring_sum, 'zl', 0, 0, tiled=True)  5.89 us
  transfers between devices with their start and end apart: 21, of which 5 were waited for; matrix products, arithmetic and copies ran while one was open for 3% of the time, Pallas kernels for 13%

profile of v6, /device:TPU:6, one launch (start us, length us, event | category | flops | bytes accessed | tf_op | source)
XLA Modules:
  0.0 148.7 jit_solution(13995963045165447519)
XLA Ops:
  1.4 1.0 copy-done.10
  2.4 1.6 %live_sets.1 = (bf16[4,384,256]{2,1,0:T(8,128)(2,1)}, bf16[384,256]{1,0:T(8,128)(2,1)}) custom-call(s32[5]{0:T(128)S(1)} %stack.19.place, bf16[768,256]{1,0:T(8,128)(2,1)S(1)} %copy-done.10), custom_call_target="tpu_custom_call" | custom-call | bytes 393236 | tf_op jit(solution)/shard_map/live_sets/pallas_call | solution.py:197
  4.0 4.5 %all-to-all-start = ((bf16[4,384,256]{2,1,0:T(8,128)(2,1)}), bf16[4,384,256]{2,1,0:T(8,128)(2,1)S(1)}, u32[]{:S(2)}, u32[]{:S(2)}) async-start(bf16[4,384,256]{2,1,0:T(8,128)(2,1)} %get-tuple-element.31), calls=%async_computation | async-start | bytes 1572864 | tf_op jit(solution)/shard_map/all_to_all | solution.py:214
  8.5 2.9 %collective-permute-start = (bf16[384,256]{1,0:T(8,128)(2,1)}, bf16[384,256]{1,0:T(8,128)(2,1)S(1)}, u32[]{:S(2)}, u32[]{:S(2)}) collective-permute-start(bf16[384,256]{1,0:T(8,128)(2,1)} %get-tuple-element.33), channel_id=1, source_target_pairs={{0,1},{1,0},{2,3},{3,2},{4,5},{5,4},{6,7},{7,6},{8,9},{9,8},{10,11... | collective-permute-start | bytes 589832 | tf_op jit(solution)/shard_map/ppermute | solution.py:218
  11.3 1.3 pre_sent.1
  12.6 3.1 %collective-permute-start.1 = (bf16[384,384]{1,0:T(8,128)(2,1)}, bf16[384,384]{1,0:T(8,128)(2,1)S(1)}, u32[]{:S(2)}, u32[]{:S(2)}) collective-permute-start(bf16[384,384]{1,0:T(8,128)(2,1)} %pre_sent.1), channel_id=1, source_target_pairs={{0,1},{1,0},{2,3},{3,2},{4,5},{5,4},{6,7},{7,6},{8,9},{9,8},{10,11... | collective-permute-start | bytes 884744 | tf_op jit(solution)/shard_map/ppermute | solution.py:216
  15.7 2.1 %dynamic-slice_bitcast_fusion.1 = bf16[1024,384]{1,0:T(8,128)(2,1)} fusion(bf16[2,1024,384]{2,1,0:T(8,128)(2,1)} %bitcast.14, s32[]{:T(128)S(6)} %select_n.6), kind=kLoop, calls=%fused_computation.3 | loop fusion | bytes 1572868 | tf_op jit(solution)/shard_map/jit(dynamic_index_in_dim)/squeeze | solution.py:175
  17.8 6.8 %collective-permute-start.2 = (bf16[1024,384]{1,0:T(8,128)(2,1)}, bf16[1024,384]{1,0:T(8,128)(2,1)}, u32[]{:S(2)}, u32[]{:S(2)}) collective-permute-start(bf16[1024,384]{1,0:T(8,128)(2,1)} %dynamic-slice_bitcast_fusion.1), channel_id=1, source_target_pairs={{0,17},{17,0},{1,16},{16,1},{2,19},{19,2},{3,18},{18,3},{4,21},{21... | collective-permute-start | bytes 2359304 | tf_op jit(solution)/shard_map/ppermute | solution.py:223
  24.7 0.9 copy-done.2
  25.6 1.0 dynamic-slice_bitcast_fusion
  26.6 1.9 %collective-permute-start.3 = (bf16[192,2048]{1,0:T(8,128)(2,1)}, bf16[192,2048]{1,0:T(8,128)(2,1)}, u32[]{:S(2)}, u32[]{:S(2)}) collective-permute-start(bf16[192,2048]{1,0:T(8,128)(2,1)} %dynamic-slice_bitcast_fusion), channel_id=1, source_target_pairs={{0,1},{1,0},{8,25},{9,24},{16,17},{17,16},{24,9},{25,8},{2,3},{3,2... | collective-permute-start | bytes 2359304 | tf_op jit(solution)/shard_map/ppermute | solution.py:224
  28.5 4.8 %all-to-all-start.1 = ((bf16[4,384,256]{2,1,0:T(8,128)(2,1)}), bf16[4,384,256]{2,1,0:T(8,128)(2,1)S(1)}, u32[]{:S(2)}, u32[]{:S(2)}) async-start(bf16[4,384,256]{2,1,0:T(8,128)(2,1)} %copy-done.2), calls=%async_computation.1 | async-start | bytes 1572864 | tf_op jit(solution)/shard_map/all_to_all | solution.py:222
  33.3 1.1 copy-done.4
  34.3 1.6 %down_own.1 = (bf16[4,2,4,32,384]{4,3,2,1,0:T(8,128)(2,1)S(1)}, bf16[4,2,4,32,384]{4,3,2,1,0:T(8,128)(2,1)S(1)}) custom-call(s32[5]{0:T(128)S(1)} %stack.19.place, bf16[4,384,256]{2,1,0:T(8,128)(2,1)S(1)} %all-to-all-done.grads, bf16[768,384]{1,0:T(8,128)(2,1)S(1)} %copy-done.4, bf16[384,384]{1,0:T(8,128)(2,1)S(1)} %collective-permute-done.1.pre_far), custom_call_target="tpu_custom_call" | custom-call | flops 120795955200 | bytes 1671188 | tf_op jit(solution)/shard_map/down_own/pallas_call | solution.py:197
  36.0 0.9 copy-done.6
  36.8 0.9 copy-done.14
  37.7 5.7 %collective-permute-done.2.down_mine = bf16[1024,384]{1,0:T(8,128)(2,1)} collective-permute-done((bf16[1024,384]{1,0:T(8,128)(2,1)}, bf16[1024,384]{1,0:T(8,128)(2,1)}, u32[]{:S(2)}, u32[]{:S(2)}) %collective-permute-start.2) | collective-permute-done | bytes 786464 | tf_op jit(solution)/shard_map/ppermute | solution.py:223
  43.4 6.5 %collective-permute-start.4 = (bf16[1024,384]{1,0:T(8,128)(2,1)}, bf16[1024,384]{1,0:T(8,128)(2,1)S(1)}, u32[]{:S(2)}, u32[]{:S(2)}) collective-permute-start(bf16[1024,384]{1,0:T(8,128)(2,1)} %collective-permute-done.2.down_mine), channel_id=1, source_target_pairs={{0,8},{8,0},{1,9},{9,1},{2,10},{10,2},{3,11},{11,3},{4,12},{12,4},... | collective-permute-start | bytes 2359304 | tf_op jit(solution)/shard_map/ppermute | solution.py:233
  50.0 1.9 %collective-permute-start.5 = (bf16[192,2048]{1,0:T(8,128)(2,1)}, bf16[192,2048]{1,0:T(8,128)(2,1)S(1)}, u32[]{:S(2)}, u32[]{:S(2)}) collective-permute-start(bf16[192,2048]{1,0:T(8,128)(2,1)} %collective-permute-done.3.up_mine), channel_id=1, source_target_pairs={{0,8},{8,0},{1,9},{9,1},{2,10},{10,2},{3,11},{11,3},{4,12},{12,4},... | collective-permute-start | bytes 2359304 | tf_op jit(solution)/shard_map/ppermute | solution.py:234
  51.9 1.1 copy-done.5
  53.0 2.5 %down_near.1 = (bf16[4,2,4,32,384]{4,3,2,1,0:T(8,128)(2,1)S(1)}, bf16[4,2,4,32,384]{4,3,2,1,0:T(8,128)(2,1)}) custom-call(s32[5]{0:T(128)S(1)} %stack.19.place, bf16[4,384,256]{2,1,0:T(8,128)(2,1)S(1)} %all-to-all-done.1.grads_near.grads, bf16[768,384]{1,0:T(8,128)(2,1)S(1)} %copy-done.5, bf16[384,384]{1,0:T(8,128)(2,1)S(1)} %collective-permute-done.1.pre_far), custom_call_target="tpu_custom_call" | custom-call | flops 603979776 | bytes 1671188 | tf_op jit(solution)/shard_map/down_near/pallas_call | solution.py:197
  55.5 2.4 %collective-permute-start.12 = (bf16[4,2,4,32,384]{4,3,2,1,0:T(8,128)(2,1)}, bf16[4,2,4,32,384]{4,3,2,1,0:T(8,128)(2,1)}, u32[]{:S(2)}, u32[]{:S(2)}) collective-permute-start(bf16[4,2,4,32,384]{4,3,2,1,0:T(8,128)(2,1)} %get-tuple-element.42), channel_id=1, source_target_pairs={{0,8},{8,0},{1,9},{9,1},{2,10},{10,2},{3,11},{11,3},{4,12},{12,4},... | collective-permute-start | bytes 2359304 | tf_op jit(solution)/shard_map/ppermute | solution.py:239
  57.9 1.9 %collective-permute-start.11 = (bf16[4,2,4,32,384]{4,3,2,1,0:T(8,128)(2,1)}, bf16[4,2,4,32,384]{4,3,2,1,0:T(8,128)(2,1)}, u32[]{:S(2)}, u32[]{:S(2)}) collective-permute-start(bf16[4,2,4,32,384]{4,3,2,1,0:T(8,128)(2,1)} %copy-done.14), channel_id=1, source_target_pairs={{0,8},{8,0},{1,9},{9,1},{2,10},{10,2},{3,11},{11,3},{4,12},{12,4},... | collective-permute-start | bytes 2359304 | tf_op jit(solution)/shard_map/ppermute | solution.py:235
  59.8 1.5 %own_grad.1.own = bf16[384,384]{1,0:T(8,128)(2,1)S(1)} custom-call(s32[5]{0:T(128)S(1)} %stack.19.place, bf16[4,384,256]{2,1,0:T(8,128)(2,1)S(1)} %all-to-all-done.grads, bf16[4,384,256]{2,1,0:T(8,128)(2,1)S(1)} %all-to-all-done.1.grads_near.grads, bf16[768,384]{1,0:T(8,128)(2,1)S(1)} %copy-done.5, bf16[2048,384]{1,0:T(8,128)(2,1)S(1)} %copy-done.1), custom_call_target="tpu_custom_call" | custom-call | flops 603979776 | bytes 3735572 | tf_op jit(solution)/shard_map/own_grad/pallas_call | solution.py:197
  61.4 5.2 %terms.1 = bf16[384,2048]{1,0:T(8,128)(2,1)} custom-call(s32[5]{0:T(128)S(1)} %stack.19.place, bf16[4,384,256]{2,1,0:T(8,128)(2,1)S(1)} %all-to-all-done.grads, bf16[4,384,256]{2,1,0:T(8,128)(2,1)S(1)} %all-to-all-done.1.grads_near.grads, bf16[384,384]{1,0:T(8,128)(2,1)S(1)} %own_grad.1.own, bf16[384,384]{1,0:T(8,128)(2,1)S(1)} %collective-permute-done.1.pre_far, ...), custom_call_target="tpu_custom_call" | custom-call | flops 1811939328 | bytes 6881300 | tf_op jit(solution)/shard_map/terms/pallas_call | solution.py:197
  66.5 4.7 %all-to-all-start.2 = ((bf16[4,96,2048]{2,1,0:T(8,128)(2,1)}), bf16[4,96,2048]{2,1,0:T(8,128)(2,1)S(1)}, u32[]{:S(2)}, u32[]{:S(2)}) async-start(bf16[4,96,2048]{2,1,0:T(8,128)(2,1)} %bitcast.8), calls=%async_computation.2 | async-start | bytes 3145728 | tf_op jit(solution)/shard_map/all_to_all | solution.py:251
  71.2 2.6 %chip_sum.1 = (bf16[4,4,32,384]{3,2,1,0:T(8,128)(2,1)S(1)}, bf16[4,4,32,384]{3,2,1,0:T(8,128)(2,1)}, bf16[4,4,32,384]{3,2,1,0:T(8,128)(2,1)}, bf16[4,4,32,384]{3,2,1,0:T(8,128)(2,1)}) custom-call(s32[5]{0:T(128)S(1)} %stack.19.place, bf16[4,2,4,32,384]{4,3,2,1,0:T(8,128)(2,1)S(1)} %copy-done.7, bf16[4,2,4,32,384]{4,3,2,1,0:T(8,128)(2,1)} %collective-permute-done.11.came, ...), custom_call_target="tpu_custom_call" | custom-call | bytes 3145748 | tf_op jit(solution)/shard_map/chip_sum/pallas_call | solution.py:197
  73.8 0.8 copy-done.12
  74.6 2.0 %collective-permute-start.13 = (bf16[4,4,32,384]{3,2,1,0:T(8,128)(2,1)}, bf16[4,4,32,384]{3,2,1,0:T(8,128)(2,1)S(1)}, u32[]{:S(2)}, u32[]{:S(2)}) collective-permute-start(bf16[4,4,32,384]{3,2,1,0:T(8,128)(2,1)} %get-tuple-element.53), channel_id=1, source_target_pairs={{0,1},{1,0},{2,3},{3,2},{4,5},{5,4},{6,7},{7,6},{8,9},{9,8},{10,11... | collective-permute-start | bytes 1179656 | tf_op jit(solution)/shard_map/ppermute | solution.py:259
  76.6 2.7 %collective-permute-start.14 = (bf16[4,4,32,384]{3,2,1,0:T(8,128)(2,1)}, bf16[4,4,32,384]{3,2,1,0:T(8,128)(2,1)S(1)}, u32[]{:S(2)}, u32[]{:S(2)}) collective-permute-start(bf16[4,4,32,384]{3,2,1,0:T(8,128)(2,1)} %get-tuple-element.54), channel_id=1, source_target_pairs={{0,17},{17,0},{1,16},{16,1},{2,19},{19,2},{3,18},{18,3},{4,21},{21... | collective-permute-start | bytes 1179656 | tf_op jit(solution)/shard_map/ppermute | solution.py:260
  79.3 5.2 %collective-permute-start.15 = (bf16[4,4,32,384]{3,2,1,0:T(8,128)(2,1)}, bf16[4,4,32,384]{3,2,1,0:T(8,128)(2,1)S(1)}, u32[]{:S(2)}, u32[]{:S(2)}) collective-permute-start(bf16[4,4,32,384]{3,2,1,0:T(8,128)(2,1)} %get-tuple-element.55), channel_id=1, source_target_pairs={{0,16},{16,0},{1,17},{17,1},{2,18},{18,2},{3,19},{19,3},{4,20},{20... | collective-permute-start | bytes 1179656 | tf_op jit(solution)/shard_map/ppermute | solution.py:261
  84.5 8.0 %all-to-all-done.2.came = bf16[4,96,2048]{2,1,0:T(8,128)(2,1)S(1)} async-done(((bf16[4,96,2048]{2,1,0:T(8,128)(2,1)}), bf16[4,96,2048]{2,1,0:T(8,128)(2,1)S(1)}, u32[]{:S(2)}, u32[]{:S(2)}) %all-to-all-start.2) | async-done | bytes 1572896 | tf_op jit(solution)/shard_map/all_to_all | solution.py:251
  92.8 1.9 %collective-permute-start.6 = (bf16[96,2048]{1,0:T(8,128)(2,1)S(1)}, bf16[96,2048]{1,0:T(8,128)(2,1)S(1)}, u32[]{:S(2)}, u32[]{:S(2)}) collective-permute-start(bf16[96,2048]{1,0:T(8,128)(2,1)S(1)} %own_rows.1.own), channel_id=1, source_target_pairs={{0,1},{1,0},{2,3},{3,2},{4,5},{5,4},{6,7},{7,6},{8,9},{9,8},{10,11... | collective-permute-start | bytes 1179656 | tf_op jit(solution)/shard_map/ppermute | solution.py:264
  94.7 2.5 %collective-permute-start.7 = (bf16[96,2048]{1,0:T(8,128)(2,1)S(1)}, bf16[96,2048]{1,0:T(8,128)(2,1)S(1)}, u32[]{:S(2)}, u32[]{:S(2)}) collective-permute-start(bf16[96,2048]{1,0:T(8,128)(2,1)S(1)} %own_rows.1.own), channel_id=1, source_target_pairs={{0,2},{2,4},{4,6},{6,0},{1,3},{3,5},{5,7},{7,1},{8,10},{10,12},{12... | collective-permute-start | bytes 1179656 | tf_op jit(solution)/shard_map/ppermute | solution.py:265
  97.2 4.6 %collective-permute-start.8 = (bf16[96,2048]{1,0:T(8,128)(2,1)S(1)}, bf16[96,2048]{1,0:T(8,128)(2,1)S(1)}, u32[]{:S(2)}, u32[]{:S(2)}) collective-permute-start(bf16[96,2048]{1,0:T(8,128)(2,1)S(1)} %own_rows.1.own), channel_id=1, source_target_pairs={{0,6},{2,0},{4,2},{6,4},{1,7},{3,1},{5,3},{7,5},{8,14},{10,8},{12,... | collective-permute-start | bytes 1179656 | tf_op jit(solution)/shard_map/ppermute | solution.py:266
  101.8 0.9 ring_sum.1
  102.7 5.9 %all-to-all-start.3 = ((bf16[4,4,32,384]{3,2,1,0:T(8,128)(2,1)}), bf16[4,4,32,384]{3,2,1,0:T(8,128)(2,1)S(1)}, u32[]{:S(2)}, u32[]{:S(2)}) async-start(bf16[4,4,32,384]{3,2,1,0:T(8,128)(2,1)} %ring_sum.1), calls=%async_computation.3 | async-start | bytes 786432 | tf_op jit(solution)/shard_map/all_to_all | solution.py:270
  108.6 0.8 collective-permute-done.8.above
  109.4 0.9 pad_maximum_fusion.1
  110.3 3.6 %collective-permute-start.10 = (bf16[192,2048]{1,0:T(8,128)(2,1)}, bf16[192,2048]{1,0:T(8,128)(2,1)S(1)}, u32[]{:S(2)}, u32[]{:S(2)}) collective-permute-start(bf16[192,2048]{1,0:T(8,128)(2,1)} %pad_maximum_fusion.1), channel_id=1, source_target_pairs={{0,1},{1,0},{2,3},{3,2},{4,5},{5,4},{6,7},{7,6},{8,9},{9,8},{10,11... | collective-permute-start | bytes 2359304 | tf_op jit(solution)/shard_map/ppermute | solution.py:277
  114.0 1.0 pad_maximum_fusion
  114.9 4.1 %collective-permute-start.9 = (bf16[192,2048]{1,0:T(8,128)(2,1)}, bf16[192,2048]{1,0:T(8,128)(2,1)S(1)}, u32[]{:S(2)}, u32[]{:S(2)}) collective-permute-start(bf16[192,2048]{1,0:T(8,128)(2,1)} %pad_maximum_fusion), channel_id=1, source_target_pairs={{0,4},{2,6},{4,0},{6,2},{1,5},{3,7},{5,1},{7,3},{8,12},{10,14},{12... | collective-permute-start | bytes 2359304 | tf_op jit(solution)/shard_map/ppermute | solution.py:276
  119.4 0.6 copy-done.11
  120.0 14.8 %all-to-all-start.4 = ((bf16[4,32,384]{2,1,0:T(8,128)(2,1)}), bf16[4,32,384]{2,1,0:T(8,128)(2,1)S(1)}, u32[]{:S(2)}, u32[]{:S(2)}) async-start(bf16[4,32,384]{2,1,0:T(8,128)(2,1)} %copy-done.11), calls=%async_computation.4 | async-start | bytes 196608 | tf_op jit(solution)/shard_map/all_to_all | solution.py:272
  134.8 1.7 %place_first.1.partial = bf16[768,2048]{1,0:T(8,128)(2,1)} custom-call(s32[5]{0:T(128)S(1)} %stack.19.place, bf16[96,2048]{1,0:T(8,128)(2,1)S(1)} %own_rows.1.own, bf16[96,2048]{1,0:T(8,128)(2,1)S(1)} %collective-permute-done.6.near, bf16[96,2048]{1,0:T(8,128)(2,1)S(1)} %collective-permute-done.7.below, bf16[96,2048]{1,0:T(8,128)(2,1)S(1)} %collective-permute-done.8.above), custom_call_target="tpu_custom_call" | custom-call | tf_op jit(solution)/shard_map/place_first/pallas_call | solution.py:279
  136.6 1.7 %place_last.1 = bf16[768,2048]{1,0:T(8,128)(2,1)} custom-call(s32[5]{0:T(128)S(1)} %stack.19.place, bf16[768,2048]{1,0:T(8,128)(2,1)} %place_first.1.partial, bf16[192,2048]{1,0:T(8,128)(2,1)S(1)} %collective-permute-done.9.across, bf16[192,2048]{1,0:T(8,128)(2,1)S(1)} %collective-permute-done.10.beside), custom_call_target="tpu_custom_call", output_to_operand_aliasing={{}: (1, {})} | custom-call | tf_op jit(solution)/shard_map/place_last/pallas_call | solution.py:288
  138.3 9.7 %all-to-all-done.4 = bf16[4,32,384]{2,1,0:T(8,128)(2,1)S(1)} async-done(((bf16[4,32,384]{2,1,0:T(8,128)(2,1)}), bf16[4,32,384]{2,1,0:T(8,128)(2,1)S(1)}, u32[]{:S(2)}, u32[]{:S(2)}) %all-to-all-start.4) | async-done | bytes 98336 | tf_op jit(solution)/shard_map/all_to_all | solution.py:272
  148.0 0.6 multiply_bitcast_fusion
  (43 shorter events, 0.7 us)
Async XLA Ops:
  0.6 10.7 %copy-start.3 = (bf16[768,384]{1,0:T(8,128)(2,1)S(1)}, bf16[768,384]{1,0:T(8,128)(2,1)}, u32[]{:S(2)}) copy-start(bf16[768,384]{1,0:T(8,128)(2,1)} %pre_own.3) | copy-start | bytes 1769476
  1.4 1.0 copy-start.10
  4.0 24.5 %all-to-all-start = ((bf16[4,384,256]{2,1,0:T(8,128)(2,1)}), bf16[4,384,256]{2,1,0:T(8,128)(2,1)S(1)}, u32[]{:S(2)}, u32[]{:S(2)}) async-start(bf16[4,384,256]{2,1,0:T(8,128)(2,1)} %get-tuple-element.31), calls=%async_computation | async-start | bytes 1572864 | tf_op jit(solution)/shard_map/all_to_all | solution.py:214
  8.5 17.1 %copy-start = (bf16[384,2048]{1,0:T(8,128)(2,1)S(1)}, bf16[384,2048]{1,0:T(8,128)(2,1)}, u32[]{:S(2)}) copy-start(bf16[384,2048]{1,0:T(8,128)(2,1)} %up_own.1) | copy-start | bytes 4718596
  8.5 16.2 %collective-permute-start = (bf16[384,256]{1,0:T(8,128)(2,1)}, bf16[384,256]{1,0:T(8,128)(2,1)S(1)}, u32[]{:S(2)}, u32[]{:S(2)}) collective-permute-start(bf16[384,256]{1,0:T(8,128)(2,1)} %get-tuple-element.33), channel_id=1, source_target_pairs={{0,1},{1,0},{2,3},{3,2},{4,5},{5,4},{6,7},{7,6},{8,9},{9,8},{10,11... | collective-permute-start | bytes 589832 | tf_op jit(solution)/shard_map/ppermute | solution.py:218
  12.6 15.9 %collective-permute-start.1 = (bf16[384,384]{1,0:T(8,128)(2,1)}, bf16[384,384]{1,0:T(8,128)(2,1)S(1)}, u32[]{:S(2)}, u32[]{:S(2)}) collective-permute-start(bf16[384,384]{1,0:T(8,128)(2,1)} %pre_sent.1), channel_id=1, source_target_pairs={{0,1},{1,0},{2,3},{3,2},{4,5},{5,4},{6,7},{7,6},{8,9},{9,8},{10,11... | collective-permute-start | bytes 884744 | tf_op jit(solution)/shard_map/ppermute | solution.py:216
  17.8 25.6 %collective-permute-start.2 = (bf16[1024,384]{1,0:T(8,128)(2,1)}, bf16[1024,384]{1,0:T(8,128)(2,1)}, u32[]{:S(2)}, u32[]{:S(2)}) collective-permute-start(bf16[1024,384]{1,0:T(8,128)(2,1)} %dynamic-slice_bitcast_fusion.1), channel_id=1, source_target_pairs={{0,17},{17,0},{1,16},{16,1},{2,19},{19,2},{3,18},{18,3},{4,21},{21... | collective-permute-start | bytes 2359304 | tf_op jit(solution)/shard_map/ppermute | solution.py:223
  24.7 0.9 copy-start.2
  26.6 16.8 %collective-permute-start.3 = (bf16[192,2048]{1,0:T(8,128)(2,1)}, bf16[192,2048]{1,0:T(8,128)(2,1)}, u32[]{:S(2)}, u32[]{:S(2)}) collective-permute-start(bf16[192,2048]{1,0:T(8,128)(2,1)} %dynamic-slice_bitcast_fusion), channel_id=1, source_target_pairs={{0,1},{1,0},{8,25},{9,24},{16,17},{17,16},{24,9},{25,8},{2,3},{3,2... | collective-permute-start | bytes 2359304 | tf_op jit(solution)/shard_map/ppermute | solution.py:224
  28.5 14.9 %all-to-all-start.1 = ((bf16[4,384,256]{2,1,0:T(8,128)(2,1)}), bf16[4,384,256]{2,1,0:T(8,128)(2,1)S(1)}, u32[]{:S(2)}, u32[]{:S(2)}) async-start(bf16[4,384,256]{2,1,0:T(8,128)(2,1)} %copy-done.2), calls=%async_computation.1 | async-start | bytes 1572864 | tf_op jit(solution)/shard_map/all_to_all | solution.py:222
  33.3 1.1 copy-start.4
  36.0 0.9 copy-start.6
  36.8 0.9 copy-start.14
  43.4 16.4 %copy-start.1 = (bf16[2048,384]{1,0:T(8,128)(2,1)S(1)}, bf16[2048,384]{1,0:T(8,128)(2,1)}, u32[]{:S(2)}) copy-start(bf16[2048,384]{1,0:T(8,128)(2,1)} %down.1) | copy-start | bytes 4718596
  43.4 17.9 %collective-permute-start.4 = (bf16[1024,384]{1,0:T(8,128)(2,1)}, bf16[1024,384]{1,0:T(8,128)(2,1)S(1)}, u32[]{:S(2)}, u32[]{:S(2)}) collective-permute-start(bf16[1024,384]{1,0:T(8,128)(2,1)} %collective-permute-done.2.down_mine), channel_id=1, source_target_pairs={{0,8},{8,0},{1,9},{9,1},{2,10},{10,2},{3,11},{11,3},{4,12},{12,4},... | collective-permute-start | bytes 2359304 | tf_op jit(solution)/shard_map/ppermute | solution.py:233
  50.0 11.4 %collective-permute-start.5 = (bf16[192,2048]{1,0:T(8,128)(2,1)}, bf16[192,2048]{1,0:T(8,128)(2,1)S(1)}, u32[]{:S(2)}, u32[]{:S(2)}) collective-permute-start(bf16[192,2048]{1,0:T(8,128)(2,1)} %collective-permute-done.3.up_mine), channel_id=1, source_target_pairs={{0,8},{8,0},{1,9},{9,1},{2,10},{10,2},{3,11},{11,3},{4,12},{12,4},... | collective-permute-start | bytes 2359304 | tf_op jit(solution)/shard_map/ppermute | solution.py:234
  51.9 1.1 copy-start.5
  55.5 5.9 %copy-start.8 = (bf16[4,2,4,32,384]{4,3,2,1,0:T(8,128)(2,1)}, bf16[4,2,4,32,384]{4,3,2,1,0:T(8,128)(2,1)S(1)}, u32[]{:S(2)}) copy-start(bf16[4,2,4,32,384]{4,3,2,1,0:T(8,128)(2,1)S(1)} %get-tuple-element.51.kept_near) | copy-start | bytes 2359300
  55.5 15.7 %collective-permute-start.12 = (bf16[4,2,4,32,384]{4,3,2,1,0:T(8,128)(2,1)}, bf16[4,2,4,32,384]{4,3,2,1,0:T(8,128)(2,1)}, u32[]{:S(2)}, u32[]{:S(2)}) collective-permute-start(bf16[4,2,4,32,384]{4,3,2,1,0:T(8,128)(2,1)} %get-tuple-element.42), channel_id=1, source_target_pairs={{0,8},{8,0},{1,9},{9,1},{2,10},{10,2},{3,11},{11,3},{4,12},{12,4},... | collective-permute-start | bytes 2359304 | tf_op jit(solution)/shard_map/ppermute | solution.py:239
  57.9 13.3 %collective-permute-start.11 = (bf16[4,2,4,32,384]{4,3,2,1,0:T(8,128)(2,1)}, bf16[4,2,4,32,384]{4,3,2,1,0:T(8,128)(2,1)}, u32[]{:S(2)}, u32[]{:S(2)}) collective-permute-start(bf16[4,2,4,32,384]{4,3,2,1,0:T(8,128)(2,1)} %copy-done.14), channel_id=1, source_target_pairs={{0,8},{8,0},{1,9},{9,1},{2,10},{10,2},{3,11},{11,3},{4,12},{12,4},... | collective-permute-start | bytes 2359304 | tf_op jit(solution)/shard_map/ppermute | solution.py:235
  66.5 4.7 %copy-start.7 = (bf16[4,2,4,32,384]{4,3,2,1,0:T(8,128)(2,1)S(1)}, bf16[4,2,4,32,384]{4,3,2,1,0:T(8,128)(2,1)}, u32[]{:S(2)}) copy-start(bf16[4,2,4,32,384]{4,3,2,1,0:T(8,128)(2,1)} %copy-done.6) | copy-start | bytes 2359300
  66.5 4.7 %copy-start.9 = (bf16[4,2,4,32,384]{4,3,2,1,0:T(8,128)(2,1)S(1)}, bf16[4,2,4,32,384]{4,3,2,1,0:T(8,128)(2,1)}, u32[]{:S(2)}) copy-start(bf16[4,2,4,32,384]{4,3,2,1,0:T(8,128)(2,1)} %copy-done.8) | copy-start | bytes 2359300
  66.5 26.0 %all-to-all-start.2 = ((bf16[4,96,2048]{2,1,0:T(8,128)(2,1)}), bf16[4,96,2048]{2,1,0:T(8,128)(2,1)S(1)}, u32[]{:S(2)}, u32[]{:S(2)}) async-start(bf16[4,96,2048]{2,1,0:T(8,128)(2,1)} %bitcast.8), calls=%async_computation.2 | async-start | bytes 3145728 | tf_op jit(solution)/shard_map/all_to_all | solution.py:251
  73.8 0.8 copy-start.12
  74.6 27.2 %copy-start.13 = (bf16[4,4,32,384]{3,2,1,0:T(8,128)(2,1)S(1)}, bf16[4,4,32,384]{3,2,1,0:T(8,128)(2,1)}, u32[]{:S(2)}) copy-start(bf16[4,4,32,384]{3,2,1,0:T(8,128)(2,1)} %copy-done.12) | copy-start | bytes 1179652
  74.6 22.6 %collective-permute-start.13 = (bf16[4,4,32,384]{3,2,1,0:T(8,128)(2,1)}, bf16[4,4,32,384]{3,2,1,0:T(8,128)(2,1)S(1)}, u32[]{:S(2)}, u32[]{:S(2)}) collective-permute-start(bf16[4,4,32,384]{3,2,1,0:T(8,128)(2,1)} %get-tuple-element.53), channel_id=1, source_target_pairs={{0,1},{1,0},{2,3},{3,2},{4,5},{5,4},{6,7},{7,6},{8,9},{9,8},{10,11... | collective-permute-start | bytes 1179656 | tf_op jit(solution)/shard_map/ppermute | solution.py:259
  76.6 25.2 %collective-permute-start.14 = (bf16[4,4,32,384]{3,2,1,0:T(8,128)(2,1)}, bf16[4,4,32,384]{3,2,1,0:T(8,128)(2,1)S(1)}, u32[]{:S(2)}, u32[]{:S(2)}) collective-permute-start(bf16[4,4,32,384]{3,2,1,0:T(8,128)(2,1)} %get-tuple-element.54), channel_id=1, source_target_pairs={{0,17},{17,0},{1,16},{16,1},{2,19},{19,2},{3,18},{18,3},{4,21},{21... | collective-permute-start | bytes 1179656 | tf_op jit(solution)/shard_map/ppermute | solution.py:260
  79.3 22.5 %collective-permute-start.15 = (bf16[4,4,32,384]{3,2,1,0:T(8,128)(2,1)}, bf16[4,4,32,384]{3,2,1,0:T(8,128)(2,1)S(1)}, u32[]{:S(2)}, u32[]{:S(2)}) collective-permute-start(bf16[4,4,32,384]{3,2,1,0:T(8,128)(2,1)} %get-tuple-element.55), channel_id=1, source_target_pairs={{0,16},{16,0},{1,17},{17,1},{2,18},{18,2},{3,19},{19,3},{4,20},{20... | collective-permute-start | bytes 1179656 | tf_op jit(solution)/shard_map/ppermute | solution.py:261
  92.8 15.9 %collective-permute-start.6 = (bf16[96,2048]{1,0:T(8,128)(2,1)S(1)}, bf16[96,2048]{1,0:T(8,128)(2,1)S(1)}, u32[]{:S(2)}, u32[]{:S(2)}) collective-permute-start(bf16[96,2048]{1,0:T(8,128)(2,1)S(1)} %own_rows.1.own), channel_id=1, source_target_pairs={{0,1},{1,0},{2,3},{3,2},{4,5},{5,4},{6,7},{7,6},{8,9},{9,8},{10,11... | collective-permute-start | bytes 1179656 | tf_op jit(solution)/shard_map/ppermute | solution.py:264
  94.7 14.0 %collective-permute-start.7 = (bf16[96,2048]{1,0:T(8,128)(2,1)S(1)}, bf16[96,2048]{1,0:T(8,128)(2,1)S(1)}, u32[]{:S(2)}, u32[]{:S(2)}) collective-permute-start(bf16[96,2048]{1,0:T(8,128)(2,1)S(1)} %own_rows.1.own), channel_id=1, source_target_pairs={{0,2},{2,4},{4,6},{6,0},{1,3},{3,5},{5,7},{7,1},{8,10},{10,12},{12... | collective-permute-start | bytes 1179656 | tf_op jit(solution)/shard_map/ppermute | solution.py:265
  97.2 12.2 %collective-permute-start.8 = (bf16[96,2048]{1,0:T(8,128)(2,1)S(1)}, bf16[96,2048]{1,0:T(8,128)(2,1)S(1)}, u32[]{:S(2)}, u32[]{:S(2)}) collective-permute-start(bf16[96,2048]{1,0:T(8,128)(2,1)S(1)} %own_rows.1.own), channel_id=1, source_target_pairs={{0,6},{2,0},{4,2},{6,4},{1,7},{3,1},{5,3},{7,5},{8,14},{10,8},{12,... | collective-permute-start | bytes 1179656 | tf_op jit(solution)/shard_map/ppermute | solution.py:266
  102.7 16.6 %all-to-all-start.3 = ((bf16[4,4,32,384]{3,2,1,0:T(8,128)(2,1)}), bf16[4,4,32,384]{3,2,1,0:T(8,128)(2,1)S(1)}, u32[]{:S(2)}, u32[]{:S(2)}) async-start(bf16[4,4,32,384]{3,2,1,0:T(8,128)(2,1)} %ring_sum.1), calls=%async_computation.3 | async-start | bytes 786432 | tf_op jit(solution)/shard_map/all_to_all | solution.py:270
  110.3 26.2 %collective-permute-start.10 = (bf16[192,2048]{1,0:T(8,128)(2,1)}, bf16[192,2048]{1,0:T(8,128)(2,1)S(1)}, u32[]{:S(2)}, u32[]{:S(2)}) collective-permute-start(bf16[192,2048]{1,0:T(8,128)(2,1)} %pad_maximum_fusion.1), channel_id=1, source_target_pairs={{0,1},{1,0},{2,3},{3,2},{4,5},{5,4},{6,7},{7,6},{8,9},{9,8},{10,11... | collective-permute-start | bytes 2359304 | tf_op jit(solution)/shard_map/ppermute | solution.py:277
  114.9 21.6 %collective-permute-start.9 = (bf16[192,2048]{1,0:T(8,128)(2,1)}, bf16[192,2048]{1,0:T(8,128)(2,1)S(1)}, u32[]{:S(2)}, u32[]{:S(2)}) collective-permute-start(bf16[192,2048]{1,0:T(8,128)(2,1)} %pad_maximum_fusion), channel_id=1, source_target_pairs={{0,4},{2,6},{4,0},{6,2},{1,5},{3,7},{5,1},{7,3},{8,12},{10,14},{12... | collective-permute-start | bytes 2359304 | tf_op jit(solution)/shard_map/ppermute | solution.py:276
  119.4 0.6 copy-start.11
  120.0 28.0 %all-to-all-start.4 = ((bf16[4,32,384]{2,1,0:T(8,128)(2,1)}), bf16[4,32,384]{2,1,0:T(8,128)(2,1)S(1)}, u32[]{:S(2)}, u32[]{:S(2)}) async-start(bf16[4,32,384]{2,1,0:T(8,128)(2,1)} %copy-done.11), calls=%async_computation.4 | async-start | bytes 196608 | tf_op jit(solution)/shard_map/all_to_all | solution.py:272

commit v7 on v5

--- a/solution.py
+++ b/solution.py
@@ -6,7 +6,7 @@
 from jax.sharding import Mesh
 from jax.sharding import PartitionSpec as P
 
-DP = ("zh", "zl", "xh", "core")
+DP = ("z", "xh", "core")
 REP = ("y", "xl")
 RING = ("xh", "xl")
 NEAR = [(0, 1), (1, 0)]
@@ -16,6 +16,7 @@
 VMEM = pl.BlockSpec(memory_space=pltpu.VMEM)
 SMEM = pl.BlockSpec(memory_space=pltpu.SMEM)
 ANY = pl.BlockSpec(memory_space=pl.ANY)
+HBM = pl.BlockSpec(memory_space=pltpu.HBM)
 LIMIT = 12 * 1024 * 1024
 
 
@@ -23,12 +24,15 @@
     return jnp.dot(a, b, preferred_element_type=jnp.float32)
 
 
-def split_kernel(place, whole, own, other):
-    xl = place[2]
-    part = own.shape[0] // 4
-    for y in range(4):
-        for x, out in ((xl, own), (1 - xl, other)):
-            out[y * part:(y + 1) * part, :] = whole[pl.ds(pl.multiple_of((y * 2 + x) * part, 16), part), :]
+def own_rows(ref, xl):
+    part = ref.shape[0] // 8
+    return jnp.concatenate(
+        [ref[pl.ds(pl.multiple_of((y * 2 + xl) * part, 16), part), :] for y in range(4)], axis=0
+    )
+
+
+def sent_kernel(place, whole, other):
+    other[...] = own_rows(whole, 1 - place[2])
 
 
 def live_kernel(place, whole, own, other):
@@ -48,13 +52,13 @@
         out[y, 1 - xl] = near_set[...]
 
 
-def own_kernel(grads, pre, down, out):
+def own_kernel(place, grads, pre, down, out):
     blocks, _, features = grads.shape
     hidden = sum(dot(grads[j], down[j * features:(j + 1) * features, :]) for j in range(blocks))
-    out[...] = jnp.where(pre[...] > 0, hidden, 0.0).astype(out.dtype)
-
-
-def terms_kernel(place, grads, own, pre_far, down_mine, down_other, up_own, up_mine, up_other, terms, up_far):
+    out[...] = jnp.where(own_rows(pre, place[2]) > 0, hidden, 0.0).astype(out.dtype)
+
+
+def terms_kernel(place, grads, own, pre_far, down_mine, down_other, up_own, up_mine, up_other, out, up_far, terms, sems):
     core = place[0]
     blocks, features = grads.shape[0], grads.shape[2]
     half = blocks // 2
@@ -67,29 +71,39 @@
         dot(grads[(1 - core) * half + j], down_other[j * features:(j + 1) * features, :]) for j in range(half)
     )
     far = jnp.where(pre_far[...] > 0, far, 0.0).astype(jnp.bfloat16)
-    terms[...] = (dot(own[...], up_own[...]) + dot(far, up_far[...])).astype(terms.dtype)
-
-
-def down_kernel(place, grads, pre_own, pre_far, kept, sent):
+    parts = sems.shape[0]
+    columns = terms.shape[1] // parts
+    running = []
+    for i in range(parts):
+        at = pl.ds(i * columns, columns)
+        terms[:, at] = (dot(own[...], up_own[:, at]) + dot(far, up_far[:, at])).astype(terms.dtype)
+        copy = pltpu.make_async_copy(terms.at[:, at], out.at[:, at], sems.at[i])
+        copy.start()
+        running.append(copy)
+    for copy in running:
+        copy.wait()
+
+
+def down_kernel(place, grads, pre_own, pre_far, kept_out, sent_out, kept, sent, sems):
     core, xh, xl, live = place[0], place[1], place[2], place[3]
     blocks, rows, features = grads.shape
-    units = pre_own.shape[1]
+    units = pre_far.shape[1]
     share = kept.shape[2]
     groups = features // (4 * share)
-    at = lax.broadcasted_iota(jnp.int32, pre_own.shape, 0)
+    at = lax.broadcasted_iota(jnp.int32, pre_far.shape, 0)
     part = rows // 4
     row = at + (at // part + xl) * part
     hidden = jnp.concatenate(
-        [jnp.where(row < live, jnp.maximum(pre[...], 0), 0).astype(jnp.bfloat16) for pre in (pre_own, pre_far)],
+        [jnp.where(row < live, jnp.maximum(pre, 0), 0).astype(jnp.bfloat16) for pre in (own_rows(pre_own, xl), pre_far[...])],
         axis=1,
     )
+    running = []
     for j in range(blocks):
         block = lax.dot_general(
             grads[j], hidden, (((0,), (0,)), ((), ())), preferred_element_type=jnp.float32
         ).astype(kept.dtype)
         for g in range(groups):
-            zh, zl = divmod(j * groups + g, 4)
-            z = zl * (kept.shape[1] // 4) + zh
+            z = j * groups + g
             for h in range(2):
                 first = (g * 4 + h * 2) * share
                 low = block[first:first + share, :]
@@ -100,11 +114,27 @@
                     kind = t * 2 + jnp.abs(xh - h)
                     kept[kind, z] = mine[:, t * units:(t + 1) * units]
                     sent[kind, z] = other[:, t * units:(t + 1) * units]
+        at = pl.ds(j * groups, groups)
+        for i, (source, out) in enumerate(((sent, sent_out), (kept, kept_out))):
+            copy = pltpu.make_async_copy(source.at[:, at], out.at[:, at], sems.at[i, j])
+            copy.start()
+            running.append(copy)
+    for copy in running:
+        copy.wait()
 
 
 def ring_kernel(own, near, far, across, out):
     total = own[...].astype(jnp.float32) + near[...].astype(jnp.float32)
     out[...] = (total + far[...].astype(jnp.float32) + across[...].astype(jnp.float32)).astype(out.dtype)
+
+
+def rows_kernel(came, out):
+    out[...] = sum(came[i].astype(jnp.float32) for i in range(came.shape[0])).astype(out.dtype)
+
+
+def chip_kernel(kept, came, *outs):
+    for kind, out in enumerate(outs):
+        out[...] = (kept[kind].astype(jnp.float32) + came[kind].astype(jnp.float32)).astype(out.dtype)
 
 
 def put(place, blocks, out, sems):
@@ -144,7 +174,7 @@
 def on_device(grad_out, pre_act, up_weight, down_weight, slot_counts):
     slot_rows, features = grad_out.shape
     hidden_units = pre_act.shape[1]
-    ys, zs = lax.axis_size("y"), lax.axis_size(("zh", "zl"))
+    ys, zs = lax.axis_size("y"), lax.axis_size("z")
     reps = 2 * ys
     width = features * reps
     rows = slot_rows // reps
@@ -167,15 +197,17 @@
         compiler_params=params,
         name="live_sets",
     )(place, grad_out)
-    pre_own, pre_sent = pl.pallas_call(
-        split_kernel,
-        out_shape=(pre_shape, pre_shape),
+    pre_sent = pl.pallas_call(
+        sent_kernel,
+        out_shape=pre_shape,
         in_specs=[SMEM, VMEM],
-        out_specs=(VMEM, VMEM),
-        compiler_params=params,
-        name="pre_sets",
+        out_specs=VMEM,
+        compiler_params=params,
+        name="pre_sent",
     )(place, pre_act)
     near_set = lax.ppermute(other_set, "xl", NEAR)
+    down_sent = own_part(down_weight.reshape(2, width // 2, hidden_units), core, 0)
+    near_set, _ = lax.optimization_barrier((near_set, down_sent))
     grads = pl.pallas_call(
         spread_kernel,
         out_shape=jax.ShapeDtypeStruct((ys, 2, half_rows, features), bf16),
@@ -187,7 +219,7 @@
     grads = lax.all_to_all(grads, "y", 0, 0, tiled=True).reshape(reps, half_rows, features)
     pre_far = lax.ppermute(pre_sent, "xl", NEAR)
 
-    down_mine = lax.ppermute(own_part(down_weight.reshape(2, width // 2, hidden_units), core, 0), RING, FAR)
+    down_mine = lax.ppermute(down_sent, RING, FAR)
     up_mine = lax.ppermute(
         own_part(up_weight.reshape(2, hidden_units // 2, width), core, 0), ("xh", "core", "xl"), MIXED
     )
@@ -197,49 +229,40 @@
     pre_grad = pl.pallas_call(
         own_kernel,
         out_shape=jax.ShapeDtypeStruct((half_rows, hidden_units), bf16),
-        in_specs=[VMEM] * 3,
+        in_specs=[SMEM] + [VMEM] * 3,
         out_specs=VMEM,
         compiler_params=pltpu.CompilerParams(vmem_limit_bytes=LIMIT),
         cost_estimate=pl.CostEstimate(
             flops=2 * half_rows * width * hidden_units, bytes_accessed=4 * width * hidden_units, transcendentals=0
         ),
         name="own_grad",
-    )(grads, pre_own, down_weight)
+    )(place, grads, pre_act, down_weight)
     share = width // (4 * zs)
     laid_out = jax.ShapeDtypeStruct((4, zs, share, hidden_units), bf16)
     kept, sent = pl.pallas_call(
         down_kernel,
         out_shape=(laid_out, laid_out),
         in_specs=[SMEM] + [VMEM] * 3,
-        out_specs=(VMEM, VMEM),
+        out_specs=(HBM, HBM),
+        scratch_shapes=[pltpu.VMEM(laid_out.shape, bf16)] * 2 + [pltpu.SemaphoreType.DMA((2, reps))],
         compiler_params=pltpu.CompilerParams(vmem_limit_bytes=LIMIT),
         cost_estimate=pl.CostEstimate(
             flops=4 * half_rows * width * hidden_units, bytes_accessed=8 * width * hidden_units, transcendentals=0
         ),
         name="down_terms",
-    )(place, grads, pre_own, pre_far)
-
-    share = width // (4 * zs)
-    laid_out = jax.ShapeDtypeStruct((4, zs, share, hidden_units), bf16)
-    kept, sent = pl.pallas_call(
-        down_kernel,
-        out_shape=(laid_out, laid_out),
-        in_specs=[SMEM] + [VMEM] * 3,
-        out_specs=(VMEM, VMEM),
-        compiler_params=pltpu.CompilerParams(vmem_limit_bytes=LIMIT),
-        cost_estimate=pl.CostEstimate(
-            flops=4 * half_rows * width * hidden_units, bytes_accessed=8 * width * hidden_units, transcendentals=0
-        ),
-        name="down_terms",
-    )(place, grads, pre_own, pre_far)
+    )(place, grads, pre_act, pre_far)
 
     pre_later, sent = lax.optimization_barrier((pre_far, sent))
     terms = pl.pallas_call(
         terms_kernel,
         out_shape=jax.ShapeDtypeStruct((half_rows, width), bf16),
         in_specs=[SMEM] + [VMEM] * 8,
-        out_specs=VMEM,
-        scratch_shapes=[pltpu.VMEM((hidden_units, width), bf16)],
+        out_specs=HBM,
+        scratch_shapes=[
+            pltpu.VMEM((hidden_units, width), bf16),
+            pltpu.VMEM((half_rows, width), bf16),
+            pltpu.SemaphoreType.DMA((4,)),
+        ],
         compiler_params=pltpu.CompilerParams(vmem_limit_bytes=LIMIT),
         cost_estimate=pl.CostEstimate(
             flops=6 * half_rows * width * hidden_units, bytes_accessed=12 * width * hidden_units, transcendentals=0
@@ -249,21 +272,36 @@
 
     f32 = jnp.float32
     came = lax.all_to_all(terms.reshape(ys, rows, width), "y", 0, 0, tiled=True)
-    own = sum(came[i].astype(f32) for i in range(ys)).astype(bf16)
+    own = pl.pallas_call(
+        rows_kernel,
+        out_shape=jax.ShapeDtypeStruct((rows, width), bf16),
+        in_specs=[VMEM],
+        out_specs=VMEM,
+        compiler_params=params,
+        name="own_rows",
+    )(came)
 
     other = lax.ppermute(sent, "core", NEAR)
-    chip = [(kept[k].astype(f32) + other[k].astype(f32)) for k in range(4)]
+    kind = jax.ShapeDtypeStruct((zs, share, hidden_units), bf16)
+    own_chip, across_chip, near_chip, far_chip = pl.pallas_call(
+        chip_kernel,
+        out_shape=(kind,) * 4,
+        in_specs=[VMEM] * 2,
+        out_specs=(VMEM,) * 4,
+        compiler_params=params,
+        name="chip_sum",
+    )(kept, other)
     ring = [
-        lax.ppermute(chip[2].astype(bf16), "xl", NEAR),
-        lax.ppermute(chip[3].astype(bf16), RING, FAR),
-        lax.ppermute(chip[1].astype(bf16), RING, ACROSS),
+        lax.ppermute(near_chip, "xl", NEAR),
+        lax.ppermute(far_chip, RING, FAR),
+        lax.ppermute(across_chip, RING, ACROSS),
     ]
 
     near = lax.ppermute(own, "xl", NEAR)
     below = lax.ppermute(own, "y", turn(1))
     above = lax.ppermute(own, "y", turn(-1))
 
-    own_chip, ring, _ = lax.optimization_barrier((chip[0].astype(bf16), ring, own))
+    own_chip, ring, _ = lax.optimization_barrier((own_chip, ring, own))
     ring_sum = pl.pallas_call(
         ring_kernel,
         out_shape=jax.ShapeDtypeStruct((zs, share, hidden_units), bf16),
@@ -273,15 +311,8 @@
         cost_estimate=pl.CostEstimate(flops=2 * width * hidden_units, bytes_accessed=10 * width * hidden_units, transcendentals=0),
         name="ring_sum",
     )(own_chip, *ring)
-    low_terms = lax.all_to_all(ring_sum, "zl", 0, 0, tiled=True).reshape(4, zs // 4, share, hidden_units)
-    low_sum = sum(low_terms[i].astype(f32) for i in range(4))
-    highs = zs // 4
-    high = lax.axis_index("zh")
-    high_sum = own_part(low_sum, high, 0)
-    for step in range(1, highs):
-        part = own_part(low_sum, lax.rem(high + step, highs), 0)
-        high_sum += lax.ppermute(part, "zh", [(i, (i + step) % highs) for i in range(highs)])
-    down_grad = high_sum / (4 * zs)
+    z_terms = lax.all_to_all(ring_sum, "z", 0, 0, tiled=True)
+    down_grad = jnp.sum(z_terms.astype(f32), axis=0) / (4 * zs)
 
     near, below, above = lax.optimization_barrier((near, below, above))
     across = lax.ppermute(jnp.concatenate([own, near]), "y", turn(2))
@@ -312,7 +343,7 @@
 def solution(mesh):
     zs = mesh.shape["dp"] // 4
     ys = mesh.shape["rep"] // 2
-    finer = Mesh(mesh.devices.reshape(zs // 4, 4, 2, 2, ys, 2), (*DP, *REP))
+    finer = Mesh(mesh.devices.reshape(zs, 2, 2, ys, 2), (*DP, *REP))
     in_specs = (P(DP, REP), P(DP, REP), P(REP, None), P(None, REP), P(DP))
     out_specs = (P(DP, None), P(DP, REP))
     return jax.shard_map(

time: 145 us -> 146 us (level)
  the two profiles are of different devices: /device:TPU:40 before, /device:TPU:6 now
where the time goes in v7:
time: 146 us; the launch traced here: 145 us
  starting transfers between devices  72.6 us (50%)
  waiting for transfers between devices  42.1 us (29%)
  Pallas kernels  22.4 us (15%)
  local copies, waits for them, and re-layouts  5.5 us (4%)
  between operations  1.65 us (1%)
    all_to_all x1, starting transfers between devices, on_device(): z_terms = lax.all_to_all(ring_sum, 'z', 0, 0, tiled=True)  15.2 us
    ppermute x1, waiting for transfers between devices, on_device(): beside = lax.ppermute(jnp.concatenate([below, above]), 'xl', NEAR)  12.2 us
    ppermute x1, waiting for transfers between devices, on_device(): down_mine = lax.ppermute(down_sent, RING, FAR)  12.2 us
    all_to_all x1, waiting for transfers between devices, on_device(): came = lax.all_to_all(terms.reshape(ys, rows, width), 'y', 0, 0, tiled=True)  9.01 us
    ppermute x1, starting transfers between devices, on_device(): down_mine = lax.ppermute(down_sent, RING, FAR)  6.04 us
    pallas_call x1, Pallas kernels, on_device(): pl.pallas_call(down_kernel, out_shape=(laid_out, laid_out), in_specs=[SME...  5.54 us
    pallas_call x1, Pallas kernels, on_device(): pl.pallas_call(terms_kernel, out_shape=jax.ShapeDtypeStruct((half_rows, w...  5.28 us
    ppermute x1, starting transfers between devices, on_device(): lax.ppermute(across_chip, RING, ACROSS)  5.22 us
  transfers between devices with their start and end apart: 18, of which 5 were waited for; matrix products, arithmetic and copies ran while one was open for 2% of the time, Pallas kernels for 14%

profile of v7, /device:TPU:6, one launch (start us, length us, event | category | flops | bytes accessed | tf_op | source)
XLA Modules:
  0.0 145.1 jit_solution(18385842586587434987)
XLA Ops:
  1.3 0.1 stack.19.place
  1.4 1.0 copy-done.6
  2.4 0.6 live_sets.1
  3.0 2.7 %collective-permute-start = (bf16[384,256]{1,0:T(8,128)(2,1)S(1)}, bf16[384,256]{1,0:T(8,128)(2,1)S(1)}, u32[]{:S(2)}, u32[]{:S(2)}) collective-permute-start(bf16[384,256]{1,0:T(8,128)(2,1)S(1)} %get-tuple-element.21), channel_id=1, source_target_pairs={{0,1},{1,0},{2,3},{3,2},{4,5},{5,4},{6,7},{7,6},{8,9},{9,8},{10,11... | collective-permute-start | bytes 589832 | tf_op jit(solution)/shard_map/ppermute | solution.py:208
  5.7 2.1 %dynamic-slice_bitcast_fusion.1 = bf16[1024,384]{1,0:T(8,128)(2,1)} fusion(bf16[2,1024,384]{2,1,0:T(8,128)(2,1)} %bitcast.16, s32[]{:T(128)S(6)} %select_n.6), kind=kLoop, calls=%fused_computation.4 | loop fusion | bytes 1572868 | tf_op jit(solution)/shard_map/jit(dynamic_index_in_dim)/squeeze | solution.py:171
  7.8 3.7 %collective-permute-done.near_set = bf16[384,256]{1,0:T(8,128)(2,1)S(1)} collective-permute-done((bf16[384,256]{1,0:T(8,128)(2,1)S(1)}, bf16[384,256]{1,0:T(8,128)(2,1)S(1)}, u32[]{:S(2)}, u32[]{:S(2)}) %collective-permute-start) | collective-permute-done | bytes 196640 | tf_op jit(solution)/shard_map/ppermute | solution.py:208
  11.5 1.8 %spread.1 = bf16[4,2,384,256]{3,2,1,0:T(8,128)(2,1)} custom-call(s32[5]{0:T(128)S(1)} %stack.19.place, bf16[384,256]{1,0:T(8,128)(2,1)S(1)} %get-tuple-element.20.own_set, bf16[384,256]{1,0:T(8,128)(2,1)S(1)} %collective-permute-done.near_set), custom_call_target="tpu_custom_call" | custom-call | tf_op jit(solution)/shard_map/spread/pallas_call | solution.py:211
  13.3 4.6 %all-to-all-start = ((bf16[4,2,384,256]{3,2,1,0:T(8,128)(2,1)}), bf16[4,2,384,256]{3,2,1,0:T(8,128)(2,1)S(1)}, u32[]{:S(2)}, u32[]{:S(2)}) async-start(bf16[4,2,384,256]{3,2,1,0:T(8,128)(2,1)} %spread.1), calls=%async_computation | async-start | bytes 3145728 | tf_op jit(solution)/shard_map/all_to_all | solution.py:219
  17.9 6.0 %collective-permute-start.2 = (bf16[1024,384]{1,0:T(8,128)(2,1)}, bf16[1024,384]{1,0:T(8,128)(2,1)}, u32[]{:S(2)}, u32[]{:S(2)}) collective-permute-start(bf16[1024,384]{1,0:T(8,128)(2,1)} %dynamic-slice_bitcast_fusion.1), channel_id=1, source_target_pairs={{0,17},{17,0},{1,16},{16,1},{2,19},{19,2},{3,18},{18,3},{4,21},{21... | collective-permute-start | bytes 2359304 | tf_op jit(solution)/shard_map/ppermute | solution.py:222
  24.0 0.1 dynamic-slice_bitcast_fusion
  24.0 1.9 %collective-permute-start.4 = (bf16[192,2048]{1,0:T(8,128)(2,1)S(1)}, bf16[192,2048]{1,0:T(8,128)(2,1)}, u32[]{:S(2)}, u32[]{:S(2)}) collective-permute-start(bf16[192,2048]{1,0:T(8,128)(2,1)S(1)} %dynamic-slice_bitcast_fusion), channel_id=1, source_target_pairs={{0,1},{1,0},{8,25},{9,24},{16,17},{17,16},{24,9},{25,8},{2,3},{3,2... | collective-permute-start | bytes 2359304 | tf_op jit(solution)/shard_map/ppermute | solution.py:223
  26.0 0.6 pre_sent.1
  26.6 3.9 %collective-permute-start.1 = (bf16[384,384]{1,0:T(8,128)(2,1)S(1)}, bf16[384,384]{1,0:T(8,128)(2,1)S(1)}, u32[]{:S(2)}, u32[]{:S(2)}) collective-permute-start(bf16[384,384]{1,0:T(8,128)(2,1)S(1)} %pre_sent.1), channel_id=1, source_target_pairs={{0,1},{1,0},{2,3},{3,2},{4,5},{5,4},{6,7},{7,6},{8,9},{9,8},{10,11... | collective-permute-start | bytes 884744 | tf_op jit(solution)/shard_map/ppermute | solution.py:220
  30.5 12.2 %collective-permute-done.2.down_mine = bf16[1024,384]{1,0:T(8,128)(2,1)} collective-permute-done((bf16[1024,384]{1,0:T(8,128)(2,1)}, bf16[1024,384]{1,0:T(8,128)(2,1)}, u32[]{:S(2)}, u32[]{:S(2)}) %collective-permute-start.2) | collective-permute-done | bytes 786464 | tf_op jit(solution)/shard_map/ppermute | solution.py:222
  42.7 1.9 %collective-permute-start.3 = (bf16[1024,384]{1,0:T(8,128)(2,1)}, bf16[1024,384]{1,0:T(8,128)(2,1)}, u32[]{:S(2)}, u32[]{:S(2)}) collective-permute-start(bf16[1024,384]{1,0:T(8,128)(2,1)} %collective-permute-done.2.down_mine), channel_id=1, source_target_pairs={{0,8},{8,0},{1,9},{9,1},{2,10},{10,2},{3,11},{11,3},{4,12},{12,4},... | collective-permute-start | bytes 2359304 | tf_op jit(solution)/shard_map/ppermute | solution.py:226
  44.6 0.0 collective-permute-done.4.up_mine
  44.6 5.1 %collective-permute-start.5 = (bf16[192,2048]{1,0:T(8,128)(2,1)}, bf16[192,2048]{1,0:T(8,128)(2,1)}, u32[]{:S(2)}, u32[]{:S(2)}) collective-permute-start(bf16[192,2048]{1,0:T(8,128)(2,1)} %collective-permute-done.4.up_mine), channel_id=1, source_target_pairs={{0,8},{8,0},{1,9},{9,1},{2,10},{10,2},{3,11},{11,3},{4,12},{12,4},... | collective-permute-start | bytes 2359304 | tf_op jit(solution)/shard_map/ppermute | solution.py:227
  49.7 0.0 all-to-all-done
  49.8 0.0 copy-start.3
  49.8 1.1 copy-done.3
  50.8 5.5 %down_terms.1 = (bf16[4,16,32,384]{3,2,1,0:T(8,128)(2,1)S(1)}, bf16[4,16,32,384]{3,2,1,0:T(8,128)(2,1)}) custom-call(s32[5]{0:T(128)S(1)} %stack.19.place, bf16[8,384,256]{2,1,0:T(8,128)(2,1)S(1)} %bitcast.12, bf16[768,384]{1,0:T(8,128)(2,1)S(1)} %copy-done.3, bf16[384,384]{1,0:T(8,128)(2,1)S(1)} %collective-permute-done.1.pre_far), custom_call_target="tpu_custom_call" | custom-call | flops 1207959552 | bytes 6291456 | tf_op jit(solution)/shard_map/down_terms/pallas_call | solution.py:242
  56.4 1.2 copy-done.4
  57.5 1.9 %collective-permute-start.11 = (bf16[4,16,32,384]{3,2,1,0:T(8,128)(2,1)}, bf16[4,16,32,384]{3,2,1,0:T(8,128)(2,1)}, u32[]{:S(2)}, u32[]{:S(2)}) collective-permute-start(bf16[4,16,32,384]{3,2,1,0:T(8,128)(2,1)} %get-tuple-element.29), channel_id=1, source_target_pairs={{0,8},{8,0},{1,9},{9,1},{2,10},{10,2},{3,11},{11,3},{4,12},{12,4},... | collective-permute-start | bytes 4718600 | tf_op jit(solution)/shard_map/ppermute | solution.py:284
  59.5 1.5 %own_grad.1.own = bf16[384,384]{1,0:T(8,128)(2,1)S(1)} custom-call(s32[5]{0:T(128)S(1)} %stack.19.place, bf16[8,384,256]{2,1,0:T(8,128)(2,1)S(1)} %bitcast.13, bf16[768,384]{1,0:T(8,128)(2,1)S(1)} %copy-done.3, bf16[2048,384]{1,0:T(8,128)(2,1)S(1)} %copy-done.1), custom_call_target="tpu_custom_call" | custom-call | flops 603979776 | bytes 3145728 | tf_op jit(solution)/shard_map/own_grad/pallas_call | solution.py:229
  61.0 0.0 collective-permute-done.3.down_other
  61.0 5.3 %terms.1 = bf16[384,2048]{1,0:T(8,128)(2,1)} custom-call(s32[5]{0:T(128)S(1)} %stack.19.place, bf16[8,384,256]{2,1,0:T(8,128)(2,1)S(1)} %bitcast.14, bf16[384,384]{1,0:T(8,128)(2,1)S(1)} %own_grad.1.own, bf16[384,384]{1,0:T(8,128)(2,1)S(1)} %collective-permute-done.1.pre_far, bf16[1024,384]{1,0:T(8,128)(2,1)} %collective-permute-done.2.down_mine, ...), custom_call_target="tpu_custom_call" | custom-call | flops 1811939328 | bytes 9437184 | tf_op jit(solution)/shard_map/terms/pallas_call | solution.py:256
  66.3 4.7 %all-to-all-start.1 = ((bf16[4,96,2048]{2,1,0:T(8,128)(2,1)}), bf16[4,96,2048]{2,1,0:T(8,128)(2,1)S(1)}, u32[]{:S(2)}, u32[]{:S(2)}) async-start(bf16[4,96,2048]{2,1,0:T(8,128)(2,1)} %bitcast.9), calls=%async_computation.1 | async-start | bytes 3145728 | tf_op jit(solution)/shard_map/all_to_all | solution.py:274
  71.0 2.5 %chip_sum.1 = (bf16[16,32,384]{2,1,0:T(8,128)(2,1)S(1)}, bf16[16,32,384]{2,1,0:T(8,128)(2,1)}, bf16[16,32,384]{2,1,0:T(8,128)(2,1)}, bf16[16,32,384]{2,1,0:T(8,128)(2,1)}) custom-call(bf16[4,16,32,384]{3,2,1,0:T(8,128)(2,1)S(1)} %copy-done.5, bf16[4,16,32,384]{3,2,1,0:T(8,128)(2,1)} %collective-permute-done.11.came), custom_call_target="tpu_custom_call" | custom-call | tf_op jit(solution)/shard_map/chip_sum/pallas_call | solution.py:286
  73.5 1.9 %collective-permute-start.12 = (bf16[16,32,384]{2,1,0:T(8,128)(2,1)}, bf16[16,32,384]{2,1,0:T(8,128)(2,1)S(1)}, u32[]{:S(2)}, u32[]{:S(2)}) collective-permute-start(bf16[16,32,384]{2,1,0:T(8,128)(2,1)} %get-tuple-element.31), channel_id=1, source_target_pairs={{0,1},{1,0},{2,3},{3,2},{4,5},{5,4},{6,7},{7,6},{8,9},{9,8},{10,11... | collective-permute-start | bytes 1179656 | tf_op jit(solution)/shard_map/ppermute | solution.py:295
  75.4 2.7 %collective-permute-start.13 = (bf16[16,32,384]{2,1,0:T(8,128)(2,1)}, bf16[16,32,384]{2,1,0:T(8,128)(2,1)S(1)}, u32[]{:S(2)}, u32[]{:S(2)}) collective-permute-start(bf16[16,32,384]{2,1,0:T(8,128)(2,1)} %get-tuple-element.32), channel_id=1, source_target_pairs={{0,17},{17,0},{1,16},{16,1},{2,19},{19,2},{3,18},{18,3},{4,21},{21... | collective-permute-start | bytes 1179656 | tf_op jit(solution)/shard_map/ppermute | solution.py:296
  78.1 5.2 %collective-permute-start.14 = (bf16[16,32,384]{2,1,0:T(8,128)(2,1)}, bf16[16,32,384]{2,1,0:T(8,128)(2,1)S(1)}, u32[]{:S(2)}, u32[]{:S(2)}) collective-permute-start(bf16[16,32,384]{2,1,0:T(8,128)(2,1)} %get-tuple-element.33), channel_id=1, source_target_pairs={{0,16},{16,0},{1,17},{17,1},{2,18},{18,2},{3,19},{19,3},{4,20},{20... | collective-permute-start | bytes 1179656 | tf_op jit(solution)/shard_map/ppermute | solution.py:297
  83.4 9.0 %all-to-all-done.1.came = bf16[4,96,2048]{2,1,0:T(8,128)(2,1)S(1)} async-done(((bf16[4,96,2048]{2,1,0:T(8,128)(2,1)}), bf16[4,96,2048]{2,1,0:T(8,128)(2,1)S(1)}, u32[]{:S(2)}, u32[]{:S(2)}) %all-to-all-start.1) | async-done | bytes 1572896 | tf_op jit(solution)/shard_map/all_to_all | solution.py:274
  92.4 0.2 own_rows.1.own
  92.6 1.9 %collective-permute-start.6 = (bf16[96,2048]{1,0:T(8,128)(2,1)S(1)}, bf16[96,2048]{1,0:T(8,128)(2,1)S(1)}, u32[]{:S(2)}, u32[]{:S(2)}) collective-permute-start(bf16[96,2048]{1,0:T(8,128)(2,1)S(1)} %own_rows.1.own), channel_id=1, source_target_pairs={{0,1},{1,0},{2,3},{3,2},{4,5},{5,4},{6,7},{7,6},{8,9},{9,8},{10,11... | collective-permute-start | bytes 1179656 | tf_op jit(solution)/shard_map/ppermute | solution.py:300
  94.5 2.5 %collective-permute-start.7 = (bf16[96,2048]{1,0:T(8,128)(2,1)S(1)}, bf16[96,2048]{1,0:T(8,128)(2,1)S(1)}, u32[]{:S(2)}, u32[]{:S(2)}) collective-permute-start(bf16[96,2048]{1,0:T(8,128)(2,1)S(1)} %own_rows.1.own), channel_id=1, source_target_pairs={{0,2},{2,4},{4,6},{6,0},{1,3},{3,5},{5,7},{7,1},{8,10},{10,12},{12... | collective-permute-start | bytes 1179656 | tf_op jit(solution)/shard_map/ppermute | solution.py:301
  97.0 4.6 %collective-permute-start.8 = (bf16[96,2048]{1,0:T(8,128)(2,1)S(1)}, bf16[96,2048]{1,0:T(8,128)(2,1)S(1)}, u32[]{:S(2)}, u32[]{:S(2)}) collective-permute-start(bf16[96,2048]{1,0:T(8,128)(2,1)S(1)} %own_rows.1.own), channel_id=1, source_target_pairs={{0,6},{2,0},{4,2},{6,4},{1,7},{3,1},{5,3},{7,5},{8,14},{10,8},{12,... | collective-permute-start | bytes 1179656 | tf_op jit(solution)/shard_map/ppermute | solution.py:302
  101.6 1.0 ring_sum.1
  102.5 15.2 %all-to-all-start.2 = ((bf16[16,32,384]{2,1,0:T(8,128)(2,1)}), bf16[16,32,384]{2,1,0:T(8,128)(2,1)S(1)}, u32[]{:S(2)}, u32[]{:S(2)}) async-start(bf16[16,32,384]{2,1,0:T(8,128)(2,1)} %ring_sum.1), calls=%async_computation.2 | async-start | bytes 786432 | tf_op jit(solution)/shard_map/all_to_all | solution.py:314
  117.8 0.1 pad_maximum_fusion.1
  117.9 3.9 %collective-permute-start.10 = (bf16[192,2048]{1,0:T(8,128)(2,1)S(1)}, bf16[192,2048]{1,0:T(8,128)(2,1)S(1)}, u32[]{:S(2)}, u32[]{:S(2)}) collective-permute-start(bf16[192,2048]{1,0:T(8,128)(2,1)S(1)} %pad_maximum_fusion.1), channel_id=1, source_target_pairs={{0,1},{1,0},{2,3},{3,2},{4,5},{5,4},{6,7},{7,6},{8,9},{9,8},{10,11... | collective-permute-start | bytes 2359304 | tf_op jit(solution)/shard_map/ppermute | solution.py:319
  121.8 0.1 pad_maximum_fusion
  121.9 1.9 %collective-permute-start.9 = (bf16[192,2048]{1,0:T(8,128)(2,1)S(1)}, bf16[192,2048]{1,0:T(8,128)(2,1)S(1)}, u32[]{:S(2)}, u32[]{:S(2)}) collective-permute-start(bf16[192,2048]{1,0:T(8,128)(2,1)S(1)} %pad_maximum_fusion), channel_id=1, source_target_pairs={{0,4},{2,6},{4,0},{6,2},{1,5},{3,7},{5,1},{7,3},{8,12},{10,14},{12... | collective-permute-start | bytes 2359304 | tf_op jit(solution)/shard_map/ppermute | solution.py:318
  123.8 1.7 %place_first.1.partial = bf16[768,2048]{1,0:T(8,128)(2,1)} custom-call(s32[5]{0:T(128)S(1)} %stack.19.place, bf16[96,2048]{1,0:T(8,128)(2,1)S(1)} %own_rows.1.own, bf16[96,2048]{1,0:T(8,128)(2,1)S(1)} %collective-permute-done.6.near, bf16[96,2048]{1,0:T(8,128)(2,1)S(1)} %collective-permute-done.7.below, bf16[96,2048]{1,0:T(8,128)(2,1)S(1)} %collective-permute-done.8.above), custom_call_target="tpu_custom_call" | custom-call | tf_op jit(solution)/shard_map/place_first/pallas_call | solution.py:321
  125.5 12.2 %collective-permute-done.10.beside = bf16[192,2048]{1,0:T(8,128)(2,1)S(1)} collective-permute-done((bf16[192,2048]{1,0:T(8,128)(2,1)S(1)}, bf16[192,2048]{1,0:T(8,128)(2,1)S(1)}, u32[]{:S(2)}, u32[]{:S(2)}) %collective-permute-start.10) | collective-permute-done | bytes 786464 | tf_op jit(solution)/shard_map/ppermute | solution.py:319
  137.8 5.0 %collective-permute-done.9.across = bf16[192,2048]{1,0:T(8,128)(2,1)S(1)} collective-permute-done((bf16[192,2048]{1,0:T(8,128)(2,1)S(1)}, bf16[192,2048]{1,0:T(8,128)(2,1)S(1)}, u32[]{:S(2)}, u32[]{:S(2)}) %collective-permute-start.9) | collective-permute-done | bytes 786464 | tf_op jit(solution)/shard_map/ppermute | solution.py:318
  142.7 1.7 %place_last.1 = bf16[768,2048]{1,0:T(8,128)(2,1)} custom-call(s32[5]{0:T(128)S(1)} %stack.19.place, bf16[768,2048]{1,0:T(8,128)(2,1)} %place_first.1.partial, bf16[192,2048]{1,0:T(8,128)(2,1)S(1)} %collective-permute-done.9.across, bf16[192,2048]{1,0:T(8,128)(2,1)S(1)} %collective-permute-done.10.beside), custom_call_target="tpu_custom_call", output_to_operand_aliasing={{}: (1, {})} | custom-call | tf_op jit(solution)/shard_map/place_last/pallas_call | solution.py:330
  144.5 0.1 convert_reduce_fusion
  144.5 0.6 broadcast_multiply_fusion
  (20 shorter events, 0.0 us)
Async XLA Ops:
  1.4 1.0 copy-start.6
  3.0 8.5 %collective-permute-start = (bf16[384,256]{1,0:T(8,128)(2,1)S(1)}, bf16[384,256]{1,0:T(8,128)(2,1)S(1)}, u32[]{:S(2)}, u32[]{:S(2)}) collective-permute-start(bf16[384,256]{1,0:T(8,128)(2,1)S(1)} %get-tuple-element.21), channel_id=1, source_target_pairs={{0,1},{1,0},{2,3},{3,2},{4,5},{5,4},{6,7},{7,6},{8,9},{9,8},{10,11... | collective-permute-start | bytes 589832 | tf_op jit(solution)/shard_map/ppermute | solution.py:208
  13.3 10.6 %copy-start = (bf16[384,2048]{1,0:T(8,128)(2,1)S(1)}, bf16[384,2048]{1,0:T(8,128)(2,1)}, u32[]{:S(2)}) copy-start(bf16[384,2048]{1,0:T(8,128)(2,1)} %up_own.1) | copy-start | bytes 4718596
  13.3 36.4 %all-to-all-start = ((bf16[4,2,384,256]{3,2,1,0:T(8,128)(2,1)}), bf16[4,2,384,256]{3,2,1,0:T(8,128)(2,1)S(1)}, u32[]{:S(2)}, u32[]{:S(2)}) async-start(bf16[4,2,384,256]{3,2,1,0:T(8,128)(2,1)} %spread.1), calls=%async_computation | async-start | bytes 3145728 | tf_op jit(solution)/shard_map/all_to_all | solution.py:219
  17.9 8.1 %copy-start.2 = (bf16[768,384]{1,0:T(8,128)(2,1)S(1)}, bf16[768,384]{1,0:T(8,128)(2,1)}, u32[]{:S(2)}) copy-start(bf16[768,384]{1,0:T(8,128)(2,1)} %pre_own.1) | copy-start | bytes 1769476
  17.9 24.8 %collective-permute-start.2 = (bf16[1024,384]{1,0:T(8,128)(2,1)}, bf16[1024,384]{1,0:T(8,128)(2,1)}, u32[]{:S(2)}, u32[]{:S(2)}) collective-permute-start(bf16[1024,384]{1,0:T(8,128)(2,1)} %dynamic-slice_bitcast_fusion.1), channel_id=1, source_target_pairs={{0,17},{17,0},{1,16},{16,1},{2,19},{19,2},{3,18},{18,3},{4,21},{21... | collective-permute-start | bytes 2359304 | tf_op jit(solution)/shard_map/ppermute | solution.py:222
  24.0 20.6 %collective-permute-start.4 = (bf16[192,2048]{1,0:T(8,128)(2,1)S(1)}, bf16[192,2048]{1,0:T(8,128)(2,1)}, u32[]{:S(2)}, u32[]{:S(2)}) collective-permute-start(bf16[192,2048]{1,0:T(8,128)(2,1)S(1)} %dynamic-slice_bitcast_fusion), channel_id=1, source_target_pairs={{0,1},{1,0},{8,25},{9,24},{16,17},{17,16},{24,9},{25,8},{2,3},{3,2... | collective-permute-start | bytes 2359304 | tf_op jit(solution)/shard_map/ppermute | solution.py:223
  26.6 23.2 %collective-permute-start.1 = (bf16[384,384]{1,0:T(8,128)(2,1)S(1)}, bf16[384,384]{1,0:T(8,128)(2,1)S(1)}, u32[]{:S(2)}, u32[]{:S(2)}) collective-permute-start(bf16[384,384]{1,0:T(8,128)(2,1)S(1)} %pre_sent.1), channel_id=1, source_target_pairs={{0,1},{1,0},{2,3},{3,2},{4,5},{5,4},{6,7},{7,6},{8,9},{9,8},{10,11... | collective-permute-start | bytes 884744 | tf_op jit(solution)/shard_map/ppermute | solution.py:220
  42.7 18.3 %collective-permute-start.3 = (bf16[1024,384]{1,0:T(8,128)(2,1)}, bf16[1024,384]{1,0:T(8,128)(2,1)}, u32[]{:S(2)}, u32[]{:S(2)}) collective-permute-start(bf16[1024,384]{1,0:T(8,128)(2,1)} %collective-permute-done.2.down_mine), channel_id=1, source_target_pairs={{0,8},{8,0},{1,9},{9,1},{2,10},{10,2},{3,11},{11,3},{4,12},{12,4},... | collective-permute-start | bytes 2359304 | tf_op jit(solution)/shard_map/ppermute | solution.py:226
  44.6 16.4 %collective-permute-start.5 = (bf16[192,2048]{1,0:T(8,128)(2,1)}, bf16[192,2048]{1,0:T(8,128)(2,1)}, u32[]{:S(2)}, u32[]{:S(2)}) collective-permute-start(bf16[192,2048]{1,0:T(8,128)(2,1)} %collective-permute-done.4.up_mine), channel_id=1, source_target_pairs={{0,8},{8,0},{1,9},{9,1},{2,10},{10,2},{3,11},{11,3},{4,12},{12,4},... | collective-permute-start | bytes 2359304 | tf_op jit(solution)/shard_map/ppermute | solution.py:227
  49.8 1.1 copy-start.3
  50.8 8.7 %copy-start.1 = (bf16[2048,384]{1,0:T(8,128)(2,1)S(1)}, bf16[2048,384]{1,0:T(8,128)(2,1)}, u32[]{:S(2)}) copy-start(bf16[2048,384]{1,0:T(8,128)(2,1)} %down.1) | copy-start | bytes 4718596
  56.4 1.2 copy-start.4
  57.5 13.4 %collective-permute-start.11 = (bf16[4,16,32,384]{3,2,1,0:T(8,128)(2,1)}, bf16[4,16,32,384]{3,2,1,0:T(8,128)(2,1)}, u32[]{:S(2)}, u32[]{:S(2)}) collective-permute-start(bf16[4,16,32,384]{3,2,1,0:T(8,128)(2,1)} %get-tuple-element.29), channel_id=1, source_target_pairs={{0,8},{8,0},{1,9},{9,1},{2,10},{10,2},{3,11},{11,3},{4,12},{12,4},... | collective-permute-start | bytes 4718600 | tf_op jit(solution)/shard_map/ppermute | solution.py:284
  66.3 4.7 %copy-start.5 = (bf16[4,16,32,384]{3,2,1,0:T(8,128)(2,1)S(1)}, bf16[4,16,32,384]{3,2,1,0:T(8,128)(2,1)}, u32[]{:S(2)}) copy-start(bf16[4,16,32,384]{3,2,1,0:T(8,128)(2,1)} %copy-done.4) | copy-start | bytes 4718596
  66.3 26.0 %all-to-all-start.1 = ((bf16[4,96,2048]{2,1,0:T(8,128)(2,1)}), bf16[4,96,2048]{2,1,0:T(8,128)(2,1)S(1)}, u32[]{:S(2)}, u32[]{:S(2)}) async-start(bf16[4,96,2048]{2,1,0:T(8,128)(2,1)} %bitcast.9), calls=%async_computation.1 | async-start | bytes 3145728 | tf_op jit(solution)/shard_map/all_to_all | solution.py:274
  73.5 23.4 %collective-permute-start.12 = (bf16[16,32,384]{2,1,0:T(8,128)(2,1)}, bf16[16,32,384]{2,1,0:T(8,128)(2,1)S(1)}, u32[]{:S(2)}, u32[]{:S(2)}) collective-permute-start(bf16[16,32,384]{2,1,0:T(8,128)(2,1)} %get-tuple-element.31), channel_id=1, source_target_pairs={{0,1},{1,0},{2,3},{3,2},{4,5},{5,4},{6,7},{7,6},{8,9},{9,8},{10,11... | collective-permute-start | bytes 1179656 | tf_op jit(solution)/shard_map/ppermute | solution.py:295
  75.4 26.1 %collective-permute-start.13 = (bf16[16,32,384]{2,1,0:T(8,128)(2,1)}, bf16[16,32,384]{2,1,0:T(8,128)(2,1)S(1)}, u32[]{:S(2)}, u32[]{:S(2)}) collective-permute-start(bf16[16,32,384]{2,1,0:T(8,128)(2,1)} %get-tuple-element.32), channel_id=1, source_target_pairs={{0,17},{17,0},{1,16},{16,1},{2,19},{19,2},{3,18},{18,3},{4,21},{21... | collective-permute-start | bytes 1179656 | tf_op jit(solution)/shard_map/ppermute | solution.py:296
  78.1 23.5 %collective-permute-start.14 = (bf16[16,32,384]{2,1,0:T(8,128)(2,1)}, bf16[16,32,384]{2,1,0:T(8,128)(2,1)S(1)}, u32[]{:S(2)}, u32[]{:S(2)}) collective-permute-start(bf16[16,32,384]{2,1,0:T(8,128)(2,1)} %get-tuple-element.33), channel_id=1, source_target_pairs={{0,16},{16,0},{1,17},{17,1},{2,18},{18,2},{3,19},{19,3},{4,20},{20... | collective-permute-start | bytes 1179656 | tf_op jit(solution)/shard_map/ppermute | solution.py:297
  92.6 25.2 %collective-permute-start.6 = (bf16[96,2048]{1,0:T(8,128)(2,1)S(1)}, bf16[96,2048]{1,0:T(8,128)(2,1)S(1)}, u32[]{:S(2)}, u32[]{:S(2)}) collective-permute-start(bf16[96,2048]{1,0:T(8,128)(2,1)S(1)} %own_rows.1.own), channel_id=1, source_target_pairs={{0,1},{1,0},{2,3},{3,2},{4,5},{5,4},{6,7},{7,6},{8,9},{9,8},{10,11... | collective-permute-start | bytes 1179656 | tf_op jit(solution)/shard_map/ppermute | solution.py:300
  94.5 23.3 %collective-permute-start.7 = (bf16[96,2048]{1,0:T(8,128)(2,1)S(1)}, bf16[96,2048]{1,0:T(8,128)(2,1)S(1)}, u32[]{:S(2)}, u32[]{:S(2)}) collective-permute-start(bf16[96,2048]{1,0:T(8,128)(2,1)S(1)} %own_rows.1.own), channel_id=1, source_target_pairs={{0,2},{2,4},{4,6},{6,0},{1,3},{3,5},{5,7},{7,1},{8,10},{10,12},{12... | collective-permute-start | bytes 1179656 | tf_op jit(solution)/shard_map/ppermute | solution.py:301
  97.0 20.8 %collective-permute-start.8 = (bf16[96,2048]{1,0:T(8,128)(2,1)S(1)}, bf16[96,2048]{1,0:T(8,128)(2,1)S(1)}, u32[]{:S(2)}, u32[]{:S(2)}) collective-permute-start(bf16[96,2048]{1,0:T(8,128)(2,1)S(1)} %own_rows.1.own), channel_id=1, source_target_pairs={{0,6},{2,0},{4,2},{6,4},{1,7},{3,1},{5,3},{7,5},{8,14},{10,8},{12,... | collective-permute-start | bytes 1179656 | tf_op jit(solution)/shard_map/ppermute | solution.py:302
  102.5 41.9 %all-to-all-start.2 = ((bf16[16,32,384]{2,1,0:T(8,128)(2,1)}), bf16[16,32,384]{2,1,0:T(8,128)(2,1)S(1)}, u32[]{:S(2)}, u32[]{:S(2)}) async-start(bf16[16,32,384]{2,1,0:T(8,128)(2,1)} %ring_sum.1), calls=%async_computation.2 | async-start | bytes 786432 | tf_op jit(solution)/shard_map/all_to_all | solution.py:314
  117.9 19.9 %collective-permute-start.10 = (bf16[192,2048]{1,0:T(8,128)(2,1)S(1)}, bf16[192,2048]{1,0:T(8,128)(2,1)S(1)}, u32[]{:S(2)}, u32[]{:S(2)}) collective-permute-start(bf16[192,2048]{1,0:T(8,128)(2,1)S(1)} %pad_maximum_fusion.1), channel_id=1, source_target_pairs={{0,1},{1,0},{2,3},{3,2},{4,5},{5,4},{6,7},{7,6},{8,9},{9,8},{10,11... | collective-permute-start | bytes 2359304 | tf_op jit(solution)/shard_map/ppermute | solution.py:319
  121.9 20.8 %collective-permute-start.9 = (bf16[192,2048]{1,0:T(8,128)(2,1)S(1)}, bf16[192,2048]{1,0:T(8,128)(2,1)S(1)}, u32[]{:S(2)}, u32[]{:S(2)}) collective-permute-start(bf16[192,2048]{1,0:T(8,128)(2,1)S(1)} %pad_maximum_fusion), channel_id=1, source_target_pairs={{0,4},{2,6},{4,0},{6,2},{1,5},{3,7},{5,1},{7,3},{8,12},{10,14},{12... | collective-permute-start | bytes 2359304 | tf_op jit(solution)/shard_map/ppermute | solution.py:318

commit v8 on v5

--- a/solution.py
+++ b/solution.py
@@ -6,7 +6,7 @@
 from jax.sharding import Mesh
 from jax.sharding import PartitionSpec as P
 
-DP = ("zh", "zl", "xh", "core")
+DP = ("z", "xh", "core")
 REP = ("y", "xl")
 RING = ("xh", "xl")
 NEAR = [(0, 1), (1, 0)]
@@ -67,7 +67,10 @@
         dot(grads[(1 - core) * half + j], down_other[j * features:(j + 1) * features, :]) for j in range(half)
     )
     far = jnp.where(pre_far[...] > 0, far, 0.0).astype(jnp.bfloat16)
-    terms[...] = (dot(own[...], up_own[...]) + dot(far, up_far[...])).astype(terms.dtype)
+    columns = terms.shape[1] // 4
+    for i in range(4):
+        at = slice(i * columns, (i + 1) * columns)
+        terms[:, at] = (dot(own[...], up_own[:, at]) + dot(far, up_far[:, at])).astype(terms.dtype)
 
 
 def down_kernel(place, grads, pre_own, pre_far, kept, sent):
@@ -88,8 +91,7 @@
             grads[j], hidden, (((0,), (0,)), ((), ())), preferred_element_type=jnp.float32
         ).astype(kept.dtype)
         for g in range(groups):
-            zh, zl = divmod(j * groups + g, 4)
-            z = zl * (kept.shape[1] // 4) + zh
+            z = j * groups + g
             for h in range(2):
                 first = (g * 4 + h * 2) * share
                 low = block[first:first + share, :]
@@ -144,7 +146,7 @@
 def on_device(grad_out, pre_act, up_weight, down_weight, slot_counts):
     slot_rows, features = grad_out.shape
     hidden_units = pre_act.shape[1]
-    ys, zs = lax.axis_size("y"), lax.axis_size(("zh", "zl"))
+    ys, zs = lax.axis_size("y"), lax.axis_size("z")
     reps = 2 * ys
     width = features * reps
     rows = slot_rows // reps
@@ -219,20 +221,6 @@
         name="down_terms",
     )(place, grads, pre_own, pre_far)
 
-    share = width // (4 * zs)
-    laid_out = jax.ShapeDtypeStruct((4, zs, share, hidden_units), bf16)
-    kept, sent = pl.pallas_call(
-        down_kernel,
-        out_shape=(laid_out, laid_out),
-        in_specs=[SMEM] + [VMEM] * 3,
-        out_specs=(VMEM, VMEM),
-        compiler_params=pltpu.CompilerParams(vmem_limit_bytes=LIMIT),
-        cost_estimate=pl.CostEstimate(
-            flops=4 * half_rows * width * hidden_units, bytes_accessed=8 * width * hidden_units, transcendentals=0
-        ),
-        name="down_terms",
-    )(place, grads, pre_own, pre_far)
-
     pre_later, sent = lax.optimization_barrier((pre_far, sent))
     terms = pl.pallas_call(
         terms_kernel,
@@ -273,15 +261,8 @@
         cost_estimate=pl.CostEstimate(flops=2 * width * hidden_units, bytes_accessed=10 * width * hidden_units, transcendentals=0),
         name="ring_sum",
     )(own_chip, *ring)
-    low_terms = lax.all_to_all(ring_sum, "zl", 0, 0, tiled=True).reshape(4, zs // 4, share, hidden_units)
-    low_sum = sum(low_terms[i].astype(f32) for i in range(4))
-    highs = zs // 4
-    high = lax.axis_index("zh")
-    high_sum = own_part(low_sum, high, 0)
-    for step in range(1, highs):
-        part = own_part(low_sum, lax.rem(high + step, highs), 0)
-        high_sum += lax.ppermute(part, "zh", [(i, (i + step) % highs) for i in range(highs)])
-    down_grad = high_sum / (4 * zs)
+    z_terms = lax.all_to_all(ring_sum, "z", 0, 0, tiled=True)
+    down_grad = jnp.sum(z_terms.astype(f32), axis=0) / (4 * zs)
 
     near, below, above = lax.optimization_barrier((near, below, above))
     across = lax.ppermute(jnp.concatenate([own, near]), "y", turn(2))
@@ -312,7 +293,7 @@
 def solution(mesh):
     zs = mesh.shape["dp"] // 4
     ys = mesh.shape["rep"] // 2
-    finer = Mesh(mesh.devices.reshape(zs // 4, 4, 2, 2, ys, 2), (*DP, *REP))
+    finer = Mesh(mesh.devices.reshape(zs, 2, 2, ys, 2), (*DP, *REP))
     in_specs = (P(DP, REP), P(DP, REP), P(REP, None), P(None, REP), P(DP))
     out_specs = (P(DP, None), P(DP, REP))
     return jax.shard_map(

time: 145 us -> 137 us (0.945)
  the two profiles are of different devices: /device:TPU:40 before, /device:TPU:6 now
where the time goes in v8:
time: 137 us; the launch traced here: 135 us
  starting transfers between devices  70 us (51%)
  waiting for transfers between devices  34.8 us (25%)
  Pallas kernels  17.6 us (13%)
  local copies, waits for them, and re-layouts  6.15 us (4%)
  other arithmetic  5.06 us (4%)
  between operations  1.62 us (1%)
    all_to_all x1, starting transfers between devices, on_device(): z_terms = lax.all_to_all(ring_sum, 'z', 0, 0, tiled=True)  14.7 us
    ppermute x1, waiting for transfers between devices, on_device(): beside = lax.ppermute(jnp.concatenate([below, above]), 'xl', NEAR)  12.4 us
    all_to_all x1, waiting for transfers between devices, on_device(): came = lax.all_to_all(terms.reshape(ys, rows, width), 'y', 0, 0, tiled=True)  9.07 us
    ppermute x1, starting transfers between devices, on_device(): lax.ppermute(own_part(down_weight.reshape(2, width // 2, hidden_units), c...  6.93 us
    ppermute x1, waiting for transfers between devices, on_device(): lax.ppermute(own_part(down_weight.reshape(2, width // 2, hidden_units), c...  5.81 us
    pallas_call x1, Pallas kernels, on_device(): pl.pallas_call(terms_kernel, out_shape=jax.ShapeDtypeStruct((half_rows, w...  5.64 us
    ppermute x1, waiting for transfers between devices, on_device(): across = lax.ppermute(jnp.concatenate([own, near]), 'y', turn(2))  4.95 us
    all_to_all x1, starting transfers between devices, on_device(): came = lax.all_to_all(terms.reshape(ys, rows, width), 'y', 0, 0, tiled=True)  4.72 us
  transfers between devices with their start and end apart: 18, of which 6 were waited for; matrix products, arithmetic and copies ran while one was open for 5% of the time, Pallas kernels for 13%

profile of v8, /device:TPU:6, one launch (start us, length us, event | category | flops | bytes accessed | tf_op | source)
XLA Modules:
  0.0 135.2 jit_solution(635698062099106712)
XLA Ops:
  1.3 0.1 stack.19.place
  1.4 1.0 copy-done.5
  2.4 0.6 live_sets.1
  3.0 2.7 %collective-permute-start = (bf16[384,256]{1,0:T(8,128)(2,1)S(1)}, bf16[384,256]{1,0:T(8,128)(2,1)S(1)}, u32[]{:S(2)}, u32[]{:S(2)}) collective-permute-start(bf16[384,256]{1,0:T(8,128)(2,1)S(1)} %get-tuple-element.18), channel_id=1, source_target_pairs={{0,1},{1,0},{2,3},{3,2},{4,5},{5,4},{6,7},{7,6},{8,9},{9,8},{10,11... | collective-permute-start | bytes 589832 | tf_op jit(solution)/shard_map/ppermute | solution.py:180
  5.7 2.1 %dynamic-slice_bitcast_fusion.1 = bf16[1024,384]{1,0:T(8,128)(2,1)} fusion(bf16[2,1024,384]{2,1,0:T(8,128)(2,1)} %bitcast.25, s32[]{:T(128)S(6)} %select_n.6), kind=kLoop, calls=%fused_computation.9 | loop fusion | bytes 1572868 | tf_op jit(solution)/shard_map/jit(dynamic_index_in_dim)/squeeze | solution.py:143
  7.8 6.9 %collective-permute-start.2 = (bf16[1024,384]{1,0:T(8,128)(2,1)}, bf16[1024,384]{1,0:T(8,128)(2,1)}, u32[]{:S(2)}, u32[]{:S(2)}) collective-permute-start(bf16[1024,384]{1,0:T(8,128)(2,1)} %dynamic-slice_bitcast_fusion.1), channel_id=1, source_target_pairs={{0,17},{17,0},{1,16},{16,1},{2,19},{19,2},{3,18},{18,3},{4,21},{21... | collective-permute-start | bytes 2359304 | tf_op jit(solution)/shard_map/ppermute | solution.py:192
  14.8 0.0 collective-permute-done.near_set
  14.8 1.8 %spread.1 = bf16[4,2,384,256]{3,2,1,0:T(8,128)(2,1)} custom-call(s32[5]{0:T(128)S(1)} %stack.19.place, bf16[384,256]{1,0:T(8,128)(2,1)S(1)} %get-tuple-element.17.own_set, bf16[384,256]{1,0:T(8,128)(2,1)S(1)} %collective-permute-done.near_set), custom_call_target="tpu_custom_call" | custom-call | tf_op jit(solution)/shard_map/spread/pallas_call | solution.py:181
  16.6 3.7 %all-to-all-start = ((bf16[4,2,384,256]{3,2,1,0:T(8,128)(2,1)}), bf16[4,2,384,256]{3,2,1,0:T(8,128)(2,1)S(1)}, u32[]{:S(2)}, u32[]{:S(2)}) async-start(bf16[4,2,384,256]{3,2,1,0:T(8,128)(2,1)} %spread.1), calls=%async_computation | async-start | bytes 3145728 | tf_op jit(solution)/shard_map/all_to_all | solution.py:189
  20.3 0.0 copy-start.4
  20.3 0.1 dynamic-slice_bitcast_fusion
  20.4 3.4 %collective-permute-start.4 = (bf16[192,2048]{1,0:T(8,128)(2,1)S(1)}, bf16[192,2048]{1,0:T(8,128)(2,1)}, u32[]{:S(2)}, u32[]{:S(2)}) collective-permute-start(bf16[192,2048]{1,0:T(8,128)(2,1)S(1)} %dynamic-slice_bitcast_fusion), channel_id=1, source_target_pairs={{0,1},{1,0},{8,25},{9,24},{16,17},{17,16},{24,9},{25,8},{2,3},{3,2... | collective-permute-start | bytes 2359304 | tf_op jit(solution)/shard_map/ppermute | solution.py:193
  23.9 0.6 pre_sets.1
  24.5 0.7 copy-done.6
  25.2 2.5 %collective-permute-start.1 = (bf16[384,384]{1,0:T(8,128)(2,1)S(1)}, bf16[384,384]{1,0:T(8,128)(2,1)S(1)}, u32[]{:S(2)}, u32[]{:S(2)}) collective-permute-start(bf16[384,384]{1,0:T(8,128)(2,1)S(1)} %get-tuple-element.20), channel_id=1, source_target_pairs={{0,1},{1,0},{2,3},{3,2},{4,5},{5,4},{6,7},{7,6},{8,9},{9,8},{10,11... | collective-permute-start | bytes 884744 | tf_op jit(solution)/shard_map/ppermute | solution.py:190
  27.7 5.8 %collective-permute-done.2.down_mine = bf16[1024,384]{1,0:T(8,128)(2,1)} collective-permute-done((bf16[1024,384]{1,0:T(8,128)(2,1)}, bf16[1024,384]{1,0:T(8,128)(2,1)}, u32[]{:S(2)}, u32[]{:S(2)}) %collective-permute-start.2) | collective-permute-done | bytes 786464 | tf_op jit(solution)/shard_map/ppermute | solution.py:192
  33.5 1.9 %collective-permute-start.3 = (bf16[1024,384]{1,0:T(8,128)(2,1)}, bf16[1024,384]{1,0:T(8,128)(2,1)}, u32[]{:S(2)}, u32[]{:S(2)}) collective-permute-start(bf16[1024,384]{1,0:T(8,128)(2,1)} %collective-permute-done.2.down_mine), channel_id=1, source_target_pairs={{0,8},{8,0},{1,9},{9,1},{2,10},{10,2},{3,11},{11,3},{4,12},{12,4},... | collective-permute-start | bytes 2359304 | tf_op jit(solution)/shard_map/ppermute | solution.py:196
  35.5 2.2 %collective-permute-done.4.up_mine = bf16[192,2048]{1,0:T(8,128)(2,1)} collective-permute-done((bf16[192,2048]{1,0:T(8,128)(2,1)S(1)}, bf16[192,2048]{1,0:T(8,128)(2,1)}, u32[]{:S(2)}, u32[]{:S(2)}) %collective-permute-start.4) | collective-permute-done | bytes 786464 | tf_op jit(solution)/shard_map/ppermute | solution.py:193
  37.7 2.7 %collective-permute-start.5 = (bf16[192,2048]{1,0:T(8,128)(2,1)}, bf16[192,2048]{1,0:T(8,128)(2,1)}, u32[]{:S(2)}, u32[]{:S(2)}) collective-permute-start(bf16[192,2048]{1,0:T(8,128)(2,1)} %collective-permute-done.4.up_mine), channel_id=1, source_target_pairs={{0,8},{8,0},{1,9},{9,1},{2,10},{10,2},{3,11},{11,3},{4,12},{12,4},... | collective-permute-start | bytes 2359304 | tf_op jit(solution)/shard_map/ppermute | solution.py:197
  40.4 0.3 collective-permute-done.1.pre_far
  40.7 1.0 copy-done.7
  41.7 3.6 %down_terms.1 = (bf16[4,16,32,384]{3,2,1,0:T(8,128)(2,1)S(1)}, bf16[4,16,32,384]{3,2,1,0:T(8,128)(2,1)}) custom-call(s32[5]{0:T(128)S(1)} %stack.19.place, bf16[8,384,256]{2,1,0:T(8,128)(2,1)S(1)} %bitcast.22, bf16[384,384]{1,0:T(8,128)(2,1)S(1)} %copy-done.7, bf16[384,384]{1,0:T(8,128)(2,1)S(1)} %collective-permute-done.1.pre_far), custom_call_target="tpu_custom_call" | custom-call | flops 1207959552 | bytes 6291456 | tf_op jit(solution)/shard_map/down_terms/pallas_call | solution.py:212
  45.3 1.2 copy-done.2
  46.4 1.9 %collective-permute-start.11 = (bf16[4,16,32,384]{3,2,1,0:T(8,128)(2,1)}, bf16[4,16,32,384]{3,2,1,0:T(8,128)(2,1)}, u32[]{:S(2)}, u32[]{:S(2)}) collective-permute-start(bf16[4,16,32,384]{3,2,1,0:T(8,128)(2,1)} %get-tuple-element.27), channel_id=1, source_target_pairs={{0,8},{8,0},{1,9},{9,1},{2,10},{10,2},{3,11},{11,3},{4,12},{12,4},... | collective-permute-start | bytes 4718600 | tf_op jit(solution)/shard_map/ppermute | solution.py:242
  48.4 1.0 own_grad.1.own
  49.4 5.6 %terms.1 = bf16[384,2048]{1,0:T(8,128)(2,1)} custom-call(s32[5]{0:T(128)S(1)} %stack.19.place, bf16[8,384,256]{2,1,0:T(8,128)(2,1)S(1)} %bitcast.24, bf16[384,384]{1,0:T(8,128)(2,1)S(1)} %own_grad.1.own, bf16[384,384]{1,0:T(8,128)(2,1)S(1)} %collective-permute-done.1.pre_far, bf16[1024,384]{1,0:T(8,128)(2,1)} %collective-permute-done.2.down_mine, ...), custom_call_target="tpu_custom_call" | custom-call | flops 1811939328 | bytes 9437184 | tf_op jit(solution)/shard_map/terms/pallas_call | solution.py:225
  55.0 4.7 %all-to-all-start.1 = ((bf16[4,96,2048]{2,1,0:T(8,128)(2,1)}), bf16[4,96,2048]{2,1,0:T(8,128)(2,1)}, u32[]{:S(2)}, u32[]{:S(2)}) async-start(bf16[4,96,2048]{2,1,0:T(8,128)(2,1)} %bitcast.9), calls=%async_computation.1 | async-start | bytes 3145728 | tf_op jit(solution)/shard_map/all_to_all | solution.py:239
  59.7 2.7 %fusion.4 = (bf16[16,32,384]{2,1,0:T(8,128)(2,1)}, bf16[16,32,384]{2,1,0:T(8,128)(2,1)}, bf16[16,32,384]{2,1,0:T(8,128)(2,1)}, bf16[16,32,384]{2,1,0:T(8,128)(2,1)S(1)}) fusion(bf16[4,16,32,384]{3,2,1,0:T(8,128)(2,1)} %collective-permute-done.11, bf16[4,16,32,384]{3,2,1,0:T(8,128)(2,1)S(1)} %copy-done.3), kind=kLoop, calls=%fused_computation.14 | loop fusion | flops 3145728 | bytes 4718592 | tf_op jit(solution)/shard_map/convert_element_type | solution.py:247
  62.4 2.2 %collective-permute-start.12 = (bf16[16,32,384]{2,1,0:T(8,128)(2,1)}, bf16[16,32,384]{2,1,0:T(8,128)(2,1)S(1)}, u32[]{:S(2)}, u32[]{:S(2)}) collective-permute-start(bf16[16,32,384]{2,1,0:T(8,128)(2,1)} %get-tuple-element.34), channel_id=1, source_target_pairs={{0,1},{1,0},{2,3},{3,2},{4,5},{5,4},{6,7},{7,6},{8,9},{9,8},{10,11... | collective-permute-start | bytes 1179656 | tf_op jit(solution)/shard_map/ppermute | solution.py:245
  64.6 3.3 %collective-permute-start.13 = (bf16[16,32,384]{2,1,0:T(8,128)(2,1)}, bf16[16,32,384]{2,1,0:T(8,128)(2,1)S(1)}, u32[]{:S(2)}, u32[]{:S(2)}) collective-permute-start(bf16[16,32,384]{2,1,0:T(8,128)(2,1)} %get-tuple-element.33), channel_id=1, source_target_pairs={{0,17},{17,0},{1,16},{16,1},{2,19},{19,2},{3,18},{18,3},{4,21},{21... | collective-permute-start | bytes 1179656 | tf_op jit(solution)/shard_map/ppermute | solution.py:246
  68.0 4.3 %collective-permute-start.14 = (bf16[16,32,384]{2,1,0:T(8,128)(2,1)}, bf16[16,32,384]{2,1,0:T(8,128)(2,1)S(1)}, u32[]{:S(2)}, u32[]{:S(2)}) collective-permute-start(bf16[16,32,384]{2,1,0:T(8,128)(2,1)} %get-tuple-element.32), channel_id=1, source_target_pairs={{0,16},{16,0},{1,17},{17,1},{2,18},{18,2},{3,19},{19,3},{4,20},{20... | collective-permute-start | bytes 1179656 | tf_op jit(solution)/shard_map/ppermute | solution.py:247
  72.2 9.1 %all-to-all-done.1 = bf16[4,96,2048]{2,1,0:T(8,128)(2,1)} async-done(((bf16[4,96,2048]{2,1,0:T(8,128)(2,1)}), bf16[4,96,2048]{2,1,0:T(8,128)(2,1)}, u32[]{:S(2)}, u32[]{:S(2)}) %all-to-all-start.1) | async-done | bytes 1572896 | tf_op jit(solution)/shard_map/all_to_all | solution.py:239
  81.3 1.6 %fusion.own = bf16[96,2048]{1,0:T(8,128)(2,1)S(1)} fusion(bf16[4,96,2048]{2,1,0:T(8,128)(2,1)} %all-to-all-done.1), kind=kLoop, calls=%fused_computation.10 | loop fusion | flops 1572864 | bytes 1966080 | tf_op jit(solution)/shard_map/add | solution.py:240
  82.9 2.2 %collective-permute-start.6 = (bf16[96,2048]{1,0:T(8,128)(2,1)S(1)}, bf16[96,2048]{1,0:T(8,128)(2,1)S(1)}, u32[]{:S(2)}, u32[]{:S(2)}) collective-permute-start(bf16[96,2048]{1,0:T(8,128)(2,1)S(1)} %fusion.own), channel_id=1, source_target_pairs={{0,1},{1,0},{2,3},{3,2},{4,5},{5,4},{6,7},{7,6},{8,9},{9,8},{10,11... | collective-permute-start | bytes 1179656 | tf_op jit(solution)/shard_map/ppermute | solution.py:250
  85.1 2.5 %collective-permute-start.7 = (bf16[96,2048]{1,0:T(8,128)(2,1)S(1)}, bf16[96,2048]{1,0:T(8,128)(2,1)S(1)}, u32[]{:S(2)}, u32[]{:S(2)}) collective-permute-start(bf16[96,2048]{1,0:T(8,128)(2,1)S(1)} %fusion.own), channel_id=1, source_target_pairs={{0,2},{2,4},{4,6},{6,0},{1,3},{3,5},{5,7},{7,1},{8,10},{10,12},{12... | collective-permute-start | bytes 1179656 | tf_op jit(solution)/shard_map/ppermute | solution.py:251
  87.6 4.6 %collective-permute-start.8 = (bf16[96,2048]{1,0:T(8,128)(2,1)S(1)}, bf16[96,2048]{1,0:T(8,128)(2,1)S(1)}, u32[]{:S(2)}, u32[]{:S(2)}) collective-permute-start(bf16[96,2048]{1,0:T(8,128)(2,1)S(1)} %fusion.own), channel_id=1, source_target_pairs={{0,6},{2,0},{4,2},{6,4},{1,7},{3,1},{5,3},{7,5},{8,14},{10,8},{12,... | collective-permute-start | bytes 1179656 | tf_op jit(solution)/shard_map/ppermute | solution.py:252
  92.2 1.0 ring_sum.1
  93.2 14.7 %all-to-all-start.2 = ((bf16[16,32,384]{2,1,0:T(8,128)(2,1)}), bf16[16,32,384]{2,1,0:T(8,128)(2,1)S(1)}, u32[]{:S(2)}, u32[]{:S(2)}) async-start(bf16[16,32,384]{2,1,0:T(8,128)(2,1)} %ring_sum.1), calls=%async_computation.2 | async-start | bytes 786432 | tf_op jit(solution)/shard_map/all_to_all | solution.py:264
  107.9 0.1 pad_maximum_fusion.1
  108.0 3.8 %collective-permute-start.10 = (bf16[192,2048]{1,0:T(8,128)(2,1)S(1)}, bf16[192,2048]{1,0:T(8,128)(2,1)S(1)}, u32[]{:S(2)}, u32[]{:S(2)}) collective-permute-start(bf16[192,2048]{1,0:T(8,128)(2,1)S(1)} %pad_maximum_fusion.1), channel_id=1, source_target_pairs={{0,1},{1,0},{2,3},{3,2},{4,5},{5,4},{6,7},{7,6},{8,9},{9,8},{10,11... | collective-permute-start | bytes 2359304 | tf_op jit(solution)/shard_map/ppermute | solution.py:269
  111.7 0.1 pad_maximum_fusion
  111.8 1.9 %collective-permute-start.9 = (bf16[192,2048]{1,0:T(8,128)(2,1)S(1)}, bf16[192,2048]{1,0:T(8,128)(2,1)S(1)}, u32[]{:S(2)}, u32[]{:S(2)}) collective-permute-start(bf16[192,2048]{1,0:T(8,128)(2,1)S(1)} %pad_maximum_fusion), channel_id=1, source_target_pairs={{0,4},{2,6},{4,0},{6,2},{1,5},{3,7},{5,1},{7,3},{8,12},{10,14},{12... | collective-permute-start | bytes 2359304 | tf_op jit(solution)/shard_map/ppermute | solution.py:268
  113.7 1.7 %place_first.1.partial = bf16[768,2048]{1,0:T(8,128)(2,1)} custom-call(s32[5]{0:T(128)S(1)} %stack.19.place, bf16[96,2048]{1,0:T(8,128)(2,1)S(1)} %fusion.own, bf16[96,2048]{1,0:T(8,128)(2,1)S(1)} %collective-permute-done.6.near, bf16[96,2048]{1,0:T(8,128)(2,1)S(1)} %collective-permute-done.7.below, bf16[96,2048]{1,0:T(8,128)(2,1)S(1)} %collective-permute-done.8.above), custom_call_target="tpu_custom_call" | custom-call | tf_op jit(solution)/shard_map/place_first/pallas_call | solution.py:271
  115.5 12.4 %collective-permute-done.10.beside = bf16[192,2048]{1,0:T(8,128)(2,1)S(1)} collective-permute-done((bf16[192,2048]{1,0:T(8,128)(2,1)S(1)}, bf16[192,2048]{1,0:T(8,128)(2,1)S(1)}, u32[]{:S(2)}, u32[]{:S(2)}) %collective-permute-start.10) | collective-permute-done | bytes 786464 | tf_op jit(solution)/shard_map/ppermute | solution.py:269
  127.8 5.0 %collective-permute-done.9.across = bf16[192,2048]{1,0:T(8,128)(2,1)S(1)} collective-permute-done((bf16[192,2048]{1,0:T(8,128)(2,1)S(1)}, bf16[192,2048]{1,0:T(8,128)(2,1)S(1)}, u32[]{:S(2)}, u32[]{:S(2)}) %collective-permute-start.9) | collective-permute-done | bytes 786464 | tf_op jit(solution)/shard_map/ppermute | solution.py:268
  132.8 1.7 %place_last.1 = bf16[768,2048]{1,0:T(8,128)(2,1)} custom-call(s32[5]{0:T(128)S(1)} %stack.19.place, bf16[768,2048]{1,0:T(8,128)(2,1)} %place_first.1.partial, bf16[192,2048]{1,0:T(8,128)(2,1)S(1)} %collective-permute-done.9.across, bf16[192,2048]{1,0:T(8,128)(2,1)S(1)} %collective-permute-done.10.beside), custom_call_target="tpu_custom_call", output_to_operand_aliasing={{}: (1, {})} | custom-call | tf_op jit(solution)/shard_map/place_last/pallas_call | solution.py:280
  134.5 0.1 convert_reduce_fusion
  134.6 0.6 broadcast_multiply_fusion
  (22 shorter events, 0.0 us)
Async XLA Ops:
  1.4 1.0 copy-start.5
  3.0 11.8 %collective-permute-start = (bf16[384,256]{1,0:T(8,128)(2,1)S(1)}, bf16[384,256]{1,0:T(8,128)(2,1)S(1)}, u32[]{:S(2)}, u32[]{:S(2)}) collective-permute-start(bf16[384,256]{1,0:T(8,128)(2,1)S(1)} %get-tuple-element.18), channel_id=1, source_target_pairs={{0,1},{1,0},{2,3},{3,2},{4,5},{5,4},{6,7},{7,6},{8,9},{9,8},{10,11... | collective-permute-start | bytes 589832 | tf_op jit(solution)/shard_map/ppermute | solution.py:180
  7.8 25.7 %collective-permute-start.2 = (bf16[1024,384]{1,0:T(8,128)(2,1)}, bf16[1024,384]{1,0:T(8,128)(2,1)}, u32[]{:S(2)}, u32[]{:S(2)}) collective-permute-start(bf16[1024,384]{1,0:T(8,128)(2,1)} %dynamic-slice_bitcast_fusion.1), channel_id=1, source_target_pairs={{0,17},{17,0},{1,16},{16,1},{2,19},{19,2},{3,18},{18,3},{4,21},{21... | collective-permute-start | bytes 2359304 | tf_op jit(solution)/shard_map/ppermute | solution.py:192
  16.6 3.7 %copy-start.1 = (bf16[384,2048]{1,0:T(8,128)(2,1)S(1)}, bf16[384,2048]{1,0:T(8,128)(2,1)}, u32[]{:S(2)}) copy-start(bf16[384,2048]{1,0:T(8,128)(2,1)} %up_own.1) | copy-start | bytes 4718596
  16.6 24.1 %all-to-all-start = ((bf16[4,2,384,256]{3,2,1,0:T(8,128)(2,1)}), bf16[4,2,384,256]{3,2,1,0:T(8,128)(2,1)S(1)}, u32[]{:S(2)}, u32[]{:S(2)}) async-start(bf16[4,2,384,256]{3,2,1,0:T(8,128)(2,1)} %spread.1), calls=%async_computation | async-start | bytes 3145728 | tf_op jit(solution)/shard_map/all_to_all | solution.py:189
  20.3 3.5 %copy-start.4 = (bf16[768,384]{1,0:T(8,128)(2,1)S(1)}, bf16[768,384]{1,0:T(8,128)(2,1)}, u32[]{:S(2)}) copy-start(bf16[768,384]{1,0:T(8,128)(2,1)} %whole.3) | copy-start | bytes 1769476
  20.4 17.3 %collective-permute-start.4 = (bf16[192,2048]{1,0:T(8,128)(2,1)S(1)}, bf16[192,2048]{1,0:T(8,128)(2,1)}, u32[]{:S(2)}, u32[]{:S(2)}) collective-permute-start(bf16[192,2048]{1,0:T(8,128)(2,1)S(1)} %dynamic-slice_bitcast_fusion), channel_id=1, source_target_pairs={{0,1},{1,0},{8,25},{9,24},{16,17},{17,16},{24,9},{25,8},{2,3},{3,2... | collective-permute-start | bytes 2359304 | tf_op jit(solution)/shard_map/ppermute | solution.py:193
  24.5 0.7 copy-start.6
  25.2 15.5 %collective-permute-start.1 = (bf16[384,384]{1,0:T(8,128)(2,1)S(1)}, bf16[384,384]{1,0:T(8,128)(2,1)S(1)}, u32[]{:S(2)}, u32[]{:S(2)}) collective-permute-start(bf16[384,384]{1,0:T(8,128)(2,1)S(1)} %get-tuple-element.20), channel_id=1, source_target_pairs={{0,1},{1,0},{2,3},{3,2},{4,5},{5,4},{6,7},{7,6},{8,9},{9,8},{10,11... | collective-permute-start | bytes 884744 | tf_op jit(solution)/shard_map/ppermute | solution.py:190
  33.5 15.8 %collective-permute-start.3 = (bf16[1024,384]{1,0:T(8,128)(2,1)}, bf16[1024,384]{1,0:T(8,128)(2,1)}, u32[]{:S(2)}, u32[]{:S(2)}) collective-permute-start(bf16[1024,384]{1,0:T(8,128)(2,1)} %collective-permute-done.2.down_mine), channel_id=1, source_target_pairs={{0,8},{8,0},{1,9},{9,1},{2,10},{10,2},{3,11},{11,3},{4,12},{12,4},... | collective-permute-start | bytes 2359304 | tf_op jit(solution)/shard_map/ppermute | solution.py:196
  37.7 11.7 %collective-permute-start.5 = (bf16[192,2048]{1,0:T(8,128)(2,1)}, bf16[192,2048]{1,0:T(8,128)(2,1)}, u32[]{:S(2)}, u32[]{:S(2)}) collective-permute-start(bf16[192,2048]{1,0:T(8,128)(2,1)} %collective-permute-done.4.up_mine), channel_id=1, source_target_pairs={{0,8},{8,0},{1,9},{9,1},{2,10},{10,2},{3,11},{11,3},{4,12},{12,4},... | collective-permute-start | bytes 2359304 | tf_op jit(solution)/shard_map/ppermute | solution.py:197
  40.7 1.0 copy-start.7
  41.7 6.7 %copy-start = (bf16[2048,384]{1,0:T(8,128)(2,1)S(1)}, bf16[2048,384]{1,0:T(8,128)(2,1)}, u32[]{:S(2)}) copy-start(bf16[2048,384]{1,0:T(8,128)(2,1)} %down.1) | copy-start | bytes 4718596
  45.3 1.2 copy-start.2
  46.4 13.3 %collective-permute-start.11 = (bf16[4,16,32,384]{3,2,1,0:T(8,128)(2,1)}, bf16[4,16,32,384]{3,2,1,0:T(8,128)(2,1)}, u32[]{:S(2)}, u32[]{:S(2)}) collective-permute-start(bf16[4,16,32,384]{3,2,1,0:T(8,128)(2,1)} %get-tuple-element.27), channel_id=1, source_target_pairs={{0,8},{8,0},{1,9},{9,1},{2,10},{10,2},{3,11},{11,3},{4,12},{12,4},... | collective-permute-start | bytes 4718600 | tf_op jit(solution)/shard_map/ppermute | solution.py:242
  55.0 4.7 %copy-start.3 = (bf16[4,16,32,384]{3,2,1,0:T(8,128)(2,1)S(1)}, bf16[4,16,32,384]{3,2,1,0:T(8,128)(2,1)}, u32[]{:S(2)}) copy-start(bf16[4,16,32,384]{3,2,1,0:T(8,128)(2,1)} %copy-done.2) | copy-start | bytes 4718596
  55.0 26.3 %all-to-all-start.1 = ((bf16[4,96,2048]{2,1,0:T(8,128)(2,1)}), bf16[4,96,2048]{2,1,0:T(8,128)(2,1)}, u32[]{:S(2)}, u32[]{:S(2)}) async-start(bf16[4,96,2048]{2,1,0:T(8,128)(2,1)} %bitcast.9), calls=%async_computation.1 | async-start | bytes 3145728 | tf_op jit(solution)/shard_map/all_to_all | solution.py:239
  62.4 25.2 %collective-permute-start.12 = (bf16[16,32,384]{2,1,0:T(8,128)(2,1)}, bf16[16,32,384]{2,1,0:T(8,128)(2,1)S(1)}, u32[]{:S(2)}, u32[]{:S(2)}) collective-permute-start(bf16[16,32,384]{2,1,0:T(8,128)(2,1)} %get-tuple-element.34), channel_id=1, source_target_pairs={{0,1},{1,0},{2,3},{3,2},{4,5},{5,4},{6,7},{7,6},{8,9},{9,8},{10,11... | collective-permute-start | bytes 1179656 | tf_op jit(solution)/shard_map/ppermute | solution.py:245
  64.6 27.6 %collective-permute-start.13 = (bf16[16,32,384]{2,1,0:T(8,128)(2,1)}, bf16[16,32,384]{2,1,0:T(8,128)(2,1)S(1)}, u32[]{:S(2)}, u32[]{:S(2)}) collective-permute-start(bf16[16,32,384]{2,1,0:T(8,128)(2,1)} %get-tuple-element.33), channel_id=1, source_target_pairs={{0,17},{17,0},{1,16},{16,1},{2,19},{19,2},{3,18},{18,3},{4,21},{21... | collective-permute-start | bytes 1179656 | tf_op jit(solution)/shard_map/ppermute | solution.py:246
  68.0 24.2 %collective-permute-start.14 = (bf16[16,32,384]{2,1,0:T(8,128)(2,1)}, bf16[16,32,384]{2,1,0:T(8,128)(2,1)S(1)}, u32[]{:S(2)}, u32[]{:S(2)}) collective-permute-start(bf16[16,32,384]{2,1,0:T(8,128)(2,1)} %get-tuple-element.32), channel_id=1, source_target_pairs={{0,16},{16,0},{1,17},{17,1},{2,18},{18,2},{3,19},{19,3},{4,20},{20... | collective-permute-start | bytes 1179656 | tf_op jit(solution)/shard_map/ppermute | solution.py:247
  82.9 25.0 %collective-permute-start.6 = (bf16[96,2048]{1,0:T(8,128)(2,1)S(1)}, bf16[96,2048]{1,0:T(8,128)(2,1)S(1)}, u32[]{:S(2)}, u32[]{:S(2)}) collective-permute-start(bf16[96,2048]{1,0:T(8,128)(2,1)S(1)} %fusion.own), channel_id=1, source_target_pairs={{0,1},{1,0},{2,3},{3,2},{4,5},{5,4},{6,7},{7,6},{8,9},{9,8},{10,11... | collective-permute-start | bytes 1179656 | tf_op jit(solution)/shard_map/ppermute | solution.py:250
  85.1 22.8 %collective-permute-start.7 = (bf16[96,2048]{1,0:T(8,128)(2,1)S(1)}, bf16[96,2048]{1,0:T(8,128)(2,1)S(1)}, u32[]{:S(2)}, u32[]{:S(2)}) collective-permute-start(bf16[96,2048]{1,0:T(8,128)(2,1)S(1)} %fusion.own), channel_id=1, source_target_pairs={{0,2},{2,4},{4,6},{6,0},{1,3},{3,5},{5,7},{7,1},{8,10},{10,12},{12... | collective-permute-start | bytes 1179656 | tf_op jit(solution)/shard_map/ppermute | solution.py:251
  87.6 20.3 %collective-permute-start.8 = (bf16[96,2048]{1,0:T(8,128)(2,1)S(1)}, bf16[96,2048]{1,0:T(8,128)(2,1)S(1)}, u32[]{:S(2)}, u32[]{:S(2)}) collective-permute-start(bf16[96,2048]{1,0:T(8,128)(2,1)S(1)} %fusion.own), channel_id=1, source_target_pairs={{0,6},{2,0},{4,2},{6,4},{1,7},{3,1},{5,3},{7,5},{8,14},{10,8},{12,... | collective-permute-start | bytes 1179656 | tf_op jit(solution)/shard_map/ppermute | solution.py:252
  93.2 41.4 %all-to-all-start.2 = ((bf16[16,32,384]{2,1,0:T(8,128)(2,1)}), bf16[16,32,384]{2,1,0:T(8,128)(2,1)S(1)}, u32[]{:S(2)}, u32[]{:S(2)}) async-start(bf16[16,32,384]{2,1,0:T(8,128)(2,1)} %ring_sum.1), calls=%async_computation.2 | async-start | bytes 786432 | tf_op jit(solution)/shard_map/all_to_all | solution.py:264
  108.0 19.9 %collective-permute-start.10 = (bf16[192,2048]{1,0:T(8,128)(2,1)S(1)}, bf16[192,2048]{1,0:T(8,128)(2,1)S(1)}, u32[]{:S(2)}, u32[]{:S(2)}) collective-permute-start(bf16[192,2048]{1,0:T(8,128)(2,1)S(1)} %pad_maximum_fusion.1), channel_id=1, source_target_pairs={{0,1},{1,0},{2,3},{3,2},{4,5},{5,4},{6,7},{7,6},{8,9},{9,8},{10,11... | collective-permute-start | bytes 2359304 | tf_op jit(solution)/shard_map/ppermute | solution.py:269
  111.8 21.0 %collective-permute-start.9 = (bf16[192,2048]{1,0:T(8,128)(2,1)S(1)}, bf16[192,2048]{1,0:T(8,128)(2,1)S(1)}, u32[]{:S(2)}, u32[]{:S(2)}) collective-permute-start(bf16[192,2048]{1,0:T(8,128)(2,1)S(1)} %pad_maximum_fusion), channel_id=1, source_target_pairs={{0,4},{2,6},{4,0},{6,2},{1,5},{3,7},{5,1},{7,3},{8,12},{10,14},{12... | collective-permute-start | bytes 2359304 | tf_op jit(solution)/shard_map/ppermute | solution.py:268

commit v9 on v8

--- a/solution.py
+++ b/solution.py
@@ -129,14 +129,14 @@
     put(place, [(own, 0, 0), (near, 0, 1), (below, -1, 0), (above, 1, 0)], out, sems)
 
 
-def last_kernel(place, partial, across, beside, out, sems):
+def across_kernel(place, partial, across, out, sems):
     rows = across.shape[0] // 2
-    put(
-        place,
-        [(across, 2, 0, 0, rows), (across, 2, 1, rows, rows), (beside, -1, 1, 0, rows), (beside, 1, 1, rows, rows)],
-        out,
-        sems,
-    )
+    put(place, [(across, 2, 0, 0, rows), (across, 2, 1, rows, rows)], out, sems)
+
+
+def beside_kernel(place, partial, beside, out, sems):
+    rows = beside.shape[0] // 2
+    put(place, [(beside, -1, 1, 0, rows), (beside, 1, 1, rows, rows)], out, sems)
 
 
 def own_part(array, index, axis):
@@ -277,16 +277,18 @@
         compiler_params=params,
         name="place_first",
     )(place, own, near, below, above)
-    input_grad = pl.pallas_call(
-        last_kernel,
-        out_shape=whole,
-        in_specs=[SMEM, ANY] + [VMEM] * 2,
-        out_specs=ANY,
-        scratch_shapes=[pltpu.SemaphoreType.DMA((4,))],
-        input_output_aliases={1: 0},
-        compiler_params=params,
-        name="place_last",
-    )(place, first, across, beside)
+    input_grad = first
+    for kernel, pair, name in ((across_kernel, across, "place_across"), (beside_kernel, beside, "place_beside")):
+        input_grad = pl.pallas_call(
+            kernel,
+            out_shape=whole,
+            in_specs=[SMEM, ANY, VMEM],
+            out_specs=ANY,
+            scratch_shapes=[pltpu.SemaphoreType.DMA((2,))],
+            input_output_aliases={1: 0},
+            compiler_params=pltpu.CompilerParams(vmem_limit_bytes=LIMIT),
+            name=name,
+        )(place, input_grad, pair)
     return (input_grad, down_grad)
 
 

time: 137 us -> 135 us (0.985)
  waiting for transfers between devices: 34.8 us -> 31.3 us
    ppermute x1, waiting for transfers between devices: 12.4 us -> 0.01 us  [on_device(): beside = lax.ppermute(jnp.concatenate([below, above]), 'xl', NEAR)]
    ppermute x1, waiting for transfers between devices: 4.95 us -> 13.9 us  [on_device(): across = lax.ppermute(jnp.concatenate([own, near]), 'y', turn(2))]
    pallas_call x1 -> x2, Pallas kernels: 1.72 us -> 2.89 us  [on_device(): pl.pallas_call(kernel, out_shape=whole, in_specs=[SMEM, ANY, VMEM], out_s...]
  transfers between devices with their start and end apart: 18 -> 18, of which waited for: 6 -> 5; matrix products, arithmetic and copies ran while one was open for 5% -> 5% of each run, Pallas kernels for 13% -> 14%
where the time goes in v9:
time: 135 us; the launch traced here: 133 us
  starting transfers between devices  70 us (52%)
  waiting for transfers between devices  31.3 us (23%)
  Pallas kernels  18.8 us (14%)
  local copies, waits for them, and re-layouts  6.15 us (5%)
  other arithmetic  5.06 us (4%)
  between operations  1.64 us (1%)
    all_to_all x1, starting transfers between devices, on_device(): z_terms = lax.all_to_all(ring_sum, 'z', 0, 0, tiled=True)  14.7 us
    ppermute x1, waiting for transfers between devices, on_device(): across = lax.ppermute(jnp.concatenate([own, near]), 'y', turn(2))  13.9 us
    all_to_all x1, waiting for transfers between devices, on_device(): came = lax.all_to_all(terms.reshape(ys, rows, width), 'y', 0, 0, tiled=True)  9.07 us
    ppermute x1, starting transfers between devices, on_device(): lax.ppermute(own_part(down_weight.reshape(2, width // 2, hidden_units), c...  6.93 us
    ppermute x1, waiting for transfers between devices, on_device(): lax.ppermute(own_part(down_weight.reshape(2, width // 2, hidden_units), c...  5.81 us
    pallas_call x1, Pallas kernels, on_device(): pl.pallas_call(terms_kernel, out_shape=jax.ShapeDtypeStruct((half_rows, w...  5.64 us
    all_to_all x1, starting transfers between devices, on_device(): came = lax.all_to_all(terms.reshape(ys, rows, width), 'y', 0, 0, tiled=True)  4.72 us
    ppermute x1, starting transfers between devices, on_device(): above = lax.ppermute(own, 'y', turn(-1))  4.57 us
  transfers between devices with their start and end apart: 18, of which 5 were waited for; matrix products, arithmetic and copies ran while one was open for 5% of the time, Pallas kernels for 14%

profile of v9, /device:TPU:6, one launch (start us, length us, event | category | flops | bytes accessed | tf_op | source)
XLA Modules:
  0.0 133.0 jit_solution(4589355399009076341)
XLA Ops:
  1.3 0.1 stack.19.place
  1.4 1.0 copy-done.5
  2.4 0.6 live_sets.1
  3.0 2.7 %collective-permute-start = (bf16[384,256]{1,0:T(8,128)(2,1)S(1)}, bf16[384,256]{1,0:T(8,128)(2,1)S(1)}, u32[]{:S(2)}, u32[]{:S(2)}) collective-permute-start(bf16[384,256]{1,0:T(8,128)(2,1)S(1)} %get-tuple-element.18), channel_id=1, source_target_pairs={{0,1},{1,0},{2,3},{3,2},{4,5},{5,4},{6,7},{7,6},{8,9},{9,8},{10,11... | collective-permute-start | bytes 589832 | tf_op jit(solution)/shard_map/ppermute | solution.py:180
  5.7 2.1 %dynamic-slice_bitcast_fusion.1 = bf16[1024,384]{1,0:T(8,128)(2,1)} fusion(bf16[2,1024,384]{2,1,0:T(8,128)(2,1)} %bitcast.25, s32[]{:T(128)S(6)} %select_n.6), kind=kLoop, calls=%fused_computation.9 | loop fusion | bytes 1572868 | tf_op jit(solution)/shard_map/jit(dynamic_index_in_dim)/squeeze | solution.py:143
  7.8 6.9 %collective-permute-start.2 = (bf16[1024,384]{1,0:T(8,128)(2,1)}, bf16[1024,384]{1,0:T(8,128)(2,1)}, u32[]{:S(2)}, u32[]{:S(2)}) collective-permute-start(bf16[1024,384]{1,0:T(8,128)(2,1)} %dynamic-slice_bitcast_fusion.1), channel_id=1, source_target_pairs={{0,17},{17,0},{1,16},{16,1},{2,19},{19,2},{3,18},{18,3},{4,21},{21... | collective-permute-start | bytes 2359304 | tf_op jit(solution)/shard_map/ppermute | solution.py:192
  14.8 0.0 collective-permute-done.near_set
  14.8 1.8 %spread.1 = bf16[4,2,384,256]{3,2,1,0:T(8,128)(2,1)} custom-call(s32[5]{0:T(128)S(1)} %stack.19.place, bf16[384,256]{1,0:T(8,128)(2,1)S(1)} %get-tuple-element.17.own_set, bf16[384,256]{1,0:T(8,128)(2,1)S(1)} %collective-permute-done.near_set), custom_call_target="tpu_custom_call" | custom-call | tf_op jit(solution)/shard_map/spread/pallas_call | solution.py:181
  16.6 3.7 %all-to-all-start = ((bf16[4,2,384,256]{3,2,1,0:T(8,128)(2,1)}), bf16[4,2,384,256]{3,2,1,0:T(8,128)(2,1)S(1)}, u32[]{:S(2)}, u32[]{:S(2)}) async-start(bf16[4,2,384,256]{3,2,1,0:T(8,128)(2,1)} %spread.1), calls=%async_computation | async-start | bytes 3145728 | tf_op jit(solution)/shard_map/all_to_all | solution.py:189
  20.3 0.0 copy-start.4
  20.3 0.1 dynamic-slice_bitcast_fusion
  20.4 3.4 %collective-permute-start.4 = (bf16[192,2048]{1,0:T(8,128)(2,1)S(1)}, bf16[192,2048]{1,0:T(8,128)(2,1)}, u32[]{:S(2)}, u32[]{:S(2)}) collective-permute-start(bf16[192,2048]{1,0:T(8,128)(2,1)S(1)} %dynamic-slice_bitcast_fusion), channel_id=1, source_target_pairs={{0,1},{1,0},{8,25},{9,24},{16,17},{17,16},{24,9},{25,8},{2,3},{3,2... | collective-permute-start | bytes 2359304 | tf_op jit(solution)/shard_map/ppermute | solution.py:193
  23.9 0.6 pre_sets.1
  24.5 0.7 copy-done.6
  25.2 2.5 %collective-permute-start.1 = (bf16[384,384]{1,0:T(8,128)(2,1)S(1)}, bf16[384,384]{1,0:T(8,128)(2,1)S(1)}, u32[]{:S(2)}, u32[]{:S(2)}) collective-permute-start(bf16[384,384]{1,0:T(8,128)(2,1)S(1)} %get-tuple-element.20), channel_id=1, source_target_pairs={{0,1},{1,0},{2,3},{3,2},{4,5},{5,4},{6,7},{7,6},{8,9},{9,8},{10,11... | collective-permute-start | bytes 884744 | tf_op jit(solution)/shard_map/ppermute | solution.py:190
  27.7 5.8 %collective-permute-done.2.down_mine = bf16[1024,384]{1,0:T(8,128)(2,1)} collective-permute-done((bf16[1024,384]{1,0:T(8,128)(2,1)}, bf16[1024,384]{1,0:T(8,128)(2,1)}, u32[]{:S(2)}, u32[]{:S(2)}) %collective-permute-start.2) | collective-permute-done | bytes 786464 | tf_op jit(solution)/shard_map/ppermute | solution.py:192
  33.5 1.9 %collective-permute-start.3 = (bf16[1024,384]{1,0:T(8,128)(2,1)}, bf16[1024,384]{1,0:T(8,128)(2,1)}, u32[]{:S(2)}, u32[]{:S(2)}) collective-permute-start(bf16[1024,384]{1,0:T(8,128)(2,1)} %collective-permute-done.2.down_mine), channel_id=1, source_target_pairs={{0,8},{8,0},{1,9},{9,1},{2,10},{10,2},{3,11},{11,3},{4,12},{12,4},... | collective-permute-start | bytes 2359304 | tf_op jit(solution)/shard_map/ppermute | solution.py:196
  35.5 2.2 %collective-permute-done.4.up_mine = bf16[192,2048]{1,0:T(8,128)(2,1)} collective-permute-done((bf16[192,2048]{1,0:T(8,128)(2,1)S(1)}, bf16[192,2048]{1,0:T(8,128)(2,1)}, u32[]{:S(2)}, u32[]{:S(2)}) %collective-permute-start.4) | collective-permute-done | bytes 786464 | tf_op jit(solution)/shard_map/ppermute | solution.py:193
  37.7 2.7 %collective-permute-start.5 = (bf16[192,2048]{1,0:T(8,128)(2,1)}, bf16[192,2048]{1,0:T(8,128)(2,1)}, u32[]{:S(2)}, u32[]{:S(2)}) collective-permute-start(bf16[192,2048]{1,0:T(8,128)(2,1)} %collective-permute-done.4.up_mine), channel_id=1, source_target_pairs={{0,8},{8,0},{1,9},{9,1},{2,10},{10,2},{3,11},{11,3},{4,12},{12,4},... | collective-permute-start | bytes 2359304 | tf_op jit(solution)/shard_map/ppermute | solution.py:197
  40.4 0.3 collective-permute-done.1.pre_far
  40.7 1.0 copy-done.7
  41.7 3.6 %down_terms.1 = (bf16[4,16,32,384]{3,2,1,0:T(8,128)(2,1)S(1)}, bf16[4,16,32,384]{3,2,1,0:T(8,128)(2,1)}) custom-call(s32[5]{0:T(128)S(1)} %stack.19.place, bf16[8,384,256]{2,1,0:T(8,128)(2,1)S(1)} %bitcast.22, bf16[384,384]{1,0:T(8,128)(2,1)S(1)} %copy-done.7, bf16[384,384]{1,0:T(8,128)(2,1)S(1)} %collective-permute-done.1.pre_far), custom_call_target="tpu_custom_call" | custom-call | flops 1207959552 | bytes 6291456 | tf_op jit(solution)/shard_map/down_terms/pallas_call | solution.py:212
  45.3 1.2 copy-done.2
  46.4 1.9 %collective-permute-start.11 = (bf16[4,16,32,384]{3,2,1,0:T(8,128)(2,1)}, bf16[4,16,32,384]{3,2,1,0:T(8,128)(2,1)}, u32[]{:S(2)}, u32[]{:S(2)}) collective-permute-start(bf16[4,16,32,384]{3,2,1,0:T(8,128)(2,1)} %get-tuple-element.27), channel_id=1, source_target_pairs={{0,8},{8,0},{1,9},{9,1},{2,10},{10,2},{3,11},{11,3},{4,12},{12,4},... | collective-permute-start | bytes 4718600 | tf_op jit(solution)/shard_map/ppermute | solution.py:242
  48.4 1.0 own_grad.1.own
  49.4 5.6 %terms.1 = bf16[384,2048]{1,0:T(8,128)(2,1)} custom-call(s32[5]{0:T(128)S(1)} %stack.19.place, bf16[8,384,256]{2,1,0:T(8,128)(2,1)S(1)} %bitcast.24, bf16[384,384]{1,0:T(8,128)(2,1)S(1)} %own_grad.1.own, bf16[384,384]{1,0:T(8,128)(2,1)S(1)} %collective-permute-done.1.pre_far, bf16[1024,384]{1,0:T(8,128)(2,1)} %collective-permute-done.2.down_mine, ...), custom_call_target="tpu_custom_call" | custom-call | flops 1811939328 | bytes 9437184 | tf_op jit(solution)/shard_map/terms/pallas_call | solution.py:225
  55.0 4.7 %all-to-all-start.1 = ((bf16[4,96,2048]{2,1,0:T(8,128)(2,1)}), bf16[4,96,2048]{2,1,0:T(8,128)(2,1)}, u32[]{:S(2)}, u32[]{:S(2)}) async-start(bf16[4,96,2048]{2,1,0:T(8,128)(2,1)} %bitcast.9), calls=%async_computation.1 | async-start | bytes 3145728 | tf_op jit(solution)/shard_map/all_to_all | solution.py:239
  59.7 2.7 %fusion.4 = (bf16[16,32,384]{2,1,0:T(8,128)(2,1)}, bf16[16,32,384]{2,1,0:T(8,128)(2,1)}, bf16[16,32,384]{2,1,0:T(8,128)(2,1)}, bf16[16,32,384]{2,1,0:T(8,128)(2,1)S(1)}) fusion(bf16[4,16,32,384]{3,2,1,0:T(8,128)(2,1)} %collective-permute-done.11, bf16[4,16,32,384]{3,2,1,0:T(8,128)(2,1)S(1)} %copy-done.3), kind=kLoop, calls=%fused_computation.14 | loop fusion | flops 3145728 | bytes 4718592 | tf_op jit(solution)/shard_map/convert_element_type | solution.py:247
  62.4 2.2 %collective-permute-start.12 = (bf16[16,32,384]{2,1,0:T(8,128)(2,1)}, bf16[16,32,384]{2,1,0:T(8,128)(2,1)S(1)}, u32[]{:S(2)}, u32[]{:S(2)}) collective-permute-start(bf16[16,32,384]{2,1,0:T(8,128)(2,1)} %get-tuple-element.34), channel_id=1, source_target_pairs={{0,1},{1,0},{2,3},{3,2},{4,5},{5,4},{6,7},{7,6},{8,9},{9,8},{10,11... | collective-permute-start | bytes 1179656 | tf_op jit(solution)/shard_map/ppermute | solution.py:245
  64.6 3.3 %collective-permute-start.13 = (bf16[16,32,384]{2,1,0:T(8,128)(2,1)}, bf16[16,32,384]{2,1,0:T(8,128)(2,1)S(1)}, u32[]{:S(2)}, u32[]{:S(2)}) collective-permute-start(bf16[16,32,384]{2,1,0:T(8,128)(2,1)} %get-tuple-element.33), channel_id=1, source_target_pairs={{0,17},{17,0},{1,16},{16,1},{2,19},{19,2},{3,18},{18,3},{4,21},{21... | collective-permute-start | bytes 1179656 | tf_op jit(solution)/shard_map/ppermute | solution.py:246
  68.0 4.3 %collective-permute-start.14 = (bf16[16,32,384]{2,1,0:T(8,128)(2,1)}, bf16[16,32,384]{2,1,0:T(8,128)(2,1)S(1)}, u32[]{:S(2)}, u32[]{:S(2)}) collective-permute-start(bf16[16,32,384]{2,1,0:T(8,128)(2,1)} %get-tuple-element.32), channel_id=1, source_target_pairs={{0,16},{16,0},{1,17},{17,1},{2,18},{18,2},{3,19},{19,3},{4,20},{20... | collective-permute-start | bytes 1179656 | tf_op jit(solution)/shard_map/ppermute | solution.py:247
  72.2 9.1 %all-to-all-done.1 = bf16[4,96,2048]{2,1,0:T(8,128)(2,1)} async-done(((bf16[4,96,2048]{2,1,0:T(8,128)(2,1)}), bf16[4,96,2048]{2,1,0:T(8,128)(2,1)}, u32[]{:S(2)}, u32[]{:S(2)}) %all-to-all-start.1) | async-done | bytes 1572896 | tf_op jit(solution)/shard_map/all_to_all | solution.py:239
  81.3 1.6 %fusion.own = bf16[96,2048]{1,0:T(8,128)(2,1)S(1)} fusion(bf16[4,96,2048]{2,1,0:T(8,128)(2,1)} %all-to-all-done.1), kind=kLoop, calls=%fused_computation.10 | loop fusion | flops 1572864 | bytes 1966080 | tf_op jit(solution)/shard_map/add | solution.py:240
  82.9 2.2 %collective-permute-start.6 = (bf16[96,2048]{1,0:T(8,128)(2,1)S(1)}, bf16[96,2048]{1,0:T(8,128)(2,1)S(1)}, u32[]{:S(2)}, u32[]{:S(2)}) collective-permute-start(bf16[96,2048]{1,0:T(8,128)(2,1)S(1)} %fusion.own), channel_id=1, source_target_pairs={{0,1},{1,0},{2,3},{3,2},{4,5},{5,4},{6,7},{7,6},{8,9},{9,8},{10,11... | collective-permute-start | bytes 1179656 | tf_op jit(solution)/shard_map/ppermute | solution.py:250
  85.1 2.5 %collective-permute-start.7 = (bf16[96,2048]{1,0:T(8,128)(2,1)S(1)}, bf16[96,2048]{1,0:T(8,128)(2,1)S(1)}, u32[]{:S(2)}, u32[]{:S(2)}) collective-permute-start(bf16[96,2048]{1,0:T(8,128)(2,1)S(1)} %fusion.own), channel_id=1, source_target_pairs={{0,2},{2,4},{4,6},{6,0},{1,3},{3,5},{5,7},{7,1},{8,10},{10,12},{12... | collective-permute-start | bytes 1179656 | tf_op jit(solution)/shard_map/ppermute | solution.py:251
  87.6 4.6 %collective-permute-start.8 = (bf16[96,2048]{1,0:T(8,128)(2,1)S(1)}, bf16[96,2048]{1,0:T(8,128)(2,1)S(1)}, u32[]{:S(2)}, u32[]{:S(2)}) collective-permute-start(bf16[96,2048]{1,0:T(8,128)(2,1)S(1)} %fusion.own), channel_id=1, source_target_pairs={{0,6},{2,0},{4,2},{6,4},{1,7},{3,1},{5,3},{7,5},{8,14},{10,8},{12,... | collective-permute-start | bytes 1179656 | tf_op jit(solution)/shard_map/ppermute | solution.py:252
  92.2 1.0 ring_sum.1
  93.2 14.7 %all-to-all-start.2 = ((bf16[16,32,384]{2,1,0:T(8,128)(2,1)}), bf16[16,32,384]{2,1,0:T(8,128)(2,1)S(1)}, u32[]{:S(2)}, u32[]{:S(2)}) async-start(bf16[16,32,384]{2,1,0:T(8,128)(2,1)} %ring_sum.1), calls=%async_computation.2 | async-start | bytes 786432 | tf_op jit(solution)/shard_map/all_to_all | solution.py:264
  107.9 0.1 pad_maximum_fusion
  108.0 1.9 %collective-permute-start.9 = (bf16[192,2048]{1,0:T(8,128)(2,1)S(1)}, bf16[192,2048]{1,0:T(8,128)(2,1)S(1)}, u32[]{:S(2)}, u32[]{:S(2)}) collective-permute-start(bf16[192,2048]{1,0:T(8,128)(2,1)S(1)} %pad_maximum_fusion), channel_id=1, source_target_pairs={{0,4},{2,6},{4,0},{6,2},{1,5},{3,7},{5,1},{7,3},{8,12},{10,14},{12... | collective-permute-start | bytes 2359304 | tf_op jit(solution)/shard_map/ppermute | solution.py:268
  109.9 0.1 pad_maximum_fusion.1
  110.0 3.8 %collective-permute-start.10 = (bf16[192,2048]{1,0:T(8,128)(2,1)S(1)}, bf16[192,2048]{1,0:T(8,128)(2,1)S(1)}, u32[]{:S(2)}, u32[]{:S(2)}) collective-permute-start(bf16[192,2048]{1,0:T(8,128)(2,1)S(1)} %pad_maximum_fusion.1), channel_id=1, source_target_pairs={{0,1},{1,0},{2,3},{3,2},{4,5},{5,4},{6,7},{7,6},{8,9},{9,8},{10,11... | collective-permute-start | bytes 2359304 | tf_op jit(solution)/shard_map/ppermute | solution.py:269
  113.7 1.7 %place_first.1.partial = bf16[768,2048]{1,0:T(8,128)(2,1)} custom-call(s32[5]{0:T(128)S(1)} %stack.19.place, bf16[96,2048]{1,0:T(8,128)(2,1)S(1)} %fusion.own, bf16[96,2048]{1,0:T(8,128)(2,1)S(1)} %collective-permute-done.6.near, bf16[96,2048]{1,0:T(8,128)(2,1)S(1)} %collective-permute-done.7.below, bf16[96,2048]{1,0:T(8,128)(2,1)S(1)} %collective-permute-done.8.above), custom_call_target="tpu_custom_call" | custom-call | tf_op jit(solution)/shard_map/place_first/pallas_call | solution.py:271
  115.5 13.9 %collective-permute-done.9.across = bf16[192,2048]{1,0:T(8,128)(2,1)S(1)} collective-permute-done((bf16[192,2048]{1,0:T(8,128)(2,1)S(1)}, bf16[192,2048]{1,0:T(8,128)(2,1)S(1)}, u32[]{:S(2)}, u32[]{:S(2)}) %collective-permute-start.9) | collective-permute-done | bytes 786464 | tf_op jit(solution)/shard_map/ppermute | solution.py:268
  129.3 1.4 %place_across.1.partial = bf16[768,2048]{1,0:T(8,128)(2,1)} custom-call(s32[5]{0:T(128)S(1)} %stack.19.place, bf16[768,2048]{1,0:T(8,128)(2,1)} %place_first.1.partial, bf16[192,2048]{1,0:T(8,128)(2,1)S(1)} %collective-permute-done.9.across), custom_call_target="tpu_custom_call", output_to_operand_aliasing={{}: (1, {})} | custom-call | tf_op jit(solution)/shard_map/place_across/pallas_call | solution.py:282
  130.8 1.4 %place_beside.1 = bf16[768,2048]{1,0:T(8,128)(2,1)} custom-call(s32[5]{0:T(128)S(1)} %stack.19.place, bf16[768,2048]{1,0:T(8,128)(2,1)} %place_across.1.partial, bf16[192,2048]{1,0:T(8,128)(2,1)S(1)} %collective-permute-done.10.beside), custom_call_target="tpu_custom_call", output_to_operand_aliasing={{}: (1, {})} | custom-call | tf_op jit(solution)/shard_map/place_beside/pallas_call | solution.py:282
  132.3 0.1 convert_reduce_fusion
  132.3 0.6 broadcast_multiply_fusion
  (23 shorter events, 0.1 us)
Async XLA Ops:
  1.4 1.0 copy-start.5
  3.0 11.8 %collective-permute-start = (bf16[384,256]{1,0:T(8,128)(2,1)S(1)}, bf16[384,256]{1,0:T(8,128)(2,1)S(1)}, u32[]{:S(2)}, u32[]{:S(2)}) collective-permute-start(bf16[384,256]{1,0:T(8,128)(2,1)S(1)} %get-tuple-element.18), channel_id=1, source_target_pairs={{0,1},{1,0},{2,3},{3,2},{4,5},{5,4},{6,7},{7,6},{8,9},{9,8},{10,11... | collective-permute-start | bytes 589832 | tf_op jit(solution)/shard_map/ppermute | solution.py:180
  7.8 25.7 %collective-permute-start.2 = (bf16[1024,384]{1,0:T(8,128)(2,1)}, bf16[1024,384]{1,0:T(8,128)(2,1)}, u32[]{:S(2)}, u32[]{:S(2)}) collective-permute-start(bf16[1024,384]{1,0:T(8,128)(2,1)} %dynamic-slice_bitcast_fusion.1), channel_id=1, source_target_pairs={{0,17},{17,0},{1,16},{16,1},{2,19},{19,2},{3,18},{18,3},{4,21},{21... | collective-permute-start | bytes 2359304 | tf_op jit(solution)/shard_map/ppermute | solution.py:192
  16.6 3.7 %copy-start.1 = (bf16[384,2048]{1,0:T(8,128)(2,1)S(1)}, bf16[384,2048]{1,0:T(8,128)(2,1)}, u32[]{:S(2)}) copy-start(bf16[384,2048]{1,0:T(8,128)(2,1)} %up_own.1) | copy-start | bytes 4718596
  16.6 24.1 %all-to-all-start = ((bf16[4,2,384,256]{3,2,1,0:T(8,128)(2,1)}), bf16[4,2,384,256]{3,2,1,0:T(8,128)(2,1)S(1)}, u32[]{:S(2)}, u32[]{:S(2)}) async-start(bf16[4,2,384,256]{3,2,1,0:T(8,128)(2,1)} %spread.1), calls=%async_computation | async-start | bytes 3145728 | tf_op jit(solution)/shard_map/all_to_all | solution.py:189
  20.3 3.5 %copy-start.4 = (bf16[768,384]{1,0:T(8,128)(2,1)S(1)}, bf16[768,384]{1,0:T(8,128)(2,1)}, u32[]{:S(2)}) copy-start(bf16[768,384]{1,0:T(8,128)(2,1)} %whole.3) | copy-start | bytes 1769476
  20.4 17.3 %collective-permute-start.4 = (bf16[192,2048]{1,0:T(8,128)(2,1)S(1)}, bf16[192,2048]{1,0:T(8,128)(2,1)}, u32[]{:S(2)}, u32[]{:S(2)}) collective-permute-start(bf16[192,2048]{1,0:T(8,128)(2,1)S(1)} %dynamic-slice_bitcast_fusion), channel_id=1, source_target_pairs={{0,1},{1,0},{8,25},{9,24},{16,17},{17,16},{24,9},{25,8},{2,3},{3,2... | collective-permute-start | bytes 2359304 | tf_op jit(solution)/shard_map/ppermute | solution.py:193
  24.5 0.7 copy-start.6
  25.2 15.5 %collective-permute-start.1 = (bf16[384,384]{1,0:T(8,128)(2,1)S(1)}, bf16[384,384]{1,0:T(8,128)(2,1)S(1)}, u32[]{:S(2)}, u32[]{:S(2)}) collective-permute-start(bf16[384,384]{1,0:T(8,128)(2,1)S(1)} %get-tuple-element.20), channel_id=1, source_target_pairs={{0,1},{1,0},{2,3},{3,2},{4,5},{5,4},{6,7},{7,6},{8,9},{9,8},{10,11... | collective-permute-start | bytes 884744 | tf_op jit(solution)/shard_map/ppermute | solution.py:190
  33.5 15.8 %collective-permute-start.3 = (bf16[1024,384]{1,0:T(8,128)(2,1)}, bf16[1024,384]{1,0:T(8,128)(2,1)}, u32[]{:S(2)}, u32[]{:S(2)}) collective-permute-start(bf16[1024,384]{1,0:T(8,128)(2,1)} %collective-permute-done.2.down_mine), channel_id=1, source_target_pairs={{0,8},{8,0},{1,9},{9,1},{2,10},{10,2},{3,11},{11,3},{4,12},{12,4},... | collective-permute-start | bytes 2359304 | tf_op jit(solution)/shard_map/ppermute | solution.py:196
  37.7 11.7 %collective-permute-start.5 = (bf16[192,2048]{1,0:T(8,128)(2,1)}, bf16[192,2048]{1,0:T(8,128)(2,1)}, u32[]{:S(2)}, u32[]{:S(2)}) collective-permute-start(bf16[192,2048]{1,0:T(8,128)(2,1)} %collective-permute-done.4.up_mine), channel_id=1, source_target_pairs={{0,8},{8,0},{1,9},{9,1},{2,10},{10,2},{3,11},{11,3},{4,12},{12,4},... | collective-permute-start | bytes 2359304 | tf_op jit(solution)/shard_map/ppermute | solution.py:197
  40.7 1.0 copy-start.7
  41.7 6.7 %copy-start = (bf16[2048,384]{1,0:T(8,128)(2,1)S(1)}, bf16[2048,384]{1,0:T(8,128)(2,1)}, u32[]{:S(2)}) copy-start(bf16[2048,384]{1,0:T(8,128)(2,1)} %down.1) | copy-start | bytes 4718596
  45.3 1.2 copy-start.2
  46.4 13.3 %collective-permute-start.11 = (bf16[4,16,32,384]{3,2,1,0:T(8,128)(2,1)}, bf16[4,16,32,384]{3,2,1,0:T(8,128)(2,1)}, u32[]{:S(2)}, u32[]{:S(2)}) collective-permute-start(bf16[4,16,32,384]{3,2,1,0:T(8,128)(2,1)} %get-tuple-element.27), channel_id=1, source_target_pairs={{0,8},{8,0},{1,9},{9,1},{2,10},{10,2},{3,11},{11,3},{4,12},{12,4},... | collective-permute-start | bytes 4718600 | tf_op jit(solution)/shard_map/ppermute | solution.py:242
  55.0 4.7 %copy-start.3 = (bf16[4,16,32,384]{3,2,1,0:T(8,128)(2,1)S(1)}, bf16[4,16,32,384]{3,2,1,0:T(8,128)(2,1)}, u32[]{:S(2)}) copy-start(bf16[4,16,32,384]{3,2,1,0:T(8,128)(2,1)} %copy-done.2) | copy-start | bytes 4718596
  55.0 26.3 %all-to-all-start.1 = ((bf16[4,96,2048]{2,1,0:T(8,128)(2,1)}), bf16[4,96,2048]{2,1,0:T(8,128)(2,1)}, u32[]{:S(2)}, u32[]{:S(2)}) async-start(bf16[4,96,2048]{2,1,0:T(8,128)(2,1)} %bitcast.9), calls=%async_computation.1 | async-start | bytes 3145728 | tf_op jit(solution)/shard_map/all_to_all | solution.py:239
  62.4 25.2 %collective-permute-start.12 = (bf16[16,32,384]{2,1,0:T(8,128)(2,1)}, bf16[16,32,384]{2,1,0:T(8,128)(2,1)S(1)}, u32[]{:S(2)}, u32[]{:S(2)}) collective-permute-start(bf16[16,32,384]{2,1,0:T(8,128)(2,1)} %get-tuple-element.34), channel_id=1, source_target_pairs={{0,1},{1,0},{2,3},{3,2},{4,5},{5,4},{6,7},{7,6},{8,9},{9,8},{10,11... | collective-permute-start | bytes 1179656 | tf_op jit(solution)/shard_map/ppermute | solution.py:245
  64.6 27.6 %collective-permute-start.13 = (bf16[16,32,384]{2,1,0:T(8,128)(2,1)}, bf16[16,32,384]{2,1,0:T(8,128)(2,1)S(1)}, u32[]{:S(2)}, u32[]{:S(2)}) collective-permute-start(bf16[16,32,384]{2,1,0:T(8,128)(2,1)} %get-tuple-element.33), channel_id=1, source_target_pairs={{0,17},{17,0},{1,16},{16,1},{2,19},{19,2},{3,18},{18,3},{4,21},{21... | collective-permute-start | bytes 1179656 | tf_op jit(solution)/shard_map/ppermute | solution.py:246
  68.0 24.2 %collective-permute-start.14 = (bf16[16,32,384]{2,1,0:T(8,128)(2,1)}, bf16[16,32,384]{2,1,0:T(8,128)(2,1)S(1)}, u32[]{:S(2)}, u32[]{:S(2)}) collective-permute-start(bf16[16,32,384]{2,1,0:T(8,128)(2,1)} %get-tuple-element.32), channel_id=1, source_target_pairs={{0,16},{16,0},{1,17},{17,1},{2,18},{18,2},{3,19},{19,3},{4,20},{20... | collective-permute-start | bytes 1179656 | tf_op jit(solution)/shard_map/ppermute | solution.py:247
  82.9 25.0 %collective-permute-start.6 = (bf16[96,2048]{1,0:T(8,128)(2,1)S(1)}, bf16[96,2048]{1,0:T(8,128)(2,1)S(1)}, u32[]{:S(2)}, u32[]{:S(2)}) collective-permute-start(bf16[96,2048]{1,0:T(8,128)(2,1)S(1)} %fusion.own), channel_id=1, source_target_pairs={{0,1},{1,0},{2,3},{3,2},{4,5},{5,4},{6,7},{7,6},{8,9},{9,8},{10,11... | collective-permute-start | bytes 1179656 | tf_op jit(solution)/shard_map/ppermute | solution.py:250
  85.1 22.8 %collective-permute-start.7 = (bf16[96,2048]{1,0:T(8,128)(2,1)S(1)}, bf16[96,2048]{1,0:T(8,128)(2,1)S(1)}, u32[]{:S(2)}, u32[]{:S(2)}) collective-permute-start(bf16[96,2048]{1,0:T(8,128)(2,1)S(1)} %fusion.own), channel_id=1, source_target_pairs={{0,2},{2,4},{4,6},{6,0},{1,3},{3,5},{5,7},{7,1},{8,10},{10,12},{12... | collective-permute-start | bytes 1179656 | tf_op jit(solution)/shard_map/ppermute | solution.py:251
  87.6 20.3 %collective-permute-start.8 = (bf16[96,2048]{1,0:T(8,128)(2,1)S(1)}, bf16[96,2048]{1,0:T(8,128)(2,1)S(1)}, u32[]{:S(2)}, u32[]{:S(2)}) collective-permute-start(bf16[96,2048]{1,0:T(8,128)(2,1)S(1)} %fusion.own), channel_id=1, source_target_pairs={{0,6},{2,0},{4,2},{6,4},{1,7},{3,1},{5,3},{7,5},{8,14},{10,8},{12,... | collective-permute-start | bytes 1179656 | tf_op jit(solution)/shard_map/ppermute | solution.py:252
  93.2 39.1 %all-to-all-start.2 = ((bf16[16,32,384]{2,1,0:T(8,128)(2,1)}), bf16[16,32,384]{2,1,0:T(8,128)(2,1)S(1)}, u32[]{:S(2)}, u32[]{:S(2)}) async-start(bf16[16,32,384]{2,1,0:T(8,128)(2,1)} %ring_sum.1), calls=%async_computation.2 | async-start | bytes 786432 | tf_op jit(solution)/shard_map/all_to_all | solution.py:264
  108.0 21.4 %collective-permute-start.9 = (bf16[192,2048]{1,0:T(8,128)(2,1)S(1)}, bf16[192,2048]{1,0:T(8,128)(2,1)S(1)}, u32[]{:S(2)}, u32[]{:S(2)}) collective-permute-start(bf16[192,2048]{1,0:T(8,128)(2,1)S(1)} %pad_maximum_fusion), channel_id=1, source_target_pairs={{0,4},{2,6},{4,0},{6,2},{1,5},{3,7},{5,1},{7,3},{8,12},{10,14},{12... | collective-permute-start | bytes 2359304 | tf_op jit(solution)/shard_map/ppermute | solution.py:268
  110.0 20.8 %collective-permute-start.10 = (bf16[192,2048]{1,0:T(8,128)(2,1)S(1)}, bf16[192,2048]{1,0:T(8,128)(2,1)S(1)}, u32[]{:S(2)}, u32[]{:S(2)}) collective-permute-start(bf16[192,2048]{1,0:T(8,128)(2,1)S(1)} %pad_maximum_fusion.1), channel_id=1, source_target_pairs={{0,1},{1,0},{2,3},{3,2},{4,5},{5,4},{6,7},{7,6},{8,9},{9,8},{10,11... | collective-permute-start | bytes 2359304 | tf_op jit(solution)/shard_map/ppermute | solution.py:269

commit v10 on v9

--- a/solution.py
+++ b/solution.py
@@ -41,11 +41,19 @@
             out[y * part:(y + 1) * part, :] = jnp.where(row < live, whole[pl.ds(first, part), :], 0).astype(out.dtype)
 
 
-def spread_kernel(place, own_set, near_set, out):
-    xl = place[2]
+def own_spread_kernel(place, own_set, out):
     for y in range(out.shape[0]):
-        out[y, xl] = own_set[...]
-        out[y, 1 - xl] = near_set[...]
+        out[y, place[2]] = own_set[...]
+
+
+def near_spread_kernel(place, partial, near_set, out, sems):
+    copies = [
+        pltpu.make_async_copy(near_set, out.at[y, 1 - place[2]], sems.at[y]) for y in range(out.shape[0])
+    ]
+    for copy in copies:
+        copy.start()
+    for copy in copies:
+        copy.wait()
 
 
 def own_kernel(grads, pre, down, out):
@@ -178,14 +186,25 @@
         name="pre_sets",
     )(place, pre_act)
     near_set = lax.ppermute(other_set, "xl", NEAR)
+    spread = jax.ShapeDtypeStruct((ys, 2, half_rows, features), bf16)
     grads = pl.pallas_call(
-        spread_kernel,
-        out_shape=jax.ShapeDtypeStruct((ys, 2, half_rows, features), bf16),
-        in_specs=[SMEM] + [VMEM] * 2,
+        own_spread_kernel,
+        out_shape=spread,
+        in_specs=[SMEM, VMEM],
         out_specs=VMEM,
-        compiler_params=params,
-        name="spread",
-    )(place, own_set, near_set)
+        compiler_params=pltpu.CompilerParams(vmem_limit_bytes=LIMIT),
+        name="spread_own",
+    )(place, own_set)
+    grads = pl.pallas_call(
+        near_spread_kernel,
+        out_shape=spread,
+        in_specs=[SMEM, ANY, VMEM],
+        out_specs=ANY,
+        scratch_shapes=[pltpu.SemaphoreType.DMA((ys,))],
+        input_output_aliases={1: 0},
+        compiler_params=pltpu.CompilerParams(vmem_limit_bytes=LIMIT),
+        name="spread_near",
+    )(place, grads, near_set)
     grads = lax.all_to_all(grads, "y", 0, 0, tiled=True).reshape(reps, half_rows, features)
     pre_far = lax.ppermute(pre_sent, "xl", NEAR)
 

time: 135 us -> 135 us (level)
  starting transfers between devices: 70 us -> 68 us
    ppermute x1, waiting for transfers between devices: 5.81 us -> 4.41 us  [on_device(): lax.ppermute(own_part(down_weight.reshape(2, width // 2, hidden_units), c...]
    ppermute x1, waiting for transfers between devices: 2.21 us -> 3.62 us  [on_device(): lax.ppermute(own_part(up_weight.reshape(2, hidden_units // 2, width), cor...]
    pallas_call x1 -> x2, Pallas kernels: 1.8 us -> 3.19 us  [the longest x1 1.74 us: on_device(): pl.pallas_call(own_spread_kernel, out_shape=spread, in_specs=[SMEM, VMEM]...]
    all_to_all x1, starting transfers between devices: 14.7 us -> 13.3 us  [on_device(): z_terms = lax.all_to_all(ring_sum, 'z', 0, 0, tiled=True)]
  transfers between devices with their start and end apart: 18 -> 18, of which waited for: 5 -> 5; matrix products, arithmetic and copies ran while one was open for 5% -> 5% of each run, Pallas kernels for 14% -> 15%
where the time goes in v10:
time: 135 us; the launch traced here: 133 us
  starting transfers between devices  68 us (50%)
  waiting for transfers between devices  32.3 us (24%)
  Pallas kernels  20.1 us (15%)
  local copies, waits for them, and re-layouts  6.15 us (5%)
  other arithmetic  5.06 us (4%)
  between operations  1.65 us (1%)
    ppermute x1, waiting for transfers between devices, on_device(): across = lax.ppermute(jnp.concatenate([own, near]), 'y', turn(2))  14.1 us
    all_to_all x1, starting transfers between devices, on_device(): z_terms = lax.all_to_all(ring_sum, 'z', 0, 0, tiled=True)  13.3 us
    all_to_all x1, waiting for transfers between devices, on_device(): came = lax.all_to_all(terms.reshape(ys, rows, width), 'y', 0, 0, tiled=True)  9.07 us
    ppermute x1, starting transfers between devices, on_device(): lax.ppermute(own_part(down_weight.reshape(2, width // 2, hidden_units), c...  6.93 us
    pallas_call x1, Pallas kernels, on_device(): pl.pallas_call(terms_kernel, out_shape=jax.ShapeDtypeStruct((half_rows, w...  5.64 us
    all_to_all x1, starting transfers between devices, on_device(): came = lax.all_to_all(terms.reshape(ys, rows, width), 'y', 0, 0, tiled=True)  4.72 us
    ppermute x1, starting transfers between devices, on_device(): lax.ppermute(chip[1].astype(bf16), RING, ACROSS)  4.57 us
    ppermute x1, starting transfers between devices, on_device(): above = lax.ppermute(own, 'y', turn(-1))  4.56 us
  transfers between devices with their start and end apart: 18, of which 5 were waited for; matrix products, arithmetic and copies ran while one was open for 5% of the time, Pallas kernels for 15%

profile of v10, /device:TPU:6, one launch (start us, length us, event | category | flops | bytes accessed | tf_op | source)
XLA Modules:
  0.0 133.3 jit_solution(14793778383983737765)
XLA Ops:
  1.3 0.1 stack.19.place
  1.4 1.0 copy-done.5
  2.4 0.6 live_sets.1
  3.0 2.7 %collective-permute-start = (bf16[384,256]{1,0:T(8,128)(2,1)S(1)}, bf16[384,256]{1,0:T(8,128)(2,1)S(1)}, u32[]{:S(2)}, u32[]{:S(2)}) collective-permute-start(bf16[384,256]{1,0:T(8,128)(2,1)S(1)} %get-tuple-element.18), channel_id=1, source_target_pairs={{0,1},{1,0},{2,3},{3,2},{4,5},{5,4},{6,7},{7,6},{8,9},{9,8},{10,11... | collective-permute-start | bytes 589832 | tf_op jit(solution)/shard_map/ppermute | solution.py:188
  5.7 2.1 %dynamic-slice_bitcast_fusion.1 = bf16[1024,384]{1,0:T(8,128)(2,1)} fusion(bf16[2,1024,384]{2,1,0:T(8,128)(2,1)} %bitcast.25, s32[]{:T(128)S(6)} %select_n.6), kind=kLoop, calls=%fused_computation.9 | loop fusion | bytes 1572868 | tf_op jit(solution)/shard_map/jit(dynamic_index_in_dim)/squeeze | solution.py:151
  7.8 6.9 %collective-permute-start.2 = (bf16[1024,384]{1,0:T(8,128)(2,1)}, bf16[1024,384]{1,0:T(8,128)(2,1)}, u32[]{:S(2)}, u32[]{:S(2)}) collective-permute-start(bf16[1024,384]{1,0:T(8,128)(2,1)} %dynamic-slice_bitcast_fusion.1), channel_id=1, source_target_pairs={{0,17},{17,0},{1,16},{16,1},{2,19},{19,2},{3,18},{18,3},{4,21},{21... | collective-permute-start | bytes 2359304 | tf_op jit(solution)/shard_map/ppermute | solution.py:211
  14.8 1.7 %spread_own.1.partial = bf16[4,2,384,256]{3,2,1,0:T(8,128)(2,1)} custom-call(s32[5]{0:T(128)S(1)} %stack.19.place, bf16[384,256]{1,0:T(8,128)(2,1)S(1)} %get-tuple-element.17.own_set), custom_call_target="tpu_custom_call" | custom-call | tf_op jit(solution)/shard_map/spread_own/pallas_call | solution.py:190
  16.5 1.4 %spread_near.1 = bf16[4,2,384,256]{3,2,1,0:T(8,128)(2,1)} custom-call(s32[5]{0:T(128)S(1)} %stack.19.place, bf16[4,2,384,256]{3,2,1,0:T(8,128)(2,1)} %spread_own.1.partial, bf16[384,256]{1,0:T(8,128)(2,1)S(1)} %collective-permute-done.near_set), custom_call_target="tpu_custom_call", output_to_operand_aliasing={{}: (1, {})} | custom-call | tf_op jit(solution)/shard_map/spread_near/pallas_call | solution.py:198
  18.0 0.0 copy-start.1
  18.0 3.7 %all-to-all-start = ((bf16[4,2,384,256]{3,2,1,0:T(8,128)(2,1)}), bf16[4,2,384,256]{3,2,1,0:T(8,128)(2,1)S(1)}, u32[]{:S(2)}, u32[]{:S(2)}) async-start(bf16[4,2,384,256]{3,2,1,0:T(8,128)(2,1)} %spread_near.1), calls=%async_computation | async-start | bytes 3145728 | tf_op jit(solution)/shard_map/all_to_all | solution.py:208
  21.7 0.1 dynamic-slice_bitcast_fusion
  21.8 3.4 %collective-permute-start.4 = (bf16[192,2048]{1,0:T(8,128)(2,1)S(1)}, bf16[192,2048]{1,0:T(8,128)(2,1)}, u32[]{:S(2)}, u32[]{:S(2)}) collective-permute-start(bf16[192,2048]{1,0:T(8,128)(2,1)S(1)} %dynamic-slice_bitcast_fusion), channel_id=1, source_target_pairs={{0,1},{1,0},{8,25},{9,24},{16,17},{17,16},{24,9},{25,8},{2,3},{3,2... | collective-permute-start | bytes 2359304 | tf_op jit(solution)/shard_map/ppermute | solution.py:212
  25.3 0.6 pre_sets.1
  25.9 0.7 copy-done.6
  26.6 2.5 %collective-permute-start.1 = (bf16[384,384]{1,0:T(8,128)(2,1)S(1)}, bf16[384,384]{1,0:T(8,128)(2,1)S(1)}, u32[]{:S(2)}, u32[]{:S(2)}) collective-permute-start(bf16[384,384]{1,0:T(8,128)(2,1)S(1)} %get-tuple-element.20), channel_id=1, source_target_pairs={{0,1},{1,0},{2,3},{3,2},{4,5},{5,4},{6,7},{7,6},{8,9},{9,8},{10,11... | collective-permute-start | bytes 884744 | tf_op jit(solution)/shard_map/ppermute | solution.py:209
  29.1 4.4 %collective-permute-done.2.down_mine = bf16[1024,384]{1,0:T(8,128)(2,1)} collective-permute-done((bf16[1024,384]{1,0:T(8,128)(2,1)}, bf16[1024,384]{1,0:T(8,128)(2,1)}, u32[]{:S(2)}, u32[]{:S(2)}) %collective-permute-start.2) | collective-permute-done | bytes 786464 | tf_op jit(solution)/shard_map/ppermute | solution.py:211
  33.5 1.9 %collective-permute-start.3 = (bf16[1024,384]{1,0:T(8,128)(2,1)}, bf16[1024,384]{1,0:T(8,128)(2,1)}, u32[]{:S(2)}, u32[]{:S(2)}) collective-permute-start(bf16[1024,384]{1,0:T(8,128)(2,1)} %collective-permute-done.2.down_mine), channel_id=1, source_target_pairs={{0,8},{8,0},{1,9},{9,1},{2,10},{10,2},{3,11},{11,3},{4,12},{12,4},... | collective-permute-start | bytes 2359304 | tf_op jit(solution)/shard_map/ppermute | solution.py:215
  35.5 3.6 %collective-permute-done.4.up_mine = bf16[192,2048]{1,0:T(8,128)(2,1)} collective-permute-done((bf16[192,2048]{1,0:T(8,128)(2,1)S(1)}, bf16[192,2048]{1,0:T(8,128)(2,1)}, u32[]{:S(2)}, u32[]{:S(2)}) %collective-permute-start.4) | collective-permute-done | bytes 786464 | tf_op jit(solution)/shard_map/ppermute | solution.py:212
  39.1 1.9 %collective-permute-start.5 = (bf16[192,2048]{1,0:T(8,128)(2,1)}, bf16[192,2048]{1,0:T(8,128)(2,1)}, u32[]{:S(2)}, u32[]{:S(2)}) collective-permute-start(bf16[192,2048]{1,0:T(8,128)(2,1)} %collective-permute-done.4.up_mine), channel_id=1, source_target_pairs={{0,8},{8,0},{1,9},{9,1},{2,10},{10,2},{3,11},{11,3},{4,12},{12,4},... | collective-permute-start | bytes 2359304 | tf_op jit(solution)/shard_map/ppermute | solution.py:216
  41.0 1.1 collective-permute-done.1.pre_far
  42.1 1.0 copy-done.7
  43.1 3.6 %down_terms.1 = (bf16[4,16,32,384]{3,2,1,0:T(8,128)(2,1)S(1)}, bf16[4,16,32,384]{3,2,1,0:T(8,128)(2,1)}) custom-call(s32[5]{0:T(128)S(1)} %stack.19.place, bf16[8,384,256]{2,1,0:T(8,128)(2,1)S(1)} %bitcast.22, bf16[384,384]{1,0:T(8,128)(2,1)S(1)} %copy-done.7, bf16[384,384]{1,0:T(8,128)(2,1)S(1)} %collective-permute-done.1.pre_far), custom_call_target="tpu_custom_call" | custom-call | flops 1207959552 | bytes 6291456 | tf_op jit(solution)/shard_map/down_terms/pallas_call | solution.py:231
  46.7 1.2 copy-done.2
  47.8 1.9 %collective-permute-start.11 = (bf16[4,16,32,384]{3,2,1,0:T(8,128)(2,1)}, bf16[4,16,32,384]{3,2,1,0:T(8,128)(2,1)}, u32[]{:S(2)}, u32[]{:S(2)}) collective-permute-start(bf16[4,16,32,384]{3,2,1,0:T(8,128)(2,1)} %get-tuple-element.27), channel_id=1, source_target_pairs={{0,8},{8,0},{1,9},{9,1},{2,10},{10,2},{3,11},{11,3},{4,12},{12,4},... | collective-permute-start | bytes 4718600 | tf_op jit(solution)/shard_map/ppermute | solution.py:261
  49.8 1.0 own_grad.1.own
  50.8 5.6 %terms.1 = bf16[384,2048]{1,0:T(8,128)(2,1)} custom-call(s32[5]{0:T(128)S(1)} %stack.19.place, bf16[8,384,256]{2,1,0:T(8,128)(2,1)S(1)} %bitcast.24, bf16[384,384]{1,0:T(8,128)(2,1)S(1)} %own_grad.1.own, bf16[384,384]{1,0:T(8,128)(2,1)S(1)} %collective-permute-done.1.pre_far, bf16[1024,384]{1,0:T(8,128)(2,1)} %collective-permute-done.2.down_mine, ...), custom_call_target="tpu_custom_call" | custom-call | flops 1811939328 | bytes 9437184 | tf_op jit(solution)/shard_map/terms/pallas_call | solution.py:244
  56.4 4.7 %all-to-all-start.1 = ((bf16[4,96,2048]{2,1,0:T(8,128)(2,1)}), bf16[4,96,2048]{2,1,0:T(8,128)(2,1)}, u32[]{:S(2)}, u32[]{:S(2)}) async-start(bf16[4,96,2048]{2,1,0:T(8,128)(2,1)} %bitcast.9), calls=%async_computation.1 | async-start | bytes 3145728 | tf_op jit(solution)/shard_map/all_to_all | solution.py:258
  61.2 2.7 %fusion.4 = (bf16[16,32,384]{2,1,0:T(8,128)(2,1)}, bf16[16,32,384]{2,1,0:T(8,128)(2,1)}, bf16[16,32,384]{2,1,0:T(8,128)(2,1)}, bf16[16,32,384]{2,1,0:T(8,128)(2,1)S(1)}) fusion(bf16[4,16,32,384]{3,2,1,0:T(8,128)(2,1)} %collective-permute-done.11, bf16[4,16,32,384]{3,2,1,0:T(8,128)(2,1)S(1)} %copy-done.3), kind=kLoop, calls=%fused_computation.14 | loop fusion | flops 3145728 | bytes 4718592 | tf_op jit(solution)/shard_map/convert_element_type | solution.py:266
  63.8 2.2 %collective-permute-start.12 = (bf16[16,32,384]{2,1,0:T(8,128)(2,1)}, bf16[16,32,384]{2,1,0:T(8,128)(2,1)S(1)}, u32[]{:S(2)}, u32[]{:S(2)}) collective-permute-start(bf16[16,32,384]{2,1,0:T(8,128)(2,1)} %get-tuple-element.34), channel_id=1, source_target_pairs={{0,1},{1,0},{2,3},{3,2},{4,5},{5,4},{6,7},{7,6},{8,9},{9,8},{10,11... | collective-permute-start | bytes 1179656 | tf_op jit(solution)/shard_map/ppermute | solution.py:264
  66.0 3.1 %collective-permute-start.13 = (bf16[16,32,384]{2,1,0:T(8,128)(2,1)}, bf16[16,32,384]{2,1,0:T(8,128)(2,1)S(1)}, u32[]{:S(2)}, u32[]{:S(2)}) collective-permute-start(bf16[16,32,384]{2,1,0:T(8,128)(2,1)} %get-tuple-element.33), channel_id=1, source_target_pairs={{0,17},{17,0},{1,16},{16,1},{2,19},{19,2},{3,18},{18,3},{4,21},{21... | collective-permute-start | bytes 1179656 | tf_op jit(solution)/shard_map/ppermute | solution.py:265
  69.1 4.6 %collective-permute-start.14 = (bf16[16,32,384]{2,1,0:T(8,128)(2,1)}, bf16[16,32,384]{2,1,0:T(8,128)(2,1)S(1)}, u32[]{:S(2)}, u32[]{:S(2)}) collective-permute-start(bf16[16,32,384]{2,1,0:T(8,128)(2,1)} %get-tuple-element.32), channel_id=1, source_target_pairs={{0,16},{16,0},{1,17},{17,1},{2,18},{18,2},{3,19},{19,3},{4,20},{20... | collective-permute-start | bytes 1179656 | tf_op jit(solution)/shard_map/ppermute | solution.py:266
  73.6 9.1 %all-to-all-done.1 = bf16[4,96,2048]{2,1,0:T(8,128)(2,1)} async-done(((bf16[4,96,2048]{2,1,0:T(8,128)(2,1)}), bf16[4,96,2048]{2,1,0:T(8,128)(2,1)}, u32[]{:S(2)}, u32[]{:S(2)}) %all-to-all-start.1) | async-done | bytes 1572896 | tf_op jit(solution)/shard_map/all_to_all | solution.py:258
  82.7 1.6 %fusion.own = bf16[96,2048]{1,0:T(8,128)(2,1)S(1)} fusion(bf16[4,96,2048]{2,1,0:T(8,128)(2,1)} %all-to-all-done.1), kind=kLoop, calls=%fused_computation.10 | loop fusion | flops 1572864 | bytes 1966080 | tf_op jit(solution)/shard_map/add | solution.py:259
  84.3 2.2 %collective-permute-start.6 = (bf16[96,2048]{1,0:T(8,128)(2,1)S(1)}, bf16[96,2048]{1,0:T(8,128)(2,1)S(1)}, u32[]{:S(2)}, u32[]{:S(2)}) collective-permute-start(bf16[96,2048]{1,0:T(8,128)(2,1)S(1)} %fusion.own), channel_id=1, source_target_pairs={{0,1},{1,0},{2,3},{3,2},{4,5},{5,4},{6,7},{7,6},{8,9},{9,8},{10,11... | collective-permute-start | bytes 1179656 | tf_op jit(solution)/shard_map/ppermute | solution.py:269
  86.5 2.5 %collective-permute-start.7 = (bf16[96,2048]{1,0:T(8,128)(2,1)S(1)}, bf16[96,2048]{1,0:T(8,128)(2,1)S(1)}, u32[]{:S(2)}, u32[]{:S(2)}) collective-permute-start(bf16[96,2048]{1,0:T(8,128)(2,1)S(1)} %fusion.own), channel_id=1, source_target_pairs={{0,2},{2,4},{4,6},{6,0},{1,3},{3,5},{5,7},{7,1},{8,10},{10,12},{12... | collective-permute-start | bytes 1179656 | tf_op jit(solution)/shard_map/ppermute | solution.py:270
  89.0 4.6 %collective-permute-start.8 = (bf16[96,2048]{1,0:T(8,128)(2,1)S(1)}, bf16[96,2048]{1,0:T(8,128)(2,1)S(1)}, u32[]{:S(2)}, u32[]{:S(2)}) collective-permute-start(bf16[96,2048]{1,0:T(8,128)(2,1)S(1)} %fusion.own), channel_id=1, source_target_pairs={{0,6},{2,0},{4,2},{6,4},{1,7},{3,1},{5,3},{7,5},{8,14},{10,8},{12,... | collective-permute-start | bytes 1179656 | tf_op jit(solution)/shard_map/ppermute | solution.py:271
  93.6 1.0 ring_sum.1
  94.6 13.3 %all-to-all-start.2 = ((bf16[16,32,384]{2,1,0:T(8,128)(2,1)}), bf16[16,32,384]{2,1,0:T(8,128)(2,1)S(1)}, u32[]{:S(2)}, u32[]{:S(2)}) async-start(bf16[16,32,384]{2,1,0:T(8,128)(2,1)} %ring_sum.1), calls=%async_computation.2 | async-start | bytes 786432 | tf_op jit(solution)/shard_map/all_to_all | solution.py:283
  107.9 0.1 pad_maximum_fusion
  108.0 1.9 %collective-permute-start.9 = (bf16[192,2048]{1,0:T(8,128)(2,1)S(1)}, bf16[192,2048]{1,0:T(8,128)(2,1)S(1)}, u32[]{:S(2)}, u32[]{:S(2)}) collective-permute-start(bf16[192,2048]{1,0:T(8,128)(2,1)S(1)} %pad_maximum_fusion), channel_id=1, source_target_pairs={{0,4},{2,6},{4,0},{6,2},{1,5},{3,7},{5,1},{7,3},{8,12},{10,14},{12... | collective-permute-start | bytes 2359304 | tf_op jit(solution)/shard_map/ppermute | solution.py:287
  109.9 0.1 pad_maximum_fusion.1
  110.0 3.9 %collective-permute-start.10 = (bf16[192,2048]{1,0:T(8,128)(2,1)S(1)}, bf16[192,2048]{1,0:T(8,128)(2,1)S(1)}, u32[]{:S(2)}, u32[]{:S(2)}) collective-permute-start(bf16[192,2048]{1,0:T(8,128)(2,1)S(1)} %pad_maximum_fusion.1), channel_id=1, source_target_pairs={{0,1},{1,0},{2,3},{3,2},{4,5},{5,4},{6,7},{7,6},{8,9},{9,8},{10,11... | collective-permute-start | bytes 2359304 | tf_op jit(solution)/shard_map/ppermute | solution.py:288
  113.9 1.7 %place_first.1.partial = bf16[768,2048]{1,0:T(8,128)(2,1)} custom-call(s32[5]{0:T(128)S(1)} %stack.19.place, bf16[96,2048]{1,0:T(8,128)(2,1)S(1)} %fusion.own, bf16[96,2048]{1,0:T(8,128)(2,1)S(1)} %collective-permute-done.6.near, bf16[96,2048]{1,0:T(8,128)(2,1)S(1)} %collective-permute-done.7.below, bf16[96,2048]{1,0:T(8,128)(2,1)S(1)} %collective-permute-done.8.above), custom_call_target="tpu_custom_call" | custom-call | tf_op jit(solution)/shard_map/place_first/pallas_call | solution.py:290
  115.7 14.1 %collective-permute-done.9.across = bf16[192,2048]{1,0:T(8,128)(2,1)S(1)} collective-permute-done((bf16[192,2048]{1,0:T(8,128)(2,1)S(1)}, bf16[192,2048]{1,0:T(8,128)(2,1)S(1)}, u32[]{:S(2)}, u32[]{:S(2)}) %collective-permute-start.9) | collective-permute-done | bytes 786464 | tf_op jit(solution)/shard_map/ppermute | solution.py:287
  129.7 1.4 %place_across.1.partial = bf16[768,2048]{1,0:T(8,128)(2,1)} custom-call(s32[5]{0:T(128)S(1)} %stack.19.place, bf16[768,2048]{1,0:T(8,128)(2,1)} %place_first.1.partial, bf16[192,2048]{1,0:T(8,128)(2,1)S(1)} %collective-permute-done.9.across), custom_call_target="tpu_custom_call", output_to_operand_aliasing={{}: (1, {})} | custom-call | tf_op jit(solution)/shard_map/place_across/pallas_call | solution.py:301
  131.2 1.4 %place_beside.1 = bf16[768,2048]{1,0:T(8,128)(2,1)} custom-call(s32[5]{0:T(128)S(1)} %stack.19.place, bf16[768,2048]{1,0:T(8,128)(2,1)} %place_across.1.partial, bf16[192,2048]{1,0:T(8,128)(2,1)S(1)} %collective-permute-done.10.beside), custom_call_target="tpu_custom_call", output_to_operand_aliasing={{}: (1, {})} | custom-call | tf_op jit(solution)/shard_map/place_beside/pallas_call | solution.py:301
  132.6 0.1 convert_reduce_fusion
  132.7 0.6 broadcast_multiply_fusion
  (24 shorter events, 0.1 us)
Async XLA Ops:
  1.4 1.0 copy-start.5
  3.0 13.5 %collective-permute-start = (bf16[384,256]{1,0:T(8,128)(2,1)S(1)}, bf16[384,256]{1,0:T(8,128)(2,1)S(1)}, u32[]{:S(2)}, u32[]{:S(2)}) collective-permute-start(bf16[384,256]{1,0:T(8,128)(2,1)S(1)} %get-tuple-element.18), channel_id=1, source_target_pairs={{0,1},{1,0},{2,3},{3,2},{4,5},{5,4},{6,7},{7,6},{8,9},{9,8},{10,11... | collective-permute-start | bytes 589832 | tf_op jit(solution)/shard_map/ppermute | solution.py:188
  7.8 25.7 %collective-permute-start.2 = (bf16[1024,384]{1,0:T(8,128)(2,1)}, bf16[1024,384]{1,0:T(8,128)(2,1)}, u32[]{:S(2)}, u32[]{:S(2)}) collective-permute-start(bf16[1024,384]{1,0:T(8,128)(2,1)} %dynamic-slice_bitcast_fusion.1), channel_id=1, source_target_pairs={{0,17},{17,0},{1,16},{16,1},{2,19},{19,2},{3,18},{18,3},{4,21},{21... | collective-permute-start | bytes 2359304 | tf_op jit(solution)/shard_map/ppermute | solution.py:211
  18.0 3.7 %copy-start.1 = (bf16[384,2048]{1,0:T(8,128)(2,1)S(1)}, bf16[384,2048]{1,0:T(8,128)(2,1)}, u32[]{:S(2)}) copy-start(bf16[384,2048]{1,0:T(8,128)(2,1)} %up_own.1) | copy-start | bytes 4718596
  18.0 24.1 %all-to-all-start = ((bf16[4,2,384,256]{3,2,1,0:T(8,128)(2,1)}), bf16[4,2,384,256]{3,2,1,0:T(8,128)(2,1)S(1)}, u32[]{:S(2)}, u32[]{:S(2)}) async-start(bf16[4,2,384,256]{3,2,1,0:T(8,128)(2,1)} %spread_near.1), calls=%async_computation | async-start | bytes 3145728 | tf_op jit(solution)/shard_map/all_to_all | solution.py:208
  21.7 3.5 %copy-start.4 = (bf16[768,384]{1,0:T(8,128)(2,1)S(1)}, bf16[768,384]{1,0:T(8,128)(2,1)}, u32[]{:S(2)}) copy-start(bf16[768,384]{1,0:T(8,128)(2,1)} %whole.3) | copy-start | bytes 1769476
  21.8 17.3 %collective-permute-start.4 = (bf16[192,2048]{1,0:T(8,128)(2,1)S(1)}, bf16[192,2048]{1,0:T(8,128)(2,1)}, u32[]{:S(2)}, u32[]{:S(2)}) collective-permute-start(bf16[192,2048]{1,0:T(8,128)(2,1)S(1)} %dynamic-slice_bitcast_fusion), channel_id=1, source_target_pairs={{0,1},{1,0},{8,25},{9,24},{16,17},{17,16},{24,9},{25,8},{2,3},{3,2... | collective-permute-start | bytes 2359304 | tf_op jit(solution)/shard_map/ppermute | solution.py:212
  25.9 0.7 copy-start.6
  26.6 15.5 %collective-permute-start.1 = (bf16[384,384]{1,0:T(8,128)(2,1)S(1)}, bf16[384,384]{1,0:T(8,128)(2,1)S(1)}, u32[]{:S(2)}, u32[]{:S(2)}) collective-permute-start(bf16[384,384]{1,0:T(8,128)(2,1)S(1)} %get-tuple-element.20), channel_id=1, source_target_pairs={{0,1},{1,0},{2,3},{3,2},{4,5},{5,4},{6,7},{7,6},{8,9},{9,8},{10,11... | collective-permute-start | bytes 884744 | tf_op jit(solution)/shard_map/ppermute | solution.py:209
  33.5 17.2 %collective-permute-start.3 = (bf16[1024,384]{1,0:T(8,128)(2,1)}, bf16[1024,384]{1,0:T(8,128)(2,1)}, u32[]{:S(2)}, u32[]{:S(2)}) collective-permute-start(bf16[1024,384]{1,0:T(8,128)(2,1)} %collective-permute-done.2.down_mine), channel_id=1, source_target_pairs={{0,8},{8,0},{1,9},{9,1},{2,10},{10,2},{3,11},{11,3},{4,12},{12,4},... | collective-permute-start | bytes 2359304 | tf_op jit(solution)/shard_map/ppermute | solution.py:215
  39.1 11.7 %collective-permute-start.5 = (bf16[192,2048]{1,0:T(8,128)(2,1)}, bf16[192,2048]{1,0:T(8,128)(2,1)}, u32[]{:S(2)}, u32[]{:S(2)}) collective-permute-start(bf16[192,2048]{1,0:T(8,128)(2,1)} %collective-permute-done.4.up_mine), channel_id=1, source_target_pairs={{0,8},{8,0},{1,9},{9,1},{2,10},{10,2},{3,11},{11,3},{4,12},{12,4},... | collective-permute-start | bytes 2359304 | tf_op jit(solution)/shard_map/ppermute | solution.py:216
  42.1 1.0 copy-start.7
  43.1 6.7 %copy-start = (bf16[2048,384]{1,0:T(8,128)(2,1)S(1)}, bf16[2048,384]{1,0:T(8,128)(2,1)}, u32[]{:S(2)}) copy-start(bf16[2048,384]{1,0:T(8,128)(2,1)} %down.1) | copy-start | bytes 4718596
  46.7 1.2 copy-start.2
  47.8 13.3 %collective-permute-start.11 = (bf16[4,16,32,384]{3,2,1,0:T(8,128)(2,1)}, bf16[4,16,32,384]{3,2,1,0:T(8,128)(2,1)}, u32[]{:S(2)}, u32[]{:S(2)}) collective-permute-start(bf16[4,16,32,384]{3,2,1,0:T(8,128)(2,1)} %get-tuple-element.27), channel_id=1, source_target_pairs={{0,8},{8,0},{1,9},{9,1},{2,10},{10,2},{3,11},{11,3},{4,12},{12,4},... | collective-permute-start | bytes 4718600 | tf_op jit(solution)/shard_map/ppermute | solution.py:261
  56.4 4.7 %copy-start.3 = (bf16[4,16,32,384]{3,2,1,0:T(8,128)(2,1)S(1)}, bf16[4,16,32,384]{3,2,1,0:T(8,128)(2,1)}, u32[]{:S(2)}) copy-start(bf16[4,16,32,384]{3,2,1,0:T(8,128)(2,1)} %copy-done.2) | copy-start | bytes 4718596
  56.4 26.3 %all-to-all-start.1 = ((bf16[4,96,2048]{2,1,0:T(8,128)(2,1)}), bf16[4,96,2048]{2,1,0:T(8,128)(2,1)}, u32[]{:S(2)}, u32[]{:S(2)}) async-start(bf16[4,96,2048]{2,1,0:T(8,128)(2,1)} %bitcast.9), calls=%async_computation.1 | async-start | bytes 3145728 | tf_op jit(solution)/shard_map/all_to_all | solution.py:258
  63.8 25.2 %collective-permute-start.12 = (bf16[16,32,384]{2,1,0:T(8,128)(2,1)}, bf16[16,32,384]{2,1,0:T(8,128)(2,1)S(1)}, u32[]{:S(2)}, u32[]{:S(2)}) collective-permute-start(bf16[16,32,384]{2,1,0:T(8,128)(2,1)} %get-tuple-element.34), channel_id=1, source_target_pairs={{0,1},{1,0},{2,3},{3,2},{4,5},{5,4},{6,7},{7,6},{8,9},{9,8},{10,11... | collective-permute-start | bytes 1179656 | tf_op jit(solution)/shard_map/ppermute | solution.py:264
  66.0 27.6 %collective-permute-start.13 = (bf16[16,32,384]{2,1,0:T(8,128)(2,1)}, bf16[16,32,384]{2,1,0:T(8,128)(2,1)S(1)}, u32[]{:S(2)}, u32[]{:S(2)}) collective-permute-start(bf16[16,32,384]{2,1,0:T(8,128)(2,1)} %get-tuple-element.33), channel_id=1, source_target_pairs={{0,17},{17,0},{1,16},{16,1},{2,19},{19,2},{3,18},{18,3},{4,21},{21... | collective-permute-start | bytes 1179656 | tf_op jit(solution)/shard_map/ppermute | solution.py:265
  69.1 24.5 %collective-permute-start.14 = (bf16[16,32,384]{2,1,0:T(8,128)(2,1)}, bf16[16,32,384]{2,1,0:T(8,128)(2,1)S(1)}, u32[]{:S(2)}, u32[]{:S(2)}) collective-permute-start(bf16[16,32,384]{2,1,0:T(8,128)(2,1)} %get-tuple-element.32), channel_id=1, source_target_pairs={{0,16},{16,0},{1,17},{17,1},{2,18},{18,2},{3,19},{19,3},{4,20},{20... | collective-permute-start | bytes 1179656 | tf_op jit(solution)/shard_map/ppermute | solution.py:266
  84.3 23.6 %collective-permute-start.6 = (bf16[96,2048]{1,0:T(8,128)(2,1)S(1)}, bf16[96,2048]{1,0:T(8,128)(2,1)S(1)}, u32[]{:S(2)}, u32[]{:S(2)}) collective-permute-start(bf16[96,2048]{1,0:T(8,128)(2,1)S(1)} %fusion.own), channel_id=1, source_target_pairs={{0,1},{1,0},{2,3},{3,2},{4,5},{5,4},{6,7},{7,6},{8,9},{9,8},{10,11... | collective-permute-start | bytes 1179656 | tf_op jit(solution)/shard_map/ppermute | solution.py:269
  86.5 21.4 %collective-permute-start.7 = (bf16[96,2048]{1,0:T(8,128)(2,1)S(1)}, bf16[96,2048]{1,0:T(8,128)(2,1)S(1)}, u32[]{:S(2)}, u32[]{:S(2)}) collective-permute-start(bf16[96,2048]{1,0:T(8,128)(2,1)S(1)} %fusion.own), channel_id=1, source_target_pairs={{0,2},{2,4},{4,6},{6,0},{1,3},{3,5},{5,7},{7,1},{8,10},{10,12},{12... | collective-permute-start | bytes 1179656 | tf_op jit(solution)/shard_map/ppermute | solution.py:270
  89.0 18.9 %collective-permute-start.8 = (bf16[96,2048]{1,0:T(8,128)(2,1)S(1)}, bf16[96,2048]{1,0:T(8,128)(2,1)S(1)}, u32[]{:S(2)}, u32[]{:S(2)}) collective-permute-start(bf16[96,2048]{1,0:T(8,128)(2,1)S(1)} %fusion.own), channel_id=1, source_target_pairs={{0,6},{2,0},{4,2},{6,4},{1,7},{3,1},{5,3},{7,5},{8,14},{10,8},{12,... | collective-permute-start | bytes 1179656 | tf_op jit(solution)/shard_map/ppermute | solution.py:271
  94.6 38.1 %all-to-all-start.2 = ((bf16[16,32,384]{2,1,0:T(8,128)(2,1)}), bf16[16,32,384]{2,1,0:T(8,128)(2,1)S(1)}, u32[]{:S(2)}, u32[]{:S(2)}) async-start(bf16[16,32,384]{2,1,0:T(8,128)(2,1)} %ring_sum.1), calls=%async_computation.2 | async-start | bytes 786432 | tf_op jit(solution)/shard_map/all_to_all | solution.py:283
  108.0 21.7 %collective-permute-start.9 = (bf16[192,2048]{1,0:T(8,128)(2,1)S(1)}, bf16[192,2048]{1,0:T(8,128)(2,1)S(1)}, u32[]{:S(2)}, u32[]{:S(2)}) collective-permute-start(bf16[192,2048]{1,0:T(8,128)(2,1)S(1)} %pad_maximum_fusion), channel_id=1, source_target_pairs={{0,4},{2,6},{4,0},{6,2},{1,5},{3,7},{5,1},{7,3},{8,12},{10,14},{12... | collective-permute-start | bytes 2359304 | tf_op jit(solution)/shard_map/ppermute | solution.py:287
  110.0 21.2 %collective-permute-start.10 = (bf16[192,2048]{1,0:T(8,128)(2,1)S(1)}, bf16[192,2048]{1,0:T(8,128)(2,1)S(1)}, u32[]{:S(2)}, u32[]{:S(2)}) collective-permute-start(bf16[192,2048]{1,0:T(8,128)(2,1)S(1)} %pad_maximum_fusion.1), channel_id=1, source_target_pairs={{0,1},{1,0},{2,3},{3,2},{4,5},{5,4},{6,7},{7,6},{8,9},{9,8},{10,11... | collective-permute-start | bytes 2359304 | tf_op jit(solution)/shard_map/ppermute | solution.py:288

commit v11 on v8

--- a/solution.py
+++ b/solution.py
@@ -129,7 +129,7 @@
     put(place, [(own, 0, 0), (near, 0, 1), (below, -1, 0), (above, 1, 0)], out, sems)
 
 
-def last_kernel(place, partial, across, beside, out, sems):
+def last_kernel(place, partial, beside, across, out, sems):
     rows = across.shape[0] // 2
     put(
         place,
@@ -286,7 +286,7 @@
         input_output_aliases={1: 0},
         compiler_params=params,
         name="place_last",
-    )(place, first, across, beside)
+    )(place, first, beside, across)
     return (input_grad, down_grad)
 
 

time: 137 us -> 134 us (0.978)
  waiting for transfers between devices: 34.8 us -> 31.8 us
    ppermute x1, waiting for transfers between devices: 12.4 us -> 0.5 us  [on_device(): beside = lax.ppermute(jnp.concatenate([below, above]), 'xl', NEAR)]
    ppermute x1, waiting for transfers between devices: 4.95 us -> 13.9 us  [on_device(): across = lax.ppermute(jnp.concatenate([own, near]), 'y', turn(2))]
where the time goes in v11:
time: 134 us; the launch traced here: 132 us
  starting transfers between devices  70 us (52%)
  waiting for transfers between devices  31.8 us (24%)
  Pallas kernels  17.6 us (13%)
  local copies, waits for them, and re-layouts  6.15 us (5%)
  other arithmetic  5.06 us (4%)
  between operations  1.62 us (1%)
    all_to_all x1, starting transfers between devices, on_device(): z_terms = lax.all_to_all(ring_sum, 'z', 0, 0, tiled=True)  14.7 us
    ppermute x1, waiting for transfers between devices, on_device(): across = lax.ppermute(jnp.concatenate([own, near]), 'y', turn(2))  13.9 us
    all_to_all x1, waiting for transfers between devices, on_device(): came = lax.all_to_all(terms.reshape(ys, rows, width), 'y', 0, 0, tiled=True)  9.07 us
    ppermute x1, starting transfers between devices, on_device(): lax.ppermute(own_part(down_weight.reshape(2, width // 2, hidden_units), c...  6.93 us
    ppermute x1, waiting for transfers between devices, on_device(): lax.ppermute(own_part(down_weight.reshape(2, width // 2, hidden_units), c...  5.81 us
    pallas_call x1, Pallas kernels, on_device(): pl.pallas_call(terms_kernel, out_shape=jax.ShapeDtypeStruct((half_rows, w...  5.64 us
    all_to_all x1, starting transfers between devices, on_device(): came = lax.all_to_all(terms.reshape(ys, rows, width), 'y', 0, 0, tiled=True)  4.72 us
    ppermute x1, starting transfers between devices, on_device(): above = lax.ppermute(own, 'y', turn(-1))  4.57 us
  transfers between devices with their start and end apart: 18, of which 6 were waited for; matrix products, arithmetic and copies ran while one was open for 5% of the time, Pallas kernels for 13%

profile of v11, /device:TPU:6, one launch (start us, length us, event | category | flops | bytes accessed | tf_op | source)
XLA Modules:
  0.0 132.3 jit_solution(6568185581748252068)
XLA Ops:
  1.3 0.1 stack.19.place
  1.4 1.0 copy-done.5
  2.4 0.6 live_sets.1
  3.0 2.7 %collective-permute-start = (bf16[384,256]{1,0:T(8,128)(2,1)S(1)}, bf16[384,256]{1,0:T(8,128)(2,1)S(1)}, u32[]{:S(2)}, u32[]{:S(2)}) collective-permute-start(bf16[384,256]{1,0:T(8,128)(2,1)S(1)} %get-tuple-element.18), channel_id=1, source_target_pairs={{0,1},{1,0},{2,3},{3,2},{4,5},{5,4},{6,7},{7,6},{8,9},{9,8},{10,11... | collective-permute-start | bytes 589832 | tf_op jit(solution)/shard_map/ppermute | solution.py:180
  5.7 2.1 %dynamic-slice_bitcast_fusion.1 = bf16[1024,384]{1,0:T(8,128)(2,1)} fusion(bf16[2,1024,384]{2,1,0:T(8,128)(2,1)} %bitcast.25, s32[]{:T(128)S(6)} %select_n.6), kind=kLoop, calls=%fused_computation.9 | loop fusion | bytes 1572868 | tf_op jit(solution)/shard_map/jit(dynamic_index_in_dim)/squeeze | solution.py:143
  7.8 6.9 %collective-permute-start.2 = (bf16[1024,384]{1,0:T(8,128)(2,1)}, bf16[1024,384]{1,0:T(8,128)(2,1)}, u32[]{:S(2)}, u32[]{:S(2)}) collective-permute-start(bf16[1024,384]{1,0:T(8,128)(2,1)} %dynamic-slice_bitcast_fusion.1), channel_id=1, source_target_pairs={{0,17},{17,0},{1,16},{16,1},{2,19},{19,2},{3,18},{18,3},{4,21},{21... | collective-permute-start | bytes 2359304 | tf_op jit(solution)/shard_map/ppermute | solution.py:192
  14.8 1.8 %spread.1 = bf16[4,2,384,256]{3,2,1,0:T(8,128)(2,1)} custom-call(s32[5]{0:T(128)S(1)} %stack.19.place, bf16[384,256]{1,0:T(8,128)(2,1)S(1)} %get-tuple-element.17.own_set, bf16[384,256]{1,0:T(8,128)(2,1)S(1)} %collective-permute-done.near_set), custom_call_target="tpu_custom_call" | custom-call | tf_op jit(solution)/shard_map/spread/pallas_call | solution.py:181
  16.6 3.7 %all-to-all-start = ((bf16[4,2,384,256]{3,2,1,0:T(8,128)(2,1)}), bf16[4,2,384,256]{3,2,1,0:T(8,128)(2,1)S(1)}, u32[]{:S(2)}, u32[]{:S(2)}) async-start(bf16[4,2,384,256]{3,2,1,0:T(8,128)(2,1)} %spread.1), calls=%async_computation | async-start | bytes 3145728 | tf_op jit(solution)/shard_map/all_to_all | solution.py:189
  20.3 0.0 copy-start.4
  20.3 0.1 dynamic-slice_bitcast_fusion
  20.4 3.4 %collective-permute-start.4 = (bf16[192,2048]{1,0:T(8,128)(2,1)S(1)}, bf16[192,2048]{1,0:T(8,128)(2,1)}, u32[]{:S(2)}, u32[]{:S(2)}) collective-permute-start(bf16[192,2048]{1,0:T(8,128)(2,1)S(1)} %dynamic-slice_bitcast_fusion), channel_id=1, source_target_pairs={{0,1},{1,0},{8,25},{9,24},{16,17},{17,16},{24,9},{25,8},{2,3},{3,2... | collective-permute-start | bytes 2359304 | tf_op jit(solution)/shard_map/ppermute | solution.py:193
  23.9 0.6 pre_sets.1
  24.5 0.7 copy-done.6
  25.2 2.5 %collective-permute-start.1 = (bf16[384,384]{1,0:T(8,128)(2,1)S(1)}, bf16[384,384]{1,0:T(8,128)(2,1)S(1)}, u32[]{:S(2)}, u32[]{:S(2)}) collective-permute-start(bf16[384,384]{1,0:T(8,128)(2,1)S(1)} %get-tuple-element.20), channel_id=1, source_target_pairs={{0,1},{1,0},{2,3},{3,2},{4,5},{5,4},{6,7},{7,6},{8,9},{9,8},{10,11... | collective-permute-start | bytes 884744 | tf_op jit(solution)/shard_map/ppermute | solution.py:190
  27.7 5.8 %collective-permute-done.2.down_mine = bf16[1024,384]{1,0:T(8,128)(2,1)} collective-permute-done((bf16[1024,384]{1,0:T(8,128)(2,1)}, bf16[1024,384]{1,0:T(8,128)(2,1)}, u32[]{:S(2)}, u32[]{:S(2)}) %collective-permute-start.2) | collective-permute-done | bytes 786464 | tf_op jit(solution)/shard_map/ppermute | solution.py:192
  33.5 1.9 %collective-permute-start.3 = (bf16[1024,384]{1,0:T(8,128)(2,1)}, bf16[1024,384]{1,0:T(8,128)(2,1)}, u32[]{:S(2)}, u32[]{:S(2)}) collective-permute-start(bf16[1024,384]{1,0:T(8,128)(2,1)} %collective-permute-done.2.down_mine), channel_id=1, source_target_pairs={{0,8},{8,0},{1,9},{9,1},{2,10},{10,2},{3,11},{11,3},{4,12},{12,4},... | collective-permute-start | bytes 2359304 | tf_op jit(solution)/shard_map/ppermute | solution.py:196
  35.5 2.2 %collective-permute-done.4.up_mine = bf16[192,2048]{1,0:T(8,128)(2,1)} collective-permute-done((bf16[192,2048]{1,0:T(8,128)(2,1)S(1)}, bf16[192,2048]{1,0:T(8,128)(2,1)}, u32[]{:S(2)}, u32[]{:S(2)}) %collective-permute-start.4) | collective-permute-done | bytes 786464 | tf_op jit(solution)/shard_map/ppermute | solution.py:193
  37.7 2.7 %collective-permute-start.5 = (bf16[192,2048]{1,0:T(8,128)(2,1)}, bf16[192,2048]{1,0:T(8,128)(2,1)}, u32[]{:S(2)}, u32[]{:S(2)}) collective-permute-start(bf16[192,2048]{1,0:T(8,128)(2,1)} %collective-permute-done.4.up_mine), channel_id=1, source_target_pairs={{0,8},{8,0},{1,9},{9,1},{2,10},{10,2},{3,11},{11,3},{4,12},{12,4},... | collective-permute-start | bytes 2359304 | tf_op jit(solution)/shard_map/ppermute | solution.py:197
  40.4 0.3 collective-permute-done.1.pre_far
  40.7 1.0 copy-done.7
  41.7 3.6 %down_terms.1 = (bf16[4,16,32,384]{3,2,1,0:T(8,128)(2,1)S(1)}, bf16[4,16,32,384]{3,2,1,0:T(8,128)(2,1)}) custom-call(s32[5]{0:T(128)S(1)} %stack.19.place, bf16[8,384,256]{2,1,0:T(8,128)(2,1)S(1)} %bitcast.22, bf16[384,384]{1,0:T(8,128)(2,1)S(1)} %copy-done.7, bf16[384,384]{1,0:T(8,128)(2,1)S(1)} %collective-permute-done.1.pre_far), custom_call_target="tpu_custom_call" | custom-call | flops 1207959552 | bytes 6291456 | tf_op jit(solution)/shard_map/down_terms/pallas_call | solution.py:212
  45.3 1.2 copy-done.2
  46.4 1.9 %collective-permute-start.11 = (bf16[4,16,32,384]{3,2,1,0:T(8,128)(2,1)}, bf16[4,16,32,384]{3,2,1,0:T(8,128)(2,1)}, u32[]{:S(2)}, u32[]{:S(2)}) collective-permute-start(bf16[4,16,32,384]{3,2,1,0:T(8,128)(2,1)} %get-tuple-element.27), channel_id=1, source_target_pairs={{0,8},{8,0},{1,9},{9,1},{2,10},{10,2},{3,11},{11,3},{4,12},{12,4},... | collective-permute-start | bytes 4718600 | tf_op jit(solution)/shard_map/ppermute | solution.py:242
  48.4 1.0 own_grad.1.own
  49.4 0.0 collective-permute-done.5.up_other
  49.4 5.6 %terms.1 = bf16[384,2048]{1,0:T(8,128)(2,1)} custom-call(s32[5]{0:T(128)S(1)} %stack.19.place, bf16[8,384,256]{2,1,0:T(8,128)(2,1)S(1)} %bitcast.24, bf16[384,384]{1,0:T(8,128)(2,1)S(1)} %own_grad.1.own, bf16[384,384]{1,0:T(8,128)(2,1)S(1)} %collective-permute-done.1.pre_far, bf16[1024,384]{1,0:T(8,128)(2,1)} %collective-permute-done.2.down_mine, ...), custom_call_target="tpu_custom_call" | custom-call | flops 1811939328 | bytes 9437184 | tf_op jit(solution)/shard_map/terms/pallas_call | solution.py:225
  55.0 4.7 %all-to-all-start.1 = ((bf16[4,96,2048]{2,1,0:T(8,128)(2,1)}), bf16[4,96,2048]{2,1,0:T(8,128)(2,1)}, u32[]{:S(2)}, u32[]{:S(2)}) async-start(bf16[4,96,2048]{2,1,0:T(8,128)(2,1)} %bitcast.9), calls=%async_computation.1 | async-start | bytes 3145728 | tf_op jit(solution)/shard_map/all_to_all | solution.py:239
  59.7 2.7 %fusion.4 = (bf16[16,32,384]{2,1,0:T(8,128)(2,1)}, bf16[16,32,384]{2,1,0:T(8,128)(2,1)}, bf16[16,32,384]{2,1,0:T(8,128)(2,1)}, bf16[16,32,384]{2,1,0:T(8,128)(2,1)S(1)}) fusion(bf16[4,16,32,384]{3,2,1,0:T(8,128)(2,1)} %collective-permute-done.11, bf16[4,16,32,384]{3,2,1,0:T(8,128)(2,1)S(1)} %copy-done.3), kind=kLoop, calls=%fused_computation.14 | loop fusion | flops 3145728 | bytes 4718592 | tf_op jit(solution)/shard_map/convert_element_type | solution.py:247
  62.4 2.2 %collective-permute-start.12 = (bf16[16,32,384]{2,1,0:T(8,128)(2,1)}, bf16[16,32,384]{2,1,0:T(8,128)(2,1)S(1)}, u32[]{:S(2)}, u32[]{:S(2)}) collective-permute-start(bf16[16,32,384]{2,1,0:T(8,128)(2,1)} %get-tuple-element.34), channel_id=1, source_target_pairs={{0,1},{1,0},{2,3},{3,2},{4,5},{5,4},{6,7},{7,6},{8,9},{9,8},{10,11... | collective-permute-start | bytes 1179656 | tf_op jit(solution)/shard_map/ppermute | solution.py:245
  64.6 3.3 %collective-permute-start.13 = (bf16[16,32,384]{2,1,0:T(8,128)(2,1)}, bf16[16,32,384]{2,1,0:T(8,128)(2,1)S(1)}, u32[]{:S(2)}, u32[]{:S(2)}) collective-permute-start(bf16[16,32,384]{2,1,0:T(8,128)(2,1)} %get-tuple-element.33), channel_id=1, source_target_pairs={{0,17},{17,0},{1,16},{16,1},{2,19},{19,2},{3,18},{18,3},{4,21},{21... | collective-permute-start | bytes 1179656 | tf_op jit(solution)/shard_map/ppermute | solution.py:246
  68.0 4.3 %collective-permute-start.14 = (bf16[16,32,384]{2,1,0:T(8,128)(2,1)}, bf16[16,32,384]{2,1,0:T(8,128)(2,1)S(1)}, u32[]{:S(2)}, u32[]{:S(2)}) collective-permute-start(bf16[16,32,384]{2,1,0:T(8,128)(2,1)} %get-tuple-element.32), channel_id=1, source_target_pairs={{0,16},{16,0},{1,17},{17,1},{2,18},{18,2},{3,19},{19,3},{4,20},{20... | collective-permute-start | bytes 1179656 | tf_op jit(solution)/shard_map/ppermute | solution.py:247
  72.2 9.1 %all-to-all-done.1 = bf16[4,96,2048]{2,1,0:T(8,128)(2,1)} async-done(((bf16[4,96,2048]{2,1,0:T(8,128)(2,1)}), bf16[4,96,2048]{2,1,0:T(8,128)(2,1)}, u32[]{:S(2)}, u32[]{:S(2)}) %all-to-all-start.1) | async-done | bytes 1572896 | tf_op jit(solution)/shard_map/all_to_all | solution.py:239
  81.3 1.6 %fusion.own = bf16[96,2048]{1,0:T(8,128)(2,1)S(1)} fusion(bf16[4,96,2048]{2,1,0:T(8,128)(2,1)} %all-to-all-done.1), kind=kLoop, calls=%fused_computation.10 | loop fusion | flops 1572864 | bytes 1966080 | tf_op jit(solution)/shard_map/add | solution.py:240
  82.9 2.2 %collective-permute-start.6 = (bf16[96,2048]{1,0:T(8,128)(2,1)S(1)}, bf16[96,2048]{1,0:T(8,128)(2,1)S(1)}, u32[]{:S(2)}, u32[]{:S(2)}) collective-permute-start(bf16[96,2048]{1,0:T(8,128)(2,1)S(1)} %fusion.own), channel_id=1, source_target_pairs={{0,1},{1,0},{2,3},{3,2},{4,5},{5,4},{6,7},{7,6},{8,9},{9,8},{10,11... | collective-permute-start | bytes 1179656 | tf_op jit(solution)/shard_map/ppermute | solution.py:250
  85.1 2.5 %collective-permute-start.7 = (bf16[96,2048]{1,0:T(8,128)(2,1)S(1)}, bf16[96,2048]{1,0:T(8,128)(2,1)S(1)}, u32[]{:S(2)}, u32[]{:S(2)}) collective-permute-start(bf16[96,2048]{1,0:T(8,128)(2,1)S(1)} %fusion.own), channel_id=1, source_target_pairs={{0,2},{2,4},{4,6},{6,0},{1,3},{3,5},{5,7},{7,1},{8,10},{10,12},{12... | collective-permute-start | bytes 1179656 | tf_op jit(solution)/shard_map/ppermute | solution.py:251
  87.6 4.6 %collective-permute-start.8 = (bf16[96,2048]{1,0:T(8,128)(2,1)S(1)}, bf16[96,2048]{1,0:T(8,128)(2,1)S(1)}, u32[]{:S(2)}, u32[]{:S(2)}) collective-permute-start(bf16[96,2048]{1,0:T(8,128)(2,1)S(1)} %fusion.own), channel_id=1, source_target_pairs={{0,6},{2,0},{4,2},{6,4},{1,7},{3,1},{5,3},{7,5},{8,14},{10,8},{12,... | collective-permute-start | bytes 1179656 | tf_op jit(solution)/shard_map/ppermute | solution.py:252
  92.2 1.0 ring_sum.1
  93.2 14.7 %all-to-all-start.2 = ((bf16[16,32,384]{2,1,0:T(8,128)(2,1)}), bf16[16,32,384]{2,1,0:T(8,128)(2,1)S(1)}, u32[]{:S(2)}, u32[]{:S(2)}) async-start(bf16[16,32,384]{2,1,0:T(8,128)(2,1)} %ring_sum.1), calls=%async_computation.2 | async-start | bytes 786432 | tf_op jit(solution)/shard_map/all_to_all | solution.py:264
  107.9 0.1 pad_maximum_fusion.1
  108.0 1.9 %collective-permute-start.10 = (bf16[192,2048]{1,0:T(8,128)(2,1)S(1)}, bf16[192,2048]{1,0:T(8,128)(2,1)S(1)}, u32[]{:S(2)}, u32[]{:S(2)}) collective-permute-start(bf16[192,2048]{1,0:T(8,128)(2,1)S(1)} %pad_maximum_fusion.1), channel_id=1, source_target_pairs={{0,4},{2,6},{4,0},{6,2},{1,5},{3,7},{5,1},{7,3},{8,12},{10,14},{12... | collective-permute-start | bytes 2359304 | tf_op jit(solution)/shard_map/ppermute | solution.py:268
  109.9 0.1 pad_maximum_fusion
  110.0 3.8 %collective-permute-start.9 = (bf16[192,2048]{1,0:T(8,128)(2,1)S(1)}, bf16[192,2048]{1,0:T(8,128)(2,1)S(1)}, u32[]{:S(2)}, u32[]{:S(2)}) collective-permute-start(bf16[192,2048]{1,0:T(8,128)(2,1)S(1)} %pad_maximum_fusion), channel_id=1, source_target_pairs={{0,1},{1,0},{2,3},{3,2},{4,5},{5,4},{6,7},{7,6},{8,9},{9,8},{10,11... | collective-permute-start | bytes 2359304 | tf_op jit(solution)/shard_map/ppermute | solution.py:269
  113.7 1.7 %place_first.1.partial = bf16[768,2048]{1,0:T(8,128)(2,1)} custom-call(s32[5]{0:T(128)S(1)} %stack.19.place, bf16[96,2048]{1,0:T(8,128)(2,1)S(1)} %fusion.own, bf16[96,2048]{1,0:T(8,128)(2,1)S(1)} %collective-permute-done.6.near, bf16[96,2048]{1,0:T(8,128)(2,1)S(1)} %collective-permute-done.7.below, bf16[96,2048]{1,0:T(8,128)(2,1)S(1)} %collective-permute-done.8.above), custom_call_target="tpu_custom_call" | custom-call | tf_op jit(solution)/shard_map/place_first/pallas_call | solution.py:271
  115.5 13.9 %collective-permute-done.10.across = bf16[192,2048]{1,0:T(8,128)(2,1)S(1)} collective-permute-done((bf16[192,2048]{1,0:T(8,128)(2,1)S(1)}, bf16[192,2048]{1,0:T(8,128)(2,1)S(1)}, u32[]{:S(2)}, u32[]{:S(2)}) %collective-permute-start.10) | collective-permute-done | bytes 786464 | tf_op jit(solution)/shard_map/ppermute | solution.py:268
  129.3 0.5 collective-permute-done.9.beside
  129.8 1.7 %place_last.1 = bf16[768,2048]{1,0:T(8,128)(2,1)} custom-call(s32[5]{0:T(128)S(1)} %stack.19.place, bf16[768,2048]{1,0:T(8,128)(2,1)} %place_first.1.partial, bf16[192,2048]{1,0:T(8,128)(2,1)S(1)} %collective-permute-done.9.beside, bf16[192,2048]{1,0:T(8,128)(2,1)S(1)} %collective-permute-done.10.across), custom_call_target="tpu_custom_call", output_to_operand_aliasing={{}: (1, {})} | custom-call | tf_op jit(solution)/shard_map/place_last/pallas_call | solution.py:280
  131.6 0.1 convert_reduce_fusion
  131.6 0.6 broadcast_multiply_fusion
  (22 shorter events, 0.0 us)
Async XLA Ops:
  1.4 1.0 copy-start.5
  3.0 11.8 %collective-permute-start = (bf16[384,256]{1,0:T(8,128)(2,1)S(1)}, bf16[384,256]{1,0:T(8,128)(2,1)S(1)}, u32[]{:S(2)}, u32[]{:S(2)}) collective-permute-start(bf16[384,256]{1,0:T(8,128)(2,1)S(1)} %get-tuple-element.18), channel_id=1, source_target_pairs={{0,1},{1,0},{2,3},{3,2},{4,5},{5,4},{6,7},{7,6},{8,9},{9,8},{10,11... | collective-permute-start | bytes 589832 | tf_op jit(solution)/shard_map/ppermute | solution.py:180
  7.8 25.7 %collective-permute-start.2 = (bf16[1024,384]{1,0:T(8,128)(2,1)}, bf16[1024,384]{1,0:T(8,128)(2,1)}, u32[]{:S(2)}, u32[]{:S(2)}) collective-permute-start(bf16[1024,384]{1,0:T(8,128)(2,1)} %dynamic-slice_bitcast_fusion.1), channel_id=1, source_target_pairs={{0,17},{17,0},{1,16},{16,1},{2,19},{19,2},{3,18},{18,3},{4,21},{21... | collective-permute-start | bytes 2359304 | tf_op jit(solution)/shard_map/ppermute | solution.py:192
  16.6 3.7 %copy-start.1 = (bf16[384,2048]{1,0:T(8,128)(2,1)S(1)}, bf16[384,2048]{1,0:T(8,128)(2,1)}, u32[]{:S(2)}) copy-start(bf16[384,2048]{1,0:T(8,128)(2,1)} %up_own.1) | copy-start | bytes 4718596
  16.6 24.1 %all-to-all-start = ((bf16[4,2,384,256]{3,2,1,0:T(8,128)(2,1)}), bf16[4,2,384,256]{3,2,1,0:T(8,128)(2,1)S(1)}, u32[]{:S(2)}, u32[]{:S(2)}) async-start(bf16[4,2,384,256]{3,2,1,0:T(8,128)(2,1)} %spread.1), calls=%async_computation | async-start | bytes 3145728 | tf_op jit(solution)/shard_map/all_to_all | solution.py:189
  20.3 3.5 %copy-start.4 = (bf16[768,384]{1,0:T(8,128)(2,1)S(1)}, bf16[768,384]{1,0:T(8,128)(2,1)}, u32[]{:S(2)}) copy-start(bf16[768,384]{1,0:T(8,128)(2,1)} %whole.3) | copy-start | bytes 1769476
  20.4 17.3 %collective-permute-start.4 = (bf16[192,2048]{1,0:T(8,128)(2,1)S(1)}, bf16[192,2048]{1,0:T(8,128)(2,1)}, u32[]{:S(2)}, u32[]{:S(2)}) collective-permute-start(bf16[192,2048]{1,0:T(8,128)(2,1)S(1)} %dynamic-slice_bitcast_fusion), channel_id=1, source_target_pairs={{0,1},{1,0},{8,25},{9,24},{16,17},{17,16},{24,9},{25,8},{2,3},{3,2... | collective-permute-start | bytes 2359304 | tf_op jit(solution)/shard_map/ppermute | solution.py:193
  24.5 0.7 copy-start.6
  25.2 15.5 %collective-permute-start.1 = (bf16[384,384]{1,0:T(8,128)(2,1)S(1)}, bf16[384,384]{1,0:T(8,128)(2,1)S(1)}, u32[]{:S(2)}, u32[]{:S(2)}) collective-permute-start(bf16[384,384]{1,0:T(8,128)(2,1)S(1)} %get-tuple-element.20), channel_id=1, source_target_pairs={{0,1},{1,0},{2,3},{3,2},{4,5},{5,4},{6,7},{7,6},{8,9},{9,8},{10,11... | collective-permute-start | bytes 884744 | tf_op jit(solution)/shard_map/ppermute | solution.py:190
  33.5 15.8 %collective-permute-start.3 = (bf16[1024,384]{1,0:T(8,128)(2,1)}, bf16[1024,384]{1,0:T(8,128)(2,1)}, u32[]{:S(2)}, u32[]{:S(2)}) collective-permute-start(bf16[1024,384]{1,0:T(8,128)(2,1)} %collective-permute-done.2.down_mine), channel_id=1, source_target_pairs={{0,8},{8,0},{1,9},{9,1},{2,10},{10,2},{3,11},{11,3},{4,12},{12,4},... | collective-permute-start | bytes 2359304 | tf_op jit(solution)/shard_map/ppermute | solution.py:196
  37.7 11.7 %collective-permute-start.5 = (bf16[192,2048]{1,0:T(8,128)(2,1)}, bf16[192,2048]{1,0:T(8,128)(2,1)}, u32[]{:S(2)}, u32[]{:S(2)}) collective-permute-start(bf16[192,2048]{1,0:T(8,128)(2,1)} %collective-permute-done.4.up_mine), channel_id=1, source_target_pairs={{0,8},{8,0},{1,9},{9,1},{2,10},{10,2},{3,11},{11,3},{4,12},{12,4},... | collective-permute-start | bytes 2359304 | tf_op jit(solution)/shard_map/ppermute | solution.py:197
  40.7 1.0 copy-start.7
  41.7 6.7 %copy-start = (bf16[2048,384]{1,0:T(8,128)(2,1)S(1)}, bf16[2048,384]{1,0:T(8,128)(2,1)}, u32[]{:S(2)}) copy-start(bf16[2048,384]{1,0:T(8,128)(2,1)} %down.1) | copy-start | bytes 4718596
  45.3 1.2 copy-start.2
  46.4 13.3 %collective-permute-start.11 = (bf16[4,16,32,384]{3,2,1,0:T(8,128)(2,1)}, bf16[4,16,32,384]{3,2,1,0:T(8,128)(2,1)}, u32[]{:S(2)}, u32[]{:S(2)}) collective-permute-start(bf16[4,16,32,384]{3,2,1,0:T(8,128)(2,1)} %get-tuple-element.27), channel_id=1, source_target_pairs={{0,8},{8,0},{1,9},{9,1},{2,10},{10,2},{3,11},{11,3},{4,12},{12,4},... | collective-permute-start | bytes 4718600 | tf_op jit(solution)/shard_map/ppermute | solution.py:242
  55.0 4.7 %copy-start.3 = (bf16[4,16,32,384]{3,2,1,0:T(8,128)(2,1)S(1)}, bf16[4,16,32,384]{3,2,1,0:T(8,128)(2,1)}, u32[]{:S(2)}) copy-start(bf16[4,16,32,384]{3,2,1,0:T(8,128)(2,1)} %copy-done.2) | copy-start | bytes 4718596
  55.0 26.3 %all-to-all-start.1 = ((bf16[4,96,2048]{2,1,0:T(8,128)(2,1)}), bf16[4,96,2048]{2,1,0:T(8,128)(2,1)}, u32[]{:S(2)}, u32[]{:S(2)}) async-start(bf16[4,96,2048]{2,1,0:T(8,128)(2,1)} %bitcast.9), calls=%async_computation.1 | async-start | bytes 3145728 | tf_op jit(solution)/shard_map/all_to_all | solution.py:239
  62.4 25.2 %collective-permute-start.12 = (bf16[16,32,384]{2,1,0:T(8,128)(2,1)}, bf16[16,32,384]{2,1,0:T(8,128)(2,1)S(1)}, u32[]{:S(2)}, u32[]{:S(2)}) collective-permute-start(bf16[16,32,384]{2,1,0:T(8,128)(2,1)} %get-tuple-element.34), channel_id=1, source_target_pairs={{0,1},{1,0},{2,3},{3,2},{4,5},{5,4},{6,7},{7,6},{8,9},{9,8},{10,11... | collective-permute-start | bytes 1179656 | tf_op jit(solution)/shard_map/ppermute | solution.py:245
  64.6 27.6 %collective-permute-start.13 = (bf16[16,32,384]{2,1,0:T(8,128)(2,1)}, bf16[16,32,384]{2,1,0:T(8,128)(2,1)S(1)}, u32[]{:S(2)}, u32[]{:S(2)}) collective-permute-start(bf16[16,32,384]{2,1,0:T(8,128)(2,1)} %get-tuple-element.33), channel_id=1, source_target_pairs={{0,17},{17,0},{1,16},{16,1},{2,19},{19,2},{3,18},{18,3},{4,21},{21... | collective-permute-start | bytes 1179656 | tf_op jit(solution)/shard_map/ppermute | solution.py:246
  68.0 24.2 %collective-permute-start.14 = (bf16[16,32,384]{2,1,0:T(8,128)(2,1)}, bf16[16,32,384]{2,1,0:T(8,128)(2,1)S(1)}, u32[]{:S(2)}, u32[]{:S(2)}) collective-permute-start(bf16[16,32,384]{2,1,0:T(8,128)(2,1)} %get-tuple-element.32), channel_id=1, source_target_pairs={{0,16},{16,0},{1,17},{17,1},{2,18},{18,2},{3,19},{19,3},{4,20},{20... | collective-permute-start | bytes 1179656 | tf_op jit(solution)/shard_map/ppermute | solution.py:247
  82.9 25.0 %collective-permute-start.6 = (bf16[96,2048]{1,0:T(8,128)(2,1)S(1)}, bf16[96,2048]{1,0:T(8,128)(2,1)S(1)}, u32[]{:S(2)}, u32[]{:S(2)}) collective-permute-start(bf16[96,2048]{1,0:T(8,128)(2,1)S(1)} %fusion.own), channel_id=1, source_target_pairs={{0,1},{1,0},{2,3},{3,2},{4,5},{5,4},{6,7},{7,6},{8,9},{9,8},{10,11... | collective-permute-start | bytes 1179656 | tf_op jit(solution)/shard_map/ppermute | solution.py:250
  85.1 22.8 %collective-permute-start.7 = (bf16[96,2048]{1,0:T(8,128)(2,1)S(1)}, bf16[96,2048]{1,0:T(8,128)(2,1)S(1)}, u32[]{:S(2)}, u32[]{:S(2)}) collective-permute-start(bf16[96,2048]{1,0:T(8,128)(2,1)S(1)} %fusion.own), channel_id=1, source_target_pairs={{0,2},{2,4},{4,6},{6,0},{1,3},{3,5},{5,7},{7,1},{8,10},{10,12},{12... | collective-permute-start | bytes 1179656 | tf_op jit(solution)/shard_map/ppermute | solution.py:251
  87.6 20.3 %collective-permute-start.8 = (bf16[96,2048]{1,0:T(8,128)(2,1)S(1)}, bf16[96,2048]{1,0:T(8,128)(2,1)S(1)}, u32[]{:S(2)}, u32[]{:S(2)}) collective-permute-start(bf16[96,2048]{1,0:T(8,128)(2,1)S(1)} %fusion.own), channel_id=1, source_target_pairs={{0,6},{2,0},{4,2},{6,4},{1,7},{3,1},{5,3},{7,5},{8,14},{10,8},{12,... | collective-permute-start | bytes 1179656 | tf_op jit(solution)/shard_map/ppermute | solution.py:252
  93.2 38.4 %all-to-all-start.2 = ((bf16[16,32,384]{2,1,0:T(8,128)(2,1)}), bf16[16,32,384]{2,1,0:T(8,128)(2,1)S(1)}, u32[]{:S(2)}, u32[]{:S(2)}) async-start(bf16[16,32,384]{2,1,0:T(8,128)(2,1)} %ring_sum.1), calls=%async_computation.2 | async-start | bytes 786432 | tf_op jit(solution)/shard_map/all_to_all | solution.py:264
  108.0 21.4 %collective-permute-start.10 = (bf16[192,2048]{1,0:T(8,128)(2,1)S(1)}, bf16[192,2048]{1,0:T(8,128)(2,1)S(1)}, u32[]{:S(2)}, u32[]{:S(2)}) collective-permute-start(bf16[192,2048]{1,0:T(8,128)(2,1)S(1)} %pad_maximum_fusion.1), channel_id=1, source_target_pairs={{0,4},{2,6},{4,0},{6,2},{1,5},{3,7},{5,1},{7,3},{8,12},{10,14},{12... | collective-permute-start | bytes 2359304 | tf_op jit(solution)/shard_map/ppermute | solution.py:268
  110.0 19.9 %collective-permute-start.9 = (bf16[192,2048]{1,0:T(8,128)(2,1)S(1)}, bf16[192,2048]{1,0:T(8,128)(2,1)S(1)}, u32[]{:S(2)}, u32[]{:S(2)}) collective-permute-start(bf16[192,2048]{1,0:T(8,128)(2,1)S(1)} %pad_maximum_fusion), channel_id=1, source_target_pairs={{0,1},{1,0},{2,3},{3,2},{4,5},{5,4},{6,7},{7,6},{8,9},{9,8},{10,11... | collective-permute-start | bytes 2359304 | tf_op jit(solution)/shard_map/ppermute | solution.py:269

commit v12 on v11

--- a/solution.py
+++ b/solution.py
@@ -117,10 +117,14 @@
     for i, (block, dy, dx, *rest) in enumerate(blocks):
         at = ((y + dy + ranks) % ranks) * 2 + (1 - xl if dx else xl)
         start = pl.multiple_of(at * rows, 16)
-        source = block.at[pl.ds(rest[0], rows)] if rest else block
-        copy = pltpu.make_async_copy(source, out.at[pl.ds(start, rows)], sems.at[i])
-        copy.start()
-        running.append(copy)
+        for part in range(2):
+            half = rows // 2
+            source = block.at[pl.ds((rest[0] if rest else 0) + part * half, half)]
+            copy = pltpu.make_async_copy(
+                source, out.at[pl.ds(pl.multiple_of(start + part * half, 16), half)], sems.at[2 * i + part]
+            )
+            copy.start()
+            running.append(copy)
     for copy in running:
         copy.wait()
 
@@ -273,7 +277,7 @@
         out_shape=whole,
         in_specs=[SMEM] + [VMEM] * 4,
         out_specs=ANY,
-        scratch_shapes=[pltpu.SemaphoreType.DMA((4,))],
+        scratch_shapes=[pltpu.SemaphoreType.DMA((8,))],
         compiler_params=params,
         name="place_first",
     )(place, own, near, below, above)
@@ -282,7 +286,7 @@
         out_shape=whole,
         in_specs=[SMEM, ANY] + [VMEM] * 2,
         out_specs=ANY,
-        scratch_shapes=[pltpu.SemaphoreType.DMA((4,))],
+        scratch_shapes=[pltpu.SemaphoreType.DMA((8,))],
         input_output_aliases={1: 0},
         compiler_params=params,
         name="place_last",

time: 134 us -> 134 us (level)
  no operation moved by 1% of the time
where the time goes in v12:
time: 134 us; the launch traced here: 132 us
  starting transfers between devices  70 us (52%)
  waiting for transfers between devices  31.8 us (24%)
  Pallas kernels  17.6 us (13%)
  local copies, waits for them, and re-layouts  6.15 us (5%)
  other arithmetic  5.06 us (4%)
  between operations  1.62 us (1%)
    all_to_all x1, starting transfers between devices, on_device(): z_terms = lax.all_to_all(ring_sum, 'z', 0, 0, tiled=True)  14.7 us
    ppermute x1, waiting for transfers between devices, on_device(): across = lax.ppermute(jnp.concatenate([own, near]), 'y', turn(2))  13.8 us
    all_to_all x1, waiting for transfers between devices, on_device(): came = lax.all_to_all(terms.reshape(ys, rows, width), 'y', 0, 0, tiled=True)  9.07 us
    ppermute x1, starting transfers between devices, on_device(): lax.ppermute(own_part(down_weight.reshape(2, width // 2, hidden_units), c...  6.93 us
    ppermute x1, waiting for transfers between devices, on_device(): lax.ppermute(own_part(down_weight.reshape(2, width // 2, hidden_units), c...  5.81 us
    pallas_call x1, Pallas kernels, on_device(): pl.pallas_call(terms_kernel, out_shape=jax.ShapeDtypeStruct((half_rows, w...  5.64 us
    all_to_all x1, starting transfers between devices, on_device(): came = lax.all_to_all(terms.reshape(ys, rows, width), 'y', 0, 0, tiled=True)  4.72 us
    ppermute x1, starting transfers between devices, on_device(): above = lax.ppermute(own, 'y', turn(-1))  4.57 us
  transfers between devices with their start and end apart: 18, of which 6 were waited for; matrix products, arithmetic and copies ran while one was open for 5% of the time, Pallas kernels for 13%

profile of v12, /device:TPU:6, one launch (start us, length us, event | category | flops | bytes accessed | tf_op | source)
XLA Modules:
  0.0 132.3 jit_solution(5554001420133944503)
XLA Ops:
  1.3 0.1 stack.19.place
  1.4 1.0 copy-done.5
  2.4 0.6 live_sets.1
  3.0 2.7 %collective-permute-start = (bf16[384,256]{1,0:T(8,128)(2,1)S(1)}, bf16[384,256]{1,0:T(8,128)(2,1)S(1)}, u32[]{:S(2)}, u32[]{:S(2)}) collective-permute-start(bf16[384,256]{1,0:T(8,128)(2,1)S(1)} %get-tuple-element.18), channel_id=1, source_target_pairs={{0,1},{1,0},{2,3},{3,2},{4,5},{5,4},{6,7},{7,6},{8,9},{9,8},{10,11... | collective-permute-start | bytes 589832 | tf_op jit(solution)/shard_map/ppermute | solution.py:184
  5.7 2.1 %dynamic-slice_bitcast_fusion.1 = bf16[1024,384]{1,0:T(8,128)(2,1)} fusion(bf16[2,1024,384]{2,1,0:T(8,128)(2,1)} %bitcast.25, s32[]{:T(128)S(6)} %select_n.6), kind=kLoop, calls=%fused_computation.9 | loop fusion | bytes 1572868 | tf_op jit(solution)/shard_map/jit(dynamic_index_in_dim)/squeeze | solution.py:147
  7.8 6.9 %collective-permute-start.2 = (bf16[1024,384]{1,0:T(8,128)(2,1)}, bf16[1024,384]{1,0:T(8,128)(2,1)}, u32[]{:S(2)}, u32[]{:S(2)}) collective-permute-start(bf16[1024,384]{1,0:T(8,128)(2,1)} %dynamic-slice_bitcast_fusion.1), channel_id=1, source_target_pairs={{0,17},{17,0},{1,16},{16,1},{2,19},{19,2},{3,18},{18,3},{4,21},{21... | collective-permute-start | bytes 2359304 | tf_op jit(solution)/shard_map/ppermute | solution.py:196
  14.8 1.8 %spread.1 = bf16[4,2,384,256]{3,2,1,0:T(8,128)(2,1)} custom-call(s32[5]{0:T(128)S(1)} %stack.19.place, bf16[384,256]{1,0:T(8,128)(2,1)S(1)} %get-tuple-element.17.own_set, bf16[384,256]{1,0:T(8,128)(2,1)S(1)} %collective-permute-done.near_set), custom_call_target="tpu_custom_call" | custom-call | tf_op jit(solution)/shard_map/spread/pallas_call | solution.py:185
  16.6 3.7 %all-to-all-start = ((bf16[4,2,384,256]{3,2,1,0:T(8,128)(2,1)}), bf16[4,2,384,256]{3,2,1,0:T(8,128)(2,1)S(1)}, u32[]{:S(2)}, u32[]{:S(2)}) async-start(bf16[4,2,384,256]{3,2,1,0:T(8,128)(2,1)} %spread.1), calls=%async_computation | async-start | bytes 3145728 | tf_op jit(solution)/shard_map/all_to_all | solution.py:193
  20.3 0.0 copy-start.4
  20.3 0.1 dynamic-slice_bitcast_fusion
  20.4 3.4 %collective-permute-start.4 = (bf16[192,2048]{1,0:T(8,128)(2,1)S(1)}, bf16[192,2048]{1,0:T(8,128)(2,1)}, u32[]{:S(2)}, u32[]{:S(2)}) collective-permute-start(bf16[192,2048]{1,0:T(8,128)(2,1)S(1)} %dynamic-slice_bitcast_fusion), channel_id=1, source_target_pairs={{0,1},{1,0},{8,25},{9,24},{16,17},{17,16},{24,9},{25,8},{2,3},{3,2... | collective-permute-start | bytes 2359304 | tf_op jit(solution)/shard_map/ppermute | solution.py:197
  23.9 0.6 pre_sets.1
  24.5 0.7 copy-done.6
  25.2 2.5 %collective-permute-start.1 = (bf16[384,384]{1,0:T(8,128)(2,1)S(1)}, bf16[384,384]{1,0:T(8,128)(2,1)S(1)}, u32[]{:S(2)}, u32[]{:S(2)}) collective-permute-start(bf16[384,384]{1,0:T(8,128)(2,1)S(1)} %get-tuple-element.20), channel_id=1, source_target_pairs={{0,1},{1,0},{2,3},{3,2},{4,5},{5,4},{6,7},{7,6},{8,9},{9,8},{10,11... | collective-permute-start | bytes 884744 | tf_op jit(solution)/shard_map/ppermute | solution.py:194
  27.7 5.8 %collective-permute-done.2.down_mine = bf16[1024,384]{1,0:T(8,128)(2,1)} collective-permute-done((bf16[1024,384]{1,0:T(8,128)(2,1)}, bf16[1024,384]{1,0:T(8,128)(2,1)}, u32[]{:S(2)}, u32[]{:S(2)}) %collective-permute-start.2) | collective-permute-done | bytes 786464 | tf_op jit(solution)/shard_map/ppermute | solution.py:196
  33.5 1.9 %collective-permute-start.3 = (bf16[1024,384]{1,0:T(8,128)(2,1)}, bf16[1024,384]{1,0:T(8,128)(2,1)}, u32[]{:S(2)}, u32[]{:S(2)}) collective-permute-start(bf16[1024,384]{1,0:T(8,128)(2,1)} %collective-permute-done.2.down_mine), channel_id=1, source_target_pairs={{0,8},{8,0},{1,9},{9,1},{2,10},{10,2},{3,11},{11,3},{4,12},{12,4},... | collective-permute-start | bytes 2359304 | tf_op jit(solution)/shard_map/ppermute | solution.py:200
  35.5 2.2 %collective-permute-done.4.up_mine = bf16[192,2048]{1,0:T(8,128)(2,1)} collective-permute-done((bf16[192,2048]{1,0:T(8,128)(2,1)S(1)}, bf16[192,2048]{1,0:T(8,128)(2,1)}, u32[]{:S(2)}, u32[]{:S(2)}) %collective-permute-start.4) | collective-permute-done | bytes 786464 | tf_op jit(solution)/shard_map/ppermute | solution.py:197
  37.7 2.7 %collective-permute-start.5 = (bf16[192,2048]{1,0:T(8,128)(2,1)}, bf16[192,2048]{1,0:T(8,128)(2,1)}, u32[]{:S(2)}, u32[]{:S(2)}) collective-permute-start(bf16[192,2048]{1,0:T(8,128)(2,1)} %collective-permute-done.4.up_mine), channel_id=1, source_target_pairs={{0,8},{8,0},{1,9},{9,1},{2,10},{10,2},{3,11},{11,3},{4,12},{12,4},... | collective-permute-start | bytes 2359304 | tf_op jit(solution)/shard_map/ppermute | solution.py:201
  40.4 0.3 collective-permute-done.1.pre_far
  40.7 1.0 copy-done.7
  41.7 3.6 %down_terms.1 = (bf16[4,16,32,384]{3,2,1,0:T(8,128)(2,1)S(1)}, bf16[4,16,32,384]{3,2,1,0:T(8,128)(2,1)}) custom-call(s32[5]{0:T(128)S(1)} %stack.19.place, bf16[8,384,256]{2,1,0:T(8,128)(2,1)S(1)} %bitcast.22, bf16[384,384]{1,0:T(8,128)(2,1)S(1)} %copy-done.7, bf16[384,384]{1,0:T(8,128)(2,1)S(1)} %collective-permute-done.1.pre_far), custom_call_target="tpu_custom_call" | custom-call | flops 1207959552 | bytes 6291456 | tf_op jit(solution)/shard_map/down_terms/pallas_call | solution.py:216
  45.3 1.2 copy-done.2
  46.4 1.9 %collective-permute-start.11 = (bf16[4,16,32,384]{3,2,1,0:T(8,128)(2,1)}, bf16[4,16,32,384]{3,2,1,0:T(8,128)(2,1)}, u32[]{:S(2)}, u32[]{:S(2)}) collective-permute-start(bf16[4,16,32,384]{3,2,1,0:T(8,128)(2,1)} %get-tuple-element.27), channel_id=1, source_target_pairs={{0,8},{8,0},{1,9},{9,1},{2,10},{10,2},{3,11},{11,3},{4,12},{12,4},... | collective-permute-start | bytes 4718600 | tf_op jit(solution)/shard_map/ppermute | solution.py:246
  48.4 1.0 own_grad.1.own
  49.4 0.0 collective-permute-done.5.up_other
  49.4 5.6 %terms.1 = bf16[384,2048]{1,0:T(8,128)(2,1)} custom-call(s32[5]{0:T(128)S(1)} %stack.19.place, bf16[8,384,256]{2,1,0:T(8,128)(2,1)S(1)} %bitcast.24, bf16[384,384]{1,0:T(8,128)(2,1)S(1)} %own_grad.1.own, bf16[384,384]{1,0:T(8,128)(2,1)S(1)} %collective-permute-done.1.pre_far, bf16[1024,384]{1,0:T(8,128)(2,1)} %collective-permute-done.2.down_mine, ...), custom_call_target="tpu_custom_call" | custom-call | flops 1811939328 | bytes 9437184 | tf_op jit(solution)/shard_map/terms/pallas_call | solution.py:229
  55.0 4.7 %all-to-all-start.1 = ((bf16[4,96,2048]{2,1,0:T(8,128)(2,1)}), bf16[4,96,2048]{2,1,0:T(8,128)(2,1)}, u32[]{:S(2)}, u32[]{:S(2)}) async-start(bf16[4,96,2048]{2,1,0:T(8,128)(2,1)} %bitcast.9), calls=%async_computation.1 | async-start | bytes 3145728 | tf_op jit(solution)/shard_map/all_to_all | solution.py:243
  59.7 2.7 %fusion.4 = (bf16[16,32,384]{2,1,0:T(8,128)(2,1)}, bf16[16,32,384]{2,1,0:T(8,128)(2,1)}, bf16[16,32,384]{2,1,0:T(8,128)(2,1)}, bf16[16,32,384]{2,1,0:T(8,128)(2,1)S(1)}) fusion(bf16[4,16,32,384]{3,2,1,0:T(8,128)(2,1)} %collective-permute-done.11, bf16[4,16,32,384]{3,2,1,0:T(8,128)(2,1)S(1)} %copy-done.3), kind=kLoop, calls=%fused_computation.14 | loop fusion | flops 3145728 | bytes 4718592 | tf_op jit(solution)/shard_map/convert_element_type | solution.py:251
  62.4 2.2 %collective-permute-start.12 = (bf16[16,32,384]{2,1,0:T(8,128)(2,1)}, bf16[16,32,384]{2,1,0:T(8,128)(2,1)S(1)}, u32[]{:S(2)}, u32[]{:S(2)}) collective-permute-start(bf16[16,32,384]{2,1,0:T(8,128)(2,1)} %get-tuple-element.34), channel_id=1, source_target_pairs={{0,1},{1,0},{2,3},{3,2},{4,5},{5,4},{6,7},{7,6},{8,9},{9,8},{10,11... | collective-permute-start | bytes 1179656 | tf_op jit(solution)/shard_map/ppermute | solution.py:249
  64.6 3.3 %collective-permute-start.13 = (bf16[16,32,384]{2,1,0:T(8,128)(2,1)}, bf16[16,32,384]{2,1,0:T(8,128)(2,1)S(1)}, u32[]{:S(2)}, u32[]{:S(2)}) collective-permute-start(bf16[16,32,384]{2,1,0:T(8,128)(2,1)} %get-tuple-element.33), channel_id=1, source_target_pairs={{0,17},{17,0},{1,16},{16,1},{2,19},{19,2},{3,18},{18,3},{4,21},{21... | collective-permute-start | bytes 1179656 | tf_op jit(solution)/shard_map/ppermute | solution.py:250
  68.0 4.3 %collective-permute-start.14 = (bf16[16,32,384]{2,1,0:T(8,128)(2,1)}, bf16[16,32,384]{2,1,0:T(8,128)(2,1)S(1)}, u32[]{:S(2)}, u32[]{:S(2)}) collective-permute-start(bf16[16,32,384]{2,1,0:T(8,128)(2,1)} %get-tuple-element.32), channel_id=1, source_target_pairs={{0,16},{16,0},{1,17},{17,1},{2,18},{18,2},{3,19},{19,3},{4,20},{20... | collective-permute-start | bytes 1179656 | tf_op jit(solution)/shard_map/ppermute | solution.py:251
  72.2 9.1 %all-to-all-done.1 = bf16[4,96,2048]{2,1,0:T(8,128)(2,1)} async-done(((bf16[4,96,2048]{2,1,0:T(8,128)(2,1)}), bf16[4,96,2048]{2,1,0:T(8,128)(2,1)}, u32[]{:S(2)}, u32[]{:S(2)}) %all-to-all-start.1) | async-done | bytes 1572896 | tf_op jit(solution)/shard_map/all_to_all | solution.py:243
  81.3 1.6 %fusion.own = bf16[96,2048]{1,0:T(8,128)(2,1)S(1)} fusion(bf16[4,96,2048]{2,1,0:T(8,128)(2,1)} %all-to-all-done.1), kind=kLoop, calls=%fused_computation.10 | loop fusion | flops 1572864 | bytes 1966080 | tf_op jit(solution)/shard_map/add | solution.py:244
  82.9 2.2 %collective-permute-start.6 = (bf16[96,2048]{1,0:T(8,128)(2,1)S(1)}, bf16[96,2048]{1,0:T(8,128)(2,1)S(1)}, u32[]{:S(2)}, u32[]{:S(2)}) collective-permute-start(bf16[96,2048]{1,0:T(8,128)(2,1)S(1)} %fusion.own), channel_id=1, source_target_pairs={{0,1},{1,0},{2,3},{3,2},{4,5},{5,4},{6,7},{7,6},{8,9},{9,8},{10,11... | collective-permute-start | bytes 1179656 | tf_op jit(solution)/shard_map/ppermute | solution.py:254
  85.1 2.5 %collective-permute-start.7 = (bf16[96,2048]{1,0:T(8,128)(2,1)S(1)}, bf16[96,2048]{1,0:T(8,128)(2,1)S(1)}, u32[]{:S(2)}, u32[]{:S(2)}) collective-permute-start(bf16[96,2048]{1,0:T(8,128)(2,1)S(1)} %fusion.own), channel_id=1, source_target_pairs={{0,2},{2,4},{4,6},{6,0},{1,3},{3,5},{5,7},{7,1},{8,10},{10,12},{12... | collective-permute-start | bytes 1179656 | tf_op jit(solution)/shard_map/ppermute | solution.py:255
  87.6 4.6 %collective-permute-start.8 = (bf16[96,2048]{1,0:T(8,128)(2,1)S(1)}, bf16[96,2048]{1,0:T(8,128)(2,1)S(1)}, u32[]{:S(2)}, u32[]{:S(2)}) collective-permute-start(bf16[96,2048]{1,0:T(8,128)(2,1)S(1)} %fusion.own), channel_id=1, source_target_pairs={{0,6},{2,0},{4,2},{6,4},{1,7},{3,1},{5,3},{7,5},{8,14},{10,8},{12,... | collective-permute-start | bytes 1179656 | tf_op jit(solution)/shard_map/ppermute | solution.py:256
  92.2 1.0 ring_sum.1
  93.2 14.7 %all-to-all-start.2 = ((bf16[16,32,384]{2,1,0:T(8,128)(2,1)}), bf16[16,32,384]{2,1,0:T(8,128)(2,1)S(1)}, u32[]{:S(2)}, u32[]{:S(2)}) async-start(bf16[16,32,384]{2,1,0:T(8,128)(2,1)} %ring_sum.1), calls=%async_computation.2 | async-start | bytes 786432 | tf_op jit(solution)/shard_map/all_to_all | solution.py:268
  107.9 0.1 pad_maximum_fusion.1
  108.0 1.9 %collective-permute-start.10 = (bf16[192,2048]{1,0:T(8,128)(2,1)S(1)}, bf16[192,2048]{1,0:T(8,128)(2,1)S(1)}, u32[]{:S(2)}, u32[]{:S(2)}) collective-permute-start(bf16[192,2048]{1,0:T(8,128)(2,1)S(1)} %pad_maximum_fusion.1), channel_id=1, source_target_pairs={{0,4},{2,6},{4,0},{6,2},{1,5},{3,7},{5,1},{7,3},{8,12},{10,14},{12... | collective-permute-start | bytes 2359304 | tf_op jit(solution)/shard_map/ppermute | solution.py:272
  109.9 0.1 pad_maximum_fusion
  110.0 3.8 %collective-permute-start.9 = (bf16[192,2048]{1,0:T(8,128)(2,1)S(1)}, bf16[192,2048]{1,0:T(8,128)(2,1)S(1)}, u32[]{:S(2)}, u32[]{:S(2)}) collective-permute-start(bf16[192,2048]{1,0:T(8,128)(2,1)S(1)} %pad_maximum_fusion), channel_id=1, source_target_pairs={{0,1},{1,0},{2,3},{3,2},{4,5},{5,4},{6,7},{7,6},{8,9},{9,8},{10,11... | collective-permute-start | bytes 2359304 | tf_op jit(solution)/shard_map/ppermute | solution.py:273
  113.7 1.7 %place_first.1.partial = bf16[768,2048]{1,0:T(8,128)(2,1)} custom-call(s32[5]{0:T(128)S(1)} %stack.19.place, bf16[96,2048]{1,0:T(8,128)(2,1)S(1)} %fusion.own, bf16[96,2048]{1,0:T(8,128)(2,1)S(1)} %collective-permute-done.6.near, bf16[96,2048]{1,0:T(8,128)(2,1)S(1)} %collective-permute-done.7.below, bf16[96,2048]{1,0:T(8,128)(2,1)S(1)} %collective-permute-done.8.above), custom_call_target="tpu_custom_call" | custom-call | tf_op jit(solution)/shard_map/place_first/pallas_call | solution.py:275
  115.5 13.8 %collective-permute-done.10.across = bf16[192,2048]{1,0:T(8,128)(2,1)S(1)} collective-permute-done((bf16[192,2048]{1,0:T(8,128)(2,1)S(1)}, bf16[192,2048]{1,0:T(8,128)(2,1)S(1)}, u32[]{:S(2)}, u32[]{:S(2)}) %collective-permute-start.10) | collective-permute-done | bytes 786464 | tf_op jit(solution)/shard_map/ppermute | solution.py:272
  129.3 0.5 collective-permute-done.9.beside
  129.8 1.7 %place_last.1 = bf16[768,2048]{1,0:T(8,128)(2,1)} custom-call(s32[5]{0:T(128)S(1)} %stack.19.place, bf16[768,2048]{1,0:T(8,128)(2,1)} %place_first.1.partial, bf16[192,2048]{1,0:T(8,128)(2,1)S(1)} %collective-permute-done.9.beside, bf16[192,2048]{1,0:T(8,128)(2,1)S(1)} %collective-permute-done.10.across), custom_call_target="tpu_custom_call", output_to_operand_aliasing={{}: (1, {})} | custom-call | tf_op jit(solution)/shard_map/place_last/pallas_call | solution.py:284
  131.6 0.1 convert_reduce_fusion
  131.7 0.6 broadcast_multiply_fusion
  (22 shorter events, 0.0 us)
Async XLA Ops:
  1.4 1.0 copy-start.5
  3.0 11.8 %collective-permute-start = (bf16[384,256]{1,0:T(8,128)(2,1)S(1)}, bf16[384,256]{1,0:T(8,128)(2,1)S(1)}, u32[]{:S(2)}, u32[]{:S(2)}) collective-permute-start(bf16[384,256]{1,0:T(8,128)(2,1)S(1)} %get-tuple-element.18), channel_id=1, source_target_pairs={{0,1},{1,0},{2,3},{3,2},{4,5},{5,4},{6,7},{7,6},{8,9},{9,8},{10,11... | collective-permute-start | bytes 589832 | tf_op jit(solution)/shard_map/ppermute | solution.py:184
  7.8 25.7 %collective-permute-start.2 = (bf16[1024,384]{1,0:T(8,128)(2,1)}, bf16[1024,384]{1,0:T(8,128)(2,1)}, u32[]{:S(2)}, u32[]{:S(2)}) collective-permute-start(bf16[1024,384]{1,0:T(8,128)(2,1)} %dynamic-slice_bitcast_fusion.1), channel_id=1, source_target_pairs={{0,17},{17,0},{1,16},{16,1},{2,19},{19,2},{3,18},{18,3},{4,21},{21... | collective-permute-start | bytes 2359304 | tf_op jit(solution)/shard_map/ppermute | solution.py:196
  16.6 3.7 %copy-start.1 = (bf16[384,2048]{1,0:T(8,128)(2,1)S(1)}, bf16[384,2048]{1,0:T(8,128)(2,1)}, u32[]{:S(2)}) copy-start(bf16[384,2048]{1,0:T(8,128)(2,1)} %up_own.1) | copy-start | bytes 4718596
  16.6 24.1 %all-to-all-start = ((bf16[4,2,384,256]{3,2,1,0:T(8,128)(2,1)}), bf16[4,2,384,256]{3,2,1,0:T(8,128)(2,1)S(1)}, u32[]{:S(2)}, u32[]{:S(2)}) async-start(bf16[4,2,384,256]{3,2,1,0:T(8,128)(2,1)} %spread.1), calls=%async_computation | async-start | bytes 3145728 | tf_op jit(solution)/shard_map/all_to_all | solution.py:193
  20.3 3.5 %copy-start.4 = (bf16[768,384]{1,0:T(8,128)(2,1)S(1)}, bf16[768,384]{1,0:T(8,128)(2,1)}, u32[]{:S(2)}) copy-start(bf16[768,384]{1,0:T(8,128)(2,1)} %whole.3) | copy-start | bytes 1769476
  20.4 17.3 %collective-permute-start.4 = (bf16[192,2048]{1,0:T(8,128)(2,1)S(1)}, bf16[192,2048]{1,0:T(8,128)(2,1)}, u32[]{:S(2)}, u32[]{:S(2)}) collective-permute-start(bf16[192,2048]{1,0:T(8,128)(2,1)S(1)} %dynamic-slice_bitcast_fusion), channel_id=1, source_target_pairs={{0,1},{1,0},{8,25},{9,24},{16,17},{17,16},{24,9},{25,8},{2,3},{3,2... | collective-permute-start | bytes 2359304 | tf_op jit(solution)/shard_map/ppermute | solution.py:197
  24.5 0.7 copy-start.6
  25.2 15.5 %collective-permute-start.1 = (bf16[384,384]{1,0:T(8,128)(2,1)S(1)}, bf16[384,384]{1,0:T(8,128)(2,1)S(1)}, u32[]{:S(2)}, u32[]{:S(2)}) collective-permute-start(bf16[384,384]{1,0:T(8,128)(2,1)S(1)} %get-tuple-element.20), channel_id=1, source_target_pairs={{0,1},{1,0},{2,3},{3,2},{4,5},{5,4},{6,7},{7,6},{8,9},{9,8},{10,11... | collective-permute-start | bytes 884744 | tf_op jit(solution)/shard_map/ppermute | solution.py:194
  33.5 15.8 %collective-permute-start.3 = (bf16[1024,384]{1,0:T(8,128)(2,1)}, bf16[1024,384]{1,0:T(8,128)(2,1)}, u32[]{:S(2)}, u32[]{:S(2)}) collective-permute-start(bf16[1024,384]{1,0:T(8,128)(2,1)} %collective-permute-done.2.down_mine), channel_id=1, source_target_pairs={{0,8},{8,0},{1,9},{9,1},{2,10},{10,2},{3,11},{11,3},{4,12},{12,4},... | collective-permute-start | bytes 2359304 | tf_op jit(solution)/shard_map/ppermute | solution.py:200
  37.7 11.7 %collective-permute-start.5 = (bf16[192,2048]{1,0:T(8,128)(2,1)}, bf16[192,2048]{1,0:T(8,128)(2,1)}, u32[]{:S(2)}, u32[]{:S(2)}) collective-permute-start(bf16[192,2048]{1,0:T(8,128)(2,1)} %collective-permute-done.4.up_mine), channel_id=1, source_target_pairs={{0,8},{8,0},{1,9},{9,1},{2,10},{10,2},{3,11},{11,3},{4,12},{12,4},... | collective-permute-start | bytes 2359304 | tf_op jit(solution)/shard_map/ppermute | solution.py:201
  40.7 1.0 copy-start.7
  41.7 6.7 %copy-start = (bf16[2048,384]{1,0:T(8,128)(2,1)S(1)}, bf16[2048,384]{1,0:T(8,128)(2,1)}, u32[]{:S(2)}) copy-start(bf16[2048,384]{1,0:T(8,128)(2,1)} %down.1) | copy-start | bytes 4718596
  45.3 1.2 copy-start.2
  46.4 13.3 %collective-permute-start.11 = (bf16[4,16,32,384]{3,2,1,0:T(8,128)(2,1)}, bf16[4,16,32,384]{3,2,1,0:T(8,128)(2,1)}, u32[]{:S(2)}, u32[]{:S(2)}) collective-permute-start(bf16[4,16,32,384]{3,2,1,0:T(8,128)(2,1)} %get-tuple-element.27), channel_id=1, source_target_pairs={{0,8},{8,0},{1,9},{9,1},{2,10},{10,2},{3,11},{11,3},{4,12},{12,4},... | collective-permute-start | bytes 4718600 | tf_op jit(solution)/shard_map/ppermute | solution.py:246
  55.0 4.7 %copy-start.3 = (bf16[4,16,32,384]{3,2,1,0:T(8,128)(2,1)S(1)}, bf16[4,16,32,384]{3,2,1,0:T(8,128)(2,1)}, u32[]{:S(2)}) copy-start(bf16[4,16,32,384]{3,2,1,0:T(8,128)(2,1)} %copy-done.2) | copy-start | bytes 4718596
  55.0 26.3 %all-to-all-start.1 = ((bf16[4,96,2048]{2,1,0:T(8,128)(2,1)}), bf16[4,96,2048]{2,1,0:T(8,128)(2,1)}, u32[]{:S(2)}, u32[]{:S(2)}) async-start(bf16[4,96,2048]{2,1,0:T(8,128)(2,1)} %bitcast.9), calls=%async_computation.1 | async-start | bytes 3145728 | tf_op jit(solution)/shard_map/all_to_all | solution.py:243
  62.4 25.2 %collective-permute-start.12 = (bf16[16,32,384]{2,1,0:T(8,128)(2,1)}, bf16[16,32,384]{2,1,0:T(8,128)(2,1)S(1)}, u32[]{:S(2)}, u32[]{:S(2)}) collective-permute-start(bf16[16,32,384]{2,1,0:T(8,128)(2,1)} %get-tuple-element.34), channel_id=1, source_target_pairs={{0,1},{1,0},{2,3},{3,2},{4,5},{5,4},{6,7},{7,6},{8,9},{9,8},{10,11... | collective-permute-start | bytes 1179656 | tf_op jit(solution)/shard_map/ppermute | solution.py:249
  64.6 27.6 %collective-permute-start.13 = (bf16[16,32,384]{2,1,0:T(8,128)(2,1)}, bf16[16,32,384]{2,1,0:T(8,128)(2,1)S(1)}, u32[]{:S(2)}, u32[]{:S(2)}) collective-permute-start(bf16[16,32,384]{2,1,0:T(8,128)(2,1)} %get-tuple-element.33), channel_id=1, source_target_pairs={{0,17},{17,0},{1,16},{16,1},{2,19},{19,2},{3,18},{18,3},{4,21},{21... | collective-permute-start | bytes 1179656 | tf_op jit(solution)/shard_map/ppermute | solution.py:250
  68.0 24.2 %collective-permute-start.14 = (bf16[16,32,384]{2,1,0:T(8,128)(2,1)}, bf16[16,32,384]{2,1,0:T(8,128)(2,1)S(1)}, u32[]{:S(2)}, u32[]{:S(2)}) collective-permute-start(bf16[16,32,384]{2,1,0:T(8,128)(2,1)} %get-tuple-element.32), channel_id=1, source_target_pairs={{0,16},{16,0},{1,17},{17,1},{2,18},{18,2},{3,19},{19,3},{4,20},{20... | collective-permute-start | bytes 1179656 | tf_op jit(solution)/shard_map/ppermute | solution.py:251
  82.9 25.0 %collective-permute-start.6 = (bf16[96,2048]{1,0:T(8,128)(2,1)S(1)}, bf16[96,2048]{1,0:T(8,128)(2,1)S(1)}, u32[]{:S(2)}, u32[]{:S(2)}) collective-permute-start(bf16[96,2048]{1,0:T(8,128)(2,1)S(1)} %fusion.own), channel_id=1, source_target_pairs={{0,1},{1,0},{2,3},{3,2},{4,5},{5,4},{6,7},{7,6},{8,9},{9,8},{10,11... | collective-permute-start | bytes 1179656 | tf_op jit(solution)/shard_map/ppermute | solution.py:254
  85.1 22.8 %collective-permute-start.7 = (bf16[96,2048]{1,0:T(8,128)(2,1)S(1)}, bf16[96,2048]{1,0:T(8,128)(2,1)S(1)}, u32[]{:S(2)}, u32[]{:S(2)}) collective-permute-start(bf16[96,2048]{1,0:T(8,128)(2,1)S(1)} %fusion.own), channel_id=1, source_target_pairs={{0,2},{2,4},{4,6},{6,0},{1,3},{3,5},{5,7},{7,1},{8,10},{10,12},{12... | collective-permute-start | bytes 1179656 | tf_op jit(solution)/shard_map/ppermute | solution.py:255
  87.6 20.3 %collective-permute-start.8 = (bf16[96,2048]{1,0:T(8,128)(2,1)S(1)}, bf16[96,2048]{1,0:T(8,128)(2,1)S(1)}, u32[]{:S(2)}, u32[]{:S(2)}) collective-permute-start(bf16[96,2048]{1,0:T(8,128)(2,1)S(1)} %fusion.own), channel_id=1, source_target_pairs={{0,6},{2,0},{4,2},{6,4},{1,7},{3,1},{5,3},{7,5},{8,14},{10,8},{12,... | collective-permute-start | bytes 1179656 | tf_op jit(solution)/shard_map/ppermute | solution.py:256
  93.2 38.4 %all-to-all-start.2 = ((bf16[16,32,384]{2,1,0:T(8,128)(2,1)}), bf16[16,32,384]{2,1,0:T(8,128)(2,1)S(1)}, u32[]{:S(2)}, u32[]{:S(2)}) async-start(bf16[16,32,384]{2,1,0:T(8,128)(2,1)} %ring_sum.1), calls=%async_computation.2 | async-start | bytes 786432 | tf_op jit(solution)/shard_map/all_to_all | solution.py:268
  108.0 21.4 %collective-permute-start.10 = (bf16[192,2048]{1,0:T(8,128)(2,1)S(1)}, bf16[192,2048]{1,0:T(8,128)(2,1)S(1)}, u32[]{:S(2)}, u32[]{:S(2)}) collective-permute-start(bf16[192,2048]{1,0:T(8,128)(2,1)S(1)} %pad_maximum_fusion.1), channel_id=1, source_target_pairs={{0,4},{2,6},{4,0},{6,2},{1,5},{3,7},{5,1},{7,3},{8,12},{10,14},{12... | collective-permute-start | bytes 2359304 | tf_op jit(solution)/shard_map/ppermute | solution.py:272
  110.0 19.9 %collective-permute-start.9 = (bf16[192,2048]{1,0:T(8,128)(2,1)S(1)}, bf16[192,2048]{1,0:T(8,128)(2,1)S(1)}, u32[]{:S(2)}, u32[]{:S(2)}) collective-permute-start(bf16[192,2048]{1,0:T(8,128)(2,1)S(1)} %pad_maximum_fusion), channel_id=1, source_target_pairs={{0,1},{1,0},{2,3},{3,2},{4,5},{5,4},{6,7},{7,6},{8,9},{9,8},{10,11... | collective-permute-start | bytes 2359304 | tf_op jit(solution)/shard_map/ppermute | solution.py:273
